TPU v7x, 32 devices: a whole 2x2x4 slice. The times are simulated.
32 devices in a mesh: expert: 8 (over z, x), dp: 4 (over y, core).
Axes of the slice: x: 2, y: 2, z: 4, core: 2. Of those that a mesh axis runs over, the one named last changes fastest.
Arguments:
- tokens: bfloat16 [256, 64, 384], P(('expert', 'dp')), may hold values from -6 to 6
- router: bfloat16 [384, 8], replicated, may hold values from -8.675276 to 8.675276
- w_in: bfloat16 [8, 384, 1536], P('expert'), may hold values from -0.3125 to 0.3125
- w_out: bfloat16 [8, 384, 1536], P('expert'), may hold values from -0.15625 to 0.15625
- out_grad: bfloat16 [256, 64, 384], P(('expert', 'dp')), may hold values from -6 to 6
Outputs:
- tokens_grad: bfloat16 [256, 64, 384], P(('expert', 'dp'))
- w_in_grad: float32 [8, 384, 1536], P('expert', 'dp')
- w_out_grad: float32 [8, 384, 1536], P('expert', 'dp')
- router_grad: float32 [384, 8], P('dp')
All inputs are finite; a program needn't handle non-finite values.
Results may differ from a plain program's by a relative error of at most 0.029.
Values may be sent and summed in bfloat16 or wider, within the bound.
No kernel may reach another device: no remote copies, remote signals or barrier semaphores. Data moves between devices by JAX's collectives and lax.ppermute only.
A program may use at most 64 MiB of HBM per device.

v0:
```python
import math

import jax
import jax.numpy as jnp
from jax import lax
from jax.sharding import PartitionSpec as P

D = 384


def gelu_pair(value):
    coef = math.sqrt(2.0 / math.pi)
    inner = coef * (value + 0.044715 * value * value * value)
    tangent = jnp.tanh(inner)
    result = 0.5 * value * (1.0 + tangent)
    slope = 0.5 * (1.0 + tangent) + 0.5 * value * (1.0 - tangent * tangent) * coef * (
        1.0 + 3.0 * 0.044715 * value * value
    )
    return (result, slope)


def on_device(tokens, router, w_in, w_out, out_grad):
    f32 = jnp.float32
    bf16 = jnp.bfloat16
    owners = lax.axis_size("expert")
    images = tokens.shape[0]
    experts_all = router.shape[1]
    per_owner = w_in.shape[0]
    row_count = D // lax.axis_size("dp")
    logits = jnp.einsum("bmd,de->bme", tokens, router, preferred_element_type=f32)
    dispatch = jax.nn.softmax(logits, axis=1)
    combine = jax.nn.softmax(logits, axis=2)
    dispatch_b = dispatch.astype(bf16)
    combine_b = combine.astype(bf16)
    slot_in = jnp.einsum("bme,bmd->bed", dispatch_b, tokens, preferred_element_type=f32).astype(
        bf16
    )
    slot_grad = jnp.einsum("bme,bmd->bed", combine_b, out_grad, preferred_element_type=f32).astype(
        bf16
    )
    slot_in = slot_in.reshape(images, owners, per_owner, D)
    slot_grad = slot_grad.reshape(images, owners, per_owner, D)
    recv_in, recv_grad = (
        lax.all_to_all(slot_in, "expert", split_axis=1, concat_axis=1, tiled=True),
        lax.all_to_all(slot_grad, "expert", split_axis=1, concat_axis=1, tiled=True),
    )
    pre_act = jnp.einsum("bskd,kdf->bskf", recv_in, w_in, preferred_element_type=f32)
    value, slope = gelu_pair(pre_act)
    hidden = value.astype(bf16)
    slot_out = jnp.einsum("bskf,kdf->bskd", hidden, w_out, preferred_element_type=f32).astype(bf16)
    hid_grad = jnp.einsum("bskd,kdf->bskf", recv_grad, w_out, preferred_element_type=f32)
    pre_grad = (hid_grad * slope).astype(bf16)
    back_grad = jnp.einsum("bskf,kdf->bskd", pre_grad, w_in, preferred_element_type=f32).astype(
        bf16
    )
    win_term = jnp.einsum("bskd,bskf->dkf", recv_in, pre_grad, preferred_element_type=f32)
    wout_term = jnp.einsum("bskd,bskf->dkf", recv_grad, hidden, preferred_element_type=f32)
    win_part, wout_part = (
        lax.psum_scatter(
            win_term.astype(jnp.bfloat16), "dp", scatter_dimension=0, tiled=True
        ).astype(jnp.float32),
        lax.psum_scatter(
            wout_term.astype(jnp.bfloat16), "dp", scatter_dimension=0, tiled=True
        ).astype(jnp.float32),
    )
    slot_back, slot_in_grad = (
        lax.all_to_all(slot_out, "expert", split_axis=1, concat_axis=1, tiled=True),
        lax.all_to_all(back_grad, "expert", split_axis=1, concat_axis=1, tiled=True),
    )
    slot_back = slot_back.reshape(images, experts_all, D)
    slot_in_grad = slot_in_grad.reshape(images, experts_all, D)
    comb_grad = jnp.einsum("bmd,bed->bme", out_grad, slot_back, preferred_element_type=f32)
    disp_grad = jnp.einsum("bmd,bed->bme", tokens, slot_in_grad, preferred_element_type=f32)
    logit_grad = combine * (comb_grad - jnp.sum(combine * comb_grad, axis=2, keepdims=True))
    logit_grad = logit_grad + dispatch * (
        disp_grad - jnp.sum(dispatch * disp_grad, axis=1, keepdims=True)
    )
    logit_grad = logit_grad.astype(bf16)
    tokens_grad = jnp.einsum("bme,bed->bmd", dispatch_b, slot_in_grad, preferred_element_type=f32)
    tokens_grad = tokens_grad + jnp.einsum(
        "bme,de->bmd", logit_grad, router, preferred_element_type=f32
    )
    tokens_grad = tokens_grad.astype(bf16)
    router_local = jnp.einsum("bmd,bme->de", tokens, logit_grad, preferred_element_type=f32)
    router_full = lax.psum(router_local, ("expert", "dp"))
    router_grad = lax.dynamic_slice_in_dim(
        router_full, lax.axis_index("dp") * row_count, row_count, 0
    )
    w_in_grad = jnp.transpose(win_part, (1, 0, 2))
    w_out_grad = jnp.transpose(wout_part, (1, 0, 2))
    return (tokens_grad, w_in_grad, w_out_grad, router_grad)


def solution(mesh):
    placed = (
        P(("expert", "dp"), None, None),
        P(),
        P("expert", None, None),
        P("expert", None, None),
        P(("expert", "dp"), None, None),
    )
    return jax.shard_map(
        on_device,
        mesh=mesh,
        in_specs=placed,
        out_specs=(
            P(("expert", "dp"), None, None),
            P("expert", "dp", None),
            P("expert", "dp", None),
            P("dp", None),
        ),
        check_vma=False,
    )
```

profile of v0, /device:TPU:0, one launch (start us, length us, event | category | flops | bytes accessed | tf_op | source)
XLA Modules:
  0.0 116.0 jit_solution(16563427244373289084)
XLA Ops:
  7.2 0.0 copy-start
  7.2 0.0 copy-start.2
  7.2 1.4 %fusion.73 = f32[8,64,8]{1,2,0:T(8,128)S(1)} fusion(bf16[8,64,384]{2,1,0:T(8,128)(2,1)} %param.5, bf16[384,8]{0,1:T(8,128)(2,1)} %param.6), kind=kOutput, calls=%fused_computation.82 | convolution fusion | flops 3145728 | bytes 415744 | tf_op jit(solution)/shard_map/bmd,de->bme/dot_general | solution.py:30
  8.6 1.3 %fusion.77 = (f32[8,8]{1,0:T(8,128)S(1)}, f32[8,64,8]{1,2,0:T(8,128)S(1)}) fusion(f32[8,64,8]{1,2,0:T(8,128)S(1)} %fusion.73), kind=kOutput, calls=%fused_computation.87 | output fusion | flops 8255 | bytes 33024 | tf_op jit(solution)/shard_map/sub | solution.py:31
  9.9 1.3 %fusion.33 = bf16[8,8,1,384]{3,1,0,2:T(8,128)(2,1)S(1)} fusion(bf16[8,64,384]{2,1,0:T(8,128)(2,1)} %param.5, f32[8,8]{1,0:T(8,128)S(1)} %get-tuple-element.12, f32[8,64,8]{1,2,0:T(8,128)S(1)} %fusion.73), kind=kOutput, calls=%fused_computation.32 | convolution fusion | flops 3182719 | bytes 459008 | tf_op jit(solution)/shard_map/bme,bmd->bed/dot_general | solution.py:35
  11.2 0.6 copy.13
  11.8 7.3 %all-to-all-start.1 = ((bf16[8,8,1,384]{3,0,2,1:T(8,128)(2,1)}), bf16[8,8,1,384]{3,0,2,1:T(8,128)(2,1)S(1)}, u32[]{:S(2)}, u32[]{:S(2)}) async-start(bf16[8,8,1,384]{3,0,2,1:T(8,128)(2,1)} %copy.13), calls=%async_computation.1 | async-start | bytes 98304 | tf_op jit(solution)/shard_map/all_to_all | solution.py:44
  19.1 0.2 fusion.78
  19.3 0.2 fusion.32
  19.5 0.6 copy.11
  20.2 5.7 %all-to-all-done.1 = bf16[8,8,1,384]{3,0,2,1:T(8,128)(2,1)S(1)} async-done(((bf16[8,8,1,384]{3,0,2,1:T(8,128)(2,1)}), bf16[8,8,1,384]{3,0,2,1:T(8,128)(2,1)S(1)}, u32[]{:S(2)}, u32[]{:S(2)}) %all-to-all-start.1) | async-done | bytes 49184 | tf_op jit(solution)/shard_map/all_to_all | solution.py:44
  25.9 3.3 %all-to-all-start = ((bf16[8,8,1,384]{3,0,2,1:T(8,128)(2,1)}), bf16[8,8,1,384]{3,0,2,1:T(8,128)(2,1)S(1)}, u32[]{:S(2)}, u32[]{:S(2)}) async-start(bf16[8,8,1,384]{3,0,2,1:T(8,128)(2,1)} %copy.11), calls=%async_computation | async-start | bytes 98304 | tf_op jit(solution)/shard_map/all_to_all | solution.py:45
  29.2 0.0 reduce-scatter.9.cloned.1.call-start
  29.3 0.3 convolution_bitcast_fusion.2
  29.6 0.0 copy-start.3
  29.6 6.3 %all-to-all-done = bf16[8,8,1,384]{3,0,2,1:T(8,128)(2,1)S(1)} async-done(((bf16[8,8,1,384]{3,0,2,1:T(8,128)(2,1)}), bf16[8,8,1,384]{3,0,2,1:T(8,128)(2,1)S(1)}, u32[]{:S(2)}, u32[]{:S(2)}) %all-to-all-start) | async-done | bytes 49184 | tf_op jit(solution)/shard_map/all_to_all | solution.py:45
  36.0 0.5 fusion.6
  36.5 1.5 %copy.27 = bf16[384,1536]{1,0:T(8,128)(2,1)} copy(bf16[384,1536]{0,1:T(8,128)(2,1)S(1)} %fusion.6) | data formatting | bytes 2359296
  38.0 0.0 reduce-scatter.9.cloned.1.call-update
  38.0 0.0 reduce-scatter.7.cloned.1.call-start
  38.1 1.7 %fusion.10 = bf16[8,8,1536]{2,1,0:T(8,128)(2,1)S(1)} fusion(bf16[1,384,1536]{2,1,0:T(8,128)(2,1)} %param.8, f32[8,8,1,1536]{3,1,0,2:T(8,128)S(1)} %convolution_bitcast_fusion.2, bf16[8,8,1,384]{3,0,2,1:T(8,128)(2,1)S(1)} %all-to-all-done), kind=kOutput, calls=%fused_computation.14 | convolution fusion | flops 77365248 | bytes 1818624 | tf_op jit(solution)/shard_map/bskd,kdf->bskf/dot_general | solution.py:51
  39.8 0.5 fusion.7
  40.4 1.5 %copy.25 = bf16[384,1536]{1,0:T(8,128)(2,1)} copy(bf16[384,1536]{0,1:T(8,128)(2,1)S(1)} %fusion.7) | data formatting | bytes 2359296
  41.9 0.0 reduce-scatter.7.cloned.1.call-update
  41.9 0.5 fusion.24
  42.4 0.0 copy-start.1
  42.5 0.6 copy.15
  43.1 3.3 %all-to-all-start.2 = ((bf16[8,8,1,384]{3,0,2,1:T(8,128)(2,1)}), bf16[8,8,1,384]{3,0,2,1:T(8,128)(2,1)S(1)}, u32[]{:S(2)}, u32[]{:S(2)}) async-start(bf16[8,8,1,384]{3,0,2,1:T(8,128)(2,1)} %copy.15), calls=%async_computation.2 | async-start | bytes 98304 | tf_op jit(solution)/shard_map/all_to_all | solution.py:68
  46.4 0.0 copy-done.4
  46.5 1.8 %fusion.27 = bf16[8,8,1,384]{3,1,0,2:T(8,128)(2,1)S(1)} fusion(bf16[1,384,1536]{2,1,0:T(8,128)(2,1)} %param.8, f32[8,8,1,1536]{3,1,0,2:T(8,128)S(1)} %copy-done.4), kind=kOutput, calls=%fused_computation.28 | convolution fusion | flops 76406784 | bytes 1622016 | tf_op jit(solution)/shard_map/bskf,kdf->bskd/dot_general | solution.py:50
  48.2 0.6 copy.17
  48.9 4.3 %all-to-all-done.2 = bf16[8,8,1,384]{3,0,2,1:T(8,128)(2,1)S(1)} async-done(((bf16[8,8,1,384]{3,0,2,1:T(8,128)(2,1)}), bf16[8,8,1,384]{3,0,2,1:T(8,128)(2,1)S(1)}, u32[]{:S(2)}, u32[]{:S(2)}) %all-to-all-start.2) | async-done | bytes 49184 | tf_op jit(solution)/shard_map/all_to_all | solution.py:68
  53.2 3.3 %all-to-all-start.3 = ((bf16[8,8,1,384]{3,0,2,1:T(8,128)(2,1)}), bf16[8,8,1,384]{3,0,2,1:T(8,128)(2,1)S(1)}, u32[]{:S(2)}, u32[]{:S(2)}) async-start(bf16[8,8,1,384]{3,0,2,1:T(8,128)(2,1)} %copy.17), calls=%async_computation.3 | async-start | bytes 98304 | tf_op jit(solution)/shard_map/all_to_all | solution.py:67
  56.5 0.2 convolution_bitcast_fusion.4
  56.8 1.2 %fusion.40 = f32[8,64,8]{1,2,0:T(8,128)S(1)} fusion(f32[8,64,8]{1,2,0:T(8,128)S(1)} %convolution_bitcast_fusion.4, f32[8,64,8]{1,2,0:T(8,128)S(1)} %get-tuple-element.13, f32[8,8]{1,0:T(8,128)S(1)} %get-tuple-element.12), kind=kOutput, calls=%fused_computation.39 | output fusion | flops 20607 | bytes 49408 | tf_op jit(solution)/shard_map/sub | solution.py:76
  58.0 5.3 %all-to-all-done.3 = bf16[8,8,1,384]{3,0,2,1:T(8,128)(2,1)S(1)} async-done(((bf16[8,8,1,384]{3,0,2,1:T(8,128)(2,1)}), bf16[8,8,1,384]{3,0,2,1:T(8,128)(2,1)S(1)}, u32[]{:S(2)}, u32[]{:S(2)}) %all-to-all-start.3) | async-done | bytes 49184 | tf_op jit(solution)/shard_map/all_to_all | solution.py:67
  63.3 0.2 convolution_bitcast_fusion.5
  63.5 0.2 convolution_bitcast_fusion.6
  63.7 38.5 %psum.7 = f32[384,8]{0,1:T(8,128)S(1)} all-reduce(f32[384,8]{0,1:T(8,128)S(1)} %convolution_bitcast_fusion.6), channel_id=1, replica_groups=mesh['expert'=8,'dp'=4] {'expert','dp'}, use_global_device_ids=true, to_apply=%region_8.0 | all-reduce | flops 3072 | bytes 24576 | tf_op jit(solution)/shard_map/psum | solution.py:85
  102.2 0.7 constant_dynamic-slice_fusion
  102.9 0.5 fusion.55
  103.4 1.1 fusion.11
  104.5 1.2 %copy.28 = bf16[96,1536]{0,1:T(8,128)(2,1)S(1)} copy(bf16[96,1536]{1,0:T(8,128)(2,1)} %reduce-scatter.9.cloned.1.call-done) | data formatting | bytes 589824
  105.6 0.1 bitcast_convert_fusion
  105.7 1.1 copy.20
  106.8 1.2 %copy.26 = bf16[96,1536]{0,1:T(8,128)(2,1)S(1)} copy(bf16[96,1536]{1,0:T(8,128)(2,1)} %reduce-scatter.7.cloned.1.call-done) | data formatting | bytes 589824
  108.0 0.1 bitcast_convert_fusion.1
  108.0 1.1 copy.19
  (9 shorter events, 0.0 us)
Async XLA Ops:
  7.2 22.1 %copy-start = (bf16[1,384,1536]{2,1,0:T(8,128)(2,1)S(1)}, bf16[1,384,1536]{2,1,0:T(8,128)(2,1)}, u32[]{:S(2)}) copy-start(bf16[1,384,1536]{2,1,0:T(8,128)(2,1)} %param.7) | copy-start | bytes 3538948
  7.2 12.1 %copy-start.2 = (bf16[8,64,384]{2,1,0:T(8,128)(2,1)S(1)}, bf16[8,64,384]{2,1,0:T(8,128)(2,1)}, u32[]{:S(2)}) copy-start(bf16[8,64,384]{2,1,0:T(8,128)(2,1)} %param.9) | copy-start | bytes 1179652
  11.8 14.0 %all-to-all-start.1 = ((bf16[8,8,1,384]{3,0,2,1:T(8,128)(2,1)}), bf16[8,8,1,384]{3,0,2,1:T(8,128)(2,1)S(1)}, u32[]{:S(2)}, u32[]{:S(2)}) async-start(bf16[8,8,1,384]{3,0,2,1:T(8,128)(2,1)} %copy.13), calls=%async_computation.1 | async-start | bytes 98304 | tf_op jit(solution)/shard_map/all_to_all | solution.py:44
  25.9 10.1 %all-to-all-start = ((bf16[8,8,1,384]{3,0,2,1:T(8,128)(2,1)}), bf16[8,8,1,384]{3,0,2,1:T(8,128)(2,1)S(1)}, u32[]{:S(2)}, u32[]{:S(2)}) async-start(bf16[8,8,1,384]{3,0,2,1:T(8,128)(2,1)} %copy.11), calls=%async_computation | async-start | bytes 98304 | tf_op jit(solution)/shard_map/all_to_all | solution.py:45
  29.2 75.2 %reduce-scatter.9.cloned.1.call-start = ((), (), s32[]{:S(2)}) async-start(), calls=%async_computation.7 | async-start | bytes 1474560
  29.6 8.5 %copy-start.3 = (f32[8,8,1,1536]{3,1,0,2:T(8,128)}, f32[8,8,1,1536]{3,1,0,2:T(8,128)S(1)}, u32[]{:S(2)}) copy-start(f32[8,8,1,1536]{3,1,0,2:T(8,128)S(1)} %convolution_bitcast_fusion.2) | copy-start | bytes 1179652
  38.0 68.8 %reduce-scatter.7.cloned.1.call-start = ((), (), s32[]{:S(2)}) async-start(), calls=%async_computation.6 | async-start | bytes 1474560
  41.9 4.5 %copy-start.4 = (f32[8,8,1,1536]{3,1,0,2:T(8,128)S(1)}, f32[8,8,1,1536]{3,1,0,2:T(8,128)}, u32[]{:S(2)}) copy-start(f32[8,8,1,1536]{3,1,0,2:T(8,128)} %copy-done.3) | copy-start | bytes 1179652
  42.4 14.1 %copy-start.1 = (bf16[8,64,384]{2,1,0:T(8,128)(2,1)S(1)}, bf16[8,64,384]{2,1,0:T(8,128)(2,1)}, u32[]{:S(2)}) copy-start(bf16[8,64,384]{2,1,0:T(8,128)(2,1)} %param.5) | copy-start | bytes 1179652
  43.1 10.1 %all-to-all-start.2 = ((bf16[8,8,1,384]{3,0,2,1:T(8,128)(2,1)}), bf16[8,8,1,384]{3,0,2,1:T(8,128)(2,1)S(1)}, u32[]{:S(2)}, u32[]{:S(2)}) async-start(bf16[8,8,1,384]{3,0,2,1:T(8,128)(2,1)} %copy.15), calls=%async_computation.2 | async-start | bytes 98304 | tf_op jit(solution)/shard_map/all_to_all | solution.py:68
  53.2 10.1 %all-to-all-start.3 = ((bf16[8,8,1,384]{3,0,2,1:T(8,128)(2,1)}), bf16[8,8,1,384]{3,0,2,1:T(8,128)(2,1)S(1)}, u32[]{:S(2)}, u32[]{:S(2)}) async-start(bf16[8,8,1,384]{3,0,2,1:T(8,128)(2,1)} %copy.17), calls=%async_computation.3 | async-start | bytes 98304 | tf_op jit(solution)/shard_map/all_to_all | solution.py:67
  56.8 46.6 %copy-start.5 = (bf16[384,8]{0,1:T(8,128)(2,1)S(1)}, bf16[384,8]{0,1:T(8,128)(2,1)}, u32[]{:S(2)}) copy-start(bf16[384,8]{0,1:T(8,128)(2,1)} %param.6) | copy-start | bytes 18436
Sparse Core Ops, SparseCore 0:
  38.2 23.1 reduce-scatter.8
  64.1 25.7 reduce-scatter.6
where the time goes:
time: 117 us; the launch traced here: 116 us
  blocking collectives  38.5 us (33%)
  waiting for transfers between devices  21.7 us (19%)
  starting transfers between devices  17.4 us (15%)
  between operations  14.2 us (12%)
  local copies, waits for them, and re-layouts  10.8 us (9%)
  matrix products  10.5 us (9%)
  other arithmetic  2.82 us (2%)
    psum x1, blocking collectives, on_device(): router_full = lax.psum(router_local, ('expert', 'dp'))  38.5 us
    unnamed x18, local copies, waits for them, and re-layouts  7.6 us
    all_to_all x1, starting transfers between devices, on_device(): lax.all_to_all(slot_in, 'expert', split_axis=1, concat_axis=1, tiled=True)  7.25 us
    all_to_all x1, waiting for transfers between devices, on_device(): lax.all_to_all(slot_grad, 'expert', split_axis=1, concat_axis=1, tiled=True)  6.34 us
    all_to_all x1, waiting for transfers between devices, on_device(): lax.all_to_all(slot_in, 'expert', split_axis=1, concat_axis=1, tiled=True)  5.73 us
    all_to_all x1, waiting for transfers between devices, on_device(): lax.all_to_all(slot_out, 'expert', split_axis=1, concat_axis=1, tiled=True)  5.27 us
    all_to_all x1, waiting for transfers between devices, on_device(): lax.all_to_all(back_grad, 'expert', split_axis=1, concat_axis=1, tiled=True)  4.31 us
    all_to_all x1, starting transfers between devices, on_device(): lax.all_to_all(slot_grad, 'expert', split_axis=1, concat_axis=1, tiled=True)  3.35 us
  transfers between devices with their start and end apart: 6, of which 4 were waited for; matrix products, arithmetic and copies ran while one was open for 13% of the time, Pallas kernels for 0%

commit v1 on v0

--- a/solution.py
+++ b/solution.py
@@ -38,37 +38,40 @@
     slot_grad = jnp.einsum("bme,bmd->bed", combine_b, out_grad, preferred_element_type=f32).astype(
         bf16
     )
-    slot_in = slot_in.reshape(images, owners, per_owner, D)
-    slot_grad = slot_grad.reshape(images, owners, per_owner, D)
-    recv_in, recv_grad = (
-        lax.all_to_all(slot_in, "expert", split_axis=1, concat_axis=1, tiled=True),
-        lax.all_to_all(slot_grad, "expert", split_axis=1, concat_axis=1, tiled=True),
+    def to_owner(part):
+        part = part.reshape(images, owners, per_owner, D)
+        return jnp.transpose(part, (1, 2, 0, 3))
+
+    sent = jnp.stack((to_owner(slot_in), to_owner(slot_grad)), axis=2)
+    recv = lax.all_to_all(sent, "expert", split_axis=0, concat_axis=0, tiled=True)
+    spread = lax.all_gather(recv, "dp", axis=0, tiled=False)
+
+    def expert_pass(slots, cotan):
+        pre_act = jnp.einsum("kbd,kdf->kbf", slots, w_in, preferred_element_type=f32)
+        value, slope = gelu_pair(pre_act)
+        hid_grad = jnp.einsum("kbd,kdf->kbf", cotan, w_out, preferred_element_type=f32)
+        return value.astype(bf16), (hid_grad * slope).astype(bf16)
+
+    def by_expert(part):
+        return jnp.moveaxis(part, -3, 0).reshape(per_owner, -1, D)
+
+    hidden, pre_grad = expert_pass(by_expert(recv[:, :, 0]), by_expert(recv[:, :, 1]))
+    slot_out = jnp.einsum("kbf,kdf->kbd", hidden, w_out, preferred_element_type=f32).astype(bf16)
+    back_grad = jnp.einsum("kbf,kdf->kbd", pre_grad, w_in, preferred_element_type=f32).astype(bf16)
+    back = jnp.stack((slot_out, back_grad), axis=1).reshape(per_owner, 2, owners, images, D)
+    back = lax.all_to_all(
+        jnp.transpose(back, (2, 0, 1, 3, 4)), "expert", split_axis=0, concat_axis=0, tiled=True
     )
-    pre_act = jnp.einsum("bskd,kdf->bskf", recv_in, w_in, preferred_element_type=f32)
-    value, slope = gelu_pair(pre_act)
-    hidden = value.astype(bf16)
-    slot_out = jnp.einsum("bskf,kdf->bskd", hidden, w_out, preferred_element_type=f32).astype(bf16)
-    hid_grad = jnp.einsum("bskd,kdf->bskf", recv_grad, w_out, preferred_element_type=f32)
-    pre_grad = (hid_grad * slope).astype(bf16)
-    back_grad = jnp.einsum("bskf,kdf->bskd", pre_grad, w_in, preferred_element_type=f32).astype(
-        bf16
-    )
-    win_term = jnp.einsum("bskd,bskf->dkf", recv_in, pre_grad, preferred_element_type=f32)
-    wout_term = jnp.einsum("bskd,bskf->dkf", recv_grad, hidden, preferred_element_type=f32)
-    win_part, wout_part = (
-        lax.psum_scatter(
-            win_term.astype(jnp.bfloat16), "dp", scatter_dimension=0, tiled=True
-        ).astype(jnp.float32),
-        lax.psum_scatter(
-            wout_term.astype(jnp.bfloat16), "dp", scatter_dimension=0, tiled=True
-        ).astype(jnp.float32),
-    )
-    slot_back, slot_in_grad = (
-        lax.all_to_all(slot_out, "expert", split_axis=1, concat_axis=1, tiled=True),
-        lax.all_to_all(back_grad, "expert", split_axis=1, concat_axis=1, tiled=True),
-    )
-    slot_back = slot_back.reshape(images, experts_all, D)
-    slot_in_grad = slot_in_grad.reshape(images, experts_all, D)
+    slot_back = jnp.transpose(back[:, :, 0].reshape(experts_all, images, D), (1, 0, 2))
+    slot_in_grad = jnp.transpose(back[:, :, 1].reshape(experts_all, images, D), (1, 0, 2))
+
+    all_in, all_cot = by_expert(spread[:, :, :, 0]), by_expert(spread[:, :, :, 1])
+    all_hidden, all_pre_grad = expert_pass(all_in, all_cot)
+    first_row = lax.axis_index("dp") * row_count
+    own_in = lax.dynamic_slice_in_dim(all_in, first_row, row_count, 2)
+    own_cot = lax.dynamic_slice_in_dim(all_cot, first_row, row_count, 2)
+    w_in_grad = jnp.einsum("kbd,kbf->kdf", own_in, all_pre_grad, preferred_element_type=f32)
+    w_out_grad = jnp.einsum("kbd,kbf->kdf", own_cot, all_hidden, preferred_element_type=f32)
     comb_grad = jnp.einsum("bmd,bed->bme", out_grad, slot_back, preferred_element_type=f32)
     disp_grad = jnp.einsum("bmd,bed->bme", tokens, slot_in_grad, preferred_element_type=f32)
     logit_grad = combine * (comb_grad - jnp.sum(combine * comb_grad, axis=2, keepdims=True))
@@ -86,8 +89,6 @@
     router_grad = lax.dynamic_slice_in_dim(
         router_full, lax.axis_index("dp") * row_count, row_count, 0
     )
-    w_in_grad = jnp.transpose(win_part, (1, 0, 2))
-    w_out_grad = jnp.transpose(wout_part, (1, 0, 2))
     return (tokens_grad, w_in_grad, w_out_grad, router_grad)
 
 

time: 117 us -> 89.8 us (0.77)
  between operations: 14.2 us -> 0.72 us
  waiting for transfers between devices: 21.7 us -> 8.3 us
  local copies, waits for them, and re-layouts: 10.8 us -> 2.47 us
  blocking collectives: 38.5 us -> 46 us
  starting transfers between devices: 17.4 us -> 10.6 us
  matrix products: 10.5 us -> 16.8 us
  other arithmetic: 2.82 us -> 4.25 us
    all_to_all x4 -> x2, waiting for transfers between devices: 21.6 us -> 8.3 us  [the longest x1 7.12 us: on_device(): lax.all_to_all(sent, 'expert', split_axis=0, concat_axis=0, tiled=True)]
    unnamed x18 -> x10, local copies, waits for them, and re-layouts: 7.6 us -> 0.38 us
    all_to_all x4 -> x2, starting transfers between devices: 17.3 us -> 10.6 us  [the longest x1 7.25 us: on_device(): lax.all_to_all(sent, 'expert', split_axis=0, concat_axis=0, tiled=True)]
    all_gather x0 -> x1, blocking collectives: none -> 6.47 us  [on_device(): spread = lax.all_gather(recv, 'dp', axis=0, tiled=False)]
    dot_general x6, matrix products: 5.37 us -> 10.7 us  [the longest x1 3.6 us: on_device(): jnp.einsum('kbd,kbf->kdf', own_in, all_pre_grad, preferred_element_type=f32)]
    transpose x2 -> x1, other arithmetic: 0.11 us -> 1.46 us  [on_device(): jnp.transpose(back, (2, 0, 1, 3, 4))]
    reshape x2 -> x0, local copies, waits for them, and re-layouts: 1.28 us -> none  [the longest x1 0.64 us: on_device(): slot_grad = slot_grad.reshape(images, owners, per_owner, D)]
    convert_element_type x2 -> x0, local copies, waits for them, and re-layouts: 1.26 us -> none  [the longest x1 0.63 us: on_device(): jnp.einsum('bskf,kdf->bskd', hidden, w_out, preferred_element_type=f32)]
  transfers between devices with their start and end apart: 6 -> 2, of which waited for: 4 -> 2; matrix products, arithmetic and copies ran while one was open for 13% -> 7% of each run, Pallas kernels for 0% -> 0%
where the time goes in v1:
time: 89.8 us; the launch traced here: 89.2 us
  blocking collectives  46 us (51%)
  matrix products  16.8 us (19%)
  starting transfers between devices  10.6 us (12%)
  waiting for transfers between devices  8.3 us (9%)
  other arithmetic  4.25 us (5%)
  local copies, waits for them, and re-layouts  2.47 us (3%)
    psum x1, blocking collectives, on_device(): router_full = lax.psum(router_local, ('expert', 'dp'))  39.6 us
    all_to_all x1, starting transfers between devices, on_device(): lax.all_to_all(sent, 'expert', split_axis=0, concat_axis=0, tiled=True)  7.25 us
    all_to_all x1, waiting for transfers between devices, on_device(): lax.all_to_all(sent, 'expert', split_axis=0, concat_axis=0, tiled=True)  7.12 us
    all_gather x1, blocking collectives, on_device(): spread = lax.all_gather(recv, 'dp', axis=0, tiled=False)  6.47 us
    dot_general x1, matrix products, on_device(): jnp.einsum('kbd,kbf->kdf', own_in, all_pre_grad, preferred_element_type=f32)  3.6 us
    all_to_all x1, starting transfers between devices, on_device(): lax.all_to_all(jnp.transpose(back, (2, 0, 1, 3, 4)), 'expert', split_axis...  3.36 us
    dot_general x1, matrix products, on_device(): jnp.einsum('kbf,kdf->kbd', pre_grad, w_in, preferred_element_type=f32)  2.59 us
    dot_general x1, matrix products, on_device(): jnp.einsum('kbd,kbf->kdf', own_cot, all_hidden, preferred_element_type=f32)  2.45 us
  transfers between devices with their start and end apart: 2, of which 2 were waited for; matrix products, arithmetic and copies ran while one was open for 7% of the time, Pallas kernels for 0%

profile of v1, /device:TPU:0, one launch (start us, length us, event | category | flops | bytes accessed | tf_op | source)
XLA Modules:
  0.0 89.2 jit_solution(14511386567733699859)
XLA Ops:
  0.6 0.0 copy-start
  0.6 1.4 %fusion.91 = f32[8,64,8]{1,2,0:T(8,128)S(1)} fusion(bf16[8,64,384]{2,1,0:T(8,128)(2,1)} %param.5, bf16[384,8]{0,1:T(8,128)(2,1)} %param.6), kind=kOutput, calls=%fused_computation.97 | convolution fusion | flops 3145728 | bytes 415744 | tf_op jit(solution)/shard_map/bmd,de->bme/dot_general | solution.py:30
  2.0 1.3 %fusion.118 = (f32[8,8]{1,0:T(8,128)S(1)}, f32[8,64,8]{1,2,0:T(8,128)S(1)}) fusion(f32[8,64,8]{1,2,0:T(8,128)S(1)} %fusion.91), kind=kOutput, calls=%fused_computation.125 | output fusion | flops 8255 | bytes 33024 | tf_op jit(solution)/shard_map/sub | solution.py:31
  3.3 0.3 fusion.117
  3.6 1.3 %fusion.42 = bf16[8,1,1,8,384]{4,0,3,2,1:T(8,128)(2,1)S(1)} fusion(bf16[8,64,384]{2,1,0:T(8,128)(2,1)} %param.5, f32[8,8]{1,0:T(8,128)S(1)} %get-tuple-element.10, f32[8,64,8]{1,2,0:T(8,128)S(1)} %fusion.91), kind=kOutput, calls=%fused_computation.38 | convolution fusion | flops 3182719 | bytes 459008 | tf_op jit(solution)/shard_map/bme,bmd->bed/dot_general | solution.py:35
  4.9 1.2 %fusion.43 = bf16[8,1,1,8,384]{4,0,3,2,1:T(8,128)(2,1)S(1)} fusion(bf16[8,64,384]{2,1,0:T(8,128)(2,1)} %param.9, f32[8,64]{1,0:T(8,128)S(1)} %get-tuple-element.8, f32[8,64,8]{1,2,0:T(8,128)S(1)} %fusion.91), kind=kOutput, calls=%fused_computation.39 | convolution fusion | flops 3183111 | bytes 460800 | tf_op jit(solution)/shard_map/bme,bmd->bed/dot_general | solution.py:38
  6.1 0.7 copy.25
  6.7 7.3 %all-to-all-start = ((bf16[8,1,2,8,384]{4,3,2,1,0:T(8,128)(2,1)}), bf16[8,1,2,8,384]{4,3,2,1,0:T(8,128)(2,1)S(1)}, u32[]{:S(2)}, u32[]{:S(2)}) async-start(bf16[8,1,2,8,384]{4,3,2,1,0:T(8,128)(2,1)} %copy.25), calls=%async_computation | async-start | bytes 196608 | tf_op jit(solution)/shard_map/all_to_all | solution.py:46
  14.0 7.1 %all-to-all-done = bf16[8,1,2,8,384]{4,3,2,1,0:T(8,128)(2,1)S(1)} async-done(((bf16[8,1,2,8,384]{4,3,2,1,0:T(8,128)(2,1)}), bf16[8,1,2,8,384]{4,3,2,1,0:T(8,128)(2,1)S(1)}, u32[]{:S(2)}, u32[]{:S(2)}) %all-to-all-start) | async-done | bytes 98336 | tf_op jit(solution)/shard_map/all_to_all | solution.py:46
  21.1 6.5 %all-gather = bf16[32,1,2,8,384]{4,3,2,1,0:T(8,128)(2,1)S(1)} all-gather(bf16[8,1,2,8,384]{4,3,2,1,0:T(8,128)(2,1)S(1)} %all-to-all-done), channel_id=2, replica_groups=mesh['expert'=8,'dp'=4] {'dp'}, dimensions={0}, use_global_device_ids=true | all-gather | bytes 491520 | tf_op jit(solution)/shard_map/all_gather | solution.py:47
  27.6 0.7 fusion.115
  28.3 0.0 copy-done
  28.3 0.0 copy-start.4
  28.3 0.6 fusion.16
  28.9 0.3 fusion.20
  29.3 0.4 copy-done.4
  29.6 1.1 %fusion.32 = bf16[1,1,8,8,384]{4,3,1,0,2:T(8,128)(2,1)} fusion(bf16[1,384,1536]{2,1,0:T(8,128)(2,1)S(1)} %copy-done.4, f32[64,1536]{1,0:T(8,128)S(1)} %fusion.20), kind=kOutput, calls=%fused_computation.34 | convolution fusion | flops 76406784 | bytes 1622016 | tf_op jit(solution)/shard_map/kbf,kdf->kbd/dot_general | solution.py:59
  30.7 2.6 %fusion.35 = bf16[1,1,8,8,384]{4,3,1,0,2:T(8,128)(2,1)} fusion(bf16[1,384,1536]{2,1,0:T(8,128)(2,1)S(1)} %copy-done, bf16[1,384,1536]{2,1,0:T(8,128)(2,1)} %param.8, f32[64,1536]{1,0:T(8,128)S(1)} %fusion.20, bf16[8,1,2,8,384]{4,3,2,1,0:T(8,128)(2,1)S(1)} %all-to-all-done), kind=kOutput, calls=%fused_computation.35 | convolution fusion | flops 152887296 | bytes 2850816 | tf_op jit(solution)/shard_map/kbf,kdf->kbd/dot_general | solution.py:60
  33.3 1.5 %maximum_bitcast_fusion = bf16[8,1,2,8,384]{4,3,2,1,0:T(8,128)(2,1)} fusion(bf16[1,1,8,8,384]{4,3,1,0,2:T(8,128)(2,1)} %fusion.35, bf16[1,1,8,8,384]{4,3,1,0,2:T(8,128)(2,1)} %fusion.32), kind=kLoop, calls=%fused_computation.76 | loop fusion | flops 49152 | bytes 196608 | tf_op jit(solution)/shard_map/transpose | solution.py:63
  34.8 3.4 %all-to-all-start.1 = ((bf16[8,1,2,8,384]{4,3,2,1,0:T(8,128)(2,1)}), bf16[8,1,2,8,384]{4,3,2,1,0:T(8,128)(2,1)S(1)}, u32[]{:S(2)}, u32[]{:S(2)}) async-start(bf16[8,1,2,8,384]{4,3,2,1,0:T(8,128)(2,1)} %maximum_bitcast_fusion), calls=%async_computation.1 | async-start | bytes 196608 | tf_op jit(solution)/shard_map/all_to_all | solution.py:62
  38.2 3.6 %convolution_bitcast_fusion.1 = f32[1,96,1536]{2,1,0:T(8,128)} fusion(bf16[256,384]{1,0:T(8,128)(2,1)} %bitcast.118, f32[256,1536]{1,0:T(8,128)S(1)} %fusion.16, bf16[1,384,1536]{2,1,0:T(8,128)(2,1)} %param.8, bf16[1,256,384]{2,1,0:T(8,128)(2,1)S(1)} %bitcast.117, s32[]{:T(128)S(6)} %select_n.2), kind=kOutput, calls=%fused_computation.7 | convolution fusion | flops 384958464 | bytes 3604484 | tf_op jit(solution)/shard_map/kbd,kbf->kdf/dot_general | solution.py:73
  41.8 0.0 copy-start.1
  41.8 2.5 %convolution_bitcast_fusion = f32[1,96,1536]{2,1,0:T(8,128)} fusion(f32[256,1536]{1,0:T(8,128)S(1)} %fusion.16, bf16[1,256,384]{2,1,0:T(8,128)(2,1)} %bitcast.119, s32[]{:T(128)S(6)} %select_n.2), kind=kOutput, calls=%fused_computation.6 | convolution fusion | flops 79036416 | bytes 2228228 | tf_op jit(solution)/shard_map/kbd,kbf->kdf/dot_general | solution.py:74
  44.2 0.0 copy-start.2
  44.2 0.0 copy-start.3
  44.2 1.2 %all-to-all-done.1 = bf16[8,1,2,8,384]{4,3,2,1,0:T(8,128)(2,1)S(1)} async-done(((bf16[8,1,2,8,384]{4,3,2,1,0:T(8,128)(2,1)}), bf16[8,1,2,8,384]{4,3,2,1,0:T(8,128)(2,1)S(1)}, u32[]{:S(2)}, u32[]{:S(2)}) %all-to-all-start.1) | async-done | bytes 98336 | tf_op jit(solution)/shard_map/all_to_all | solution.py:62
  45.4 0.0 copy-done.1
  45.4 0.2 convolution_bitcast_fusion.2
  45.7 0.5 fusion.85
  46.1 0.0 copy-done.2
  46.2 0.2 convolution_bitcast_fusion.3
  46.4 1.2 %fusion.50 = f32[8,64,8]{1,2,0:T(8,128)S(1)} fusion(f32[8,64,8]{1,2,0:T(8,128)S(1)} %convolution_bitcast_fusion.2, f32[8,64,8]{1,2,0:T(8,128)S(1)} %get-tuple-element.11, f32[8,8]{1,0:T(8,128)S(1)} %get-tuple-element.10), kind=kOutput, calls=%fused_computation.46 | output fusion | flops 20607 | bytes 49408 | tf_op jit(solution)/shard_map/sub | solution.py:79
  47.6 0.3 convolution_bitcast_fusion.4
  47.9 39.6 %psum.7 = f32[384,8]{0,1:T(8,128)S(1)} all-reduce(f32[384,8]{0,1:T(8,128)S(1)} %convolution_bitcast_fusion.4), channel_id=1, replica_groups=mesh['expert'=8,'dp'=4] {'expert','dp'}, use_global_device_ids=true, to_apply=%region_6.0 | all-reduce | flops 3072 | bytes 24576 | tf_op jit(solution)/shard_map/psum | solution.py:88
  87.4 0.7 constant_dynamic-slice_fusion
  88.1 0.0 copy-done.3
  88.1 1.1 %fusion.11 = bf16[8,64,384]{2,1,0:T(8,128)(2,1)} fusion(f32[8,64,384]{2,1,0:T(8,128)S(1)} %fusion.85, f32[8,64,8]{1,2,0:T(8,128)S(1)} %fusion.50, f32[8,64,8]{1,2,0:T(8,128)S(1)} %convolution_bitcast_fusion.3, bf16[384,8]{0,1:T(8,128)(2,1)S(1)} %copy-done.3, f32[8,64,8]{1,2,0:T(8,128)S(1)} %get-tuple-element.9, f32[8,64]{1,0:T(8,128)S(1)} %get-tuple-element.8), kind=kOutput, calls=%fused_computation.19 | convolution fusion | flops 3568135 | bytes 1236992 | tf_op jit(solution)/shard_map/bme,de->bmd/dot_general | solution.py:83
  (3 shorter events, 0.1 us)
Async XLA Ops:
  0.6 27.7 %copy-start = (bf16[1,384,1536]{2,1,0:T(8,128)(2,1)S(1)}, bf16[1,384,1536]{2,1,0:T(8,128)(2,1)}, u32[]{:S(2)}) copy-start(bf16[1,384,1536]{2,1,0:T(8,128)(2,1)} %param.7) | copy-start | bytes 3538948
  6.7 14.4 %all-to-all-start = ((bf16[8,1,2,8,384]{4,3,2,1,0:T(8,128)(2,1)}), bf16[8,1,2,8,384]{4,3,2,1,0:T(8,128)(2,1)S(1)}, u32[]{:S(2)}, u32[]{:S(2)}) async-start(bf16[8,1,2,8,384]{4,3,2,1,0:T(8,128)(2,1)} %copy.25), calls=%async_computation | async-start | bytes 196608 | tf_op jit(solution)/shard_map/all_to_all | solution.py:46
  28.3 1.3 %copy-start.4 = (bf16[1,384,1536]{2,1,0:T(8,128)(2,1)S(1)}, bf16[1,384,1536]{2,1,0:T(8,128)(2,1)}, u32[]{:S(2)}) copy-start(bf16[1,384,1536]{2,1,0:T(8,128)(2,1)} %param.8) | copy-start | bytes 3538948
  34.8 10.6 %all-to-all-start.1 = ((bf16[8,1,2,8,384]{4,3,2,1,0:T(8,128)(2,1)}), bf16[8,1,2,8,384]{4,3,2,1,0:T(8,128)(2,1)S(1)}, u32[]{:S(2)}, u32[]{:S(2)}) async-start(bf16[8,1,2,8,384]{4,3,2,1,0:T(8,128)(2,1)} %maximum_bitcast_fusion), calls=%async_computation.1 | async-start | bytes 196608 | tf_op jit(solution)/shard_map/all_to_all | solution.py:62
  41.8 3.6 %copy-start.1 = (bf16[8,64,384]{2,1,0:T(8,128)(2,1)S(1)}, bf16[8,64,384]{2,1,0:T(8,128)(2,1)}, u32[]{:S(2)}) copy-start(bf16[8,64,384]{2,1,0:T(8,128)(2,1)} %param.5) | copy-start | bytes 1179652
  44.2 1.9 %copy-start.2 = (bf16[8,64,384]{2,1,0:T(8,128)(2,1)S(1)}, bf16[8,64,384]{2,1,0:T(8,128)(2,1)}, u32[]{:S(2)}) copy-start(bf16[8,64,384]{2,1,0:T(8,128)(2,1)} %param.9) | copy-start | bytes 1179652
  44.2 43.9 %copy-start.3 = (bf16[384,8]{0,1:T(8,128)(2,1)S(1)}, bf16[384,8]{0,1:T(8,128)(2,1)}, u32[]{:S(2)}) copy-start(bf16[384,8]{0,1:T(8,128)(2,1)} %param.6) | copy-start | bytes 18436

commit v2 on v1

v2 whole, which is shorter than its diff:
```python
import functools
import math

import jax
import jax.numpy as jnp
from jax import lax
from jax.experimental import pallas as pl
from jax.experimental.pallas import tpu as pltpu
from jax.sharding import PartitionSpec as P

F32 = jnp.float32
BF16 = jnp.bfloat16
VMEM_BYTES = 24 * 1024 * 1024


def gelu_pair(value):
    coef = math.sqrt(2.0 / math.pi)
    square = value * value
    tangent = jnp.tanh(coef * value * (1.0 + 0.044715 * square))
    half = 0.5 * (1.0 + tangent)
    slope = half + 0.5 * coef * value * (1.0 - tangent * tangent) * (1.0 + 3.0 * 0.044715 * square)
    return value * half, slope


def dot(left, right, left_dim, right_dim):
    return lax.dot_general(
        left, right, (((left_dim,), (right_dim,)), ((), ())), preferred_element_type=F32
    )


def own_image(experts, images, columns):
    shape = (experts, images, columns)
    image = lax.broadcasted_iota(jnp.int32, shape, 1)
    token = lax.broadcasted_iota(jnp.int32, shape, 2)
    low = image * (columns // images)
    inside = (token >= low) & (token < low + columns // images)
    return inside.reshape(experts * images, columns)


def spread_rows(compact, images):
    experts, columns = compact.shape
    wide = jnp.broadcast_to(compact[:, None, :], (experts, images, columns))
    return wide.reshape(experts * images, columns)


def fold_rows(block, images):
    rows, columns = block.shape
    return jnp.sum(block.reshape(rows // images, images, columns), axis=1)


def pair_rows(first, second, groups):
    images = first.shape[0] // groups
    first = first.reshape(groups, images, first.shape[1])
    second = second.reshape(groups, images, second.shape[1])
    return jnp.concatenate((first, second), axis=1).astype(BF16)


def split_rows(pairs):
    groups, both, width = pairs.shape
    wide = pairs.astype(F32)
    first = wide[:, : both // 2].reshape(groups * both // 2, width)
    second = wide[:, both // 2 :].reshape(groups * both // 2, width)
    return first.astype(BF16), second.astype(BF16)


def slots_kernel(images, tokens_ref, router_ref, grad_ref, sent_ref, soft_ref):
    tokens = tokens_ref[...]
    columns = tokens.shape[0]
    experts = router_ref.shape[0]
    logits = dot(router_ref[...], tokens, 1, 1)
    mask = own_image(experts, images, columns)
    top = jnp.max(logits, axis=0, keepdims=True)
    combine = jnp.exp(logits - top)
    combine = combine / jnp.sum(combine, axis=0, keepdims=True)
    block = jnp.where(mask, spread_rows(logits, images), -jnp.inf)
    block = jnp.exp(block - jnp.max(block, axis=1, keepdims=True))
    block = block / jnp.sum(block, axis=1, keepdims=True)
    soft_ref[0] = fold_rows(block, images)
    soft_ref[1] = combine
    combine_block = jnp.where(mask, spread_rows(combine, images), 0.0)
    slot_in = dot(block.astype(BF16), tokens, 1, 0)
    slot_grad = dot(combine_block.astype(BF16), grad_ref[...], 1, 0)
    sent_ref[...] = pair_rows(slot_in, slot_grad, experts)


def expert_kernel(recv_ref, win_ref, wout_ref, back_ref, *, step):
    slots, cotan = split_rows(recv_ref[...])
    out = jnp.zeros(slots.shape, F32)
    back = jnp.zeros(slots.shape, F32)
    for start in range(0, win_ref.shape[1], step):
        w_in = win_ref[:, start : start + step]
        w_out = wout_ref[:, start : start + step]
        value, slope = gelu_pair(dot(slots, w_in, 1, 0))
        pre_grad = dot(cotan, w_out, 1, 0) * slope
        out = out + dot(value.astype(BF16), w_out, 1, 1)
        back = back + dot(pre_grad.astype(BF16), w_in, 1, 1)
    back_ref[...] = pair_rows(out, back, recv_ref.shape[0])


def tokens_kernel(
    images, back_ref, tokens_ref, router_ref, grad_ref, soft_ref, out_ref, send_ref
):
    tokens = tokens_ref[...]
    columns = tokens.shape[0]
    experts = router_ref.shape[0]
    slot_out, slot_in_grad = split_rows(back_ref[...])
    dispatch, combine = soft_ref[0], soft_ref[1]
    mask = own_image(experts, images, columns)
    comb = fold_rows(jnp.where(mask, dot(slot_out, grad_ref[...], 1, 1), 0.0), images)
    disp = jnp.where(mask, dot(slot_in_grad, tokens, 1, 1), 0.0)
    dispatch_block = jnp.where(mask, spread_rows(dispatch, images), 0.0)
    mean = jnp.sum(dispatch_block * disp, axis=1, keepdims=True)
    from_dispatch = fold_rows(dispatch_block * (disp - mean), images)
    from_combine = combine * (comb - jnp.sum(combine * comb, axis=0, keepdims=True))
    logit_grad = (from_combine + from_dispatch).astype(BF16)
    out = dot(dispatch_block.astype(BF16), slot_in_grad, 0, 0)
    out = out + dot(logit_grad, router_ref[...], 0, 0)
    out_ref[...] = out.astype(BF16)
    part = dot(logit_grad, tokens, 1, 0)
    owners, shares, _, width = send_ref.shape
    for share in range(shares):
        piece = part[:, share * width : (share + 1) * width]
        for owner in range(owners):
            send_ref[owner, share] = piece


def weights_kernel(share_ref, spread_ref, win_ref, wout_ref, win_out, wout_out, *, step):
    width = spread_ref.shape[-1]
    row_count = win_out.shape[0]
    slots, cotan = split_rows(spread_ref[...].reshape((-1,) + spread_ref.shape[2:]))
    shape = (row_count, width)
    row = lax.broadcasted_iota(jnp.int32, shape, 0) + share_ref[0] * row_count
    pick = jnp.where(lax.broadcasted_iota(jnp.int32, shape, 1) == row, 1.0, 0.0).astype(BF16)
    own_slots = dot(pick, slots, 1, 1).astype(BF16)
    own_cotan = dot(pick, cotan, 1, 1).astype(BF16)

    @pl.when(pl.program_id(0) == 0)
    def _():
        win_out[...] = jnp.zeros_like(win_out)
        wout_out[...] = jnp.zeros_like(wout_out)

    for start in range(0, win_ref.shape[1], step):
        part = slice(start, start + step)
        value, slope = gelu_pair(dot(slots, win_ref[:, part], 1, 0))
        pre_grad = dot(cotan, wout_ref[:, part], 1, 0) * slope
        win_out[:, part] += dot(own_slots, pre_grad.astype(BF16), 1, 0)
        wout_out[:, part] += dot(own_cotan, value.astype(BF16), 1, 0)


def on_device(tokens, router, w_in, w_out, out_grad):
    owners, shares = lax.axis_size("expert"), lax.axis_size("dp")
    images, per_image, width = tokens.shape
    experts = router.shape[1]
    hidden = w_in.shape[2]
    columns = images * per_image
    row_count = width // shares
    tokens2 = tokens.reshape(columns, width)
    grad2 = out_grad.reshape(columns, width)
    router_rows = router.T
    w_in2, w_out2 = w_in.reshape(width, hidden), w_out.reshape(width, hidden)
    params = pltpu.CompilerParams(vmem_limit_bytes=VMEM_BYTES)

    def struct(shape, dtype):
        return jax.ShapeDtypeStruct(shape, dtype)

    sent, soft = pl.pallas_call(
        functools.partial(slots_kernel, images),
        out_shape=(
            struct((experts, 2 * images, width), BF16),
            struct((2, experts, columns), F32),
        ),
        compiler_params=params,
        name="slots",
    )(tokens2, router_rows, grad2)
    recv = lax.all_to_all(sent, "expert", split_axis=0, concat_axis=0, tiled=True)
    back = pl.pallas_call(
        functools.partial(expert_kernel, step=512),
        out_shape=struct(recv.shape, BF16),
        compiler_params=params,
        name="expert",
    )(recv, w_in2, w_out2)
    recv, back = lax.optimization_barrier((recv, back))
    slots_back = lax.all_to_all(back, "expert", split_axis=0, concat_axis=0, tiled=True)
    spread = lax.all_gather(recv, "dp", axis=0, tiled=False)

    tokens_grad, router_send = pl.pallas_call(
        functools.partial(tokens_kernel, images),
        out_shape=(
            struct((columns, width), BF16),
            struct((owners, shares, experts, row_count), F32),
        ),
        compiler_params=params,
        name="tokens",
    )(slots_back, tokens2, router_rows, grad2, soft)
    spread, router_send = lax.optimization_barrier((spread, router_send))
    router_parts = lax.all_to_all(
        router_send.reshape(owners * shares, experts, row_count),
        ("expert", "dp"),
        split_axis=0,
        concat_axis=0,
        tiled=True,
    )

    group = max(1, min(shares, 256 // (owners * images)))
    w_in_grad, w_out_grad = pl.pallas_call(
        functools.partial(weights_kernel, step=512),
        grid=(shares // group,),
        in_specs=[
            pl.BlockSpec(memory_space=pltpu.SMEM),
            pl.BlockSpec((group,) + recv.shape, lambda i: (i, 0, 0, 0)),
            pl.BlockSpec((width, hidden), lambda i: (0, 0)),
            pl.BlockSpec((width, hidden), lambda i: (0, 0)),
        ],
        out_specs=[pl.BlockSpec((row_count, hidden), lambda i: (0, 0))] * 2,
        out_shape=[struct((row_count, hidden), F32)] * 2,
        compiler_params=params,
        name="weights",
    )(lax.axis_index("dp").reshape(1), spread, w_in2, w_out2)
    router_grad = jnp.sum(router_parts, axis=0).T
    return (
        tokens_grad.reshape(tokens.shape),
        w_in_grad.reshape(1, row_count, hidden),
        w_out_grad.reshape(1, row_count, hidden),
        router_grad,
    )


def solution(mesh):
    placed = (
        P(("expert", "dp"), None, None),
        P(),
        P("expert", None, None),
        P("expert", None, None),
        P(("expert", "dp"), None, None),
    )
    return jax.shard_map(
        on_device,
        mesh=mesh,
        in_specs=placed,
        out_specs=(
            P(("expert", "dp"), None, None),
            P("expert", "dp", None),
            P("expert", "dp", None),
            P("dp", None),
        ),
        check_vma=False,
    )
```

time: 89.8 us -> 52.6 us (0.59)
  blocking collectives: 46 us -> 20.9 us
  matrix products: 16.8 us -> 0 us
  Pallas kernels: 0 us -> 8.27 us
  local copies, waits for them, and re-layouts: 2.47 us -> 6.71 us
  other arithmetic: 4.25 us -> 0.63 us
  waiting for transfers between devices: 8.3 us -> 5.53 us
  starting transfers between devices: 10.6 us -> 9.28 us
    psum x1 -> x0, blocking collectives: 39.6 us -> none  [on_device(): router_full = lax.psum(router_local, ('expert', 'dp'))]
    dot_general x14 -> x0, matrix products: 16.8 us -> none  [the longest x1 3.6 us: on_device(): jnp.einsum('kbd,kbf->kdf', own_in, all_pre_grad, preferred_element_type=f32)]
    all_to_all x0 -> x1, blocking collectives: none -> 14.2 us  [on_device(): lax.all_to_all(sent, 'expert', split_axis=0, concat_axis=0, tiled=True)]
    pallas_call x0 -> x4, Pallas kernels: none -> 8.27 us  [the longest x1 3.12 us: on_device(): pl.pallas_call(functools.partial(weights_kernel, step=512), grid=(shares...]
    unnamed x10 -> x28, local copies, waits for them, and re-layouts: 0.38 us -> 6.71 us
    all_to_all x2, waiting for transfers between devices: 8.3 us -> 5.53 us  [the longest x1 5.08 us: on_device(): lax.all_to_all(router_send.reshape(owners * shares, experts, row_count),...]
    sub x3 -> x0, other arithmetic: 2.76 us -> none  [the longest x1 1.27 us: on_device(): dispatch = jax.nn.softmax(logits, axis=1)]
    transpose x1 -> x0, other arithmetic: 1.46 us -> none  [on_device(): jnp.transpose(back, (2, 0, 1, 3, 4))]
  transfers between devices with their start and end apart: 2 -> 2, of which waited for: 2 -> 2; matrix products, arithmetic and copies ran while one was open for 7% -> 0% of each run, Pallas kernels for 0% -> 6%
where the time goes in v2:
time: 52.6 us; the launch traced here: 52 us
  blocking collectives  20.9 us (40%)
  starting transfers between devices  9.28 us (18%)
  Pallas kernels  8.27 us (16%)
  local copies, waits for them, and re-layouts  6.71 us (13%)
  waiting for transfers between devices  5.53 us (11%)
  between operations  0.72 us (1%)
  other arithmetic  0.63 us (1%)
    all_to_all x1, blocking collectives, on_device(): lax.all_to_all(sent, 'expert', split_axis=0, concat_axis=0, tiled=True)  14.2 us
    unnamed x28, local copies, waits for them, and re-layouts  6.71 us
    all_gather x1, blocking collectives, on_device(): spread = lax.all_gather(recv, 'dp', axis=0, tiled=False)  6.7 us
    all_to_all x1, starting transfers between devices, on_device(): lax.all_to_all(router_send.reshape(owners * shares, experts, row_count),...  5.17 us
    all_to_all x1, waiting for transfers between devices, on_device(): lax.all_to_all(router_send.reshape(owners * shares, experts, row_count),...  5.08 us
    all_to_all x1, starting transfers between devices, on_device(): lax.all_to_all(back, 'expert', split_axis=0, concat_axis=0, tiled=True)  4.12 us
    pallas_call x1, Pallas kernels, on_device(): pl.pallas_call(functools.partial(weights_kernel, step=512), grid=(shares...  3.12 us
    pallas_call x1, Pallas kernels, on_device(): pl.pallas_call(functools.partial(tokens_kernel, images), out_shape=(struc...  2.59 us
  transfers between devices with their start and end apart: 2, of which 2 were waited for; matrix products, arithmetic and copies ran while one was open for 0% of the time, Pallas kernels for 6%

profile of v2, /device:TPU:0, one launch (start us, length us, event | category | flops | bytes accessed | tf_op | source)
XLA Modules:
  0.0 52.0 jit_solution(16539797580411993870)
XLA Ops:
  0.6 0.0 copy-start.4
  0.6 1.0 %copy-done.4 = bf16[8,64,384]{2,1,0:T(8,128)(2,1)S(1)} copy-done((bf16[8,64,384]{2,1,0:T(8,128)(2,1)S(1)}, bf16[8,64,384]{2,1,0:T(8,128)(2,1)}, u32[]{:S(2)}) %copy-start.4) | copy-done | bytes 393240
  1.6 0.0 copy-start.6
  1.6 1.0 %copy-done.6 = bf16[8,64,384]{2,1,0:T(8,128)(2,1)S(1)} copy-done((bf16[8,64,384]{2,1,0:T(8,128)(2,1)S(1)}, bf16[8,64,384]{2,1,0:T(8,128)(2,1)}, u32[]{:S(2)}) %copy-start.6) | copy-done | bytes 393240
  2.6 0.0 copy-start.12
  2.6 0.7 %copy-done.12 = bf16[384,8]{0,1:T(8,128)(2,1)S(1)} copy-done((bf16[384,8]{0,1:T(8,128)(2,1)S(1)}, bf16[384,8]{0,1:T(8,128)(2,1)}, u32[]{:S(2)}) %copy-start.12) | copy-done | bytes 6168
  3.3 0.6 %slots.1 = (bf16[8,16,384]{2,1,0:T(8,128)(2,1)S(1)}, f32[2,8,512]{2,1,0:T(8,128)S(1)}) custom-call(bf16[512,384]{1,0:T(8,128)(2,1)S(1)} %bitcast.16, bf16[8,384]{1,0:T(8,128)(2,1)S(1)} %bitcast.22, bf16[512,384]{1,0:T(8,128)(2,1)S(1)} %bitcast.18), custom_call_target="tpu_custom_call" | custom-call | tf_op jit(solution)/shard_map/slots/pallas_call | solution.py:166
  3.9 0.0 copy-start.10
  4.0 14.2 %all_to_all.15.recv_ref = bf16[8,16,384]{2,1,0:T(8,128)(2,1)S(1)} all-to-all(bf16[8,16,384]{2,1,0:T(8,128)(2,1)S(1)} %get-tuple-element.14), channel_id=1, replica_groups=mesh['expert'=8,'dp'=4] {'expert'}, dimensions={0} | all-to-all | bytes 196608 | tf_op jit(solution)/shard_map/all_to_all | solution.py:175
  18.1 0.0 copy-start.8
  18.1 0.0 copy-done.10
  18.1 0.0 copy-start
  18.1 1.3 %copy-done = bf16[1,384,1536]{2,1,0:T(8,128)(2,1)S(1)} copy-done((bf16[1,384,1536]{2,1,0:T(8,128)(2,1)S(1)}, bf16[1,384,1536]{2,1,0:T(8,128)(2,1)}, u32[]{:S(2)}) %copy-start) | copy-done | bytes 1179672
  19.4 0.0 copy-start.2
  19.4 1.3 %copy-done.2 = bf16[1,384,1536]{2,1,0:T(8,128)(2,1)S(1)} copy-done((bf16[1,384,1536]{2,1,0:T(8,128)(2,1)S(1)}, bf16[1,384,1536]{2,1,0:T(8,128)(2,1)}, u32[]{:S(2)}) %copy-start.2) | copy-done | bytes 1179672
  20.7 0.0 copy-start.5
  20.7 0.0 copy-start.7
  20.7 0.0 copy-start.13
  20.7 0.0 copy-start.3
  20.7 1.9 %expert.1 = bf16[8,16,384]{2,1,0:T(8,128)(2,1)} custom-call(bf16[8,16,384]{2,1,0:T(8,128)(2,1)S(1)} %all_to_all.15.recv_ref, bf16[384,1536]{1,0:T(8,128)(2,1)S(1)} %bitcast.12, bf16[384,1536]{1,0:T(8,128)(2,1)S(1)} %bitcast.14), custom_call_target="tpu_custom_call" | custom-call | tf_op jit(solution)/shard_map/expert/pallas_call | solution.py:176
  22.7 0.0 copy-done.8
  22.7 0.0 copy-start.1
  22.7 4.1 %all-to-all-start.1 = ((bf16[8,16,384]{2,1,0:T(8,128)(2,1)}), bf16[8,16,384]{2,1,0:T(8,128)(2,1)}, u32[]{:S(2)}, u32[]{:S(2)}) async-start(bf16[8,16,384]{2,1,0:T(8,128)(2,1)} %expert.1), calls=%async_computation.1 | async-start | bytes 196608 | tf_op jit(solution)/shard_map/all_to_all | solution.py:183
  26.8 6.7 %all-gather = bf16[32,16,384]{2,1,0:T(8,128)(2,1)S(1)} all-gather(bf16[8,16,384]{2,1,0:T(8,128)(2,1)} %copy-done.8), channel_id=2, replica_groups=mesh['expert'=8,'dp'=4] {'dp'}, dimensions={0}, use_global_device_ids=true | all-gather | bytes 491520 | tf_op jit(solution)/shard_map/all_gather | solution.py:184
  33.5 0.4 all-to-all-done.1.back_ref
  33.9 0.0 copy-done.5
  33.9 0.0 copy-done.7
  33.9 0.0 copy-done.13
  33.9 0.0 copy-start.11
  34.0 0.7 %copy-done.11 = f32[2,8,512]{2,1,0:T(8,128)S(1)} copy-done((f32[2,8,512]{2,1,0:T(8,128)S(1)}, f32[2,8,512]{2,1,0:T(8,128)}, u32[]{:S(2)}) %copy-start.11) | copy-done | bytes 32792
  34.7 2.6 %tokens.1 = (bf16[512,384]{1,0:T(8,128)(2,1)}, f32[8,4,8,96]{3,2,1,0:T(8,128)S(1)}) custom-call(bf16[8,16,384]{2,1,0:T(8,128)(2,1)} %all-to-all-done.1.back_ref, bf16[512,384]{1,0:T(8,128)(2,1)S(1)} %bitcast.17, bf16[8,384]{1,0:T(8,128)(2,1)S(1)} %bitcast.23, bf16[512,384]{1,0:T(8,128)(2,1)S(1)} %bitcast.19, f32[2,8,512]{2,1,0:T(8,128)S(1)} %copy-done.11), custom_call_target="tpu_custom_call" | custom-call | tf_op jit(solution)/shard_map/tokens/pallas_call | solution.py:186
  37.3 0.0 copy-start.9
  37.3 0.7 %copy-done.9 = f32[8,4,8,96]{3,2,1,0:T(8,128)} copy-done((f32[8,4,8,96]{3,2,1,0:T(8,128)}, f32[8,4,8,96]{3,2,1,0:T(8,128)S(1)}, u32[]{:S(2)}) %copy-start.9) | copy-done | bytes 98328
  38.0 5.2 %all-to-all-start.2 = ((f32[32,8,96]{2,1,0:T(8,128)}), f32[32,8,96]{2,1,0:T(8,128)S(1)}, u32[]{:S(2)}, u32[]{:S(2)}) async-start(f32[32,8,96]{2,1,0:T(8,128)} %bitcast.21), calls=%async_computation.2 | async-start | bytes 262144 | tf_op jit(solution)/shard_map/all_to_all | solution.py:196
  43.2 0.0 copy-done.3
  43.2 0.0 copy-done.1
  43.2 3.1 %weights.1 = (f32[96,1536]{1,0:T(8,128)}, f32[96,1536]{1,0:T(8,128)}) custom-call(s32[1]{0:T(128)} %bitcast.6.share_ref, bf16[4,8,16,384]{3,2,1,0:T(8,128)(2,1)S(1)} %bitcast.20, bf16[384,1536]{1,0:T(8,128)(2,1)S(1)} %bitcast.13, bf16[384,1536]{1,0:T(8,128)(2,1)S(1)} %bitcast.15), custom_call_target="tpu_custom_call" | custom-call | tf_op jit(solution)/shard_map/weights/pallas_call | solution.py:205
  46.3 5.1 %all-to-all-done.2 = f32[32,8,96]{2,1,0:T(8,128)S(1)} async-done(((f32[32,8,96]{2,1,0:T(8,128)}), f32[32,8,96]{2,1,0:T(8,128)S(1)}, u32[]{:S(2)}, u32[]{:S(2)}) %all-to-all-start.2) | async-done | bytes 98336 | tf_op jit(solution)/shard_map/all_to_all | solution.py:196
  51.4 0.6 %reduce_sum.9 = f32[8,96]{1,0:T(8,128)} reduce(f32[32,8,96]{2,1,0:T(8,128)S(1)} %all-to-all-done.2, f32[]{:T(128)} %constant.1.clone.1), dimensions={0}, to_apply=%region_0.0 | reduce | flops 23808 | bytes 101380 | tf_op jit(solution)/shard_map/reduce_sum | solution.py:219
Async XLA Ops:
  0.6 1.0 %copy-start.4 = (bf16[8,64,384]{2,1,0:T(8,128)(2,1)S(1)}, bf16[8,64,384]{2,1,0:T(8,128)(2,1)}, u32[]{:S(2)}) copy-start(bf16[8,64,384]{2,1,0:T(8,128)(2,1)} %param.5) | copy-start | bytes 1179652
  1.6 1.0 %copy-start.6 = (bf16[8,64,384]{2,1,0:T(8,128)(2,1)S(1)}, bf16[8,64,384]{2,1,0:T(8,128)(2,1)}, u32[]{:S(2)}) copy-start(bf16[8,64,384]{2,1,0:T(8,128)(2,1)} %param.9) | copy-start | bytes 1179652
  2.6 0.7 %copy-start.12 = (bf16[384,8]{0,1:T(8,128)(2,1)S(1)}, bf16[384,8]{0,1:T(8,128)(2,1)}, u32[]{:S(2)}) copy-start(bf16[384,8]{0,1:T(8,128)(2,1)} %param.6) | copy-start | bytes 18436
  3.9 14.2 %copy-start.10 = (f32[2,8,512]{2,1,0:T(8,128)}, f32[2,8,512]{2,1,0:T(8,128)S(1)}, u32[]{:S(2)}) copy-start(f32[2,8,512]{2,1,0:T(8,128)S(1)} %get-tuple-element.16.soft_ref) | copy-start | bytes 98308
  18.1 4.5 %copy-start.8 = (bf16[8,16,384]{2,1,0:T(8,128)(2,1)}, bf16[8,16,384]{2,1,0:T(8,128)(2,1)S(1)}, u32[]{:S(2)}) copy-start(bf16[8,16,384]{2,1,0:T(8,128)(2,1)S(1)} %all_to_all.15.recv_ref) | copy-start | bytes 294916
  18.1 1.3 %copy-start = (bf16[1,384,1536]{2,1,0:T(8,128)(2,1)S(1)}, bf16[1,384,1536]{2,1,0:T(8,128)(2,1)}, u32[]{:S(2)}) copy-start(bf16[1,384,1536]{2,1,0:T(8,128)(2,1)} %param.7) | copy-start | bytes 3538948
  19.4 1.3 %copy-start.2 = (bf16[1,384,1536]{2,1,0:T(8,128)(2,1)S(1)}, bf16[1,384,1536]{2,1,0:T(8,128)(2,1)}, u32[]{:S(2)}) copy-start(bf16[1,384,1536]{2,1,0:T(8,128)(2,1)} %param.8) | copy-start | bytes 3538948
  20.7 13.2 %copy-start.5 = (bf16[8,64,384]{2,1,0:T(8,128)(2,1)S(1)}, bf16[8,64,384]{2,1,0:T(8,128)(2,1)}, u32[]{:S(2)}) copy-start(bf16[8,64,384]{2,1,0:T(8,128)(2,1)} %param.5) | copy-start | bytes 1179652
  20.7 13.2 %copy-start.7 = (bf16[8,64,384]{2,1,0:T(8,128)(2,1)S(1)}, bf16[8,64,384]{2,1,0:T(8,128)(2,1)}, u32[]{:S(2)}) copy-start(bf16[8,64,384]{2,1,0:T(8,128)(2,1)} %param.9) | copy-start | bytes 1179652
  20.7 13.2 %copy-start.13 = (bf16[384,8]{0,1:T(8,128)(2,1)S(1)}, bf16[384,8]{0,1:T(8,128)(2,1)}, u32[]{:S(2)}) copy-start(bf16[384,8]{0,1:T(8,128)(2,1)} %param.6) | copy-start | bytes 18436
  20.7 22.4 %copy-start.3 = (bf16[1,384,1536]{2,1,0:T(8,128)(2,1)S(1)}, bf16[1,384,1536]{2,1,0:T(8,128)(2,1)}, u32[]{:S(2)}) copy-start(bf16[1,384,1536]{2,1,0:T(8,128)(2,1)} %param.8) | copy-start | bytes 3538948
  22.7 20.5 %copy-start.1 = (bf16[1,384,1536]{2,1,0:T(8,128)(2,1)S(1)}, bf16[1,384,1536]{2,1,0:T(8,128)(2,1)}, u32[]{:S(2)}) copy-start(bf16[1,384,1536]{2,1,0:T(8,128)(2,1)} %param.7) | copy-start | bytes 3538948
  22.7 11.3 %all-to-all-start.1 = ((bf16[8,16,384]{2,1,0:T(8,128)(2,1)}), bf16[8,16,384]{2,1,0:T(8,128)(2,1)}, u32[]{:S(2)}, u32[]{:S(2)}) async-start(bf16[8,16,384]{2,1,0:T(8,128)(2,1)} %expert.1), calls=%async_computation.1 | async-start | bytes 196608 | tf_op jit(solution)/shard_map/all_to_all | solution.py:183
  33.9 0.8 %copy-start.11 = (f32[2,8,512]{2,1,0:T(8,128)S(1)}, f32[2,8,512]{2,1,0:T(8,128)}, u32[]{:S(2)}) copy-start(f32[2,8,512]{2,1,0:T(8,128)} %copy-done.10) | copy-start | bytes 98308
  37.3 0.7 %copy-start.9 = (f32[8,4,8,96]{3,2,1,0:T(8,128)}, f32[8,4,8,96]{3,2,1,0:T(8,128)S(1)}, u32[]{:S(2)}) copy-start(f32[8,4,8,96]{3,2,1,0:T(8,128)S(1)} %get-tuple-element.23) | copy-start | bytes 294916
  38.0 13.4 %all-to-all-start.2 = ((f32[32,8,96]{2,1,0:T(8,128)}), f32[32,8,96]{2,1,0:T(8,128)S(1)}, u32[]{:S(2)}, u32[]{:S(2)}) async-start(f32[32,8,96]{2,1,0:T(8,128)} %bitcast.21), calls=%async_computation.2 | async-start | bytes 262144 | tf_op jit(solution)/shard_map/all_to_all | solution.py:196

commit v3 on v2

--- a/solution.py
+++ b/solution.py
@@ -11,6 +11,7 @@
 F32 = jnp.float32
 BF16 = jnp.bfloat16
 VMEM_BYTES = 24 * 1024 * 1024
+WHOLE_BYTES = 56 * 1024 * 1024
 
 
 def gelu_pair(value):
@@ -48,13 +49,6 @@
     return jnp.sum(block.reshape(rows // images, images, columns), axis=1)
 
 
-def pair_rows(first, second, groups):
-    images = first.shape[0] // groups
-    first = first.reshape(groups, images, first.shape[1])
-    second = second.reshape(groups, images, second.shape[1])
-    return jnp.concatenate((first, second), axis=1).astype(BF16)
-
-
 def split_rows(pairs):
     groups, both, width = pairs.shape
     wide = pairs.astype(F32)
@@ -63,11 +57,18 @@
     return first.astype(BF16), second.astype(BF16)
 
 
-def slots_kernel(images, tokens_ref, router_ref, grad_ref, sent_ref, soft_ref):
+def order_rows(me, rows):
+    count = rows.shape[0]
+    to = lax.broadcasted_iota(jnp.int32, (count, count), 0) ^ me
+    pick = jnp.where(lax.broadcasted_iota(jnp.int32, (count, count), 1) == to, 1.0, 0.0)
+    return dot(pick.astype(BF16), rows, 1, 0).astype(BF16)
+
+
+def slots_kernel(images, me_ref, tokens_ref, router_ref, grad_ref, soft_ref, *sent):
     tokens = tokens_ref[...]
     columns = tokens.shape[0]
     experts = router_ref.shape[0]
-    logits = dot(router_ref[...], tokens, 1, 1)
+    logits = dot(order_rows(me_ref[0], router_ref[...]), tokens, 1, 1)
     mask = own_image(experts, images, columns)
     top = jnp.max(logits, axis=0, keepdims=True)
     combine = jnp.exp(logits - top)
@@ -80,30 +81,64 @@
     combine_block = jnp.where(mask, spread_rows(combine, images), 0.0)
     slot_in = dot(block.astype(BF16), tokens, 1, 0)
     slot_grad = dot(combine_block.astype(BF16), grad_ref[...], 1, 0)
-    sent_ref[...] = pair_rows(slot_in, slot_grad, experts)
-
-
-def expert_kernel(recv_ref, win_ref, wout_ref, back_ref, *, step):
-    slots, cotan = split_rows(recv_ref[...])
+    write_pairs(sent, slot_in, slot_grad)
+
+
+def write_pairs(refs, first, second):
+    images = first.shape[0] // len(refs)
+    for k, ref in enumerate(refs):
+        rows = slice(k * images, (k + 1) * images)
+        ref[...] = jnp.concatenate((first[rows], second[rows]), axis=0).astype(BF16)
+
+
+def read_pairs(refs):
+    parts = [ref[...].astype(F32) for ref in refs]
+    half = parts[0].shape[0] // 2
+    first = jnp.concatenate([part[:half] for part in parts], axis=0)
+    second = jnp.concatenate([part[half:] for part in parts], axis=0)
+    return first.astype(BF16), second.astype(BF16)
+
+
+def expert_kernel(owners, step, *refs):
+    recv, (win_hbm, wout_hbm) = refs[:owners], refs[owners : owners + 2]
+    back_refs, all_ref = refs[owners + 2 : 2 * owners + 2], refs[2 * owners + 2]
+    win_ref, wout_ref, sems = refs[2 * owners + 3 :]
+    starts = range(0, win_ref.shape[1], step)
+
+    def load(which, chunk):
+        source, target = ((win_hbm, win_ref), (wout_hbm, wout_ref))[which]
+        part = (slice(None), pl.ds(chunk * step, step))
+        return pltpu.make_async_copy(source.at[part], target.at[part], sems.at[which, chunk])
+
+    for chunk in range(len(starts)):
+        load(0, chunk).start()
+        load(1, chunk).start()
+    for k, ref in enumerate(recv):
+        all_ref[k] = ref[...]
+    slots, cotan = read_pairs(recv)
     out = jnp.zeros(slots.shape, F32)
     back = jnp.zeros(slots.shape, F32)
-    for start in range(0, win_ref.shape[1], step):
+    for chunk, start in enumerate(starts):
+        load(0, chunk).wait()
+        load(1, chunk).wait()
         w_in = win_ref[:, start : start + step]
         w_out = wout_ref[:, start : start + step]
         value, slope = gelu_pair(dot(slots, w_in, 1, 0))
         pre_grad = dot(cotan, w_out, 1, 0) * slope
         out = out + dot(value.astype(BF16), w_out, 1, 1)
         back = back + dot(pre_grad.astype(BF16), w_in, 1, 1)
-    back_ref[...] = pair_rows(out, back, recv_ref.shape[0])
+    write_pairs(back_refs, out, back)
 
 
 def tokens_kernel(
-    images, back_ref, tokens_ref, router_ref, grad_ref, soft_ref, out_ref, send_ref
+    images, me_ref, tokens_ref, router_ref, grad_ref, soft_ref, *refs
 ):
+    back_refs, (out_ref, send_ref) = refs[:-2], refs[-2:]
+    me = me_ref[0]
     tokens = tokens_ref[...]
     columns = tokens.shape[0]
     experts = router_ref.shape[0]
-    slot_out, slot_in_grad = split_rows(back_ref[...])
+    slot_out, slot_in_grad = read_pairs(back_refs)
     dispatch, combine = soft_ref[0], soft_ref[1]
     mask = own_image(experts, images, columns)
     comb = fold_rows(jnp.where(mask, dot(slot_out, grad_ref[...], 1, 1), 0.0), images)
@@ -112,23 +147,27 @@
     mean = jnp.sum(dispatch_block * disp, axis=1, keepdims=True)
     from_dispatch = fold_rows(dispatch_block * (disp - mean), images)
     from_combine = combine * (comb - jnp.sum(combine * comb, axis=0, keepdims=True))
-    logit_grad = (from_combine + from_dispatch).astype(BF16)
-    out = dot(dispatch_block.astype(BF16), slot_in_grad, 0, 0)
-    out = out + dot(logit_grad, router_ref[...], 0, 0)
-    out_ref[...] = out.astype(BF16)
+    logit_grad = order_rows(me, (from_combine + from_dispatch).astype(BF16))
     part = dot(logit_grad, tokens, 1, 0)
     owners, shares, _, width = send_ref.shape
     for share in range(shares):
         piece = part[:, share * width : (share + 1) * width]
         for owner in range(owners):
             send_ref[owner, share] = piece
-
-
-def weights_kernel(share_ref, spread_ref, win_ref, wout_ref, win_out, wout_out, *, step):
-    width = spread_ref.shape[-1]
+    out = dot(dispatch_block.astype(BF16), slot_in_grad, 0, 0)
+    out = out + dot(logit_grad, router_ref[...], 0, 0)
+    out_ref[...] = out.astype(BF16)
+
+
+def weights_kernel(share_ref, *refs, step):
+    spread, (win_ref, wout_ref, win_out, wout_out) = refs[:-4], refs[-4:]
     row_count = win_out.shape[0]
-    slots, cotan = split_rows(spread_ref[...].reshape((-1,) + spread_ref.shape[2:]))
-    shape = (row_count, width)
+    pairs = [
+        split_rows(ref[...].reshape((-1,) + ref.shape[-2:])) for ref in spread
+    ]
+    slots = jnp.concatenate([pair[0] for pair in pairs], axis=0)
+    cotan = jnp.concatenate([pair[1] for pair in pairs], axis=0)
+    shape = (row_count, slots.shape[1])
     row = lax.broadcasted_iota(jnp.int32, shape, 0) + share_ref[0] * row_count
     pick = jnp.where(lax.broadcasted_iota(jnp.int32, shape, 1) == row, 1.0, 0.0).astype(BF16)
     own_slots = dot(pick, slots, 1, 1).astype(BF16)
@@ -145,6 +184,15 @@
         pre_grad = dot(cotan, wout_ref[:, part], 1, 0) * slope
         win_out[:, part] += dot(own_slots, pre_grad.astype(BF16), 1, 0)
         wout_out[:, part] += dot(own_cotan, value.astype(BF16), 1, 0)
+
+
+def exchange(chunks, axis):
+    count = len(chunks)
+    got = [None] * count
+    got[0] = chunks[0]
+    for k in range(count - 1, 0, -1):
+        got[k] = lax.ppermute(chunks[k], axis, [(i, i ^ k) for i in range(count)])
+    return got
 
 
 def on_device(tokens, router, w_in, w_out, out_grad):
@@ -159,40 +207,56 @@
     router_rows = router.T
     w_in2, w_out2 = w_in.reshape(width, hidden), w_out.reshape(width, hidden)
     params = pltpu.CompilerParams(vmem_limit_bytes=VMEM_BYTES)
+    whole = pltpu.CompilerParams(vmem_limit_bytes=WHOLE_BYTES)
 
     def struct(shape, dtype):
         return jax.ShapeDtypeStruct(shape, dtype)
 
-    sent, soft = pl.pallas_call(
+    me = lax.axis_index("expert").reshape(1)
+    share = lax.axis_index("dp").reshape(1)
+    in_smem = pl.BlockSpec(memory_space=pltpu.SMEM)
+    in_vmem = pl.BlockSpec(memory_space=pltpu.VMEM)
+    in_place = pl.BlockSpec(memory_space=pl.ANY)
+    chunk = struct((2 * images, width), BF16)
+    soft, *sent = pl.pallas_call(
         functools.partial(slots_kernel, images),
-        out_shape=(
-            struct((experts, 2 * images, width), BF16),
-            struct((2, experts, columns), F32),
-        ),
-        compiler_params=params,
+        in_specs=[in_smem] + [in_vmem] * 3,
+        out_shape=[struct((2, experts, columns), F32)] + [chunk] * owners,
+        compiler_params=whole,
         name="slots",
-    )(tokens2, router_rows, grad2)
-    recv = lax.all_to_all(sent, "expert", split_axis=0, concat_axis=0, tiled=True)
-    back = pl.pallas_call(
-        functools.partial(expert_kernel, step=512),
-        out_shape=struct(recv.shape, BF16),
-        compiler_params=params,
+    )(me, tokens2, router_rows, grad2)
+    recv = exchange(sent, "expert")
+    step = 512
+    *back, recv_all = pl.pallas_call(
+        functools.partial(expert_kernel, owners, step),
+        in_specs=[in_vmem] * owners + [in_place] * 2,
+        out_shape=[chunk] * owners + [struct((owners, 2 * images, width), BF16)],
+        scratch_shapes=[
+            pltpu.VMEM((width, hidden), BF16),
+            pltpu.VMEM((width, hidden), BF16),
+            pltpu.SemaphoreType.DMA((2, hidden // step)),
+        ],
+        compiler_params=whole,
         name="expert",
-    )(recv, w_in2, w_out2)
-    recv, back = lax.optimization_barrier((recv, back))
-    slots_back = lax.all_to_all(back, "expert", split_axis=0, concat_axis=0, tiled=True)
-    spread = lax.all_gather(recv, "dp", axis=0, tiled=False)
+    )(*recv, w_in2, w_out2)
+    slots_back = exchange(back, "expert")
+    few = shares * owners * images <= 512
+    if few:
+        spread = exchange([recv_all] * shares, "dp")
+    else:
+        spread = [lax.all_gather(recv_all, "dp", axis=0, tiled=False)]
 
     tokens_grad, router_send = pl.pallas_call(
         functools.partial(tokens_kernel, images),
+        in_specs=[in_smem] + [in_vmem] * (4 + owners),
         out_shape=(
             struct((columns, width), BF16),
             struct((owners, shares, experts, row_count), F32),
         ),
         compiler_params=params,
         name="tokens",
-    )(slots_back, tokens2, router_rows, grad2, soft)
-    spread, router_send = lax.optimization_barrier((spread, router_send))
+    )(me, tokens2, router_rows, grad2, soft, *slots_back)
+    *spread, router_send = lax.optimization_barrier((*spread, router_send))
     router_parts = lax.all_to_all(
         router_send.reshape(owners * shares, experts, row_count),
         ("expert", "dp"),
@@ -201,13 +265,16 @@
         tiled=True,
     )
 
-    group = max(1, min(shares, 256 // (owners * images)))
+    if few:
+        blocks = [pl.BlockSpec(recv_all.shape, lambda i: (0, 0, 0))] * shares
+    else:
+        blocks = [pl.BlockSpec((1,) + recv_all.shape, lambda i: (i, 0, 0, 0))]
     w_in_grad, w_out_grad = pl.pallas_call(
         functools.partial(weights_kernel, step=512),
-        grid=(shares // group,),
+        grid=(1 if few else shares,),
         in_specs=[
-            pl.BlockSpec(memory_space=pltpu.SMEM),
-            pl.BlockSpec((group,) + recv.shape, lambda i: (i, 0, 0, 0)),
+            in_smem,
+            *blocks,
             pl.BlockSpec((width, hidden), lambda i: (0, 0)),
             pl.BlockSpec((width, hidden), lambda i: (0, 0)),
         ],
@@ -215,7 +282,7 @@
         out_shape=[struct((row_count, hidden), F32)] * 2,
         compiler_params=params,
         name="weights",
-    )(lax.axis_index("dp").reshape(1), spread, w_in2, w_out2)
+    )(share, *spread, w_in2, w_out2)
     router_grad = jnp.sum(router_parts, axis=0).T
     return (
         tokens_grad.reshape(tokens.shape),

time: 52.6 us -> 64.3 us (1.22)
  waiting for transfers between devices: 5.53 us -> 28.7 us
  blocking collectives: 20.9 us -> 0 us
  starting transfers between devices: 9.28 us -> 20 us
  local copies, waits for them, and re-layouts: 6.71 us -> 2.19 us
  Pallas kernels: 8.27 us -> 11.6 us
    ppermute x0 -> x17, waiting for transfers between devices: none -> 24.5 us  [exchange(): got[k] = lax.ppermute(chunks[k], axis, [(i, i ^ k) for i in range(count)])]
    ppermute x0 -> x17, starting transfers between devices: none -> 17.4 us  [exchange(): got[k] = lax.ppermute(chunks[k], axis, [(i, i ^ k) for i in range(count)])]
    all_to_all x1 -> x0, blocking collectives: 14.2 us -> none  [on_device(): lax.all_to_all(sent, 'expert', split_axis=0, concat_axis=0, tiled=True)]
    all_gather x1 -> x0, blocking collectives: 6.7 us -> none  [on_device(): spread = lax.all_gather(recv, 'dp', axis=0, tiled=False)]
    unnamed x28 -> x30, local copies, waits for them, and re-layouts: 6.71 us -> 2.19 us
    all_to_all x1 -> x0, starting transfers between devices: 4.12 us -> none  [on_device(): lax.all_to_all(back, 'expert', split_axis=0, concat_axis=0, tiled=True)]
    pallas_call x4, Pallas kernels: 8.27 us -> 11.6 us  [the longest x1 4.27 us: on_device(): pl.pallas_call(functools.partial(expert_kernel, owners, step), in_specs=[...]
    all_to_all x1, starting transfers between devices: 5.17 us -> 2.59 us  [on_device(): lax.all_to_all(router_send.reshape(owners * shares, experts, row_count),...]
  transfers between devices with their start and end apart: 2 -> 18, of which waited for: 2 -> 10; matrix products, arithmetic and copies ran while one was open for 0% -> 0% of each run, Pallas kernels for 6% -> 8%
where the time goes in v3:
time: 64.3 us; the launch traced here: 63.9 us
  waiting for transfers between devices  28.7 us (45%)
  starting transfers between devices  20 us (31%)
  Pallas kernels  11.6 us (18%)
  local copies, waits for them, and re-layouts  2.19 us (3%)
  between operations  0.79 us (1%)
    ppermute x17, waiting for transfers between devices, exchange(): got[k] = lax.ppermute(chunks[k], axis, [(i, i ^ k) for i in range(count)])  24.5 us
    ppermute x17, starting transfers between devices, exchange(): got[k] = lax.ppermute(chunks[k], axis, [(i, i ^ k) for i in range(count)])  17.4 us
    pallas_call x1, Pallas kernels, on_device(): pl.pallas_call(functools.partial(expert_kernel, owners, step), in_specs=[...  4.27 us
    all_to_all x1, waiting for transfers between devices, on_device(): lax.all_to_all(router_send.reshape(owners * shares, experts, row_count),...  4.19 us
    pallas_call x1, Pallas kernels, on_device(): pl.pallas_call(functools.partial(weights_kernel, step=512), grid=(1 if fe...  3.12 us
    all_to_all x1, starting transfers between devices, on_device(): lax.all_to_all(router_send.reshape(owners * shares, experts, row_count),...  2.59 us
    pallas_call x1, Pallas kernels, on_device(): pl.pallas_call(functools.partial(slots_kernel, images), in_specs=[in_smem...  2.43 us
    unnamed x30, local copies, waits for them, and re-layouts  2.19 us
  transfers between devices with their start and end apart: 18, of which 10 were waited for; matrix products, arithmetic and copies ran while one was open for 0% of the time, Pallas kernels for 8%

profile of v3, /device:TPU:0, one launch (start us, length us, event | category | flops | bytes accessed | tf_op | source)
XLA Modules:
  0.0 63.9 jit_solution(1049397556735411441)
XLA Ops:
  0.6 2.4 %slots.1 = (f32[2,8,512]{2,1,0:T(8,128)}, bf16[16,384]{1,0:T(8,128)(2,1)}, bf16[16,384]{1,0:T(8,128)(2,1)}, bf16[16,384]{1,0:T(8,128)(2,1)}, bf16[16,384]{1,0:T(...) custom-call(s32[1]{0:T(128)} %bitcast.me_ref, ...), custom_call_target="tpu_custom_call" | custom-call | tf_op jit(solution)/shard_map/slots/pallas_call | solution.py:221
  3.1 2.9 %collective-permute-start = (bf16[16,384]{1,0:T(8,128)(2,1)}, bf16[16,384]{1,0:T(8,128)(2,1)S(1)}, u32[]{:S(2)}, u32[]{:S(2)}) collective-permute-start(bf16[16,384]{1,0:T(8,128)(2,1)} %get-tuple-element.33), channel_id=1, source_target_pairs={{0,4},{4,0},{8,12},{12,8},{16,20},{20,16},{24,28},{28,24},{1,5},{5... | collective-permute-start | bytes 36872 | tf_op jit(solution)/shard_map/ppermute | solution.py:194
  6.0 1.6 %collective-permute-start.1 = (bf16[16,384]{1,0:T(8,128)(2,1)}, bf16[16,384]{1,0:T(8,128)(2,1)S(1)}, u32[]{:S(2)}, u32[]{:S(2)}) collective-permute-start(bf16[16,384]{1,0:T(8,128)(2,1)} %get-tuple-element.34), channel_id=1, source_target_pairs={{0,8},{4,12},{8,0},{12,4},{16,24},{20,28},{24,16},{28,20},{1,9},{5... | collective-permute-start | bytes 36872 | tf_op jit(solution)/shard_map/ppermute | solution.py:194
  7.6 0.0 collective-permute-start.2
  7.6 3.0 %collective-permute-start.3 = (bf16[16,384]{1,0:T(8,128)(2,1)}, bf16[16,384]{1,0:T(8,128)(2,1)S(1)}, u32[]{:S(2)}, u32[]{:S(2)}) collective-permute-start(bf16[16,384]{1,0:T(8,128)(2,1)} %get-tuple-element.36), channel_id=1, source_target_pairs={{0,16},{4,20},{8,24},{12,28},{16,0},{20,4},{24,8},{28,12},{1,17},{... | collective-permute-start | bytes 36872 | tf_op jit(solution)/shard_map/ppermute | solution.py:194
  10.6 1.3 %collective-permute-start.4 = (bf16[16,384]{1,0:T(8,128)(2,1)}, bf16[16,384]{1,0:T(8,128)(2,1)S(1)}, u32[]{:S(2)}, u32[]{:S(2)}) collective-permute-start(bf16[16,384]{1,0:T(8,128)(2,1)} %get-tuple-element.37), channel_id=1, source_target_pairs={{0,20},{4,16},{8,28},{12,24},{16,4},{20,0},{24,12},{28,8},{1,21},{... | collective-permute-start | bytes 36872 | tf_op jit(solution)/shard_map/ppermute | solution.py:194
  11.9 0.0 collective-permute-done.refs_1_
  11.9 3.6 %collective-permute-start.5 = (bf16[16,384]{1,0:T(8,128)(2,1)}, bf16[16,384]{1,0:T(8,128)(2,1)S(1)}, u32[]{:S(2)}, u32[]{:S(2)}) collective-permute-start(bf16[16,384]{1,0:T(8,128)(2,1)} %get-tuple-element.38), channel_id=1, source_target_pairs={{0,24},{4,28},{8,16},{12,20},{16,8},{20,12},{24,0},{28,4},{1,25},{... | collective-permute-start | bytes 36872 | tf_op jit(solution)/shard_map/ppermute | solution.py:194
  15.5 0.0 collective-permute-done.1.refs_2_
  15.5 0.1 collective-permute-start.6
  15.5 0.0 collective-permute-done.2.refs_3_
  15.5 0.0 collective-permute-done.3.refs_4_
  15.5 0.8 %collective-permute-done.4.refs_5_ = bf16[16,384]{1,0:T(8,128)(2,1)S(1)} collective-permute-done((bf16[16,384]{1,0:T(8,128)(2,1)}, bf16[16,384]{1,0:T(8,128)(2,1)S(1)}, u32[]{:S(2)}, u32[]{:S(2)}) %collective-permute-start.4) | collective-permute-done | bytes 12320 | tf_op jit(solution)/shard_map/ppermute | solution.py:194
  16.3 1.3 %collective-permute-done.5.refs_6_ = bf16[16,384]{1,0:T(8,128)(2,1)S(1)} collective-permute-done((bf16[16,384]{1,0:T(8,128)(2,1)}, bf16[16,384]{1,0:T(8,128)(2,1)S(1)}, u32[]{:S(2)}, u32[]{:S(2)}) %collective-permute-start.5) | collective-permute-done | bytes 12320 | tf_op jit(solution)/shard_map/ppermute | solution.py:194
  17.6 4.5 %collective-permute-done.6.refs_7_ = bf16[16,384]{1,0:T(8,128)(2,1)S(1)} collective-permute-done((bf16[16,384]{1,0:T(8,128)(2,1)}, bf16[16,384]{1,0:T(8,128)(2,1)S(1)}, u32[]{:S(2)}, u32[]{:S(2)}) %collective-permute-start.6) | collective-permute-done | bytes 12320 | tf_op jit(solution)/shard_map/ppermute | solution.py:194
  22.1 0.0 copy-done.8
  22.1 0.6 copy-done.14
  22.7 0.0 copy-start.1
  22.7 4.3 %expert.1 = (bf16[16,384]{1,0:T(8,128)(2,1)}, bf16[16,384]{1,0:T(8,128)(2,1)}, bf16[16,384]{1,0:T(8,128)(2,1)}, bf16[16,384]{1,0:T(8,128)(2,1)}, bf16[16,384]{1,...) custom-call(bf16[16,384]{1,0:T(8,128)(2,1)} %get-tuple-element.32.re, ...), custom_call_target="tpu_custom_call" | custom-call | tf_op jit(solution)/shard_map/expert/pallas_call | solution.py:230
  27.0 0.0 copy-start
  27.0 0.1 collective-permute-start.16
  27.1 1.6 %collective-permute-start.15 = (bf16[8,16,384]{2,1,0:T(8,128)(2,1)}, bf16[8,16,384]{2,1,0:T(8,128)(2,1)S(1)}, u32[]{:S(2)}, u32[]{:S(2)}) collective-permute-start(bf16[8,16,384]{2,1,0:T(8,128)(2,1)} %get-tuple-element.51.refs_0_), channel_id=1, source_target_pairs={{0,2},{1,3},{2,0},{3,1},{4,6},{5,7},{6,4},{7,5},{8,10},{9,11},{10,... | collective-permute-start | bytes 294920 | tf_op jit(solution)/shard_map/ppermute | solution.py:194
  28.7 0.3 collective-permute-start.14
  28.9 0.5 collective-permute-start.7
  29.5 0.0 collective-permute-start.8
  29.5 3.4 %collective-permute-done.7.refs_1_ = bf16[16,384]{1,0:T(8,128)(2,1)S(1)} collective-permute-done((bf16[16,384]{1,0:T(8,128)(2,1)}, bf16[16,384]{1,0:T(8,128)(2,1)S(1)}, u32[]{:S(2)}, u32[]{:S(2)}) %collective-permute-start.7) | collective-permute-done | bytes 12320 | tf_op jit(solution)/shard_map/ppermute | solution.py:194
  32.8 0.0 collective-permute-start.9
  32.8 0.5 collective-permute-done.8.refs_2_
  33.4 0.2 collective-permute-start.10
  33.5 4.1 %collective-permute-done.9.refs_3_ = bf16[16,384]{1,0:T(8,128)(2,1)S(1)} collective-permute-done((bf16[16,384]{1,0:T(8,128)(2,1)}, bf16[16,384]{1,0:T(8,128)(2,1)S(1)}, u32[]{:S(2)}, u32[]{:S(2)}) %collective-permute-start.9) | collective-permute-done | bytes 12320 | tf_op jit(solution)/shard_map/ppermute | solution.py:194
  37.6 0.0 collective-permute-start.11
  37.6 0.5 collective-permute-done.10.refs_4_
  38.2 1.8 %collective-permute-start.12 = (bf16[16,384]{1,0:T(8,128)(2,1)}, bf16[16,384]{1,0:T(8,128)(2,1)S(1)}, u32[]{:S(2)}, u32[]{:S(2)}) collective-permute-start(bf16[16,384]{1,0:T(8,128)(2,1)} %get-tuple-element.46), channel_id=1, source_target_pairs={{0,24},{4,28},{8,16},{12,20},{16,8},{20,12},{24,0},{28,4},{1,25},{... | collective-permute-start | bytes 36872 | tf_op jit(solution)/shard_map/ppermute | solution.py:194
  40.0 3.3 %collective-permute-done.11.refs_5_ = bf16[16,384]{1,0:T(8,128)(2,1)S(1)} collective-permute-done((bf16[16,384]{1,0:T(8,128)(2,1)}, bf16[16,384]{1,0:T(8,128)(2,1)S(1)}, u32[]{:S(2)}, u32[]{:S(2)}) %collective-permute-start.11) | collective-permute-done | bytes 12320 | tf_op jit(solution)/shard_map/ppermute | solution.py:194
  43.3 0.5 collective-permute-start.13
  43.8 0.0 collective-permute-done.12.refs_6_
  43.9 6.1 %collective-permute-done.13.refs_7_ = bf16[16,384]{1,0:T(8,128)(2,1)S(1)} collective-permute-done((bf16[16,384]{1,0:T(8,128)(2,1)}, bf16[16,384]{1,0:T(8,128)(2,1)S(1)}, u32[]{:S(2)}, u32[]{:S(2)}) %collective-permute-start.13) | collective-permute-done | bytes 12320 | tf_op jit(solution)/shard_map/ppermute | solution.py:194
  50.0 0.7 %copy-done.7 = bf16[16,384]{1,0:T(8,128)(2,1)S(1)} copy-done((bf16[16,384]{1,0:T(8,128)(2,1)S(1)}, bf16[16,384]{1,0:T(8,128)(2,1)}, u32[]{:S(2)}) %copy-start.7) | copy-done | bytes 12312
  50.7 1.8 %tokens.1 = (bf16[512,384]{1,0:T(8,128)(2,1)}, f32[8,4,8,96]{3,2,1,0:T(8,128)}) custom-call(s32[1]{0:T(128)} %bitcast.me_ref, bf16[512,384]{1,0:T(8,128)(2,1)S(1)} %bitcast.17, bf16[8,384]{1,0:T(8,128)(2,1)S(1)} %bitcast.21, bf16[512,384]{1,0:T(8,128)(2,1)S(1)} %bitcast.19, f32[2,8,512]{2,1,0:T(8,128)S(1)} %copy-done.5, bf16[16,384]{1,0:T(8,128)(2,1)S(1)} %copy-done.7, ...), custom_call_target="tpu_custom_call" | custom-call | tf_op jit(solution)/shard_map/tokens/pallas_call | solution.py:249
  52.4 0.0 collective-permute-done.16.refs_3_
  52.4 0.0 collective-permute-done.15.refs_2_
  52.4 0.0 collective-permute-done.14.refs_1_
  52.4 2.6 %all-to-all-start = ((f32[32,8,96]{2,1,0:T(8,128)}), f32[32,8,96]{2,1,0:T(8,128)S(1)}, u32[]{:S(2)}, u32[]{:S(2)}) async-start(f32[32,8,96]{2,1,0:T(8,128)} %bitcast.10), calls=%async_computation | async-start | bytes 262144 | tf_op jit(solution)/shard_map/all_to_all | solution.py:260
  55.0 0.0 copy-start.4
  55.1 0.9 %copy-done.4 = bf16[8,16,384]{2,1,0:T(8,128)(2,1)S(1)} copy-done((bf16[8,16,384]{2,1,0:T(8,128)(2,1)S(1)}, bf16[8,16,384]{2,1,0:T(8,128)(2,1)}, u32[]{:S(2)}) %copy-start.4) | copy-done | bytes 98328
  55.9 3.1 %weights.1 = (f32[96,1536]{1,0:T(8,128)}, f32[96,1536]{1,0:T(8,128)}) custom-call(s32[1]{0:T(128)} %bitcast.7.share_ref, bf16[8,16,384]{2,1,0:T(8,128)(2,1)S(1)} %copy-done.4, bf16[8,16,384]{2,1,0:T(8,128)(2,1)S(1)} %collective-permute-done.14.refs_1_, bf16[8,16,384]{2,1,0:T(8,128)(2,1)S(1)} %collective-permute-done.15.refs_2_, ...), custom_call_target="tpu_custom_call" | custom-call | tf_op jit(solution)/shard_map/weights/pallas_call | solution.py:272
  59.1 4.2 %all-to-all-done = f32[32,8,96]{2,1,0:T(8,128)S(1)} async-done(((f32[32,8,96]{2,1,0:T(8,128)}), f32[32,8,96]{2,1,0:T(8,128)S(1)}, u32[]{:S(2)}, u32[]{:S(2)}) %all-to-all-start) | async-done | bytes 98336 | tf_op jit(solution)/shard_map/all_to_all | solution.py:260
  63.3 0.6 reduce_sum.9
  (23 shorter events, 0.0 us)
Async XLA Ops:
  3.1 8.8 %collective-permute-start = (bf16[16,384]{1,0:T(8,128)(2,1)}, bf16[16,384]{1,0:T(8,128)(2,1)S(1)}, u32[]{:S(2)}, u32[]{:S(2)}) collective-permute-start(bf16[16,384]{1,0:T(8,128)(2,1)} %get-tuple-element.33), channel_id=1, source_target_pairs={{0,4},{4,0},{8,12},{12,8},{16,20},{20,16},{24,28},{28,24},{1,5},{5... | collective-permute-start | bytes 36872 | tf_op jit(solution)/shard_map/ppermute | solution.py:194
  6.0 9.5 %collective-permute-start.1 = (bf16[16,384]{1,0:T(8,128)(2,1)}, bf16[16,384]{1,0:T(8,128)(2,1)S(1)}, u32[]{:S(2)}, u32[]{:S(2)}) collective-permute-start(bf16[16,384]{1,0:T(8,128)(2,1)} %get-tuple-element.34), channel_id=1, source_target_pairs={{0,8},{4,12},{8,0},{12,4},{16,24},{20,28},{24,16},{28,20},{1,9},{5... | collective-permute-start | bytes 36872 | tf_op jit(solution)/shard_map/ppermute | solution.py:194
  7.6 7.9 %collective-permute-start.2 = (bf16[16,384]{1,0:T(8,128)(2,1)}, bf16[16,384]{1,0:T(8,128)(2,1)S(1)}, u32[]{:S(2)}, u32[]{:S(2)}) collective-permute-start(bf16[16,384]{1,0:T(8,128)(2,1)} %get-tuple-element.35), channel_id=1, source_target_pairs={{0,12},{4,8},{8,4},{12,0},{16,28},{20,24},{24,20},{28,16},{1,13},{... | collective-permute-start | bytes 36872 | tf_op jit(solution)/shard_map/ppermute | solution.py:194
  7.6 7.9 %collective-permute-start.3 = (bf16[16,384]{1,0:T(8,128)(2,1)}, bf16[16,384]{1,0:T(8,128)(2,1)S(1)}, u32[]{:S(2)}, u32[]{:S(2)}) collective-permute-start(bf16[16,384]{1,0:T(8,128)(2,1)} %get-tuple-element.36), channel_id=1, source_target_pairs={{0,16},{4,20},{8,24},{12,28},{16,0},{20,4},{24,8},{28,12},{1,17},{... | collective-permute-start | bytes 36872 | tf_op jit(solution)/shard_map/ppermute | solution.py:194
  10.6 5.7 %collective-permute-start.4 = (bf16[16,384]{1,0:T(8,128)(2,1)}, bf16[16,384]{1,0:T(8,128)(2,1)S(1)}, u32[]{:S(2)}, u32[]{:S(2)}) collective-permute-start(bf16[16,384]{1,0:T(8,128)(2,1)} %get-tuple-element.37), channel_id=1, source_target_pairs={{0,20},{4,16},{8,28},{12,24},{16,4},{20,0},{24,12},{28,8},{1,21},{... | collective-permute-start | bytes 36872 | tf_op jit(solution)/shard_map/ppermute | solution.py:194
  11.9 10.2 %copy-start.8 = (bf16[16,384]{1,0:T(8,128)(2,1)}, bf16[16,384]{1,0:T(8,128)(2,1)S(1)}, u32[]{:S(2)}) copy-start(bf16[16,384]{1,0:T(8,128)(2,1)S(1)} %collective-permute-done.refs_1_) | copy-start | bytes 36868
  11.9 5.7 %collective-permute-start.5 = (bf16[16,384]{1,0:T(8,128)(2,1)}, bf16[16,384]{1,0:T(8,128)(2,1)S(1)}, u32[]{:S(2)}, u32[]{:S(2)}) collective-permute-start(bf16[16,384]{1,0:T(8,128)(2,1)} %get-tuple-element.38), channel_id=1, source_target_pairs={{0,24},{4,28},{8,16},{12,20},{16,8},{20,12},{24,0},{28,4},{1,25},{... | collective-permute-start | bytes 36872 | tf_op jit(solution)/shard_map/ppermute | solution.py:194
  15.5 6.6 %copy-start.9 = (bf16[16,384]{1,0:T(8,128)(2,1)}, bf16[16,384]{1,0:T(8,128)(2,1)S(1)}, u32[]{:S(2)}) copy-start(bf16[16,384]{1,0:T(8,128)(2,1)S(1)} %collective-permute-done.1.refs_2_) | copy-start | bytes 36868
  15.5 6.6 %collective-permute-start.6 = (bf16[16,384]{1,0:T(8,128)(2,1)}, bf16[16,384]{1,0:T(8,128)(2,1)S(1)}, u32[]{:S(2)}, u32[]{:S(2)}) collective-permute-start(bf16[16,384]{1,0:T(8,128)(2,1)} %get-tuple-element.39), channel_id=1, source_target_pairs={{0,28},{4,24},{8,20},{12,16},{16,12},{20,8},{24,4},{28,0},{1,29},{... | collective-permute-start | bytes 36872 | tf_op jit(solution)/shard_map/ppermute | solution.py:194
  15.5 6.6 %copy-start.10 = (bf16[16,384]{1,0:T(8,128)(2,1)}, bf16[16,384]{1,0:T(8,128)(2,1)S(1)}, u32[]{:S(2)}) copy-start(bf16[16,384]{1,0:T(8,128)(2,1)S(1)} %collective-permute-done.2.refs_3_) | copy-start | bytes 36868
  15.5 6.6 %copy-start.11 = (bf16[16,384]{1,0:T(8,128)(2,1)}, bf16[16,384]{1,0:T(8,128)(2,1)S(1)}, u32[]{:S(2)}) copy-start(bf16[16,384]{1,0:T(8,128)(2,1)S(1)} %collective-permute-done.3.refs_4_) | copy-start | bytes 36868
  16.3 5.8 %copy-start.12 = (bf16[16,384]{1,0:T(8,128)(2,1)}, bf16[16,384]{1,0:T(8,128)(2,1)S(1)}, u32[]{:S(2)}) copy-start(bf16[16,384]{1,0:T(8,128)(2,1)S(1)} %collective-permute-done.4.refs_5_) | copy-start | bytes 36868
  17.6 4.5 %copy-start.13 = (bf16[16,384]{1,0:T(8,128)(2,1)}, bf16[16,384]{1,0:T(8,128)(2,1)S(1)}, u32[]{:S(2)}) copy-start(bf16[16,384]{1,0:T(8,128)(2,1)S(1)} %collective-permute-done.5.refs_6_) | copy-start | bytes 36868
  22.1 0.6 copy-start.14
  22.7 27.3 %copy-start.2 = (bf16[8,64,384]{2,1,0:T(8,128)(2,1)S(1)}, bf16[8,64,384]{2,1,0:T(8,128)(2,1)}, u32[]{:S(2)}) copy-start(bf16[8,64,384]{2,1,0:T(8,128)(2,1)} %param.5) | copy-start | bytes 1179652
  22.7 27.3 %copy-start.3 = (bf16[8,64,384]{2,1,0:T(8,128)(2,1)S(1)}, bf16[8,64,384]{2,1,0:T(8,128)(2,1)}, u32[]{:S(2)}) copy-start(bf16[8,64,384]{2,1,0:T(8,128)(2,1)} %param.9) | copy-start | bytes 1179652
  22.7 27.3 %copy-start.5 = (f32[2,8,512]{2,1,0:T(8,128)S(1)}, f32[2,8,512]{2,1,0:T(8,128)}, u32[]{:S(2)}) copy-start(f32[2,8,512]{2,1,0:T(8,128)} %get-tuple-element.31.soft_ref) | copy-start | bytes 98308
  22.7 27.3 %copy-start.6 = (bf16[384,8]{0,1:T(8,128)(2,1)S(1)}, bf16[384,8]{0,1:T(8,128)(2,1)}, u32[]{:S(2)}) copy-start(bf16[384,8]{0,1:T(8,128)(2,1)} %param.6) | copy-start | bytes 18436
  22.7 32.3 %copy-start.1 = (bf16[1,384,1536]{2,1,0:T(8,128)(2,1)S(1)}, bf16[1,384,1536]{2,1,0:T(8,128)(2,1)}, u32[]{:S(2)}) copy-start(bf16[1,384,1536]{2,1,0:T(8,128)(2,1)} %param.8) | copy-start | bytes 3538948
  27.0 28.1 %copy-start = (bf16[1,384,1536]{2,1,0:T(8,128)(2,1)S(1)}, bf16[1,384,1536]{2,1,0:T(8,128)(2,1)}, u32[]{:S(2)}) copy-start(bf16[1,384,1536]{2,1,0:T(8,128)(2,1)} %param.7) | copy-start | bytes 3538948
  27.0 25.4 %collective-permute-start.16 = (bf16[8,16,384]{2,1,0:T(8,128)(2,1)}, bf16[8,16,384]{2,1,0:T(8,128)(2,1)S(1)}, u32[]{:S(2)}, u32[]{:S(2)}) collective-permute-start(bf16[8,16,384]{2,1,0:T(8,128)(2,1)} %get-tuple-element.51.refs_0_), channel_id=1, source_target_pairs={{0,3},{1,2},{2,1},{3,0},{4,7},{5,6},{6,5},{7,4},{8,11},{9,10},{10,... | collective-permute-start | bytes 294920 | tf_op jit(solution)/shard_map/ppermute | solution.py:194
  27.1 25.4 %collective-permute-start.15 = (bf16[8,16,384]{2,1,0:T(8,128)(2,1)}, bf16[8,16,384]{2,1,0:T(8,128)(2,1)S(1)}, u32[]{:S(2)}, u32[]{:S(2)}) collective-permute-start(bf16[8,16,384]{2,1,0:T(8,128)(2,1)} %get-tuple-element.51.refs_0_), channel_id=1, source_target_pairs={{0,2},{1,3},{2,0},{3,1},{4,6},{5,7},{6,4},{7,5},{8,10},{9,11},{10,... | collective-permute-start | bytes 294920 | tf_op jit(solution)/shard_map/ppermute | solution.py:194
  28.7 23.8 %collective-permute-start.14 = (bf16[8,16,384]{2,1,0:T(8,128)(2,1)}, bf16[8,16,384]{2,1,0:T(8,128)(2,1)S(1)}, u32[]{:S(2)}, u32[]{:S(2)}) collective-permute-start(bf16[8,16,384]{2,1,0:T(8,128)(2,1)} %get-tuple-element.51.refs_0_), channel_id=1, source_target_pairs={{0,1},{1,0},{2,3},{3,2},{4,5},{5,4},{6,7},{7,6},{8,9},{9,8},{10,11... | collective-permute-start | bytes 294920 | tf_op jit(solution)/shard_map/ppermute | solution.py:194
  28.9 3.9 %collective-permute-start.7 = (bf16[16,384]{1,0:T(8,128)(2,1)}, bf16[16,384]{1,0:T(8,128)(2,1)S(1)}, u32[]{:S(2)}, u32[]{:S(2)}) collective-permute-start(bf16[16,384]{1,0:T(8,128)(2,1)} %get-tuple-element.41), channel_id=1, source_target_pairs={{0,4},{4,0},{8,12},{12,8},{16,20},{20,16},{24,28},{28,24},{1,5},{5... | collective-permute-start | bytes 36872 | tf_op jit(solution)/shard_map/ppermute | solution.py:194
  29.5 3.9 %collective-permute-start.8 = (bf16[16,384]{1,0:T(8,128)(2,1)}, bf16[16,384]{1,0:T(8,128)(2,1)S(1)}, u32[]{:S(2)}, u32[]{:S(2)}) collective-permute-start(bf16[16,384]{1,0:T(8,128)(2,1)} %get-tuple-element.42), channel_id=1, source_target_pairs={{0,8},{4,12},{8,0},{12,4},{16,24},{20,28},{24,16},{28,20},{1,9},{5... | collective-permute-start | bytes 36872 | tf_op jit(solution)/shard_map/ppermute | solution.py:194
  32.8 4.8 %collective-permute-start.9 = (bf16[16,384]{1,0:T(8,128)(2,1)}, bf16[16,384]{1,0:T(8,128)(2,1)S(1)}, u32[]{:S(2)}, u32[]{:S(2)}) collective-permute-start(bf16[16,384]{1,0:T(8,128)(2,1)} %get-tuple-element.43), channel_id=1, source_target_pairs={{0,12},{4,8},{8,4},{12,0},{16,28},{20,24},{24,20},{28,16},{1,13},{... | collective-permute-start | bytes 36872 | tf_op jit(solution)/shard_map/ppermute | solution.py:194
  33.4 4.8 %collective-permute-start.10 = (bf16[16,384]{1,0:T(8,128)(2,1)}, bf16[16,384]{1,0:T(8,128)(2,1)S(1)}, u32[]{:S(2)}, u32[]{:S(2)}) collective-permute-start(bf16[16,384]{1,0:T(8,128)(2,1)} %get-tuple-element.44), channel_id=1, source_target_pairs={{0,16},{4,20},{8,24},{12,28},{16,0},{20,4},{24,8},{28,12},{1,17},{... | collective-permute-start | bytes 36872 | tf_op jit(solution)/shard_map/ppermute | solution.py:194
  37.6 5.7 %collective-permute-start.11 = (bf16[16,384]{1,0:T(8,128)(2,1)}, bf16[16,384]{1,0:T(8,128)(2,1)S(1)}, u32[]{:S(2)}, u32[]{:S(2)}) collective-permute-start(bf16[16,384]{1,0:T(8,128)(2,1)} %get-tuple-element.45), channel_id=1, source_target_pairs={{0,20},{4,16},{8,28},{12,24},{16,4},{20,0},{24,12},{28,8},{1,21},{... | collective-permute-start | bytes 36872 | tf_op jit(solution)/shard_map/ppermute | solution.py:194
  38.2 5.7 %collective-permute-start.12 = (bf16[16,384]{1,0:T(8,128)(2,1)}, bf16[16,384]{1,0:T(8,128)(2,1)S(1)}, u32[]{:S(2)}, u32[]{:S(2)}) collective-permute-start(bf16[16,384]{1,0:T(8,128)(2,1)} %get-tuple-element.46), channel_id=1, source_target_pairs={{0,24},{4,28},{8,16},{12,20},{16,8},{20,12},{24,0},{28,4},{1,25},{... | collective-permute-start | bytes 36872 | tf_op jit(solution)/shard_map/ppermute | solution.py:194
  43.3 6.6 %collective-permute-start.13 = (bf16[16,384]{1,0:T(8,128)(2,1)}, bf16[16,384]{1,0:T(8,128)(2,1)S(1)}, u32[]{:S(2)}, u32[]{:S(2)}) collective-permute-start(bf16[16,384]{1,0:T(8,128)(2,1)} %get-tuple-element.47), channel_id=1, source_target_pairs={{0,28},{4,24},{8,20},{12,16},{16,12},{20,8},{24,4},{28,0},{1,29},{... | collective-permute-start | bytes 36872 | tf_op jit(solution)/shard_map/ppermute | solution.py:194
  50.0 0.7 %copy-start.7 = (bf16[16,384]{1,0:T(8,128)(2,1)S(1)}, bf16[16,384]{1,0:T(8,128)(2,1)}, u32[]{:S(2)}) copy-start(bf16[16,384]{1,0:T(8,128)(2,1)} %get-tuple-element.40.refs_0_) | copy-start | bytes 36868
  52.4 10.8 %all-to-all-start = ((f32[32,8,96]{2,1,0:T(8,128)}), f32[32,8,96]{2,1,0:T(8,128)S(1)}, u32[]{:S(2)}, u32[]{:S(2)}) async-start(f32[32,8,96]{2,1,0:T(8,128)} %bitcast.10), calls=%async_computation | async-start | bytes 262144 | tf_op jit(solution)/shard_map/all_to_all | solution.py:260
  55.0 0.9 %copy-start.4 = (bf16[8,16,384]{2,1,0:T(8,128)(2,1)S(1)}, bf16[8,16,384]{2,1,0:T(8,128)(2,1)}, u32[]{:S(2)}) copy-start(bf16[8,16,384]{2,1,0:T(8,128)(2,1)} %get-tuple-element.51.refs_0_) | copy-start | bytes 294916

commit v4 on v2

--- a/solution.py
+++ b/solution.py
@@ -11,6 +11,7 @@
 F32 = jnp.float32
 BF16 = jnp.bfloat16
 VMEM_BYTES = 24 * 1024 * 1024
+WHOLE_BYTES = 56 * 1024 * 1024
 
 
 def gelu_pair(value):
@@ -63,24 +64,48 @@
     return first.astype(BF16), second.astype(BF16)
 
 
-def slots_kernel(images, tokens_ref, router_ref, grad_ref, sent_ref, soft_ref):
-    tokens = tokens_ref[...]
-    columns = tokens.shape[0]
-    experts = router_ref.shape[0]
-    logits = dot(router_ref[...], tokens, 1, 1)
+def softmaxes(router, tokens, images):
+    logits = dot(router, tokens, 1, 1)
+    experts, columns = logits.shape
     mask = own_image(experts, images, columns)
-    top = jnp.max(logits, axis=0, keepdims=True)
-    combine = jnp.exp(logits - top)
+    combine = jnp.exp(logits - jnp.max(logits, axis=0, keepdims=True))
     combine = combine / jnp.sum(combine, axis=0, keepdims=True)
     block = jnp.where(mask, spread_rows(logits, images), -jnp.inf)
     block = jnp.exp(block - jnp.max(block, axis=1, keepdims=True))
     block = block / jnp.sum(block, axis=1, keepdims=True)
-    soft_ref[0] = fold_rows(block, images)
-    soft_ref[1] = combine
+    return block, combine, mask
+
+
+def slots_kernel(images, tokens_hbm, router_hbm, grad_hbm, sent_ref, *scratch):
+    tokens_ref, router_ref, grad_ref, sems = scratch
+    loads = [
+        pltpu.make_async_copy(source, target, sems.at[i])
+        for i, (source, target) in enumerate(
+            ((tokens_hbm, tokens_ref), (router_hbm, router_ref), (grad_hbm, grad_ref))
+        )
+    ]
+    for load in loads:
+        load.start()
+    loads[0].wait()
+    loads[1].wait()
+    tokens = tokens_ref[...]
+    block, combine, mask = softmaxes(router_ref[...], tokens, images)
     combine_block = jnp.where(mask, spread_rows(combine, images), 0.0)
     slot_in = dot(block.astype(BF16), tokens, 1, 0)
+    loads[2].wait()
     slot_grad = dot(combine_block.astype(BF16), grad_ref[...], 1, 0)
-    sent_ref[...] = pair_rows(slot_in, slot_grad, experts)
+    sent_ref[...] = pair_rows(slot_in, slot_grad, combine.shape[0])
+
+
+def stage_kernel(win_hbm, wout_hbm, win_ref, wout_ref, sems):
+    loads = (
+        pltpu.make_async_copy(win_hbm, win_ref, sems.at[0]),
+        pltpu.make_async_copy(wout_hbm, wout_ref, sems.at[1]),
+    )
+    for load in loads:
+        load.start()
+    for load in loads:
+        load.wait()
 
 
 def expert_kernel(recv_ref, win_ref, wout_ref, back_ref, *, step):
@@ -98,17 +123,13 @@
 
 
 def tokens_kernel(
-    images, back_ref, tokens_ref, router_ref, grad_ref, soft_ref, out_ref, send_ref
+    images, back_ref, tokens_ref, router_ref, grad_ref, out_ref, send_ref
 ):
     tokens = tokens_ref[...]
-    columns = tokens.shape[0]
-    experts = router_ref.shape[0]
     slot_out, slot_in_grad = split_rows(back_ref[...])
-    dispatch, combine = soft_ref[0], soft_ref[1]
-    mask = own_image(experts, images, columns)
+    dispatch_block, combine, mask = softmaxes(router_ref[...], tokens, images)
     comb = fold_rows(jnp.where(mask, dot(slot_out, grad_ref[...], 1, 1), 0.0), images)
     disp = jnp.where(mask, dot(slot_in_grad, tokens, 1, 1), 0.0)
-    dispatch_block = jnp.where(mask, spread_rows(dispatch, images), 0.0)
     mean = jnp.sum(dispatch_block * disp, axis=1, keepdims=True)
     from_dispatch = fold_rows(dispatch_block * (disp - mean), images)
     from_combine = combine * (comb - jnp.sum(combine * comb, axis=0, keepdims=True))
@@ -159,19 +180,37 @@
     router_rows = router.T
     w_in2, w_out2 = w_in.reshape(width, hidden), w_out.reshape(width, hidden)
     params = pltpu.CompilerParams(vmem_limit_bytes=VMEM_BYTES)
+    whole = pltpu.CompilerParams(vmem_limit_bytes=WHOLE_BYTES)
 
     def struct(shape, dtype):
         return jax.ShapeDtypeStruct(shape, dtype)
 
-    sent, soft = pl.pallas_call(
+    in_place = pl.BlockSpec(memory_space=pl.ANY)
+    sent = pl.pallas_call(
         functools.partial(slots_kernel, images),
-        out_shape=(
-            struct((experts, 2 * images, width), BF16),
-            struct((2, experts, columns), F32),
-        ),
-        compiler_params=params,
+        in_specs=[in_place] * 3,
+        out_shape=struct((experts, 2 * images, width), BF16),
+        scratch_shapes=[
+            pltpu.VMEM((columns, width), BF16),
+            pltpu.VMEM((experts, width), BF16),
+            pltpu.VMEM((columns, width), BF16),
+            pltpu.SemaphoreType.DMA((3,)),
+        ],
+        compiler_params=whole,
         name="slots",
     )(tokens2, router_rows, grad2)
+    w_in2, w_out2 = pl.pallas_call(
+        stage_kernel,
+        in_specs=[in_place] * 2,
+        out_specs=[in_place] * 2,
+        out_shape=[struct((width, hidden), BF16)] * 2,
+        scratch_shapes=[pltpu.SemaphoreType.DMA((2,))],
+        compiler_params=pltpu.CompilerParams(vmem_limit_bytes=1024 * 1024),
+        cost_estimate=pl.CostEstimate(
+            flops=0, bytes_accessed=8 * width * hidden, transcendentals=0
+        ),
+        name="stage",
+    )(w_in2, w_out2)
     recv = lax.all_to_all(sent, "expert", split_axis=0, concat_axis=0, tiled=True)
     back = pl.pallas_call(
         functools.partial(expert_kernel, step=512),
@@ -191,7 +230,7 @@
         ),
         compiler_params=params,
         name="tokens",
-    )(slots_back, tokens2, router_rows, grad2, soft)
+    )(slots_back, tokens2, router_rows, grad2)
     spread, router_send = lax.optimization_barrier((spread, router_send))
     router_parts = lax.all_to_all(
         router_send.reshape(owners * shares, experts, row_count),

time: 52.6 us -> 48.4 us (0.920)
  blocking collectives: 20.9 us -> 6.71 us
  starting transfers between devices: 9.28 us -> 16.4 us
  waiting for transfers between devices: 5.53 us -> 9.61 us
  local copies, waits for them, and re-layouts: 6.71 us -> 3.2 us
  Pallas kernels: 8.27 us -> 10.7 us
    all_to_all x1 -> x0, blocking collectives: 14.2 us -> none  [on_device(): lax.all_to_all(sent, 'expert', split_axis=0, concat_axis=0, tiled=True)]
    all_to_all x0 -> x1, starting transfers between devices: none -> 7.26 us  [on_device(): lax.all_to_all(sent, 'expert', split_axis=0, concat_axis=0, tiled=True)]
    all_to_all x0 -> x1, waiting for transfers between devices: none -> 4.08 us  [on_device(): lax.all_to_all(sent, 'expert', split_axis=0, concat_axis=0, tiled=True)]
    unnamed x28 -> x14, local copies, waits for them, and re-layouts: 6.71 us -> 3.2 us
    pallas_call x1 -> x2, Pallas kernels: 0.62 us -> 2.94 us  [the longest x1 2.44 us: on_device(): pl.pallas_call(functools.partial(slots_kernel, images), in_specs=[in_plac...]
  transfers between devices with their start and end apart: 2 -> 3, of which waited for: 2 -> 3; matrix products, arithmetic and copies ran while one was open for 0% -> 0% of each run, Pallas kernels for 6% -> 8%
where the time goes in v4:
time: 48.4 us; the launch traced here: 48 us
  starting transfers between devices  16.4 us (34%)
  Pallas kernels  10.7 us (22%)
  waiting for transfers between devices  9.61 us (20%)
  blocking collectives  6.71 us (14%)
  local copies, waits for them, and re-layouts  3.2 us (7%)
  between operations  0.68 us (1%)
  other arithmetic  0.63 us (1%)
    all_to_all x1, starting transfers between devices, on_device(): lax.all_to_all(sent, 'expert', split_axis=0, concat_axis=0, tiled=True)  7.26 us
    all_gather x1, blocking collectives, on_device(): spread = lax.all_gather(recv, 'dp', axis=0, tiled=False)  6.71 us
    all_to_all x1, starting transfers between devices, on_device(): lax.all_to_all(router_send.reshape(owners * shares, experts, row_count),...  5.18 us
    all_to_all x1, waiting for transfers between devices, on_device(): lax.all_to_all(router_send.reshape(owners * shares, experts, row_count),...  5.1 us
    all_to_all x1, waiting for transfers between devices, on_device(): lax.all_to_all(sent, 'expert', split_axis=0, concat_axis=0, tiled=True)  4.08 us
    all_to_all x1, starting transfers between devices, on_device(): lax.all_to_all(back, 'expert', split_axis=0, concat_axis=0, tiled=True)  3.98 us
    unnamed x14, local copies, waits for them, and re-layouts  3.2 us
    pallas_call x1, Pallas kernels, on_device(): pl.pallas_call(functools.partial(weights_kernel, step=512), grid=(shares...  3.12 us
  transfers between devices with their start and end apart: 3, of which 3 were waited for; matrix products, arithmetic and copies ran while one was open for 0% of the time, Pallas kernels for 8%

profile of v4, /device:TPU:0, one launch (start us, length us, event | category | flops | bytes accessed | tf_op | source)
XLA Modules:
  0.0 48.0 jit_solution(11874969134631076083)
XLA Ops:
  0.6 2.4 %slots.1 = bf16[8,16,384]{2,1,0:T(8,128)(2,1)} custom-call(bf16[512,384]{1,0:T(8,128)(2,1)} %bitcast.12, bf16[8,384]{1,0:T(8,128)(2,1)} %bitcast.20, bf16[512,384]{1,0:T(8,128)(2,1)} %bitcast.14), custom_call_target="tpu_custom_call" | custom-call | tf_op jit(solution)/shard_map/slots/pallas_call | solution.py:189
  3.1 7.3 %all-to-all-start = ((bf16[8,16,384]{2,1,0:T(8,128)(2,1)}), bf16[8,16,384]{2,1,0:T(8,128)(2,1)S(1)}, u32[]{:S(2)}, u32[]{:S(2)}) async-start(bf16[8,16,384]{2,1,0:T(8,128)(2,1)} %slots.1), calls=%async_computation | async-start | bytes 196608 | tf_op jit(solution)/shard_map/all_to_all | solution.py:214
  10.3 0.0 copy-start.2
  10.3 1.3 %copy-done.2 = bf16[1,384,1536]{2,1,0:T(8,128)(2,1)S(1)} copy-done((bf16[1,384,1536]{2,1,0:T(8,128)(2,1)S(1)}, bf16[1,384,1536]{2,1,0:T(8,128)(2,1)}, u32[]{:S(2)}) %copy-start.2) | copy-done | bytes 1179672
  11.6 0.0 copy-start.3
  11.6 1.3 %copy-done.3 = bf16[1,384,1536]{2,1,0:T(8,128)(2,1)S(1)} copy-done((bf16[1,384,1536]{2,1,0:T(8,128)(2,1)S(1)}, bf16[1,384,1536]{2,1,0:T(8,128)(2,1)}, u32[]{:S(2)}) %copy-start.3) | copy-done | bytes 1179672
  12.9 0.5 %stage.1 = (bf16[384,1536]{1,0:T(8,128)(2,1)S(1)}, bf16[384,1536]{1,0:T(8,128)(2,1)S(1)}) custom-call(bf16[384,1536]{1,0:T(8,128)(2,1)S(1)} %bitcast.17, bf16[384,1536]{1,0:T(8,128)(2,1)S(1)} %bitcast.18), custom_call_target="tpu_custom_call" | custom-call | bytes 4718592 | tf_op jit(solution)/shard_map/stage/pallas_call | solution.py:202
  13.4 4.1 %all-to-all-done.recv_ref = bf16[8,16,384]{2,1,0:T(8,128)(2,1)S(1)} async-done(((bf16[8,16,384]{2,1,0:T(8,128)(2,1)}), bf16[8,16,384]{2,1,0:T(8,128)(2,1)S(1)}, u32[]{:S(2)}, u32[]{:S(2)}) %all-to-all-start) | async-done | bytes 98336 | tf_op jit(solution)/shard_map/all_to_all | solution.py:214
  17.5 0.0 copy-start.4
  17.5 0.0 copy-start
  17.5 0.0 copy-start.1
  17.5 0.0 copy-start.6
  17.5 1.9 %expert.1 = bf16[8,16,384]{2,1,0:T(8,128)(2,1)} custom-call(bf16[8,16,384]{2,1,0:T(8,128)(2,1)S(1)} %all-to-all-done.recv_ref, bf16[384,1536]{1,0:T(8,128)(2,1)S(1)} %get-tuple-element.14.win_ref, bf16[384,1536]{1,0:T(8,128)(2,1)S(1)} %get-tuple-element.15.wout_ref), custom_call_target="tpu_custom_call" | custom-call | tf_op jit(solution)/shard_map/expert/pallas_call | solution.py:215
  19.4 0.0 copy-done.4
  19.4 4.0 %all-to-all-start.1 = ((bf16[8,16,384]{2,1,0:T(8,128)(2,1)}), bf16[8,16,384]{2,1,0:T(8,128)(2,1)}, u32[]{:S(2)}, u32[]{:S(2)}) async-start(bf16[8,16,384]{2,1,0:T(8,128)(2,1)} %expert.1), calls=%async_computation.1 | async-start | bytes 196608 | tf_op jit(solution)/shard_map/all_to_all | solution.py:222
  23.4 6.7 %all-gather = bf16[32,16,384]{2,1,0:T(8,128)(2,1)S(1)} all-gather(bf16[8,16,384]{2,1,0:T(8,128)(2,1)} %copy-done.4), channel_id=2, replica_groups=mesh['expert'=8,'dp'=4] {'dp'}, dimensions={0}, use_global_device_ids=true | all-gather | bytes 491520 | tf_op jit(solution)/shard_map/all_gather | solution.py:223
  30.1 0.4 all-to-all-done.1.back_ref
  30.6 0.0 copy-done
  30.6 0.0 copy-done.1
  30.6 0.0 copy-done.6
  30.6 2.7 %tokens.1 = (bf16[512,384]{1,0:T(8,128)(2,1)}, f32[8,4,8,96]{3,2,1,0:T(8,128)S(1)}) custom-call(bf16[8,16,384]{2,1,0:T(8,128)(2,1)} %all-to-all-done.1.back_ref, bf16[512,384]{1,0:T(8,128)(2,1)S(1)} %bitcast.13, bf16[8,384]{1,0:T(8,128)(2,1)S(1)} %bitcast.21, bf16[512,384]{1,0:T(8,128)(2,1)S(1)} %bitcast.15), custom_call_target="tpu_custom_call" | custom-call | tf_op jit(solution)/shard_map/tokens/pallas_call | solution.py:225
  33.3 0.0 copy-start.5
  33.3 0.6 %copy-done.5 = f32[8,4,8,96]{3,2,1,0:T(8,128)} copy-done((f32[8,4,8,96]{3,2,1,0:T(8,128)}, f32[8,4,8,96]{3,2,1,0:T(8,128)S(1)}, u32[]{:S(2)}) %copy-start.5) | copy-done | bytes 98328
  33.9 5.2 %all-to-all-start.2 = ((f32[32,8,96]{2,1,0:T(8,128)}), f32[32,8,96]{2,1,0:T(8,128)S(1)}, u32[]{:S(2)}, u32[]{:S(2)}) async-start(f32[32,8,96]{2,1,0:T(8,128)} %bitcast.19), calls=%async_computation.2 | async-start | bytes 262144 | tf_op jit(solution)/shard_map/all_to_all | solution.py:235
  39.1 3.1 %weights.1 = (f32[96,1536]{1,0:T(8,128)}, f32[96,1536]{1,0:T(8,128)}) custom-call(s32[1]{0:T(128)} %bitcast.6.share_ref, bf16[4,8,16,384]{3,2,1,0:T(8,128)(2,1)S(1)} %bitcast.16, bf16[384,1536]{1,0:T(8,128)(2,1)S(1)} %get-tuple-element.14.win_ref, bf16[384,1536]{1,0:T(8,128)(2,1)S(1)} %get-tuple-element.15.wout_ref), custom_call_target="tpu_custom_call" | custom-call | tf_op jit(solution)/shard_map/weights/pallas_call | solution.py:244
  42.2 5.1 %all-to-all-done.2 = f32[32,8,96]{2,1,0:T(8,128)S(1)} async-done(((f32[32,8,96]{2,1,0:T(8,128)}), f32[32,8,96]{2,1,0:T(8,128)S(1)}, u32[]{:S(2)}, u32[]{:S(2)}) %all-to-all-start.2) | async-done | bytes 98336 | tf_op jit(solution)/shard_map/all_to_all | solution.py:235
  47.3 0.6 %reduce_sum.9 = f32[8,96]{1,0:T(8,128)} reduce(f32[32,8,96]{2,1,0:T(8,128)S(1)} %all-to-all-done.2, f32[]{:T(128)} %constant.1.clone.1), dimensions={0}, to_apply=%region_0.0 | reduce | flops 23808 | bytes 101380 | tf_op jit(solution)/shard_map/reduce_sum | solution.py:258
Async XLA Ops:
  3.1 14.4 %all-to-all-start = ((bf16[8,16,384]{2,1,0:T(8,128)(2,1)}), bf16[8,16,384]{2,1,0:T(8,128)(2,1)S(1)}, u32[]{:S(2)}, u32[]{:S(2)}) async-start(bf16[8,16,384]{2,1,0:T(8,128)(2,1)} %slots.1), calls=%async_computation | async-start | bytes 196608 | tf_op jit(solution)/shard_map/all_to_all | solution.py:214
  10.3 1.3 %copy-start.2 = (bf16[1,384,1536]{2,1,0:T(8,128)(2,1)S(1)}, bf16[1,384,1536]{2,1,0:T(8,128)(2,1)}, u32[]{:S(2)}) copy-start(bf16[1,384,1536]{2,1,0:T(8,128)(2,1)} %param.7) | copy-start | bytes 3538948
  11.6 1.3 %copy-start.3 = (bf16[1,384,1536]{2,1,0:T(8,128)(2,1)S(1)}, bf16[1,384,1536]{2,1,0:T(8,128)(2,1)}, u32[]{:S(2)}) copy-start(bf16[1,384,1536]{2,1,0:T(8,128)(2,1)} %param.8) | copy-start | bytes 3538948
  17.5 2.0 %copy-start.4 = (bf16[8,16,384]{2,1,0:T(8,128)(2,1)}, bf16[8,16,384]{2,1,0:T(8,128)(2,1)S(1)}, u32[]{:S(2)}) copy-start(bf16[8,16,384]{2,1,0:T(8,128)(2,1)S(1)} %all-to-all-done.recv_ref) | copy-start | bytes 294916
  17.5 13.1 %copy-start = (bf16[8,64,384]{2,1,0:T(8,128)(2,1)S(1)}, bf16[8,64,384]{2,1,0:T(8,128)(2,1)}, u32[]{:S(2)}) copy-start(bf16[8,64,384]{2,1,0:T(8,128)(2,1)} %param.5) | copy-start | bytes 1179652
  17.5 13.1 %copy-start.1 = (bf16[8,64,384]{2,1,0:T(8,128)(2,1)S(1)}, bf16[8,64,384]{2,1,0:T(8,128)(2,1)}, u32[]{:S(2)}) copy-start(bf16[8,64,384]{2,1,0:T(8,128)(2,1)} %param.9) | copy-start | bytes 1179652
  17.5 13.1 %copy-start.6 = (bf16[384,8]{0,1:T(8,128)(2,1)S(1)}, bf16[384,8]{0,1:T(8,128)(2,1)}, u32[]{:S(2)}) copy-start(bf16[384,8]{0,1:T(8,128)(2,1)} %param.6) | copy-start | bytes 18436
  19.4 11.1 %all-to-all-start.1 = ((bf16[8,16,384]{2,1,0:T(8,128)(2,1)}), bf16[8,16,384]{2,1,0:T(8,128)(2,1)}, u32[]{:S(2)}, u32[]{:S(2)}) async-start(bf16[8,16,384]{2,1,0:T(8,128)(2,1)} %expert.1), calls=%async_computation.1 | async-start | bytes 196608 | tf_op jit(solution)/shard_map/all_to_all | solution.py:222
  33.3 0.7 %copy-start.5 = (f32[8,4,8,96]{3,2,1,0:T(8,128)}, f32[8,4,8,96]{3,2,1,0:T(8,128)S(1)}, u32[]{:S(2)}) copy-start(f32[8,4,8,96]{3,2,1,0:T(8,128)S(1)} %get-tuple-element.23) | copy-start | bytes 294916
  33.9 13.4 %all-to-all-start.2 = ((f32[32,8,96]{2,1,0:T(8,128)}), f32[32,8,96]{2,1,0:T(8,128)S(1)}, u32[]{:S(2)}, u32[]{:S(2)}) async-start(f32[32,8,96]{2,1,0:T(8,128)} %bitcast.19), calls=%async_computation.2 | async-start | bytes 262144 | tf_op jit(solution)/shard_map/all_to_all | solution.py:235

commit v5 on v4

--- a/solution.py
+++ b/solution.py
@@ -78,21 +78,29 @@
 
 def slots_kernel(images, tokens_hbm, router_hbm, grad_hbm, sent_ref, *scratch):
     tokens_ref, router_ref, grad_ref, sems = scratch
-    loads = [
-        pltpu.make_async_copy(source, target, sems.at[i])
-        for i, (source, target) in enumerate(
-            ((tokens_hbm, tokens_ref), (router_hbm, router_ref), (grad_hbm, grad_ref))
-        )
-    ]
-    for load in loads:
+    pieces = sems.shape[1]
+    rows = tokens_ref.shape[0] // pieces
+
+    def loads(which, source, target):
+        parts = (pl.ds(i * rows, rows) for i in range(pieces))
+        return [
+            pltpu.make_async_copy(source.at[part], target.at[part], sems.at[which, i])
+            for i, part in enumerate(parts)
+        ]
+
+    first = loads(0, tokens_hbm, tokens_ref)
+    first.append(pltpu.make_async_copy(router_hbm, router_ref, sems.at[2, 0]))
+    second = loads(1, grad_hbm, grad_ref)
+    for load in first + second:
         load.start()
-    loads[0].wait()
-    loads[1].wait()
+    for load in first:
+        load.wait()
     tokens = tokens_ref[...]
     block, combine, mask = softmaxes(router_ref[...], tokens, images)
     combine_block = jnp.where(mask, spread_rows(combine, images), 0.0)
     slot_in = dot(block.astype(BF16), tokens, 1, 0)
-    loads[2].wait()
+    for load in second:
+        load.wait()
     slot_grad = dot(combine_block.astype(BF16), grad_ref[...], 1, 0)
     sent_ref[...] = pair_rows(slot_in, slot_grad, combine.shape[0])
 
@@ -122,27 +130,37 @@
     back_ref[...] = pair_rows(out, back, recv_ref.shape[0])
 
 
-def tokens_kernel(
-    images, back_ref, tokens_ref, router_ref, grad_ref, out_ref, send_ref
+def logits_kernel(
+    images, back_hbm, tokens_ref, router_ref, grad_ref, send_ref, logit_ref, back_ref, sem
 ):
+    load = pltpu.make_async_copy(back_hbm, back_ref, sem)
+    load.start()
     tokens = tokens_ref[...]
+    dispatch, combine, mask = softmaxes(router_ref[...], tokens, images)
+    load.wait()
     slot_out, slot_in_grad = split_rows(back_ref[...])
-    dispatch_block, combine, mask = softmaxes(router_ref[...], tokens, images)
+    disp = jnp.where(mask, dot(slot_in_grad, tokens, 1, 1), 0.0)
     comb = fold_rows(jnp.where(mask, dot(slot_out, grad_ref[...], 1, 1), 0.0), images)
-    disp = jnp.where(mask, dot(slot_in_grad, tokens, 1, 1), 0.0)
-    mean = jnp.sum(dispatch_block * disp, axis=1, keepdims=True)
-    from_dispatch = fold_rows(dispatch_block * (disp - mean), images)
+    mean = jnp.sum(dispatch * disp, axis=1, keepdims=True)
+    from_dispatch = fold_rows(dispatch * (disp - mean), images)
     from_combine = combine * (comb - jnp.sum(combine * comb, axis=0, keepdims=True))
     logit_grad = (from_combine + from_dispatch).astype(BF16)
-    out = dot(dispatch_block.astype(BF16), slot_in_grad, 0, 0)
-    out = out + dot(logit_grad, router_ref[...], 0, 0)
-    out_ref[...] = out.astype(BF16)
+    logit_ref[...] = logit_grad
     part = dot(logit_grad, tokens, 1, 0)
     owners, shares, _, width = send_ref.shape
     for share in range(shares):
         piece = part[:, share * width : (share + 1) * width]
         for owner in range(owners):
             send_ref[owner, share] = piece
+
+
+def tokens_kernel(images, back_ref, tokens_ref, router_ref, logit_ref, out_ref):
+    router = router_ref[...]
+    dispatch, _, _ = softmaxes(router, tokens_ref[...], images)
+    _, slot_in_grad = split_rows(back_ref[...])
+    out = dot(dispatch.astype(BF16), slot_in_grad, 0, 0)
+    out = out + dot(logit_ref[...], router, 0, 0)
+    out_ref[...] = out.astype(BF16)
 
 
 def weights_kernel(share_ref, spread_ref, win_ref, wout_ref, win_out, wout_out, *, step):
@@ -194,7 +212,7 @@
             pltpu.VMEM((columns, width), BF16),
             pltpu.VMEM((experts, width), BF16),
             pltpu.VMEM((columns, width), BF16),
-            pltpu.SemaphoreType.DMA((3,)),
+            pltpu.SemaphoreType.DMA((3, 4)),
         ],
         compiler_params=whole,
         name="slots",
@@ -222,14 +240,17 @@
     slots_back = lax.all_to_all(back, "expert", split_axis=0, concat_axis=0, tiled=True)
     spread = lax.all_gather(recv, "dp", axis=0, tiled=False)
 
-    tokens_grad, router_send = pl.pallas_call(
-        functools.partial(tokens_kernel, images),
+    in_vmem = pl.BlockSpec(memory_space=pltpu.VMEM)
+    router_send, logit_grad = pl.pallas_call(
+        functools.partial(logits_kernel, images),
+        in_specs=[in_place] + [in_vmem] * 3,
         out_shape=(
-            struct((columns, width), BF16),
             struct((owners, shares, experts, row_count), F32),
+            struct((experts, columns), BF16),
         ),
+        scratch_shapes=[pltpu.VMEM(back.shape, BF16), pltpu.SemaphoreType.DMA],
         compiler_params=params,
-        name="tokens",
+        name="logits",
     )(slots_back, tokens2, router_rows, grad2)
     spread, router_send = lax.optimization_barrier((spread, router_send))
     router_parts = lax.all_to_all(
@@ -240,6 +261,12 @@
         tiled=True,
     )
 
+    tokens_grad = pl.pallas_call(
+        functools.partial(tokens_kernel, images),
+        out_shape=struct((columns, width), BF16),
+        compiler_params=params,
+        name="tokens",
+    )(slots_back, tokens2, router_rows, logit_grad)
     group = max(1, min(shares, 256 // (owners * images)))
     w_in_grad, w_out_grad = pl.pallas_call(
         functools.partial(weights_kernel, step=512),

time: 48.4 us -> 47.5 us (0.981)
  waiting for transfers between devices: 9.61 us -> 7.17 us
  Pallas kernels: 10.7 us -> 12.2 us
    all_to_all x1, waiting for transfers between devices: 5.1 us -> 2.66 us  [on_device(): lax.all_to_all(router_send.reshape(owners * shares, experts, row_count),...]
    pallas_call x1 -> x2, Pallas kernels: 2.69 us -> 4.07 us  [the longest x1 2.44 us: on_device(): pl.pallas_call(functools.partial(tokens_kernel, images), out_shape=struct...]
  transfers between devices with their start and end apart: 3 -> 3, of which waited for: 3 -> 3; matrix products, arithmetic and copies ran while one was open for 0% -> 0% of each run, Pallas kernels for 8% -> 13%
where the time goes in v5:
time: 47.5 us; the launch traced here: 47 us
  starting transfers between devices  16.4 us (35%)
  Pallas kernels  12.2 us (26%)
  waiting for transfers between devices  7.17 us (15%)
  blocking collectives  6.71 us (14%)
  local copies, waits for them, and re-layouts  3.2 us (7%)
  between operations  0.7 us (1%)
  other arithmetic  0.63 us (1%)
    all_to_all x1, starting transfers between devices, on_device(): lax.all_to_all(sent, 'expert', split_axis=0, concat_axis=0, tiled=True)  7.27 us
    all_gather x1, blocking collectives, on_device(): spread = lax.all_gather(recv, 'dp', axis=0, tiled=False)  6.71 us
    all_to_all x1, starting transfers between devices, on_device(): lax.all_to_all(router_send.reshape(owners * shares, experts, row_count),...  5.17 us
    all_to_all x1, waiting for transfers between devices, on_device(): lax.all_to_all(sent, 'expert', split_axis=0, concat_axis=0, tiled=True)  4.08 us
    all_to_all x1, starting transfers between devices, on_device(): lax.all_to_all(back, 'expert', split_axis=0, concat_axis=0, tiled=True)  3.98 us
    unnamed x14, local copies, waits for them, and re-layouts  3.2 us
    pallas_call x1, Pallas kernels, on_device(): pl.pallas_call(functools.partial(weights_kernel, step=512), grid=(shares...  3.12 us
    all_to_all x1, waiting for transfers between devices, on_device(): lax.all_to_all(router_send.reshape(owners * shares, experts, row_count),...  2.66 us
  transfers between devices with their start and end apart: 3, of which 3 were waited for; matrix products, arithmetic and copies ran while one was open for 0% of the time, Pallas kernels for 13%

profile of v5, /device:TPU:0, one launch (start us, length us, event | category | flops | bytes accessed | tf_op | source)
XLA Modules:
  0.0 47.0 jit_solution(9140121404956289403)
XLA Ops:
  0.6 2.6 %slots.1 = bf16[8,16,384]{2,1,0:T(8,128)(2,1)} custom-call(bf16[512,384]{1,0:T(8,128)(2,1)} %bitcast.12, bf16[8,384]{1,0:T(8,128)(2,1)} %bitcast.21, bf16[512,384]{1,0:T(8,128)(2,1)} %bitcast.15), custom_call_target="tpu_custom_call" | custom-call | tf_op jit(solution)/shard_map/slots/pallas_call | solution.py:207
  3.2 7.3 %all-to-all-start = ((bf16[8,16,384]{2,1,0:T(8,128)(2,1)}), bf16[8,16,384]{2,1,0:T(8,128)(2,1)S(1)}, u32[]{:S(2)}, u32[]{:S(2)}) async-start(bf16[8,16,384]{2,1,0:T(8,128)(2,1)} %slots.1), calls=%async_computation | async-start | bytes 196608 | tf_op jit(solution)/shard_map/all_to_all | solution.py:232
  10.5 0.0 copy-start.2
  10.5 1.3 %copy-done.2 = bf16[1,384,1536]{2,1,0:T(8,128)(2,1)S(1)} copy-done((bf16[1,384,1536]{2,1,0:T(8,128)(2,1)S(1)}, bf16[1,384,1536]{2,1,0:T(8,128)(2,1)}, u32[]{:S(2)}) %copy-start.2) | copy-done | bytes 1179672
  11.7 0.0 copy-start.3
  11.7 1.3 %copy-done.3 = bf16[1,384,1536]{2,1,0:T(8,128)(2,1)S(1)} copy-done((bf16[1,384,1536]{2,1,0:T(8,128)(2,1)S(1)}, bf16[1,384,1536]{2,1,0:T(8,128)(2,1)}, u32[]{:S(2)}) %copy-start.3) | copy-done | bytes 1179672
  13.0 0.5 %stage.1 = (bf16[384,1536]{1,0:T(8,128)(2,1)S(1)}, bf16[384,1536]{1,0:T(8,128)(2,1)S(1)}) custom-call(bf16[384,1536]{1,0:T(8,128)(2,1)S(1)} %bitcast.18, bf16[384,1536]{1,0:T(8,128)(2,1)S(1)} %bitcast.19), custom_call_target="tpu_custom_call" | custom-call | bytes 4718592 | tf_op jit(solution)/shard_map/stage/pallas_call | solution.py:220
  13.5 4.1 %all-to-all-done.recv_ref = bf16[8,16,384]{2,1,0:T(8,128)(2,1)S(1)} async-done(((bf16[8,16,384]{2,1,0:T(8,128)(2,1)}), bf16[8,16,384]{2,1,0:T(8,128)(2,1)S(1)}, u32[]{:S(2)}, u32[]{:S(2)}) %all-to-all-start) | async-done | bytes 98336 | tf_op jit(solution)/shard_map/all_to_all | solution.py:232
  17.6 0.0 copy-start.4
  17.6 0.0 copy-start
  17.6 0.0 copy-start.1
  17.6 0.0 copy-start.6
  17.6 1.9 %expert.1 = bf16[8,16,384]{2,1,0:T(8,128)(2,1)} custom-call(bf16[8,16,384]{2,1,0:T(8,128)(2,1)S(1)} %all-to-all-done.recv_ref, bf16[384,1536]{1,0:T(8,128)(2,1)S(1)} %get-tuple-element.14.win_ref, bf16[384,1536]{1,0:T(8,128)(2,1)S(1)} %get-tuple-element.15.wout_ref), custom_call_target="tpu_custom_call" | custom-call | tf_op jit(solution)/shard_map/expert/pallas_call | solution.py:233
  19.6 0.0 copy-done.4
  19.6 4.0 %all-to-all-start.1 = ((bf16[8,16,384]{2,1,0:T(8,128)(2,1)}), bf16[8,16,384]{2,1,0:T(8,128)(2,1)}, u32[]{:S(2)}, u32[]{:S(2)}) async-start(bf16[8,16,384]{2,1,0:T(8,128)(2,1)} %expert.1), calls=%async_computation.1 | async-start | bytes 196608 | tf_op jit(solution)/shard_map/all_to_all | solution.py:240
  23.5 6.7 %all-gather = bf16[32,16,384]{2,1,0:T(8,128)(2,1)S(1)} all-gather(bf16[8,16,384]{2,1,0:T(8,128)(2,1)} %copy-done.4), channel_id=2, replica_groups=mesh['expert'=8,'dp'=4] {'dp'}, dimensions={0}, use_global_device_ids=true | all-gather | bytes 491520 | tf_op jit(solution)/shard_map/all_gather | solution.py:241
  30.3 0.4 all-to-all-done.1.back_hbm.back_ref
  30.7 0.0 copy-done
  30.7 0.0 copy-done.1
  30.7 0.0 copy-done.6
  30.7 1.6 %logits.1 = (f32[8,4,8,96]{3,2,1,0:T(8,128)S(1)}, bf16[8,512]{1,0:T(8,128)(2,1)S(1)}) custom-call(bf16[8,16,384]{2,1,0:T(8,128)(2,1)} %all-to-all-done.1.back_hbm.back_ref, bf16[512,384]{1,0:T(8,128)(2,1)S(1)} %bitcast.13, bf16[8,384]{1,0:T(8,128)(2,1)S(1)} %bitcast.22, bf16[512,384]{1,0:T(8,128)(2,1)S(1)} %bitcast.16), custom_call_target="tpu_custom_call" | custom-call | tf_op jit(solution)/shard_map/logits/pallas_call | solution.py:244
  32.3 0.0 copy-start.5
  32.4 0.6 %copy-done.5 = f32[8,4,8,96]{3,2,1,0:T(8,128)} copy-done((f32[8,4,8,96]{3,2,1,0:T(8,128)}, f32[8,4,8,96]{3,2,1,0:T(8,128)S(1)}, u32[]{:S(2)}) %copy-start.5) | copy-done | bytes 98328
  33.0 5.2 %all-to-all-start.2 = ((f32[32,8,96]{2,1,0:T(8,128)}), f32[32,8,96]{2,1,0:T(8,128)S(1)}, u32[]{:S(2)}, u32[]{:S(2)}) async-start(f32[32,8,96]{2,1,0:T(8,128)} %bitcast.20), calls=%async_computation.2 | async-start | bytes 262144 | tf_op jit(solution)/shard_map/all_to_all | solution.py:256
  38.2 3.1 %weights.1 = (f32[96,1536]{1,0:T(8,128)}, f32[96,1536]{1,0:T(8,128)}) custom-call(s32[1]{0:T(128)} %bitcast.6.share_ref, bf16[4,8,16,384]{3,2,1,0:T(8,128)(2,1)S(1)} %bitcast.17, bf16[384,1536]{1,0:T(8,128)(2,1)S(1)} %get-tuple-element.14.win_ref, bf16[384,1536]{1,0:T(8,128)(2,1)S(1)} %get-tuple-element.15.wout_ref), custom_call_target="tpu_custom_call" | custom-call | tf_op jit(solution)/shard_map/weights/pallas_call | solution.py:271
  41.3 2.4 %tokens.1 = bf16[512,384]{1,0:T(8,128)(2,1)} custom-call(bf16[8,16,384]{2,1,0:T(8,128)(2,1)} %all-to-all-done.1.back_hbm.back_ref, bf16[512,384]{1,0:T(8,128)(2,1)S(1)} %bitcast.14, bf16[8,384]{1,0:T(8,128)(2,1)S(1)} %bitcast.23, bf16[8,512]{1,0:T(8,128)(2,1)S(1)} %get-tuple-element.17.logit_ref), custom_call_target="tpu_custom_call" | custom-call | tf_op jit(solution)/shard_map/tokens/pallas_call | solution.py:264
  43.7 2.7 %all-to-all-done.2 = f32[32,8,96]{2,1,0:T(8,128)S(1)} async-done(((f32[32,8,96]{2,1,0:T(8,128)}), f32[32,8,96]{2,1,0:T(8,128)S(1)}, u32[]{:S(2)}, u32[]{:S(2)}) %all-to-all-start.2) | async-done | bytes 98336 | tf_op jit(solution)/shard_map/all_to_all | solution.py:256
  46.4 0.6 %reduce_sum.9 = f32[8,96]{1,0:T(8,128)} reduce(f32[32,8,96]{2,1,0:T(8,128)S(1)} %all-to-all-done.2, f32[]{:T(128)} %constant.1.clone.1), dimensions={0}, to_apply=%region_0.0 | reduce | flops 23808 | bytes 101380 | tf_op jit(solution)/shard_map/reduce_sum | solution.py:285
Async XLA Ops:
  3.2 14.4 %all-to-all-start = ((bf16[8,16,384]{2,1,0:T(8,128)(2,1)}), bf16[8,16,384]{2,1,0:T(8,128)(2,1)S(1)}, u32[]{:S(2)}, u32[]{:S(2)}) async-start(bf16[8,16,384]{2,1,0:T(8,128)(2,1)} %slots.1), calls=%async_computation | async-start | bytes 196608 | tf_op jit(solution)/shard_map/all_to_all | solution.py:232
  10.5 1.3 %copy-start.2 = (bf16[1,384,1536]{2,1,0:T(8,128)(2,1)S(1)}, bf16[1,384,1536]{2,1,0:T(8,128)(2,1)}, u32[]{:S(2)}) copy-start(bf16[1,384,1536]{2,1,0:T(8,128)(2,1)} %param.7) | copy-start | bytes 3538948
  11.7 1.3 %copy-start.3 = (bf16[1,384,1536]{2,1,0:T(8,128)(2,1)S(1)}, bf16[1,384,1536]{2,1,0:T(8,128)(2,1)}, u32[]{:S(2)}) copy-start(bf16[1,384,1536]{2,1,0:T(8,128)(2,1)} %param.8) | copy-start | bytes 3538948
  17.6 2.0 %copy-start.4 = (bf16[8,16,384]{2,1,0:T(8,128)(2,1)}, bf16[8,16,384]{2,1,0:T(8,128)(2,1)S(1)}, u32[]{:S(2)}) copy-start(bf16[8,16,384]{2,1,0:T(8,128)(2,1)S(1)} %all-to-all-done.recv_ref) | copy-start | bytes 294916
  17.6 13.1 %copy-start = (bf16[8,64,384]{2,1,0:T(8,128)(2,1)S(1)}, bf16[8,64,384]{2,1,0:T(8,128)(2,1)}, u32[]{:S(2)}) copy-start(bf16[8,64,384]{2,1,0:T(8,128)(2,1)} %param.5) | copy-start | bytes 1179652
  17.6 13.1 %copy-start.1 = (bf16[8,64,384]{2,1,0:T(8,128)(2,1)S(1)}, bf16[8,64,384]{2,1,0:T(8,128)(2,1)}, u32[]{:S(2)}) copy-start(bf16[8,64,384]{2,1,0:T(8,128)(2,1)} %param.9) | copy-start | bytes 1179652
  17.6 13.1 %copy-start.6 = (bf16[384,8]{0,1:T(8,128)(2,1)S(1)}, bf16[384,8]{0,1:T(8,128)(2,1)}, u32[]{:S(2)}) copy-start(bf16[384,8]{0,1:T(8,128)(2,1)} %param.6) | copy-start | bytes 18436
  19.6 11.1 %all-to-all-start.1 = ((bf16[8,16,384]{2,1,0:T(8,128)(2,1)}), bf16[8,16,384]{2,1,0:T(8,128)(2,1)}, u32[]{:S(2)}, u32[]{:S(2)}) async-start(bf16[8,16,384]{2,1,0:T(8,128)(2,1)} %expert.1), calls=%async_computation.1 | async-start | bytes 196608 | tf_op jit(solution)/shard_map/all_to_all | solution.py:240
  32.3 0.7 %copy-start.5 = (f32[8,4,8,96]{3,2,1,0:T(8,128)}, f32[8,4,8,96]{3,2,1,0:T(8,128)S(1)}, u32[]{:S(2)}) copy-start(f32[8,4,8,96]{3,2,1,0:T(8,128)S(1)} %get-tuple-element.23) | copy-start | bytes 294916
  33.0 13.4 %all-to-all-start.2 = ((f32[32,8,96]{2,1,0:T(8,128)}), f32[32,8,96]{2,1,0:T(8,128)S(1)}, u32[]{:S(2)}, u32[]{:S(2)}) async-start(f32[32,8,96]{2,1,0:T(8,128)} %bitcast.20), calls=%async_computation.2 | async-start | bytes 262144 | tf_op jit(solution)/shard_map/all_to_all | solution.py:256

commit v6 on v5

--- a/solution.py
+++ b/solution.py
@@ -149,7 +149,7 @@
     part = dot(logit_grad, tokens, 1, 0)
     owners, shares, _, width = send_ref.shape
     for share in range(shares):
-        piece = part[:, share * width : (share + 1) * width]
+        piece = part[:, share * width : (share + 1) * width].astype(BF16)
         for owner in range(owners):
             send_ref[owner, share] = piece
 
@@ -163,10 +163,12 @@
     out_ref[...] = out.astype(BF16)
 
 
-def weights_kernel(share_ref, spread_ref, win_ref, wout_ref, win_out, wout_out, *, step):
-    width = spread_ref.shape[-1]
-    row_count = win_out.shape[0]
-    slots, cotan = split_rows(spread_ref[...].reshape((-1,) + spread_ref.shape[2:]))
+def weights_kernel(share_ref, *refs, step):
+    spread, (win_ref, wout_ref, win_out, wout_out) = refs[:-4], refs[-4:]
+    row_count, width = win_out.shape[0], win_ref.shape[0]
+    pairs = [split_rows(ref[...].reshape((-1,) + ref.shape[-2:])) for ref in spread]
+    slots = jnp.concatenate([pair[0] for pair in pairs], axis=0)
+    cotan = jnp.concatenate([pair[1] for pair in pairs], axis=0)
     shape = (row_count, width)
     row = lax.broadcasted_iota(jnp.int32, shape, 0) + share_ref[0] * row_count
     pick = jnp.where(lax.broadcasted_iota(jnp.int32, shape, 1) == row, 1.0, 0.0).astype(BF16)
@@ -238,21 +240,28 @@
     )(recv, w_in2, w_out2)
     recv, back = lax.optimization_barrier((recv, back))
     slots_back = lax.all_to_all(back, "expert", split_axis=0, concat_axis=0, tiled=True)
-    spread = lax.all_gather(recv, "dp", axis=0, tiled=False)
+    few = shares * owners * images <= 512
+    if few:
+        spread = [recv] + [
+            lax.ppermute(recv, "dp", [(i, i ^ k) for i in range(shares)])
+            for k in range(1, shares)
+        ]
+    else:
+        spread = [lax.all_gather(recv, "dp", axis=0, tiled=False)]
 
     in_vmem = pl.BlockSpec(memory_space=pltpu.VMEM)
     router_send, logit_grad = pl.pallas_call(
         functools.partial(logits_kernel, images),
         in_specs=[in_place] + [in_vmem] * 3,
         out_shape=(
-            struct((owners, shares, experts, row_count), F32),
+            struct((owners, shares, experts, row_count), BF16),
             struct((experts, columns), BF16),
         ),
         scratch_shapes=[pltpu.VMEM(back.shape, BF16), pltpu.SemaphoreType.DMA],
         compiler_params=params,
         name="logits",
     )(slots_back, tokens2, router_rows, grad2)
-    spread, router_send = lax.optimization_barrier((spread, router_send))
+    share, router_send = lax.optimization_barrier((lax.axis_index("dp").reshape(1), router_send))
     router_parts = lax.all_to_all(
         router_send.reshape(owners * shares, experts, row_count),
         ("expert", "dp"),
@@ -267,13 +276,16 @@
         compiler_params=params,
         name="tokens",
     )(slots_back, tokens2, router_rows, logit_grad)
-    group = max(1, min(shares, 256 // (owners * images)))
+    if few:
+        blocks = [pl.BlockSpec(recv.shape, lambda i: (0, 0, 0))] * shares
+    else:
+        blocks = [pl.BlockSpec((1,) + recv.shape, lambda i: (i, 0, 0, 0))]
     w_in_grad, w_out_grad = pl.pallas_call(
         functools.partial(weights_kernel, step=512),
-        grid=(shares // group,),
+        grid=(1 if few else shares,),
         in_specs=[
             pl.BlockSpec(memory_space=pltpu.SMEM),
-            pl.BlockSpec((group,) + recv.shape, lambda i: (i, 0, 0, 0)),
+            *blocks,
             pl.BlockSpec((width, hidden), lambda i: (0, 0)),
             pl.BlockSpec((width, hidden), lambda i: (0, 0)),
         ],
@@ -281,8 +293,8 @@
         out_shape=[struct((row_count, hidden), F32)] * 2,
         compiler_params=params,
         name="weights",
-    )(lax.axis_index("dp").reshape(1), spread, w_in2, w_out2)
-    router_grad = jnp.sum(router_parts, axis=0).T
+    )(share, *spread, w_in2, w_out2)
+    router_grad = jnp.sum(router_parts.astype(F32), axis=0).T
     return (
         tokens_grad.reshape(tokens.shape),
         w_in_grad.reshape(1, row_count, hidden),

time: 47.5 us -> 42.9 us (0.903)
  blocking collectives: 6.71 us -> 0 us
  waiting for transfers between devices: 7.17 us -> 11.1 us
  starting transfers between devices: 16.4 us -> 15.1 us
    all_gather x1 -> x0, blocking collectives: 6.71 us -> none  [on_device(): spread = lax.all_gather(recv, 'dp', axis=0, tiled=False)]
    all_to_all x1, waiting for transfers between devices: 0.43 us -> 5.13 us  [on_device(): lax.all_to_all(back, 'expert', split_axis=0, concat_axis=0, tiled=True)]
    all_to_all x1, starting transfers between devices: 5.17 us -> 2.54 us  [on_device(): lax.all_to_all(router_send.reshape(owners * shares, experts, row_count),...]
    ppermute x0 -> x3, starting transfers between devices: none -> 1.92 us  [on_device(): lax.ppermute(recv, 'dp', [(i, i ^ k) for i in range(shares)])]
    pallas_call x1, Pallas kernels: 3.12 us -> 4.01 us  [on_device(): pl.pallas_call(functools.partial(weights_kernel, step=512), grid=(1 if fe...]
    pallas_call x1, Pallas kernels: 2.44 us -> 1.55 us  [on_device(): pl.pallas_call(functools.partial(tokens_kernel, images), out_shape=struct...]
    all_to_all x1, waiting for transfers between devices: 2.66 us -> 1.83 us  [on_device(): lax.all_to_all(router_send.reshape(owners * shares, experts, row_count),...]
    all_to_all x1, starting transfers between devices: 3.98 us -> 3.36 us  [on_device(): lax.all_to_all(back, 'expert', split_axis=0, concat_axis=0, tiled=True)]
  transfers between devices with their start and end apart: 3 -> 6, of which waited for: 3 -> 3; matrix products, arithmetic and copies ran while one was open for 0% -> 0% of each run, Pallas kernels for 13% -> 17%
where the time goes in v6:
time: 42.9 us; the launch traced here: 42.4 us
  starting transfers between devices  15.1 us (35%)
  Pallas kernels  11.8 us (28%)
  waiting for transfers between devices  11.1 us (26%)
  local copies, waits for them, and re-layouts  3.16 us (7%)
  between operations  0.71 us (2%)
  other arithmetic  0.63 us (1%)
    all_to_all x1, starting transfers between devices, on_device(): lax.all_to_all(sent, 'expert', split_axis=0, concat_axis=0, tiled=True)  7.27 us
    all_to_all x1, waiting for transfers between devices, on_device(): lax.all_to_all(back, 'expert', split_axis=0, concat_axis=0, tiled=True)  5.13 us
    all_to_all x1, waiting for transfers between devices, on_device(): lax.all_to_all(sent, 'expert', split_axis=0, concat_axis=0, tiled=True)  4.08 us
    pallas_call x1, Pallas kernels, on_device(): pl.pallas_call(functools.partial(weights_kernel, step=512), grid=(1 if fe...  4.01 us
    all_to_all x1, starting transfers between devices, on_device(): lax.all_to_all(back, 'expert', split_axis=0, concat_axis=0, tiled=True)  3.36 us
    unnamed x12, local copies, waits for them, and re-layouts  3.16 us
    pallas_call x1, Pallas kernels, on_device(): pl.pallas_call(functools.partial(slots_kernel, images), in_specs=[in_plac...  2.57 us
    all_to_all x1, starting transfers between devices, on_device(): lax.all_to_all(router_send.reshape(owners * shares, experts, row_count),...  2.54 us
  transfers between devices with their start and end apart: 6, of which 3 were waited for; matrix products, arithmetic and copies ran while one was open for 0% of the time, Pallas kernels for 17%

profile of v6, /device:TPU:0, one launch (start us, length us, event | category | flops | bytes accessed | tf_op | source)
XLA Modules:
  0.0 42.4 jit_solution(14246048918696317264)
XLA Ops:
  0.6 2.6 %slots.1 = bf16[8,16,384]{2,1,0:T(8,128)(2,1)} custom-call(bf16[512,384]{1,0:T(8,128)(2,1)} %bitcast.11, bf16[8,384]{1,0:T(8,128)(2,1)} %bitcast.19, bf16[512,384]{1,0:T(8,128)(2,1)} %bitcast.14), custom_call_target="tpu_custom_call" | custom-call | tf_op jit(solution)/shard_map/slots/pallas_call | solution.py:209
  3.2 7.3 %all-to-all-start = ((bf16[8,16,384]{2,1,0:T(8,128)(2,1)}), bf16[8,16,384]{2,1,0:T(8,128)(2,1)S(1)}, u32[]{:S(2)}, u32[]{:S(2)}) async-start(bf16[8,16,384]{2,1,0:T(8,128)(2,1)} %slots.1), calls=%async_computation | async-start | bytes 196608 | tf_op jit(solution)/shard_map/all_to_all | solution.py:234
  10.5 0.0 copy-start.2
  10.5 1.3 %copy-done.2 = bf16[1,384,1536]{2,1,0:T(8,128)(2,1)S(1)} copy-done((bf16[1,384,1536]{2,1,0:T(8,128)(2,1)S(1)}, bf16[1,384,1536]{2,1,0:T(8,128)(2,1)}, u32[]{:S(2)}) %copy-start.2) | copy-done | bytes 1179672
  11.7 0.0 copy-start.3
  11.7 1.3 %copy-done.3 = bf16[1,384,1536]{2,1,0:T(8,128)(2,1)S(1)} copy-done((bf16[1,384,1536]{2,1,0:T(8,128)(2,1)S(1)}, bf16[1,384,1536]{2,1,0:T(8,128)(2,1)}, u32[]{:S(2)}) %copy-start.3) | copy-done | bytes 1179672
  13.0 0.5 %stage.1 = (bf16[384,1536]{1,0:T(8,128)(2,1)S(1)}, bf16[384,1536]{1,0:T(8,128)(2,1)S(1)}) custom-call(bf16[384,1536]{1,0:T(8,128)(2,1)S(1)} %bitcast.16, bf16[384,1536]{1,0:T(8,128)(2,1)S(1)} %bitcast.17), custom_call_target="tpu_custom_call" | custom-call | bytes 4718592 | tf_op jit(solution)/shard_map/stage/pallas_call | solution.py:222
  13.5 4.1 %all-to-all-done.recv_ref.refs_0_ = bf16[8,16,384]{2,1,0:T(8,128)(2,1)S(1)} async-done(((bf16[8,16,384]{2,1,0:T(8,128)(2,1)}), bf16[8,16,384]{2,1,0:T(8,128)(2,1)S(1)}, u32[]{:S(2)}, u32[]{:S(2)}) %all-to-all-start) | async-done | bytes 98336 | tf_op jit(solution)/shard_map/all_to_all | solution.py:234
  17.6 0.0 copy-start
  17.6 0.0 copy-start.1
  17.6 0.0 copy-start.5
  17.6 1.9 %expert.1 = bf16[8,16,384]{2,1,0:T(8,128)(2,1)} custom-call(bf16[8,16,384]{2,1,0:T(8,128)(2,1)S(1)} %all-to-all-done.recv_ref.refs_0_, bf16[384,1536]{1,0:T(8,128)(2,1)S(1)} %get-tuple-element.14.win_ref.refs_4_, bf16[384,1536]{1,0:T(8,128)(2,1)S(1)} %get-tuple-element.15.wout_ref.refs_5_), custom_call_target="tpu_custom_call" | custom-call | tf_op jit(solution)/shard_map/expert/pallas_call | solution.py:235
  19.5 3.4 %all-to-all-start.1 = ((bf16[8,16,384]{2,1,0:T(8,128)(2,1)}), bf16[8,16,384]{2,1,0:T(8,128)(2,1)S(1)}, u32[]{:S(2)}, u32[]{:S(2)}) async-start(bf16[8,16,384]{2,1,0:T(8,128)(2,1)} %expert.1), calls=%async_computation.1 | async-start | bytes 196608 | tf_op jit(solution)/shard_map/all_to_all | solution.py:242
  22.9 0.1 collective-permute-start.2
  23.0 1.6 %collective-permute-start.1 = (bf16[8,16,384]{2,1,0:T(8,128)(2,1)S(1)}, bf16[8,16,384]{2,1,0:T(8,128)(2,1)S(1)}, u32[]{:S(2)}, u32[]{:S(2)}) collective-permute-start(bf16[8,16,384]{2,1,0:T(8,128)(2,1)S(1)} %all-to-all-done.recv_ref.refs_0_), channel_id=1, source_target_pairs={{0,2},{1,3},{2,0},{3,1},{4,6},{5,7},{6,4},{7,5},{8,10},{9,11},{10,... | collective-permute-start | bytes 294920 | tf_op jit(solution)/shard_map/ppermute | solution.py:246
  24.6 0.3 collective-permute-start
  24.8 5.1 %all-to-all-done.1.back_hbm.back_ref = bf16[8,16,384]{2,1,0:T(8,128)(2,1)S(1)} async-done(((bf16[8,16,384]{2,1,0:T(8,128)(2,1)}), bf16[8,16,384]{2,1,0:T(8,128)(2,1)S(1)}, u32[]{:S(2)}, u32[]{:S(2)}) %all-to-all-start.1) | async-done | bytes 98336 | tf_op jit(solution)/shard_map/all_to_all | solution.py:242
  30.0 0.0 copy-done
  30.0 0.0 copy-done.1
  30.0 0.0 copy-done.5
  30.0 1.2 %logits.1 = (bf16[8,4,8,96]{3,2,1,0:T(8,128)(2,1)S(1)}, bf16[8,512]{1,0:T(8,128)(2,1)S(1)}) custom-call(bf16[8,16,384]{2,1,0:T(8,128)(2,1)S(1)} %all-to-all-done.1.back_hbm.back_ref, bf16[512,384]{1,0:T(8,128)(2,1)S(1)} %bitcast.12, bf16[8,384]{1,0:T(8,128)(2,1)S(1)} %bitcast.20, bf16[512,384]{1,0:T(8,128)(2,1)S(1)} %bitcast.15), custom_call_target="tpu_custom_call" | custom-call | tf_op jit(solution)/shard_map/logits/pallas_call | solution.py:253
  31.2 0.0 copy-start.4
  31.2 0.6 %copy-done.4 = bf16[8,4,8,96]{3,2,1,0:T(8,128)(2,1)} copy-done((bf16[8,4,8,96]{3,2,1,0:T(8,128)(2,1)}, bf16[8,4,8,96]{3,2,1,0:T(8,128)(2,1)S(1)}, u32[]{:S(2)}) %copy-start.4) | copy-done | bytes 49176
  31.8 2.5 %all-to-all-start.2 = ((bf16[32,8,96]{2,1,0:T(8,128)(2,1)}), bf16[32,8,96]{2,1,0:T(8,128)(2,1)S(1)}, u32[]{:S(2)}, u32[]{:S(2)}) async-start(bf16[32,8,96]{2,1,0:T(8,128)(2,1)} %bitcast.18), calls=%async_computation.2 | async-start | bytes 131072 | tf_op jit(solution)/shard_map/all_to_all | solution.py:265
  34.4 1.6 %tokens.1 = bf16[512,384]{1,0:T(8,128)(2,1)} custom-call(bf16[8,16,384]{2,1,0:T(8,128)(2,1)S(1)} %all-to-all-done.1.back_hbm.back_ref, bf16[512,384]{1,0:T(8,128)(2,1)S(1)} %bitcast.13, bf16[8,384]{1,0:T(8,128)(2,1)S(1)} %bitcast.21, bf16[8,512]{1,0:T(8,128)(2,1)S(1)} %get-tuple-element.17.logit_ref), custom_call_target="tpu_custom_call" | custom-call | tf_op jit(solution)/shard_map/tokens/pallas_call | solution.py:273
  35.9 0.0 collective-permute-done.2.refs_3_
  35.9 0.0 collective-permute-done.1.refs_2_
  35.9 0.0 collective-permute-done.refs_1_
  35.9 4.0 %weights.1 = (f32[96,1536]{1,0:T(8,128)}, f32[96,1536]{1,0:T(8,128)}) custom-call(s32[1]{0:T(128)} %bitcast.6.share_ref, bf16[8,16,384]{2,1,0:T(8,128)(2,1)S(1)} %all-to-all-done.recv_ref.refs_0_, bf16[8,16,384]{2,1,0:T(8,128)(2,1)} %collective-permute-done.refs_1_, bf16[8,16,384]{2,1,0:T(8,128)(2,1)S(1)} %collective-permute-done.1.refs_2_, ...), custom_call_target="tpu_custom_call" | custom-call | tf_op jit(solution)/shard_map/weights/pallas_call | solution.py:283
  39.9 1.8 %all-to-all-done.2 = bf16[32,8,96]{2,1,0:T(8,128)(2,1)S(1)} async-done(((bf16[32,8,96]{2,1,0:T(8,128)(2,1)}), bf16[32,8,96]{2,1,0:T(8,128)(2,1)S(1)}, u32[]{:S(2)}, u32[]{:S(2)}) %all-to-all-start.2) | async-done | bytes 49184 | tf_op jit(solution)/shard_map/all_to_all | solution.py:265
  41.8 0.6 %convert_reduce_fusion = f32[8,96]{1,0:T(8,128)} fusion(bf16[32,8,96]{2,1,0:T(8,128)(2,1)S(1)} %all-to-all-done.2), kind=kLoop, calls=%fused_computation | loop fusion | flops 48384 | bytes 52224 | tf_op jit(solution)/shard_map/reduce_sum | solution.py:297
Async XLA Ops:
  3.2 14.4 %all-to-all-start = ((bf16[8,16,384]{2,1,0:T(8,128)(2,1)}), bf16[8,16,384]{2,1,0:T(8,128)(2,1)S(1)}, u32[]{:S(2)}, u32[]{:S(2)}) async-start(bf16[8,16,384]{2,1,0:T(8,128)(2,1)} %slots.1), calls=%async_computation | async-start | bytes 196608 | tf_op jit(solution)/shard_map/all_to_all | solution.py:234
  10.5 1.3 %copy-start.2 = (bf16[1,384,1536]{2,1,0:T(8,128)(2,1)S(1)}, bf16[1,384,1536]{2,1,0:T(8,128)(2,1)}, u32[]{:S(2)}) copy-start(bf16[1,384,1536]{2,1,0:T(8,128)(2,1)} %param.7) | copy-start | bytes 3538948
  11.7 1.3 %copy-start.3 = (bf16[1,384,1536]{2,1,0:T(8,128)(2,1)S(1)}, bf16[1,384,1536]{2,1,0:T(8,128)(2,1)}, u32[]{:S(2)}) copy-start(bf16[1,384,1536]{2,1,0:T(8,128)(2,1)} %param.8) | copy-start | bytes 3538948
  17.6 12.4 %copy-start = (bf16[8,64,384]{2,1,0:T(8,128)(2,1)S(1)}, bf16[8,64,384]{2,1,0:T(8,128)(2,1)}, u32[]{:S(2)}) copy-start(bf16[8,64,384]{2,1,0:T(8,128)(2,1)} %param.5) | copy-start | bytes 1179652
  17.6 12.4 %copy-start.1 = (bf16[8,64,384]{2,1,0:T(8,128)(2,1)S(1)}, bf16[8,64,384]{2,1,0:T(8,128)(2,1)}, u32[]{:S(2)}) copy-start(bf16[8,64,384]{2,1,0:T(8,128)(2,1)} %param.9) | copy-start | bytes 1179652
  17.6 12.4 %copy-start.5 = (bf16[384,8]{0,1:T(8,128)(2,1)S(1)}, bf16[384,8]{0,1:T(8,128)(2,1)}, u32[]{:S(2)}) copy-start(bf16[384,8]{0,1:T(8,128)(2,1)} %param.6) | copy-start | bytes 18436
  19.5 10.4 %all-to-all-start.1 = ((bf16[8,16,384]{2,1,0:T(8,128)(2,1)}), bf16[8,16,384]{2,1,0:T(8,128)(2,1)S(1)}, u32[]{:S(2)}, u32[]{:S(2)}) async-start(bf16[8,16,384]{2,1,0:T(8,128)(2,1)} %expert.1), calls=%async_computation.1 | async-start | bytes 196608 | tf_op jit(solution)/shard_map/all_to_all | solution.py:242
  22.9 13.0 %collective-permute-start.2 = (bf16[8,16,384]{2,1,0:T(8,128)(2,1)S(1)}, bf16[8,16,384]{2,1,0:T(8,128)(2,1)S(1)}, u32[]{:S(2)}, u32[]{:S(2)}) collective-permute-start(bf16[8,16,384]{2,1,0:T(8,128)(2,1)S(1)} %all-to-all-done.recv_ref.refs_0_), channel_id=1, source_target_pairs={{0,3},{1,2},{2,1},{3,0},{4,7},{5,6},{6,5},{7,4},{8,11},{9,10},{10,... | collective-permute-start | bytes 294920 | tf_op jit(solution)/shard_map/ppermute | solution.py:246
  23.0 12.9 %collective-permute-start.1 = (bf16[8,16,384]{2,1,0:T(8,128)(2,1)S(1)}, bf16[8,16,384]{2,1,0:T(8,128)(2,1)S(1)}, u32[]{:S(2)}, u32[]{:S(2)}) collective-permute-start(bf16[8,16,384]{2,1,0:T(8,128)(2,1)S(1)} %all-to-all-done.recv_ref.refs_0_), channel_id=1, source_target_pairs={{0,2},{1,3},{2,0},{3,1},{4,6},{5,7},{6,4},{7,5},{8,10},{9,11},{10,... | collective-permute-start | bytes 294920 | tf_op jit(solution)/shard_map/ppermute | solution.py:246
  24.6 11.3 %collective-permute-start = (bf16[8,16,384]{2,1,0:T(8,128)(2,1)S(1)}, bf16[8,16,384]{2,1,0:T(8,128)(2,1)}, u32[]{:S(2)}, u32[]{:S(2)}) collective-permute-start(bf16[8,16,384]{2,1,0:T(8,128)(2,1)S(1)} %all-to-all-done.recv_ref.refs_0_), channel_id=1, source_target_pairs={{0,1},{1,0},{2,3},{3,2},{4,5},{5,4},{6,7},{7,6},{8,9},{9,8},{10,11... | collective-permute-start | bytes 294920 | tf_op jit(solution)/shard_map/ppermute | solution.py:246
  31.2 0.6 %copy-start.4 = (bf16[8,4,8,96]{3,2,1,0:T(8,128)(2,1)}, bf16[8,4,8,96]{3,2,1,0:T(8,128)(2,1)S(1)}, u32[]{:S(2)}) copy-start(bf16[8,4,8,96]{3,2,1,0:T(8,128)(2,1)S(1)} %get-tuple-element.23) | copy-start | bytes 147460
  31.8 10.0 %all-to-all-start.2 = ((bf16[32,8,96]{2,1,0:T(8,128)(2,1)}), bf16[32,8,96]{2,1,0:T(8,128)(2,1)S(1)}, u32[]{:S(2)}, u32[]{:S(2)}) async-start(bf16[32,8,96]{2,1,0:T(8,128)(2,1)} %bitcast.18), calls=%async_computation.2 | async-start | bytes 131072 | tf_op jit(solution)/shard_map/all_to_all | solution.py:265

commit v7 on v6

--- a/solution.py
+++ b/solution.py
@@ -16,11 +16,11 @@
 
 def gelu_pair(value):
     coef = math.sqrt(2.0 / math.pi)
+    cubic = 0.044715 * coef
     square = value * value
-    tangent = jnp.tanh(coef * value * (1.0 + 0.044715 * square))
-    half = 0.5 * (1.0 + tangent)
-    slope = half + 0.5 * coef * value * (1.0 - tangent * tangent) * (1.0 + 3.0 * 0.044715 * square)
-    return value * half, slope
+    half = 0.5 * jnp.tanh(value * (coef + cubic * square)) + 0.5
+    steep = value * (2.0 * coef + 6.0 * cubic * square) * (1.0 - half)
+    return value * half, half + half * steep
 
 
 def dot(left, right, left_dim, right_dim):
@@ -78,19 +78,11 @@
 
 def slots_kernel(images, tokens_hbm, router_hbm, grad_hbm, sent_ref, *scratch):
     tokens_ref, router_ref, grad_ref, sems = scratch
-    pieces = sems.shape[1]
-    rows = tokens_ref.shape[0] // pieces
-
-    def loads(which, source, target):
-        parts = (pl.ds(i * rows, rows) for i in range(pieces))
-        return [
-            pltpu.make_async_copy(source.at[part], target.at[part], sems.at[which, i])
-            for i, part in enumerate(parts)
-        ]
-
-    first = loads(0, tokens_hbm, tokens_ref)
-    first.append(pltpu.make_async_copy(router_hbm, router_ref, sems.at[2, 0]))
-    second = loads(1, grad_hbm, grad_ref)
+    first = [
+        pltpu.make_async_copy(tokens_hbm, tokens_ref, sems.at[0]),
+        pltpu.make_async_copy(router_hbm, router_ref, sems.at[1]),
+    ]
+    second = [pltpu.make_async_copy(grad_hbm, grad_ref, sems.at[2])]
     for load in first + second:
         load.start()
     for load in first:
@@ -147,11 +139,12 @@
     logit_grad = (from_combine + from_dispatch).astype(BF16)
     logit_ref[...] = logit_grad
     part = dot(logit_grad, tokens, 1, 0)
-    owners, shares, _, width = send_ref.shape
+    devices, _, width = send_ref.shape
+    shares = part.shape[1] // width
     for share in range(shares):
         piece = part[:, share * width : (share + 1) * width].astype(BF16)
-        for owner in range(owners):
-            send_ref[owner, share] = piece
+        for device in range(share, devices, shares):
+            send_ref[device] = piece
 
 
 def tokens_kernel(images, back_ref, tokens_ref, router_ref, logit_ref, out_ref):
@@ -163,17 +156,50 @@
     out_ref[...] = out.astype(BF16)
 
 
-def weights_kernel(share_ref, *refs, step):
-    spread, (win_ref, wout_ref, win_out, wout_out) = refs[:-4], refs[-4:]
-    row_count, width = win_out.shape[0], win_ref.shape[0]
-    pairs = [split_rows(ref[...].reshape((-1,) + ref.shape[-2:])) for ref in spread]
-    slots = jnp.concatenate([pair[0] for pair in pairs], axis=0)
-    cotan = jnp.concatenate([pair[1] for pair in pairs], axis=0)
-    shape = (row_count, width)
-    row = lax.broadcasted_iota(jnp.int32, shape, 0) + share_ref[0] * row_count
-    pick = jnp.where(lax.broadcasted_iota(jnp.int32, shape, 1) == row, 1.0, 0.0).astype(BF16)
-    own_slots = dot(pick, slots, 1, 1).astype(BF16)
-    own_cotan = dot(pick, cotan, 1, 1).astype(BF16)
+def own_rows(share, rows, row_count):
+    shape = (row_count, rows.shape[1])
+    row = lax.broadcasted_iota(jnp.int32, shape, 0) + share * row_count
+    pick = jnp.where(lax.broadcasted_iota(jnp.int32, shape, 1) == row, 1.0, 0.0)
+    return dot(pick.astype(BF16), rows, 1, 1).astype(BF16)
+
+
+def weights_kernel(count, share_ref, *refs):
+    spread, (win_ref, wout_ref, win_hbm, wout_hbm) = refs[:count], refs[count : count + 4]
+    rows_ref, win_out, wout_out, load_sems, store_sems = refs[count + 4 :]
+    chunks, row_count, step = win_out.shape
+    loads = [
+        pltpu.make_async_copy(ref, rows_ref.at[k], load_sems.at[k])
+        for k, ref in enumerate(spread)
+    ]
+    for load in loads:
+        load.start()
+    for load in loads:
+        load.wait()
+    slots, cotan = split_rows(rows_ref[...].reshape((-1,) + rows_ref.shape[2:]))
+    own_slots = own_rows(share_ref[0], slots, row_count)
+    own_cotan = own_rows(share_ref[0], cotan, row_count)
+    stores = []
+    for chunk in range(chunks):
+        part = slice(chunk * step, (chunk + 1) * step)
+        value, slope = gelu_pair(dot(slots, win_ref[:, part], 1, 0))
+        pre_grad = dot(cotan, wout_ref[:, part], 1, 0) * slope
+        win_out[chunk] = dot(own_slots, pre_grad.astype(BF16), 1, 0)
+        wout_out[chunk] = dot(own_cotan, value.astype(BF16), 1, 0)
+        where = (slice(None), pl.ds(chunk * step, step))
+        for which, (source, target) in enumerate(((win_out, win_hbm), (wout_out, wout_hbm))):
+            store = pltpu.make_async_copy(
+                source.at[chunk], target.at[where], store_sems.at[which, chunk]
+            )
+            store.start()
+            stores.append(store)
+    for store in stores:
+        store.wait()
+
+
+def long_weights_kernel(share_ref, spread_ref, win_ref, wout_ref, win_out, wout_out, *, step):
+    slots, cotan = split_rows(spread_ref[...].reshape((-1,) + spread_ref.shape[2:]))
+    own_slots = own_rows(share_ref[0], slots, win_out.shape[0])
+    own_cotan = own_rows(share_ref[0], cotan, win_out.shape[0])
 
     @pl.when(pl.program_id(0) == 0)
     def _():
@@ -214,7 +240,7 @@
             pltpu.VMEM((columns, width), BF16),
             pltpu.VMEM((experts, width), BF16),
             pltpu.VMEM((columns, width), BF16),
-            pltpu.SemaphoreType.DMA((3, 4)),
+            pltpu.SemaphoreType.DMA((3,)),
         ],
         compiler_params=whole,
         name="slots",
@@ -254,7 +280,7 @@
         functools.partial(logits_kernel, images),
         in_specs=[in_place] + [in_vmem] * 3,
         out_shape=(
-            struct((owners, shares, experts, row_count), BF16),
+            struct((owners * shares, experts, row_count), BF16),
             struct((experts, columns), BF16),
         ),
         scratch_shapes=[pltpu.VMEM(back.shape, BF16), pltpu.SemaphoreType.DMA],
@@ -263,7 +289,7 @@
     )(slots_back, tokens2, router_rows, grad2)
     share, router_send = lax.optimization_barrier((lax.axis_index("dp").reshape(1), router_send))
     router_parts = lax.all_to_all(
-        router_send.reshape(owners * shares, experts, row_count),
+        router_send,
         ("expert", "dp"),
         split_axis=0,
         concat_axis=0,
@@ -276,24 +302,40 @@
         compiler_params=params,
         name="tokens",
     )(slots_back, tokens2, router_rows, logit_grad)
+    in_smem = pl.BlockSpec(memory_space=pltpu.SMEM)
+    out_shape = [struct((row_count, hidden), F32)] * 2
     if few:
-        blocks = [pl.BlockSpec(recv.shape, lambda i: (0, 0, 0))] * shares
+        chunks, step = hidden // 512, 512
+        w_in_grad, w_out_grad = pl.pallas_call(
+            functools.partial(weights_kernel, shares),
+            in_specs=[in_smem] + [in_place] * shares + [in_vmem] * 2,
+            out_specs=[in_place] * 2,
+            out_shape=out_shape,
+            scratch_shapes=[
+                pltpu.VMEM((shares,) + recv.shape, BF16),
+                pltpu.VMEM((chunks, row_count, step), F32),
+                pltpu.VMEM((chunks, row_count, step), F32),
+                pltpu.SemaphoreType.DMA((shares,)),
+                pltpu.SemaphoreType.DMA((2, chunks)),
+            ],
+            compiler_params=params,
+            name="weights",
+        )(share, *spread, w_in2, w_out2)
     else:
-        blocks = [pl.BlockSpec((1,) + recv.shape, lambda i: (i, 0, 0, 0))]
-    w_in_grad, w_out_grad = pl.pallas_call(
-        functools.partial(weights_kernel, step=512),
-        grid=(1 if few else shares,),
-        in_specs=[
-            pl.BlockSpec(memory_space=pltpu.SMEM),
-            *blocks,
-            pl.BlockSpec((width, hidden), lambda i: (0, 0)),
-            pl.BlockSpec((width, hidden), lambda i: (0, 0)),
-        ],
-        out_specs=[pl.BlockSpec((row_count, hidden), lambda i: (0, 0))] * 2,
-        out_shape=[struct((row_count, hidden), F32)] * 2,
-        compiler_params=params,
-        name="weights",
-    )(share, *spread, w_in2, w_out2)
+        w_in_grad, w_out_grad = pl.pallas_call(
+            functools.partial(long_weights_kernel, step=512),
+            grid=(shares,),
+            in_specs=[
+                in_smem,
+                pl.BlockSpec((1,) + recv.shape, lambda i: (i, 0, 0, 0)),
+                pl.BlockSpec((width, hidden), lambda i: (0, 0)),
+                pl.BlockSpec((width, hidden), lambda i: (0, 0)),
+            ],
+            out_specs=[pl.BlockSpec((row_count, hidden), lambda i: (0, 0))] * 2,
+            out_shape=out_shape,
+            compiler_params=params,
+            name="weights",
+        )(share, *spread, w_in2, w_out2)
     router_grad = jnp.sum(router_parts.astype(F32), axis=0).T
     return (
         tokens_grad.reshape(tokens.shape),

time: 42.9 us -> 42.7 us (level)
  no operation moved by 1% of the time
where the time goes in v7:
time: 42.7 us; the launch traced here: 42.3 us
  starting transfers between devices  15.1 us (35%)
  Pallas kernels  11.4 us (27%)
  waiting for transfers between devices  11.3 us (26%)
  local copies, waits for them, and re-layouts  3.16 us (7%)
  between operations  0.71 us (2%)
  other arithmetic  0.63 us (1%)
    all_to_all x1, starting transfers between devices, on_device(): lax.all_to_all(sent, 'expert', split_axis=0, concat_axis=0, tiled=True)  7.26 us
    all_to_all x1, waiting for transfers between devices, on_device(): lax.all_to_all(back, 'expert', split_axis=0, concat_axis=0, tiled=True)  5.13 us
    all_to_all x1, waiting for transfers between devices, on_device(): lax.all_to_all(sent, 'expert', split_axis=0, concat_axis=0, tiled=True)  4.08 us
    pallas_call x1, Pallas kernels, on_device(): pl.pallas_call(functools.partial(weights_kernel, shares), in_specs=[in_sm...  3.8 us
    all_to_all x1, starting transfers between devices, on_device(): lax.all_to_all(back, 'expert', split_axis=0, concat_axis=0, tiled=True)  3.36 us
    unnamed x12, local copies, waits for them, and re-layouts  3.16 us
    all_to_all x1, starting transfers between devices, on_device(): lax.all_to_all(router_send, ('expert', 'dp'), split_axis=0, concat_axis=0...  2.54 us
    pallas_call x1, Pallas kernels, on_device(): pl.pallas_call(functools.partial(slots_kernel, images), in_specs=[in_plac...  2.44 us
  transfers between devices with their start and end apart: 6, of which 3 were waited for; matrix products, arithmetic and copies ran while one was open for 0% of the time, Pallas kernels for 17%

profile of v7, /device:TPU:0, one launch (start us, length us, event | category | flops | bytes accessed | tf_op | source)
XLA Modules:
  0.0 42.3 jit_solution(17080101757176847464)
XLA Ops:
  0.6 2.4 %slots.1 = bf16[8,16,384]{2,1,0:T(8,128)(2,1)} custom-call(bf16[512,384]{1,0:T(8,128)(2,1)} %bitcast.10, bf16[8,384]{1,0:T(8,128)(2,1)} %bitcast.17, bf16[512,384]{1,0:T(8,128)(2,1)} %bitcast.13), custom_call_target="tpu_custom_call" | custom-call | tf_op jit(solution)/shard_map/slots/pallas_call | solution.py:235
  3.1 7.3 %all-to-all-start = ((bf16[8,16,384]{2,1,0:T(8,128)(2,1)}), bf16[8,16,384]{2,1,0:T(8,128)(2,1)S(1)}, u32[]{:S(2)}, u32[]{:S(2)}) async-start(bf16[8,16,384]{2,1,0:T(8,128)(2,1)} %slots.1), calls=%async_computation | async-start | bytes 196608 | tf_op jit(solution)/shard_map/all_to_all | solution.py:260
  10.3 0.0 copy-start.2
  10.3 1.3 %copy-done.2 = bf16[1,384,1536]{2,1,0:T(8,128)(2,1)S(1)} copy-done((bf16[1,384,1536]{2,1,0:T(8,128)(2,1)S(1)}, bf16[1,384,1536]{2,1,0:T(8,128)(2,1)}, u32[]{:S(2)}) %copy-start.2) | copy-done | bytes 1179672
  11.6 0.0 copy-start.3
  11.6 1.3 %copy-done.3 = bf16[1,384,1536]{2,1,0:T(8,128)(2,1)S(1)} copy-done((bf16[1,384,1536]{2,1,0:T(8,128)(2,1)S(1)}, bf16[1,384,1536]{2,1,0:T(8,128)(2,1)}, u32[]{:S(2)}) %copy-start.3) | copy-done | bytes 1179672
  12.9 0.5 %stage.1 = (bf16[384,1536]{1,0:T(8,128)(2,1)S(1)}, bf16[384,1536]{1,0:T(8,128)(2,1)S(1)}) custom-call(bf16[384,1536]{1,0:T(8,128)(2,1)S(1)} %bitcast.15, bf16[384,1536]{1,0:T(8,128)(2,1)S(1)} %bitcast.16), custom_call_target="tpu_custom_call" | custom-call | bytes 4718592 | tf_op jit(solution)/shard_map/stage/pallas_call | solution.py:248
  13.4 4.1 %all-to-all-done.recv_ref.refs_0_ = bf16[8,16,384]{2,1,0:T(8,128)(2,1)S(1)} async-done(((bf16[8,16,384]{2,1,0:T(8,128)(2,1)}), bf16[8,16,384]{2,1,0:T(8,128)(2,1)S(1)}, u32[]{:S(2)}, u32[]{:S(2)}) %all-to-all-start) | async-done | bytes 98336 | tf_op jit(solution)/shard_map/all_to_all | solution.py:260
  17.5 0.0 copy-start
  17.5 0.0 copy-start.1
  17.5 0.0 copy-start.5
  17.5 1.9 %expert.1 = bf16[8,16,384]{2,1,0:T(8,128)(2,1)} custom-call(bf16[8,16,384]{2,1,0:T(8,128)(2,1)S(1)} %all-to-all-done.recv_ref.refs_0_, bf16[384,1536]{1,0:T(8,128)(2,1)S(1)} %get-tuple-element.14.win_ref.refs_4_, bf16[384,1536]{1,0:T(8,128)(2,1)S(1)} %get-tuple-element.15.wout_ref.refs_5_), custom_call_target="tpu_custom_call" | custom-call | tf_op jit(solution)/shard_map/expert/pallas_call | solution.py:261
  19.4 3.4 %all-to-all-start.1 = ((bf16[8,16,384]{2,1,0:T(8,128)(2,1)}), bf16[8,16,384]{2,1,0:T(8,128)(2,1)S(1)}, u32[]{:S(2)}, u32[]{:S(2)}) async-start(bf16[8,16,384]{2,1,0:T(8,128)(2,1)} %expert.1), calls=%async_computation.1 | async-start | bytes 196608 | tf_op jit(solution)/shard_map/all_to_all | solution.py:268
  22.8 0.1 collective-permute-start.2
  22.9 1.6 %collective-permute-start.1 = (bf16[8,16,384]{2,1,0:T(8,128)(2,1)S(1)}, bf16[8,16,384]{2,1,0:T(8,128)(2,1)S(1)}, u32[]{:S(2)}, u32[]{:S(2)}) collective-permute-start(bf16[8,16,384]{2,1,0:T(8,128)(2,1)S(1)} %all-to-all-done.recv_ref.refs_0_), channel_id=1, source_target_pairs={{0,2},{1,3},{2,0},{3,1},{4,6},{5,7},{6,4},{7,5},{8,10},{9,11},{10,... | collective-permute-start | bytes 294920 | tf_op jit(solution)/shard_map/ppermute | solution.py:272
  24.5 0.3 collective-permute-start
  24.7 5.1 %all-to-all-done.1.back_hbm.back_ref = bf16[8,16,384]{2,1,0:T(8,128)(2,1)S(1)} async-done(((bf16[8,16,384]{2,1,0:T(8,128)(2,1)}), bf16[8,16,384]{2,1,0:T(8,128)(2,1)S(1)}, u32[]{:S(2)}, u32[]{:S(2)}) %all-to-all-start.1) | async-done | bytes 98336 | tf_op jit(solution)/shard_map/all_to_all | solution.py:268
  29.9 0.0 copy-done
  29.9 0.0 copy-done.1
  29.9 0.0 copy-done.5
  29.9 1.2 %logits.1 = (bf16[32,8,96]{2,1,0:T(8,128)(2,1)S(1)}, bf16[8,512]{1,0:T(8,128)(2,1)S(1)}) custom-call(bf16[8,16,384]{2,1,0:T(8,128)(2,1)S(1)} %all-to-all-done.1.back_hbm.back_ref, bf16[512,384]{1,0:T(8,128)(2,1)S(1)} %bitcast.11, bf16[8,384]{1,0:T(8,128)(2,1)S(1)} %bitcast.18, bf16[512,384]{1,0:T(8,128)(2,1)S(1)} %bitcast.14), custom_call_target="tpu_custom_call" | custom-call | tf_op jit(solution)/shard_map/logits/pallas_call | solution.py:279
  31.1 0.0 copy-start.4
  31.1 0.6 %copy-done.4 = bf16[32,8,96]{2,1,0:T(8,128)(2,1)} copy-done((bf16[32,8,96]{2,1,0:T(8,128)(2,1)}, bf16[32,8,96]{2,1,0:T(8,128)(2,1)S(1)}, u32[]{:S(2)}) %copy-start.4) | copy-done | bytes 49176
  31.7 2.5 %all-to-all-start.2 = ((bf16[32,8,96]{2,1,0:T(8,128)(2,1)}), bf16[32,8,96]{2,1,0:T(8,128)(2,1)S(1)}, u32[]{:S(2)}, u32[]{:S(2)}) async-start(bf16[32,8,96]{2,1,0:T(8,128)(2,1)} %copy-done.4), calls=%async_computation.2 | async-start | bytes 131072 | tf_op jit(solution)/shard_map/all_to_all | solution.py:291
  34.2 1.5 %tokens.1 = bf16[512,384]{1,0:T(8,128)(2,1)} custom-call(bf16[8,16,384]{2,1,0:T(8,128)(2,1)S(1)} %all-to-all-done.1.back_hbm.back_ref, bf16[512,384]{1,0:T(8,128)(2,1)S(1)} %bitcast.12, bf16[8,384]{1,0:T(8,128)(2,1)S(1)} %bitcast.19, bf16[8,512]{1,0:T(8,128)(2,1)S(1)} %get-tuple-element.17.logit_ref), custom_call_target="tpu_custom_call" | custom-call | tf_op jit(solution)/shard_map/tokens/pallas_call | solution.py:299
  35.8 0.0 collective-permute-done.2.refs_3_
  35.8 0.0 collective-permute-done.1.refs_2_
  35.8 0.0 collective-permute-done.refs_1_
  35.8 3.8 %weights.1 = (f32[96,1536]{1,0:T(8,128)}, f32[96,1536]{1,0:T(8,128)}) custom-call(s32[1]{0:T(128)} %bitcast.6.share_ref, bf16[8,16,384]{2,1,0:T(8,128)(2,1)S(1)} %all-to-all-done.recv_ref.refs_0_, bf16[8,16,384]{2,1,0:T(8,128)(2,1)} %collective-permute-done.refs_1_, bf16[8,16,384]{2,1,0:T(8,128)(2,1)S(1)} %collective-permute-done.1.refs_2_, ...), custom_call_target="tpu_custom_call" | custom-call | tf_op jit(solution)/shard_map/weights/pallas_call | solution.py:309
  39.6 2.0 %all-to-all-done.2 = bf16[32,8,96]{2,1,0:T(8,128)(2,1)S(1)} async-done(((bf16[32,8,96]{2,1,0:T(8,128)(2,1)}), bf16[32,8,96]{2,1,0:T(8,128)(2,1)S(1)}, u32[]{:S(2)}, u32[]{:S(2)}) %all-to-all-start.2) | async-done | bytes 49184 | tf_op jit(solution)/shard_map/all_to_all | solution.py:291
  41.6 0.6 %convert_reduce_fusion = f32[8,96]{1,0:T(8,128)} fusion(bf16[32,8,96]{2,1,0:T(8,128)(2,1)S(1)} %all-to-all-done.2), kind=kLoop, calls=%fused_computation | loop fusion | flops 48384 | bytes 52224 | tf_op jit(solution)/shard_map/reduce_sum | solution.py:339
Async XLA Ops:
  3.1 14.4 %all-to-all-start = ((bf16[8,16,384]{2,1,0:T(8,128)(2,1)}), bf16[8,16,384]{2,1,0:T(8,128)(2,1)S(1)}, u32[]{:S(2)}, u32[]{:S(2)}) async-start(bf16[8,16,384]{2,1,0:T(8,128)(2,1)} %slots.1), calls=%async_computation | async-start | bytes 196608 | tf_op jit(solution)/shard_map/all_to_all | solution.py:260
  10.3 1.3 %copy-start.2 = (bf16[1,384,1536]{2,1,0:T(8,128)(2,1)S(1)}, bf16[1,384,1536]{2,1,0:T(8,128)(2,1)}, u32[]{:S(2)}) copy-start(bf16[1,384,1536]{2,1,0:T(8,128)(2,1)} %param.7) | copy-start | bytes 3538948
  11.6 1.3 %copy-start.3 = (bf16[1,384,1536]{2,1,0:T(8,128)(2,1)S(1)}, bf16[1,384,1536]{2,1,0:T(8,128)(2,1)}, u32[]{:S(2)}) copy-start(bf16[1,384,1536]{2,1,0:T(8,128)(2,1)} %param.8) | copy-start | bytes 3538948
  17.5 12.4 %copy-start = (bf16[8,64,384]{2,1,0:T(8,128)(2,1)S(1)}, bf16[8,64,384]{2,1,0:T(8,128)(2,1)}, u32[]{:S(2)}) copy-start(bf16[8,64,384]{2,1,0:T(8,128)(2,1)} %param.5) | copy-start | bytes 1179652
  17.5 12.4 %copy-start.1 = (bf16[8,64,384]{2,1,0:T(8,128)(2,1)S(1)}, bf16[8,64,384]{2,1,0:T(8,128)(2,1)}, u32[]{:S(2)}) copy-start(bf16[8,64,384]{2,1,0:T(8,128)(2,1)} %param.9) | copy-start | bytes 1179652
  17.5 12.4 %copy-start.5 = (bf16[384,8]{0,1:T(8,128)(2,1)S(1)}, bf16[384,8]{0,1:T(8,128)(2,1)}, u32[]{:S(2)}) copy-start(bf16[384,8]{0,1:T(8,128)(2,1)} %param.6) | copy-start | bytes 18436
  19.4 10.4 %all-to-all-start.1 = ((bf16[8,16,384]{2,1,0:T(8,128)(2,1)}), bf16[8,16,384]{2,1,0:T(8,128)(2,1)S(1)}, u32[]{:S(2)}, u32[]{:S(2)}) async-start(bf16[8,16,384]{2,1,0:T(8,128)(2,1)} %expert.1), calls=%async_computation.1 | async-start | bytes 196608 | tf_op jit(solution)/shard_map/all_to_all | solution.py:268
  22.8 13.0 %collective-permute-start.2 = (bf16[8,16,384]{2,1,0:T(8,128)(2,1)S(1)}, bf16[8,16,384]{2,1,0:T(8,128)(2,1)S(1)}, u32[]{:S(2)}, u32[]{:S(2)}) collective-permute-start(bf16[8,16,384]{2,1,0:T(8,128)(2,1)S(1)} %all-to-all-done.recv_ref.refs_0_), channel_id=1, source_target_pairs={{0,3},{1,2},{2,1},{3,0},{4,7},{5,6},{6,5},{7,4},{8,11},{9,10},{10,... | collective-permute-start | bytes 294920 | tf_op jit(solution)/shard_map/ppermute | solution.py:272
  22.9 12.9 %collective-permute-start.1 = (bf16[8,16,384]{2,1,0:T(8,128)(2,1)S(1)}, bf16[8,16,384]{2,1,0:T(8,128)(2,1)S(1)}, u32[]{:S(2)}, u32[]{:S(2)}) collective-permute-start(bf16[8,16,384]{2,1,0:T(8,128)(2,1)S(1)} %all-to-all-done.recv_ref.refs_0_), channel_id=1, source_target_pairs={{0,2},{1,3},{2,0},{3,1},{4,6},{5,7},{6,4},{7,5},{8,10},{9,11},{10,... | collective-permute-start | bytes 294920 | tf_op jit(solution)/shard_map/ppermute | solution.py:272
  24.5 11.3 %collective-permute-start = (bf16[8,16,384]{2,1,0:T(8,128)(2,1)S(1)}, bf16[8,16,384]{2,1,0:T(8,128)(2,1)}, u32[]{:S(2)}, u32[]{:S(2)}) collective-permute-start(bf16[8,16,384]{2,1,0:T(8,128)(2,1)S(1)} %all-to-all-done.recv_ref.refs_0_), channel_id=1, source_target_pairs={{0,1},{1,0},{2,3},{3,2},{4,5},{5,4},{6,7},{7,6},{8,9},{9,8},{10,11... | collective-permute-start | bytes 294920 | tf_op jit(solution)/shard_map/ppermute | solution.py:272
  31.1 0.6 %copy-start.4 = (bf16[32,8,96]{2,1,0:T(8,128)(2,1)}, bf16[32,8,96]{2,1,0:T(8,128)(2,1)S(1)}, u32[]{:S(2)}) copy-start(bf16[32,8,96]{2,1,0:T(8,128)(2,1)S(1)} %get-tuple-element.23) | copy-start | bytes 147460
  31.7 10.0 %all-to-all-start.2 = ((bf16[32,8,96]{2,1,0:T(8,128)(2,1)}), bf16[32,8,96]{2,1,0:T(8,128)(2,1)S(1)}, u32[]{:S(2)}, u32[]{:S(2)}) async-start(bf16[32,8,96]{2,1,0:T(8,128)(2,1)} %copy-done.4), calls=%async_computation.2 | async-start | bytes 131072 | tf_op jit(solution)/shard_map/all_to_all | solution.py:291

commit v8 on v7

--- a/solution.py
+++ b/solution.py
@@ -122,22 +122,29 @@
     back_ref[...] = pair_rows(out, back, recv_ref.shape[0])
 
 
+def logits_grad(router, tokens, grad, images, read_back):
+    dispatch, combine, mask = softmaxes(router, tokens, images)
+    slot_out, slot_in_grad = split_rows(read_back())
+    disp = jnp.where(mask, dot(slot_in_grad, tokens, 1, 1), 0.0)
+    comb = fold_rows(jnp.where(mask, dot(slot_out, grad, 1, 1), 0.0), images)
+    mean = jnp.sum(dispatch * disp, axis=1, keepdims=True)
+    from_dispatch = fold_rows(dispatch * (disp - mean), images)
+    from_combine = combine * (comb - jnp.sum(combine * comb, axis=0, keepdims=True))
+    return (from_combine + from_dispatch).astype(BF16), dispatch, slot_in_grad
+
+
 def logits_kernel(
-    images, back_hbm, tokens_ref, router_ref, grad_ref, send_ref, logit_ref, back_ref, sem
+    images, back_hbm, tokens_ref, router_ref, grad_ref, send_ref, back_ref, sem
 ):
     load = pltpu.make_async_copy(back_hbm, back_ref, sem)
     load.start()
+
+    def read_back():
+        load.wait()
+        return back_ref[...]
+
     tokens = tokens_ref[...]
-    dispatch, combine, mask = softmaxes(router_ref[...], tokens, images)
-    load.wait()
-    slot_out, slot_in_grad = split_rows(back_ref[...])
-    disp = jnp.where(mask, dot(slot_in_grad, tokens, 1, 1), 0.0)
-    comb = fold_rows(jnp.where(mask, dot(slot_out, grad_ref[...], 1, 1), 0.0), images)
-    mean = jnp.sum(dispatch * disp, axis=1, keepdims=True)
-    from_dispatch = fold_rows(dispatch * (disp - mean), images)
-    from_combine = combine * (comb - jnp.sum(combine * comb, axis=0, keepdims=True))
-    logit_grad = (from_combine + from_dispatch).astype(BF16)
-    logit_ref[...] = logit_grad
+    logit_grad, _, _ = logits_grad(router_ref[...], tokens, grad_ref[...], images, read_back)
     part = dot(logit_grad, tokens, 1, 0)
     devices, _, width = send_ref.shape
     shares = part.shape[1] // width
@@ -147,12 +154,13 @@
             send_ref[device] = piece
 
 
-def tokens_kernel(images, back_ref, tokens_ref, router_ref, logit_ref, out_ref):
+def tokens_kernel(images, back_ref, tokens_ref, router_ref, grad_ref, out_ref):
     router = router_ref[...]
-    dispatch, _, _ = softmaxes(router, tokens_ref[...], images)
-    _, slot_in_grad = split_rows(back_ref[...])
+    logit_grad, dispatch, slot_in_grad = logits_grad(
+        router, tokens_ref[...], grad_ref[...], images, lambda: back_ref[...]
+    )
     out = dot(dispatch.astype(BF16), slot_in_grad, 0, 0)
-    out = out + dot(logit_ref[...], router, 0, 0)
+    out = out + dot(logit_grad, router, 0, 0)
     out_ref[...] = out.astype(BF16)
 
 
@@ -276,18 +284,17 @@
         spread = [lax.all_gather(recv, "dp", axis=0, tiled=False)]
 
     in_vmem = pl.BlockSpec(memory_space=pltpu.VMEM)
-    router_send, logit_grad = pl.pallas_call(
+    router_send = pl.pallas_call(
         functools.partial(logits_kernel, images),
         in_specs=[in_place] + [in_vmem] * 3,
-        out_shape=(
-            struct((owners * shares, experts, row_count), BF16),
-            struct((experts, columns), BF16),
-        ),
+        out_shape=struct((owners * shares, experts, row_count), BF16),
         scratch_shapes=[pltpu.VMEM(back.shape, BF16), pltpu.SemaphoreType.DMA],
         compiler_params=params,
         name="logits",
     )(slots_back, tokens2, router_rows, grad2)
-    share, router_send = lax.optimization_barrier((lax.axis_index("dp").reshape(1), router_send))
+    share, slots_back, router_send = lax.optimization_barrier(
+        (lax.axis_index("dp").reshape(1), slots_back, router_send)
+    )
     router_parts = lax.all_to_all(
         router_send,
         ("expert", "dp"),
@@ -301,7 +308,7 @@
         out_shape=struct((columns, width), BF16),
         compiler_params=params,
         name="tokens",
-    )(slots_back, tokens2, router_rows, logit_grad)
+    )(slots_back, tokens2, router_rows, grad2)
     in_smem = pl.BlockSpec(memory_space=pltpu.SMEM)
     out_shape = [struct((row_count, hidden), F32)] * 2
     if few:

time: 42.7 us -> 44.4 us (1.040)
  Pallas kernels: 11.4 us -> 12.3 us
  other arithmetic: 0.63 us -> 1.47 us
  starting transfers between devices: 15.1 us -> 15.8 us
  local copies, waits for them, and re-layouts: 3.16 us -> 2.55 us
    reduce_sum x1, other arithmetic: 0.63 us -> 1.47 us  [on_device(): router_grad = jnp.sum(router_parts.astype(F32), axis=0).T]
    all_to_all x1, starting transfers between devices: 2.54 us -> 3.29 us  [on_device(): lax.all_to_all(router_send, ('expert', 'dp'), split_axis=0, concat_axis=0...]
    pallas_call x1, Pallas kernels: 1.19 us -> 1.83 us  [on_device(): pl.pallas_call(functools.partial(logits_kernel, images), in_specs=[in_pla...]
    unnamed x12 -> x10, local copies, waits for them, and re-layouts: 3.16 us -> 2.55 us
  transfers between devices with their start and end apart: 6 -> 6, of which waited for: 3 -> 3; matrix products, arithmetic and copies ran while one was open for 0% -> 0% of each run, Pallas kernels for 17% -> 18%
where the time goes in v8:
time: 44.4 us; the launch traced here: 43.9 us
  starting transfers between devices  15.8 us (36%)
  Pallas kernels  12.3 us (28%)
  waiting for transfers between devices  11 us (25%)
  local copies, waits for them, and re-layouts  2.55 us (6%)
  other arithmetic  1.47 us (3%)
  between operations  0.7 us (2%)
    all_to_all x1, starting transfers between devices, on_device(): lax.all_to_all(sent, 'expert', split_axis=0, concat_axis=0, tiled=True)  7.26 us
    all_to_all x1, waiting for transfers between devices, on_device(): lax.all_to_all(back, 'expert', split_axis=0, concat_axis=0, tiled=True)  5.13 us
    all_to_all x1, waiting for transfers between devices, on_device(): lax.all_to_all(sent, 'expert', split_axis=0, concat_axis=0, tiled=True)  4.08 us
    pallas_call x1, Pallas kernels, on_device(): pl.pallas_call(functools.partial(weights_kernel, shares), in_specs=[in_sm...  3.8 us
    all_to_all x1, starting transfers between devices, on_device(): lax.all_to_all(back, 'expert', split_axis=0, concat_axis=0, tiled=True)  3.36 us
    all_to_all x1, starting transfers between devices, on_device(): lax.all_to_all(router_send, ('expert', 'dp'), split_axis=0, concat_axis=0...  3.29 us
    unnamed x10, local copies, waits for them, and re-layouts  2.55 us
    pallas_call x1, Pallas kernels, on_device(): pl.pallas_call(functools.partial(slots_kernel, images), in_specs=[in_plac...  2.44 us
  transfers between devices with their start and end apart: 6, of which 3 were waited for; matrix products, arithmetic and copies ran while one was open for 0% of the time, Pallas kernels for 18%

profile of v8, /device:TPU:0, one launch (start us, length us, event | category | flops | bytes accessed | tf_op | source)
XLA Modules:
  0.0 43.9 jit_solution(8347272484848849880)
XLA Ops:
  0.6 2.4 %slots.1 = bf16[8,16,384]{2,1,0:T(8,128)(2,1)} custom-call(bf16[512,384]{1,0:T(8,128)(2,1)} %bitcast.10, bf16[8,384]{1,0:T(8,128)(2,1)} %bitcast.18, bf16[512,384]{1,0:T(8,128)(2,1)} %bitcast.13), custom_call_target="tpu_custom_call" | custom-call | tf_op jit(solution)/shard_map/slots/pallas_call | solution.py:243
  3.1 7.3 %all-to-all-start = ((bf16[8,16,384]{2,1,0:T(8,128)(2,1)}), bf16[8,16,384]{2,1,0:T(8,128)(2,1)S(1)}, u32[]{:S(2)}, u32[]{:S(2)}) async-start(bf16[8,16,384]{2,1,0:T(8,128)(2,1)} %slots.1), calls=%async_computation | async-start | bytes 196608 | tf_op jit(solution)/shard_map/all_to_all | solution.py:268
  10.3 0.0 copy-start.2
  10.3 1.3 %copy-done.2 = bf16[1,384,1536]{2,1,0:T(8,128)(2,1)S(1)} copy-done((bf16[1,384,1536]{2,1,0:T(8,128)(2,1)S(1)}, bf16[1,384,1536]{2,1,0:T(8,128)(2,1)}, u32[]{:S(2)}) %copy-start.2) | copy-done | bytes 1179672
  11.6 0.0 copy-start.3
  11.6 1.3 %copy-done.3 = bf16[1,384,1536]{2,1,0:T(8,128)(2,1)S(1)} copy-done((bf16[1,384,1536]{2,1,0:T(8,128)(2,1)S(1)}, bf16[1,384,1536]{2,1,0:T(8,128)(2,1)}, u32[]{:S(2)}) %copy-start.3) | copy-done | bytes 1179672
  12.9 0.5 %stage.1 = (bf16[384,1536]{1,0:T(8,128)(2,1)S(1)}, bf16[384,1536]{1,0:T(8,128)(2,1)S(1)}) custom-call(bf16[384,1536]{1,0:T(8,128)(2,1)S(1)} %bitcast.16, bf16[384,1536]{1,0:T(8,128)(2,1)S(1)} %bitcast.17), custom_call_target="tpu_custom_call" | custom-call | bytes 4718592 | tf_op jit(solution)/shard_map/stage/pallas_call | solution.py:256
  13.4 4.1 %all-to-all-done.recv_ref.refs_0_ = bf16[8,16,384]{2,1,0:T(8,128)(2,1)S(1)} async-done(((bf16[8,16,384]{2,1,0:T(8,128)(2,1)}), bf16[8,16,384]{2,1,0:T(8,128)(2,1)S(1)}, u32[]{:S(2)}, u32[]{:S(2)}) %all-to-all-start) | async-done | bytes 98336 | tf_op jit(solution)/shard_map/all_to_all | solution.py:268
  17.5 0.0 copy-start
  17.5 0.0 copy-start.1
  17.5 0.0 copy-start.4
  17.5 1.9 %expert.1 = bf16[8,16,384]{2,1,0:T(8,128)(2,1)} custom-call(bf16[8,16,384]{2,1,0:T(8,128)(2,1)S(1)} %all-to-all-done.recv_ref.refs_0_, bf16[384,1536]{1,0:T(8,128)(2,1)S(1)} %get-tuple-element.13.win_ref.refs_4_, bf16[384,1536]{1,0:T(8,128)(2,1)S(1)} %get-tuple-element.14.wout_ref.refs_5_), custom_call_target="tpu_custom_call" | custom-call | tf_op jit(solution)/shard_map/expert/pallas_call | solution.py:269
  19.4 3.4 %all-to-all-start.1 = ((bf16[8,16,384]{2,1,0:T(8,128)(2,1)}), bf16[8,16,384]{2,1,0:T(8,128)(2,1)S(1)}, u32[]{:S(2)}, u32[]{:S(2)}) async-start(bf16[8,16,384]{2,1,0:T(8,128)(2,1)} %expert.1), calls=%async_computation.1 | async-start | bytes 196608 | tf_op jit(solution)/shard_map/all_to_all | solution.py:276
  22.8 0.1 collective-permute-start.2
  22.9 1.6 %collective-permute-start.1 = (bf16[8,16,384]{2,1,0:T(8,128)(2,1)S(1)}, bf16[8,16,384]{2,1,0:T(8,128)(2,1)S(1)}, u32[]{:S(2)}, u32[]{:S(2)}) collective-permute-start(bf16[8,16,384]{2,1,0:T(8,128)(2,1)S(1)} %all-to-all-done.recv_ref.refs_0_), channel_id=1, source_target_pairs={{0,2},{1,3},{2,0},{3,1},{4,6},{5,7},{6,4},{7,5},{8,10},{9,11},{10,... | collective-permute-start | bytes 294920 | tf_op jit(solution)/shard_map/ppermute | solution.py:280
  24.5 0.3 collective-permute-start
  24.7 5.1 %all-to-all-done.1.back_hbm.back_ref = bf16[8,16,384]{2,1,0:T(8,128)(2,1)S(1)} async-done(((bf16[8,16,384]{2,1,0:T(8,128)(2,1)}), bf16[8,16,384]{2,1,0:T(8,128)(2,1)S(1)}, u32[]{:S(2)}, u32[]{:S(2)}) %all-to-all-start.1) | async-done | bytes 98336 | tf_op jit(solution)/shard_map/all_to_all | solution.py:276
  29.9 0.0 copy-done
  29.9 0.0 copy-done.1
  29.9 0.0 copy-done.4
  29.9 1.8 %logits.1 = bf16[32,8,96]{2,1,0:T(8,128)(2,1)} custom-call(bf16[8,16,384]{2,1,0:T(8,128)(2,1)S(1)} %all-to-all-done.1.back_hbm.back_ref, bf16[512,384]{1,0:T(8,128)(2,1)S(1)} %bitcast.11, bf16[8,384]{1,0:T(8,128)(2,1)S(1)} %bitcast.19, bf16[512,384]{1,0:T(8,128)(2,1)S(1)} %bitcast.14), custom_call_target="tpu_custom_call" | custom-call | tf_op jit(solution)/shard_map/logits/pallas_call | solution.py:287
  31.7 3.3 %all-to-all-start.2 = ((bf16[32,8,96]{2,1,0:T(8,128)(2,1)}), bf16[32,8,96]{2,1,0:T(8,128)(2,1)}, u32[]{:S(2)}, u32[]{:S(2)}) async-start(bf16[32,8,96]{2,1,0:T(8,128)(2,1)} %logits.1), calls=%async_computation.2 | async-start | bytes 131072 | tf_op jit(solution)/shard_map/all_to_all | solution.py:298
  35.0 1.8 %tokens.1 = bf16[512,384]{1,0:T(8,128)(2,1)} custom-call(bf16[8,16,384]{2,1,0:T(8,128)(2,1)S(1)} %all-to-all-done.1.back_hbm.back_ref, bf16[512,384]{1,0:T(8,128)(2,1)S(1)} %bitcast.12, bf16[8,384]{1,0:T(8,128)(2,1)S(1)} %bitcast.20, bf16[512,384]{1,0:T(8,128)(2,1)S(1)} %bitcast.15), custom_call_target="tpu_custom_call" | custom-call | tf_op jit(solution)/shard_map/tokens/pallas_call | solution.py:306
  36.8 0.0 collective-permute-done.2.refs_3_
  36.8 0.0 collective-permute-done.1.refs_2_
  36.8 0.0 collective-permute-done.refs_1_
  36.8 3.8 %weights.1 = (f32[96,1536]{1,0:T(8,128)}, f32[96,1536]{1,0:T(8,128)}) custom-call(s32[1]{0:T(128)} %bitcast.share_ref, bf16[8,16,384]{2,1,0:T(8,128)(2,1)S(1)} %all-to-all-done.recv_ref.refs_0_, bf16[8,16,384]{2,1,0:T(8,128)(2,1)} %collective-permute-done.refs_1_, bf16[8,16,384]{2,1,0:T(8,128)(2,1)S(1)} %collective-permute-done.1.refs_2_, ...), custom_call_target="tpu_custom_call" | custom-call | tf_op jit(solution)/shard_map/weights/pallas_call | solution.py:316
  40.6 1.7 %all-to-all-done.2 = bf16[32,8,96]{2,1,0:T(8,128)(2,1)} async-done(((bf16[32,8,96]{2,1,0:T(8,128)(2,1)}), bf16[32,8,96]{2,1,0:T(8,128)(2,1)}, u32[]{:S(2)}, u32[]{:S(2)}) %all-to-all-start.2) | async-done | bytes 49184 | tf_op jit(solution)/shard_map/all_to_all | solution.py:298
  42.4 1.5 %convert_reduce_fusion = f32[8,96]{1,0:T(8,128)} fusion(bf16[32,8,96]{2,1,0:T(8,128)(2,1)} %all-to-all-done.2), kind=kLoop, calls=%fused_computation | loop fusion | flops 48384 | bytes 52224 | tf_op jit(solution)/shard_map/reduce_sum | solution.py:346
Async XLA Ops:
  3.1 14.4 %all-to-all-start = ((bf16[8,16,384]{2,1,0:T(8,128)(2,1)}), bf16[8,16,384]{2,1,0:T(8,128)(2,1)S(1)}, u32[]{:S(2)}, u32[]{:S(2)}) async-start(bf16[8,16,384]{2,1,0:T(8,128)(2,1)} %slots.1), calls=%async_computation | async-start | bytes 196608 | tf_op jit(solution)/shard_map/all_to_all | solution.py:268
  10.3 1.3 %copy-start.2 = (bf16[1,384,1536]{2,1,0:T(8,128)(2,1)S(1)}, bf16[1,384,1536]{2,1,0:T(8,128)(2,1)}, u32[]{:S(2)}) copy-start(bf16[1,384,1536]{2,1,0:T(8,128)(2,1)} %param.7) | copy-start | bytes 3538948
  11.6 1.3 %copy-start.3 = (bf16[1,384,1536]{2,1,0:T(8,128)(2,1)S(1)}, bf16[1,384,1536]{2,1,0:T(8,128)(2,1)}, u32[]{:S(2)}) copy-start(bf16[1,384,1536]{2,1,0:T(8,128)(2,1)} %param.8) | copy-start | bytes 3538948
  17.5 12.4 %copy-start = (bf16[8,64,384]{2,1,0:T(8,128)(2,1)S(1)}, bf16[8,64,384]{2,1,0:T(8,128)(2,1)}, u32[]{:S(2)}) copy-start(bf16[8,64,384]{2,1,0:T(8,128)(2,1)} %param.5) | copy-start | bytes 1179652
  17.5 12.4 %copy-start.1 = (bf16[8,64,384]{2,1,0:T(8,128)(2,1)S(1)}, bf16[8,64,384]{2,1,0:T(8,128)(2,1)}, u32[]{:S(2)}) copy-start(bf16[8,64,384]{2,1,0:T(8,128)(2,1)} %param.9) | copy-start | bytes 1179652
  17.5 12.4 %copy-start.4 = (bf16[384,8]{0,1:T(8,128)(2,1)S(1)}, bf16[384,8]{0,1:T(8,128)(2,1)}, u32[]{:S(2)}) copy-start(bf16[384,8]{0,1:T(8,128)(2,1)} %param.6) | copy-start | bytes 18436
  19.4 10.4 %all-to-all-start.1 = ((bf16[8,16,384]{2,1,0:T(8,128)(2,1)}), bf16[8,16,384]{2,1,0:T(8,128)(2,1)S(1)}, u32[]{:S(2)}, u32[]{:S(2)}) async-start(bf16[8,16,384]{2,1,0:T(8,128)(2,1)} %expert.1), calls=%async_computation.1 | async-start | bytes 196608 | tf_op jit(solution)/shard_map/all_to_all | solution.py:276
  22.8 14.0 %collective-permute-start.2 = (bf16[8,16,384]{2,1,0:T(8,128)(2,1)S(1)}, bf16[8,16,384]{2,1,0:T(8,128)(2,1)S(1)}, u32[]{:S(2)}, u32[]{:S(2)}) collective-permute-start(bf16[8,16,384]{2,1,0:T(8,128)(2,1)S(1)} %all-to-all-done.recv_ref.refs_0_), channel_id=1, source_target_pairs={{0,3},{1,2},{2,1},{3,0},{4,7},{5,6},{6,5},{7,4},{8,11},{9,10},{10,... | collective-permute-start | bytes 294920 | tf_op jit(solution)/shard_map/ppermute | solution.py:280
  22.9 14.0 %collective-permute-start.1 = (bf16[8,16,384]{2,1,0:T(8,128)(2,1)S(1)}, bf16[8,16,384]{2,1,0:T(8,128)(2,1)S(1)}, u32[]{:S(2)}, u32[]{:S(2)}) collective-permute-start(bf16[8,16,384]{2,1,0:T(8,128)(2,1)S(1)} %all-to-all-done.recv_ref.refs_0_), channel_id=1, source_target_pairs={{0,2},{1,3},{2,0},{3,1},{4,6},{5,7},{6,4},{7,5},{8,10},{9,11},{10,... | collective-permute-start | bytes 294920 | tf_op jit(solution)/shard_map/ppermute | solution.py:280
  24.5 12.4 %collective-permute-start = (bf16[8,16,384]{2,1,0:T(8,128)(2,1)S(1)}, bf16[8,16,384]{2,1,0:T(8,128)(2,1)}, u32[]{:S(2)}, u32[]{:S(2)}) collective-permute-start(bf16[8,16,384]{2,1,0:T(8,128)(2,1)S(1)} %all-to-all-done.recv_ref.refs_0_), channel_id=1, source_target_pairs={{0,1},{1,0},{2,3},{3,2},{4,5},{5,4},{6,7},{7,6},{8,9},{9,8},{10,11... | collective-permute-start | bytes 294920 | tf_op jit(solution)/shard_map/ppermute | solution.py:280
  31.7 10.7 %all-to-all-start.2 = ((bf16[32,8,96]{2,1,0:T(8,128)(2,1)}), bf16[32,8,96]{2,1,0:T(8,128)(2,1)}, u32[]{:S(2)}, u32[]{:S(2)}) async-start(bf16[32,8,96]{2,1,0:T(8,128)(2,1)} %logits.1), calls=%async_computation.2 | async-start | bytes 131072 | tf_op jit(solution)/shard_map/all_to_all | solution.py:298

commit v9 on v7

--- a/solution.py
+++ b/solution.py
@@ -76,36 +76,34 @@
     return block, combine, mask
 
 
-def slots_kernel(images, tokens_hbm, router_hbm, grad_hbm, sent_ref, *scratch):
+def slots_kernel(
+    images, tokens_hbm, router_hbm, grad_hbm, win_hbm, wout_hbm, sent_ref, win_out, wout_out, *scratch
+):
     tokens_ref, router_ref, grad_ref, sems = scratch
-    first = [
-        pltpu.make_async_copy(tokens_hbm, tokens_ref, sems.at[0]),
-        pltpu.make_async_copy(router_hbm, router_ref, sems.at[1]),
+    pairs = (
+        (tokens_hbm, tokens_ref),
+        (router_hbm, router_ref),
+        (grad_hbm, grad_ref),
+        (win_hbm, win_out),
+        (wout_hbm, wout_out),
+    )
+    loads = [
+        pltpu.make_async_copy(source, target, sems.at[i])
+        for i, (source, target) in enumerate(pairs)
     ]
-    second = [pltpu.make_async_copy(grad_hbm, grad_ref, sems.at[2])]
-    for load in first + second:
+    for load in loads:
         load.start()
-    for load in first:
-        load.wait()
+    loads[0].wait()
+    loads[1].wait()
     tokens = tokens_ref[...]
     block, combine, mask = softmaxes(router_ref[...], tokens, images)
     combine_block = jnp.where(mask, spread_rows(combine, images), 0.0)
     slot_in = dot(block.astype(BF16), tokens, 1, 0)
-    for load in second:
-        load.wait()
+    loads[2].wait()
     slot_grad = dot(combine_block.astype(BF16), grad_ref[...], 1, 0)
     sent_ref[...] = pair_rows(slot_in, slot_grad, combine.shape[0])
-
-
-def stage_kernel(win_hbm, wout_hbm, win_ref, wout_ref, sems):
-    loads = (
-        pltpu.make_async_copy(win_hbm, win_ref, sems.at[0]),
-        pltpu.make_async_copy(wout_hbm, wout_ref, sems.at[1]),
-    )
-    for load in loads:
-        load.start()
-    for load in loads:
-        load.wait()
+    loads[3].wait()
+    loads[4].wait()
 
 
 def expert_kernel(recv_ref, win_ref, wout_ref, back_ref, *, step):
@@ -232,31 +230,24 @@
         return jax.ShapeDtypeStruct(shape, dtype)
 
     in_place = pl.BlockSpec(memory_space=pl.ANY)
-    sent = pl.pallas_call(
+    sent, w_in2, w_out2 = pl.pallas_call(
         functools.partial(slots_kernel, images),
-        in_specs=[in_place] * 3,
-        out_shape=struct((experts, 2 * images, width), BF16),
+        in_specs=[in_place] * 5,
+        out_specs=[pl.BlockSpec(memory_space=pltpu.VMEM), in_place, in_place],
+        out_shape=[
+            struct((experts, 2 * images, width), BF16),
+            struct((width, hidden), BF16),
+            struct((width, hidden), BF16),
+        ],
         scratch_shapes=[
             pltpu.VMEM((columns, width), BF16),
             pltpu.VMEM((experts, width), BF16),
             pltpu.VMEM((columns, width), BF16),
-            pltpu.SemaphoreType.DMA((3,)),
+            pltpu.SemaphoreType.DMA((5,)),
         ],
         compiler_params=whole,
         name="slots",
-    )(tokens2, router_rows, grad2)
-    w_in2, w_out2 = pl.pallas_call(
-        stage_kernel,
-        in_specs=[in_place] * 2,
-        out_specs=[in_place] * 2,
-        out_shape=[struct((width, hidden), BF16)] * 2,
-        scratch_shapes=[pltpu.SemaphoreType.DMA((2,))],
-        compiler_params=pltpu.CompilerParams(vmem_limit_bytes=1024 * 1024),
-        cost_estimate=pl.CostEstimate(
-            flops=0, bytes_accessed=8 * width * hidden, transcendentals=0
-        ),
-        name="stage",
-    )(w_in2, w_out2)
+    )(tokens2, router_rows, grad2, w_in2, w_out2)
     recv = lax.all_to_all(sent, "expert", split_axis=0, concat_axis=0, tiled=True)
     back = pl.pallas_call(
         functools.partial(expert_kernel, step=512),

time: 42.7 us -> 116 us (2.72)
  Pallas kernels: 11.4 us -> 81.7 us
  blocking collectives: 0 us -> 14.4 us
  starting transfers between devices: 15.1 us -> 7.98 us
  waiting for transfers between devices: 11.3 us -> 7.16 us
    pallas_call x1, Pallas kernels: 2.44 us -> 73.3 us  [on_device(): pl.pallas_call(functools.partial(slots_kernel, images), in_specs=[in_plac...]
    all_to_all x0 -> x1, blocking collectives: none -> 14.4 us  [on_device(): lax.all_to_all(sent, 'expert', split_axis=0, concat_axis=0, tiled=True)]
    all_to_all x1 -> x0, starting transfers between devices: 7.26 us -> none  [on_device(): lax.all_to_all(sent, 'expert', split_axis=0, concat_axis=0, tiled=True)]
    all_to_all x1 -> x0, waiting for transfers between devices: 4.08 us -> none  [on_device(): lax.all_to_all(sent, 'expert', split_axis=0, concat_axis=0, tiled=True)]
    unnamed x12 -> x16, local copies, waits for them, and re-layouts: 3.16 us -> 3.17 us
  transfers between devices with their start and end apart: 6 -> 5, of which waited for: 3 -> 2; matrix products, arithmetic and copies ran while one was open for 0% -> 0% of each run, Pallas kernels for 17% -> 6%
where the time goes in v9:
time: 116 us
  Pallas kernels  81.7 us (70%)
  blocking collectives  14.4 us (12%)
  starting transfers between devices  7.98 us (7%)
  waiting for transfers between devices  7.16 us (6%)
  local copies, waits for them, and re-layouts  3.17 us (3%)
    pallas_call x1, Pallas kernels, on_device(): pl.pallas_call(functools.partial(slots_kernel, images), in_specs=[in_plac...  73.3 us
    all_to_all x1, blocking collectives, on_device(): lax.all_to_all(sent, 'expert', split_axis=0, concat_axis=0, tiled=True)  14.4 us
    all_to_all x1, waiting for transfers between devices, on_device(): lax.all_to_all(back, 'expert', split_axis=0, concat_axis=0, tiled=True)  5.13 us
    pallas_call x1, Pallas kernels, on_device(): pl.pallas_call(functools.partial(weights_kernel, shares), in_specs=[in_sm...  3.79 us
    all_to_all x1, starting transfers between devices, on_device(): lax.all_to_all(back, 'expert', split_axis=0, concat_axis=0, tiled=True)  3.49 us
    unnamed x16, local copies, waits for them, and re-layouts  3.17 us
    all_to_all x1, starting transfers between devices, on_device(): lax.all_to_all(router_send, ('expert', 'dp'), split_axis=0, concat_axis=0...  2.57 us
  transfers between devices with their start and end apart: 5, of which 2 were waited for; matrix products, arithmetic and copies ran while one was open for 0% of the time, Pallas kernels for 6%

profile of v9, /device:TPU:0, one launch (start us, length us, event | category | flops | bytes accessed | tf_op | source)
XLA Modules:
  0.0 115.8 jit_solution(5804253081591950664)
XLA Ops:
  0.6 73.3 %slots.1 = (bf16[8,16,384]{2,1,0:T(8,128)(2,1)}, bf16[384,1536]{1,0:T(8,128)(2,1)}, bf16[384,1536]{1,0:T(8,128)(2,1)}) custom-call(bf16[512,384]{1,0:T(8,128)(2,1)} %bitcast.10, bf16[8,384]{1,0:T(8,128)(2,1)} %bitcast.15, bf16[512,384]{1,0:T(8,128)(2,1)} %bitcast.13, bf16[384,1536]{1,0:T(8,128)(2,1)} %bitcast.18, bf16[384,1536]{1,0:T(8,128)(2,1)} %bitcast.19), custom_call_target="tpu_custom_call" | custom-call | tf_op jit(solution)/shard_map/slots/pallas_call | solution.py:233
  73.9 14.4 %all_to_all.15.recv_ref.refs_0_ = bf16[8,16,384]{2,1,0:T(8,128)(2,1)S(1)} all-to-all(bf16[8,16,384]{2,1,0:T(8,128)(2,1)} %get-tuple-element.15), channel_id=1, replica_groups=mesh['expert'=8,'dp'=4] {'expert'}, dimensions={0} | all-to-all | bytes 196608 | tf_op jit(solution)/shard_map/all_to_all | solution.py:251
  88.3 0.0 copy-start
  88.3 1.3 %copy-done = bf16[384,1536]{1,0:T(8,128)(2,1)S(1)} copy-done((bf16[384,1536]{1,0:T(8,128)(2,1)S(1)}, bf16[384,1536]{1,0:T(8,128)(2,1)}, u32[]{:S(2)}) %copy-start) | copy-done | bytes 1179672
  89.6 0.0 copy-start.2
  89.6 1.3 %copy-done.2 = bf16[384,1536]{1,0:T(8,128)(2,1)S(1)} copy-done((bf16[384,1536]{1,0:T(8,128)(2,1)S(1)}, bf16[384,1536]{1,0:T(8,128)(2,1)}, u32[]{:S(2)}) %copy-start.2) | copy-done | bytes 1179672
  90.8 0.0 copy-start.4
  90.8 0.0 copy-start.5
  90.8 0.0 copy-start.7
  90.8 0.0 copy-start.3
  90.8 1.9 %expert.1 = bf16[8,16,384]{2,1,0:T(8,128)(2,1)} custom-call(bf16[8,16,384]{2,1,0:T(8,128)(2,1)S(1)} %all_to_all.15.recv_ref.refs_0_, bf16[384,1536]{1,0:T(8,128)(2,1)S(1)} %copy-done, bf16[384,1536]{1,0:T(8,128)(2,1)S(1)} %copy-done.2), custom_call_target="tpu_custom_call" | custom-call | tf_op jit(solution)/shard_map/expert/pallas_call | solution.py:252
  92.8 0.0 copy-start.1
  92.8 3.5 %all-to-all-start.1 = ((bf16[8,16,384]{2,1,0:T(8,128)(2,1)}), bf16[8,16,384]{2,1,0:T(8,128)(2,1)S(1)}, u32[]{:S(2)}, u32[]{:S(2)}) async-start(bf16[8,16,384]{2,1,0:T(8,128)(2,1)} %expert.1), calls=%async_computation.1 | async-start | bytes 196608 | tf_op jit(solution)/shard_map/all_to_all | solution.py:259
  96.3 0.1 collective-permute-start.2
  96.4 1.6 %collective-permute-start.1 = (bf16[8,16,384]{2,1,0:T(8,128)(2,1)S(1)}, bf16[8,16,384]{2,1,0:T(8,128)(2,1)S(1)}, u32[]{:S(2)}, u32[]{:S(2)}) collective-permute-start(bf16[8,16,384]{2,1,0:T(8,128)(2,1)S(1)} %all_to_all.15.recv_ref.refs_0_), channel_id=1, source_target_pairs={{0,2},{1,3},{2,0},{3,1},{4,6},{5,7},{6,4},{7,5},{8,10},{9,11},{10,... | collective-permute-start | bytes 294920 | tf_op jit(solution)/shard_map/ppermute | solution.py:263
  98.0 0.3 collective-permute-start
  98.2 5.1 %all-to-all-done.1.back_hbm.back_ref = bf16[8,16,384]{2,1,0:T(8,128)(2,1)S(1)} async-done(((bf16[8,16,384]{2,1,0:T(8,128)(2,1)}), bf16[8,16,384]{2,1,0:T(8,128)(2,1)S(1)}, u32[]{:S(2)}, u32[]{:S(2)}) %all-to-all-start.1) | async-done | bytes 98336 | tf_op jit(solution)/shard_map/all_to_all | solution.py:259
  103.4 0.0 copy-done.4
  103.4 0.0 copy-done.5
  103.4 0.0 copy-done.7
  103.4 1.2 %logits.1 = (bf16[32,8,96]{2,1,0:T(8,128)(2,1)S(1)}, bf16[8,512]{1,0:T(8,128)(2,1)S(1)}) custom-call(bf16[8,16,384]{2,1,0:T(8,128)(2,1)S(1)} %all-to-all-done.1.back_hbm.back_ref, bf16[512,384]{1,0:T(8,128)(2,1)S(1)} %bitcast.11, bf16[8,384]{1,0:T(8,128)(2,1)S(1)} %bitcast.16, bf16[512,384]{1,0:T(8,128)(2,1)S(1)} %bitcast.14), custom_call_target="tpu_custom_call" | custom-call | tf_op jit(solution)/shard_map/logits/pallas_call | solution.py:270
  104.6 0.0 copy-start.6
  104.6 0.6 copy-done.6
  105.2 2.6 %all-to-all-start.2 = ((bf16[32,8,96]{2,1,0:T(8,128)(2,1)}), bf16[32,8,96]{2,1,0:T(8,128)(2,1)S(1)}, u32[]{:S(2)}, u32[]{:S(2)}) async-start(bf16[32,8,96]{2,1,0:T(8,128)(2,1)} %copy-done.6), calls=%async_computation.2 | async-start | bytes 131072 | tf_op jit(solution)/shard_map/all_to_all | solution.py:282
  107.8 1.6 %tokens.1 = bf16[512,384]{1,0:T(8,128)(2,1)} custom-call(bf16[8,16,384]{2,1,0:T(8,128)(2,1)S(1)} %all-to-all-done.1.back_hbm.back_ref, bf16[512,384]{1,0:T(8,128)(2,1)S(1)} %bitcast.12, bf16[8,384]{1,0:T(8,128)(2,1)S(1)} %bitcast.17, bf16[8,512]{1,0:T(8,128)(2,1)S(1)} %get-tuple-element.19.logit_ref), custom_call_target="tpu_custom_call" | custom-call | tf_op jit(solution)/shard_map/tokens/pallas_call | solution.py:290
  109.3 0.0 collective-permute-done.2.refs_3_
  109.3 0.0 collective-permute-done.1.refs_2_
  109.3 0.0 collective-permute-done.refs_1_
  109.3 0.0 copy-done.3
  109.3 0.0 copy-done.1
  109.3 3.8 %weights.1 = (f32[96,1536]{1,0:T(8,128)}, f32[96,1536]{1,0:T(8,128)}) custom-call(s32[1]{0:T(128)} %bitcast.6.share_ref, bf16[8,16,384]{2,1,0:T(8,128)(2,1)S(1)} %all_to_all.15.recv_ref.refs_0_, bf16[8,16,384]{2,1,0:T(8,128)(2,1)} %collective-permute-done.refs_1_, bf16[8,16,384]{2,1,0:T(8,128)(2,1)S(1)} %collective-permute-done.1.refs_2_, ...), custom_call_target="tpu_custom_call" | custom-call | tf_op jit(solution)/shard_map/weights/pallas_call | solution.py:300
  113.1 2.0 %all-to-all-done.2 = bf16[32,8,96]{2,1,0:T(8,128)(2,1)S(1)} async-done(((bf16[32,8,96]{2,1,0:T(8,128)(2,1)}), bf16[32,8,96]{2,1,0:T(8,128)(2,1)S(1)}, u32[]{:S(2)}, u32[]{:S(2)}) %all-to-all-start.2) | async-done | bytes 49184 | tf_op jit(solution)/shard_map/all_to_all | solution.py:282
  115.2 0.6 convert_reduce_fusion
Async XLA Ops:
  88.3 1.3 %copy-start = (bf16[384,1536]{1,0:T(8,128)(2,1)S(1)}, bf16[384,1536]{1,0:T(8,128)(2,1)}, u32[]{:S(2)}) copy-start(bf16[384,1536]{1,0:T(8,128)(2,1)} %get-tuple-element.16.win_ref.refs_4_) | copy-start | bytes 3538948
  89.6 1.3 %copy-start.2 = (bf16[384,1536]{1,0:T(8,128)(2,1)S(1)}, bf16[384,1536]{1,0:T(8,128)(2,1)}, u32[]{:S(2)}) copy-start(bf16[384,1536]{1,0:T(8,128)(2,1)} %get-tuple-element.17.wout_ref.refs_5_) | copy-start | bytes 3538948
  90.8 12.5 %copy-start.4 = (bf16[8,64,384]{2,1,0:T(8,128)(2,1)S(1)}, bf16[8,64,384]{2,1,0:T(8,128)(2,1)}, u32[]{:S(2)}) copy-start(bf16[8,64,384]{2,1,0:T(8,128)(2,1)} %param.5) | copy-start | bytes 1179652
  90.8 12.5 %copy-start.5 = (bf16[8,64,384]{2,1,0:T(8,128)(2,1)S(1)}, bf16[8,64,384]{2,1,0:T(8,128)(2,1)}, u32[]{:S(2)}) copy-start(bf16[8,64,384]{2,1,0:T(8,128)(2,1)} %param.9) | copy-start | bytes 1179652
  90.8 12.5 %copy-start.7 = (bf16[384,8]{0,1:T(8,128)(2,1)S(1)}, bf16[384,8]{0,1:T(8,128)(2,1)}, u32[]{:S(2)}) copy-start(bf16[384,8]{0,1:T(8,128)(2,1)} %param.6) | copy-start | bytes 18436
  90.8 18.5 %copy-start.3 = (bf16[384,1536]{1,0:T(8,128)(2,1)S(1)}, bf16[384,1536]{1,0:T(8,128)(2,1)}, u32[]{:S(2)}) copy-start(bf16[384,1536]{1,0:T(8,128)(2,1)} %get-tuple-element.17.wout_ref.refs_5_) | copy-start | bytes 3538948
  92.8 16.5 %copy-start.1 = (bf16[384,1536]{1,0:T(8,128)(2,1)S(1)}, bf16[384,1536]{1,0:T(8,128)(2,1)}, u32[]{:S(2)}) copy-start(bf16[384,1536]{1,0:T(8,128)(2,1)} %get-tuple-element.16.win_ref.refs_4_) | copy-start | bytes 3538948
  92.8 10.6 %all-to-all-start.1 = ((bf16[8,16,384]{2,1,0:T(8,128)(2,1)}), bf16[8,16,384]{2,1,0:T(8,128)(2,1)S(1)}, u32[]{:S(2)}, u32[]{:S(2)}) async-start(bf16[8,16,384]{2,1,0:T(8,128)(2,1)} %expert.1), calls=%async_computation.1 | async-start | bytes 196608 | tf_op jit(solution)/shard_map/all_to_all | solution.py:259
  96.3 13.0 %collective-permute-start.2 = (bf16[8,16,384]{2,1,0:T(8,128)(2,1)S(1)}, bf16[8,16,384]{2,1,0:T(8,128)(2,1)S(1)}, u32[]{:S(2)}, u32[]{:S(2)}) collective-permute-start(bf16[8,16,384]{2,1,0:T(8,128)(2,1)S(1)} %all_to_all.15.recv_ref.refs_0_), channel_id=1, source_target_pairs={{0,3},{1,2},{2,1},{3,0},{4,7},{5,6},{6,5},{7,4},{8,11},{9,10},{10,... | collective-permute-start | bytes 294920 | tf_op jit(solution)/shard_map/ppermute | solution.py:263
  96.4 12.9 %collective-permute-start.1 = (bf16[8,16,384]{2,1,0:T(8,128)(2,1)S(1)}, bf16[8,16,384]{2,1,0:T(8,128)(2,1)S(1)}, u32[]{:S(2)}, u32[]{:S(2)}) collective-permute-start(bf16[8,16,384]{2,1,0:T(8,128)(2,1)S(1)} %all_to_all.15.recv_ref.refs_0_), channel_id=1, source_target_pairs={{0,2},{1,3},{2,0},{3,1},{4,6},{5,7},{6,4},{7,5},{8,10},{9,11},{10,... | collective-permute-start | bytes 294920 | tf_op jit(solution)/shard_map/ppermute | solution.py:263
  98.0 11.4 %collective-permute-start = (bf16[8,16,384]{2,1,0:T(8,128)(2,1)S(1)}, bf16[8,16,384]{2,1,0:T(8,128)(2,1)}, u32[]{:S(2)}, u32[]{:S(2)}) collective-permute-start(bf16[8,16,384]{2,1,0:T(8,128)(2,1)S(1)} %all_to_all.15.recv_ref.refs_0_), channel_id=1, source_target_pairs={{0,1},{1,0},{2,3},{3,2},{4,5},{5,4},{6,7},{7,6},{8,9},{9,8},{10,11... | collective-permute-start | bytes 294920 | tf_op jit(solution)/shard_map/ppermute | solution.py:263
  104.6 0.6 copy-start.6
  105.2 10.0 %all-to-all-start.2 = ((bf16[32,8,96]{2,1,0:T(8,128)(2,1)}), bf16[32,8,96]{2,1,0:T(8,128)(2,1)S(1)}, u32[]{:S(2)}, u32[]{:S(2)}) async-start(bf16[32,8,96]{2,1,0:T(8,128)(2,1)} %copy-done.6), calls=%async_computation.2 | async-start | bytes 131072 | tf_op jit(solution)/shard_map/all_to_all | solution.py:282

commit v10 on v7

--- a/solution.py
+++ b/solution.py
@@ -72,7 +72,7 @@
     combine = combine / jnp.sum(combine, axis=0, keepdims=True)
     block = jnp.where(mask, spread_rows(logits, images), -jnp.inf)
     block = jnp.exp(block - jnp.max(block, axis=1, keepdims=True))
-    block = block / jnp.sum(block, axis=1, keepdims=True)
+    block = block * (1.0 / jnp.sum(block, axis=1, keepdims=True))
     return block, combine, mask
 
 
@@ -112,13 +112,19 @@
     slots, cotan = split_rows(recv_ref[...])
     out = jnp.zeros(slots.shape, F32)
     back = jnp.zeros(slots.shape, F32)
-    for start in range(0, win_ref.shape[1], step):
-        w_in = win_ref[:, start : start + step]
-        w_out = wout_ref[:, start : start + step]
-        value, slope = gelu_pair(dot(slots, w_in, 1, 0))
-        pre_grad = dot(cotan, w_out, 1, 0) * slope
-        out = out + dot(value.astype(BF16), w_out, 1, 1)
-        back = back + dot(pre_grad.astype(BF16), w_in, 1, 1)
+    parts = [slice(start, start + step) for start in range(0, win_ref.shape[1], step)]
+
+    def first(part):
+        return dot(slots, win_ref[:, part], 1, 0), dot(cotan, wout_ref[:, part], 1, 0)
+
+    ahead = first(parts[0])
+    for k, part in enumerate(parts):
+        pre_act, hid_grad = ahead
+        if k + 1 < len(parts):
+            ahead = first(parts[k + 1])
+        value, slope = gelu_pair(pre_act)
+        out = out + dot(value.astype(BF16), wout_ref[:, part], 1, 1)
+        back = back + dot((hid_grad * slope).astype(BF16), win_ref[:, part], 1, 1)
     back_ref[...] = pair_rows(out, back, recv_ref.shape[0])
 
 
@@ -131,7 +137,7 @@
     dispatch, combine, mask = softmaxes(router_ref[...], tokens, images)
     load.wait()
     slot_out, slot_in_grad = split_rows(back_ref[...])
-    disp = jnp.where(mask, dot(slot_in_grad, tokens, 1, 1), 0.0)
+    disp = dot(slot_in_grad, tokens, 1, 1)
     comb = fold_rows(jnp.where(mask, dot(slot_out, grad_ref[...], 1, 1), 0.0), images)
     mean = jnp.sum(dispatch * disp, axis=1, keepdims=True)
     from_dispatch = fold_rows(dispatch * (disp - mean), images)
@@ -259,7 +265,7 @@
     )(w_in2, w_out2)
     recv = lax.all_to_all(sent, "expert", split_axis=0, concat_axis=0, tiled=True)
     back = pl.pallas_call(
-        functools.partial(expert_kernel, step=512),
+        functools.partial(expert_kernel, step=256),
         out_shape=struct(recv.shape, BF16),
         compiler_params=params,
         name="expert",

time: 42.7 us -> 42.7 us (level)
  no operation moved by 1% of the time
where the time goes in v10:
time: 42.7 us; the launch traced here: 42.2 us
  starting transfers between devices  15.1 us (35%)
  Pallas kernels  11.4 us (27%)
  waiting for transfers between devices  11.3 us (26%)
  local copies, waits for them, and re-layouts  3.16 us (7%)
  between operations  0.71 us (2%)
  other arithmetic  0.63 us (1%)
    all_to_all x1, starting transfers between devices, on_device(): lax.all_to_all(sent, 'expert', split_axis=0, concat_axis=0, tiled=True)  7.26 us
    all_to_all x1, waiting for transfers between devices, on_device(): lax.all_to_all(back, 'expert', split_axis=0, concat_axis=0, tiled=True)  5.13 us
    all_to_all x1, waiting for transfers between devices, on_device(): lax.all_to_all(sent, 'expert', split_axis=0, concat_axis=0, tiled=True)  4.08 us
    pallas_call x1, Pallas kernels, on_device(): pl.pallas_call(functools.partial(weights_kernel, shares), in_specs=[in_sm...  3.8 us
    all_to_all x1, starting transfers between devices, on_device(): lax.all_to_all(back, 'expert', split_axis=0, concat_axis=0, tiled=True)  3.36 us
    unnamed x12, local copies, waits for them, and re-layouts  3.16 us
    all_to_all x1, starting transfers between devices, on_device(): lax.all_to_all(router_send, ('expert', 'dp'), split_axis=0, concat_axis=0...  2.54 us
    pallas_call x1, Pallas kernels, on_device(): pl.pallas_call(functools.partial(slots_kernel, images), in_specs=[in_plac...  2.44 us
  transfers between devices with their start and end apart: 6, of which 3 were waited for; matrix products, arithmetic and copies ran while one was open for 0% of the time, Pallas kernels for 17%

profile of v10, /device:TPU:0, one launch (start us, length us, event | category | flops | bytes accessed | tf_op | source)
XLA Modules:
  0.0 42.2 jit_solution(11507637650364049419)
XLA Ops:
  0.6 2.4 %slots.1 = bf16[8,16,384]{2,1,0:T(8,128)(2,1)} custom-call(bf16[512,384]{1,0:T(8,128)(2,1)} %bitcast.10, bf16[8,384]{1,0:T(8,128)(2,1)} %bitcast.17, bf16[512,384]{1,0:T(8,128)(2,1)} %bitcast.13), custom_call_target="tpu_custom_call" | custom-call | tf_op jit(solution)/shard_map/slots/pallas_call | solution.py:241
  3.1 7.3 %all-to-all-start = ((bf16[8,16,384]{2,1,0:T(8,128)(2,1)}), bf16[8,16,384]{2,1,0:T(8,128)(2,1)S(1)}, u32[]{:S(2)}, u32[]{:S(2)}) async-start(bf16[8,16,384]{2,1,0:T(8,128)(2,1)} %slots.1), calls=%async_computation | async-start | bytes 196608 | tf_op jit(solution)/shard_map/all_to_all | solution.py:266
  10.3 0.0 copy-start.2
  10.3 1.3 %copy-done.2 = bf16[1,384,1536]{2,1,0:T(8,128)(2,1)S(1)} copy-done((bf16[1,384,1536]{2,1,0:T(8,128)(2,1)S(1)}, bf16[1,384,1536]{2,1,0:T(8,128)(2,1)}, u32[]{:S(2)}) %copy-start.2) | copy-done | bytes 1179672
  11.6 0.0 copy-start.3
  11.6 1.3 %copy-done.3 = bf16[1,384,1536]{2,1,0:T(8,128)(2,1)S(1)} copy-done((bf16[1,384,1536]{2,1,0:T(8,128)(2,1)S(1)}, bf16[1,384,1536]{2,1,0:T(8,128)(2,1)}, u32[]{:S(2)}) %copy-start.3) | copy-done | bytes 1179672
  12.9 0.5 %stage.1 = (bf16[384,1536]{1,0:T(8,128)(2,1)S(1)}, bf16[384,1536]{1,0:T(8,128)(2,1)S(1)}) custom-call(bf16[384,1536]{1,0:T(8,128)(2,1)S(1)} %bitcast.15, bf16[384,1536]{1,0:T(8,128)(2,1)S(1)} %bitcast.16), custom_call_target="tpu_custom_call" | custom-call | bytes 4718592 | tf_op jit(solution)/shard_map/stage/pallas_call | solution.py:254
  13.4 4.1 %all-to-all-done.recv_ref.refs_0_ = bf16[8,16,384]{2,1,0:T(8,128)(2,1)S(1)} async-done(((bf16[8,16,384]{2,1,0:T(8,128)(2,1)}), bf16[8,16,384]{2,1,0:T(8,128)(2,1)S(1)}, u32[]{:S(2)}, u32[]{:S(2)}) %all-to-all-start) | async-done | bytes 98336 | tf_op jit(solution)/shard_map/all_to_all | solution.py:266
  17.5 0.0 copy-start
  17.5 0.0 copy-start.1
  17.5 0.0 copy-start.5
  17.5 1.9 %expert.1 = bf16[8,16,384]{2,1,0:T(8,128)(2,1)} custom-call(bf16[8,16,384]{2,1,0:T(8,128)(2,1)S(1)} %all-to-all-done.recv_ref.refs_0_, bf16[384,1536]{1,0:T(8,128)(2,1)S(1)} %get-tuple-element.14.win_ref.refs_4_, bf16[384,1536]{1,0:T(8,128)(2,1)S(1)} %get-tuple-element.15.wout_ref.refs_5_), custom_call_target="tpu_custom_call" | custom-call | tf_op jit(solution)/shard_map/expert/pallas_call | solution.py:267
  19.4 3.4 %all-to-all-start.1 = ((bf16[8,16,384]{2,1,0:T(8,128)(2,1)}), bf16[8,16,384]{2,1,0:T(8,128)(2,1)S(1)}, u32[]{:S(2)}, u32[]{:S(2)}) async-start(bf16[8,16,384]{2,1,0:T(8,128)(2,1)} %expert.1), calls=%async_computation.1 | async-start | bytes 196608 | tf_op jit(solution)/shard_map/all_to_all | solution.py:274
  22.7 0.1 collective-permute-start.2
  22.8 1.6 %collective-permute-start.1 = (bf16[8,16,384]{2,1,0:T(8,128)(2,1)S(1)}, bf16[8,16,384]{2,1,0:T(8,128)(2,1)S(1)}, u32[]{:S(2)}, u32[]{:S(2)}) collective-permute-start(bf16[8,16,384]{2,1,0:T(8,128)(2,1)S(1)} %all-to-all-done.recv_ref.refs_0_), channel_id=1, source_target_pairs={{0,2},{1,3},{2,0},{3,1},{4,6},{5,7},{6,4},{7,5},{8,10},{9,11},{10,... | collective-permute-start | bytes 294920 | tf_op jit(solution)/shard_map/ppermute | solution.py:278
  24.4 0.3 collective-permute-start
  24.7 5.1 %all-to-all-done.1.back_hbm.back_ref = bf16[8,16,384]{2,1,0:T(8,128)(2,1)S(1)} async-done(((bf16[8,16,384]{2,1,0:T(8,128)(2,1)}), bf16[8,16,384]{2,1,0:T(8,128)(2,1)S(1)}, u32[]{:S(2)}, u32[]{:S(2)}) %all-to-all-start.1) | async-done | bytes 98336 | tf_op jit(solution)/shard_map/all_to_all | solution.py:274
  29.8 0.0 copy-done
  29.8 0.0 copy-done.1
  29.8 0.0 copy-done.5
  29.8 1.2 %logits.1 = (bf16[32,8,96]{2,1,0:T(8,128)(2,1)S(1)}, bf16[8,512]{1,0:T(8,128)(2,1)S(1)}) custom-call(bf16[8,16,384]{2,1,0:T(8,128)(2,1)S(1)} %all-to-all-done.1.back_hbm.back_ref, bf16[512,384]{1,0:T(8,128)(2,1)S(1)} %bitcast.11, bf16[8,384]{1,0:T(8,128)(2,1)S(1)} %bitcast.18, bf16[512,384]{1,0:T(8,128)(2,1)S(1)} %bitcast.14), custom_call_target="tpu_custom_call" | custom-call | tf_op jit(solution)/shard_map/logits/pallas_call | solution.py:285
  31.0 0.0 copy-start.4
  31.0 0.6 %copy-done.4 = bf16[32,8,96]{2,1,0:T(8,128)(2,1)} copy-done((bf16[32,8,96]{2,1,0:T(8,128)(2,1)}, bf16[32,8,96]{2,1,0:T(8,128)(2,1)S(1)}, u32[]{:S(2)}) %copy-start.4) | copy-done | bytes 49176
  31.6 2.5 %all-to-all-start.2 = ((bf16[32,8,96]{2,1,0:T(8,128)(2,1)}), bf16[32,8,96]{2,1,0:T(8,128)(2,1)S(1)}, u32[]{:S(2)}, u32[]{:S(2)}) async-start(bf16[32,8,96]{2,1,0:T(8,128)(2,1)} %copy-done.4), calls=%async_computation.2 | async-start | bytes 131072 | tf_op jit(solution)/shard_map/all_to_all | solution.py:297
  34.2 1.6 %tokens.1 = bf16[512,384]{1,0:T(8,128)(2,1)} custom-call(bf16[8,16,384]{2,1,0:T(8,128)(2,1)S(1)} %all-to-all-done.1.back_hbm.back_ref, bf16[512,384]{1,0:T(8,128)(2,1)S(1)} %bitcast.12, bf16[8,384]{1,0:T(8,128)(2,1)S(1)} %bitcast.19, bf16[8,512]{1,0:T(8,128)(2,1)S(1)} %get-tuple-element.17.logit_ref), custom_call_target="tpu_custom_call" | custom-call | tf_op jit(solution)/shard_map/tokens/pallas_call | solution.py:305
  35.7 0.0 collective-permute-done.2.refs_3_
  35.7 0.0 collective-permute-done.1.refs_2_
  35.7 0.0 collective-permute-done.refs_1_
  35.8 3.8 %weights.1 = (f32[96,1536]{1,0:T(8,128)}, f32[96,1536]{1,0:T(8,128)}) custom-call(s32[1]{0:T(128)} %bitcast.6.share_ref, bf16[8,16,384]{2,1,0:T(8,128)(2,1)S(1)} %all-to-all-done.recv_ref.refs_0_, bf16[8,16,384]{2,1,0:T(8,128)(2,1)} %collective-permute-done.refs_1_, bf16[8,16,384]{2,1,0:T(8,128)(2,1)S(1)} %collective-permute-done.1.refs_2_, ...), custom_call_target="tpu_custom_call" | custom-call | tf_op jit(solution)/shard_map/weights/pallas_call | solution.py:315
  39.6 2.0 %all-to-all-done.2 = bf16[32,8,96]{2,1,0:T(8,128)(2,1)S(1)} async-done(((bf16[32,8,96]{2,1,0:T(8,128)(2,1)}), bf16[32,8,96]{2,1,0:T(8,128)(2,1)S(1)}, u32[]{:S(2)}, u32[]{:S(2)}) %all-to-all-start.2) | async-done | bytes 49184 | tf_op jit(solution)/shard_map/all_to_all | solution.py:297
  41.6 0.6 %convert_reduce_fusion = f32[8,96]{1,0:T(8,128)} fusion(bf16[32,8,96]{2,1,0:T(8,128)(2,1)S(1)} %all-to-all-done.2), kind=kLoop, calls=%fused_computation | loop fusion | flops 48384 | bytes 52224 | tf_op jit(solution)/shard_map/reduce_sum | solution.py:345
Async XLA Ops:
  3.1 14.4 %all-to-all-start = ((bf16[8,16,384]{2,1,0:T(8,128)(2,1)}), bf16[8,16,384]{2,1,0:T(8,128)(2,1)S(1)}, u32[]{:S(2)}, u32[]{:S(2)}) async-start(bf16[8,16,384]{2,1,0:T(8,128)(2,1)} %slots.1), calls=%async_computation | async-start | bytes 196608 | tf_op jit(solution)/shard_map/all_to_all | solution.py:266
  10.3 1.3 %copy-start.2 = (bf16[1,384,1536]{2,1,0:T(8,128)(2,1)S(1)}, bf16[1,384,1536]{2,1,0:T(8,128)(2,1)}, u32[]{:S(2)}) copy-start(bf16[1,384,1536]{2,1,0:T(8,128)(2,1)} %param.7) | copy-start | bytes 3538948
  11.6 1.3 %copy-start.3 = (bf16[1,384,1536]{2,1,0:T(8,128)(2,1)S(1)}, bf16[1,384,1536]{2,1,0:T(8,128)(2,1)}, u32[]{:S(2)}) copy-start(bf16[1,384,1536]{2,1,0:T(8,128)(2,1)} %param.8) | copy-start | bytes 3538948
  17.5 12.3 %copy-start = (bf16[8,64,384]{2,1,0:T(8,128)(2,1)S(1)}, bf16[8,64,384]{2,1,0:T(8,128)(2,1)}, u32[]{:S(2)}) copy-start(bf16[8,64,384]{2,1,0:T(8,128)(2,1)} %param.5) | copy-start | bytes 1179652
  17.5 12.3 %copy-start.1 = (bf16[8,64,384]{2,1,0:T(8,128)(2,1)S(1)}, bf16[8,64,384]{2,1,0:T(8,128)(2,1)}, u32[]{:S(2)}) copy-start(bf16[8,64,384]{2,1,0:T(8,128)(2,1)} %param.9) | copy-start | bytes 1179652
  17.5 12.3 %copy-start.5 = (bf16[384,8]{0,1:T(8,128)(2,1)S(1)}, bf16[384,8]{0,1:T(8,128)(2,1)}, u32[]{:S(2)}) copy-start(bf16[384,8]{0,1:T(8,128)(2,1)} %param.6) | copy-start | bytes 18436
  19.4 10.4 %all-to-all-start.1 = ((bf16[8,16,384]{2,1,0:T(8,128)(2,1)}), bf16[8,16,384]{2,1,0:T(8,128)(2,1)S(1)}, u32[]{:S(2)}, u32[]{:S(2)}) async-start(bf16[8,16,384]{2,1,0:T(8,128)(2,1)} %expert.1), calls=%async_computation.1 | async-start | bytes 196608 | tf_op jit(solution)/shard_map/all_to_all | solution.py:274
  22.7 13.0 %collective-permute-start.2 = (bf16[8,16,384]{2,1,0:T(8,128)(2,1)S(1)}, bf16[8,16,384]{2,1,0:T(8,128)(2,1)S(1)}, u32[]{:S(2)}, u32[]{:S(2)}) collective-permute-start(bf16[8,16,384]{2,1,0:T(8,128)(2,1)S(1)} %all-to-all-done.recv_ref.refs_0_), channel_id=1, source_target_pairs={{0,3},{1,2},{2,1},{3,0},{4,7},{5,6},{6,5},{7,4},{8,11},{9,10},{10,... | collective-permute-start | bytes 294920 | tf_op jit(solution)/shard_map/ppermute | solution.py:278
  22.8 12.9 %collective-permute-start.1 = (bf16[8,16,384]{2,1,0:T(8,128)(2,1)S(1)}, bf16[8,16,384]{2,1,0:T(8,128)(2,1)S(1)}, u32[]{:S(2)}, u32[]{:S(2)}) collective-permute-start(bf16[8,16,384]{2,1,0:T(8,128)(2,1)S(1)} %all-to-all-done.recv_ref.refs_0_), channel_id=1, source_target_pairs={{0,2},{1,3},{2,0},{3,1},{4,6},{5,7},{6,4},{7,5},{8,10},{9,11},{10,... | collective-permute-start | bytes 294920 | tf_op jit(solution)/shard_map/ppermute | solution.py:278
  24.4 11.3 %collective-permute-start = (bf16[8,16,384]{2,1,0:T(8,128)(2,1)S(1)}, bf16[8,16,384]{2,1,0:T(8,128)(2,1)}, u32[]{:S(2)}, u32[]{:S(2)}) collective-permute-start(bf16[8,16,384]{2,1,0:T(8,128)(2,1)S(1)} %all-to-all-done.recv_ref.refs_0_), channel_id=1, source_target_pairs={{0,1},{1,0},{2,3},{3,2},{4,5},{5,4},{6,7},{7,6},{8,9},{9,8},{10,11... | collective-permute-start | bytes 294920 | tf_op jit(solution)/shard_map/ppermute | solution.py:278
  31.0 0.6 %copy-start.4 = (bf16[32,8,96]{2,1,0:T(8,128)(2,1)}, bf16[32,8,96]{2,1,0:T(8,128)(2,1)S(1)}, u32[]{:S(2)}) copy-start(bf16[32,8,96]{2,1,0:T(8,128)(2,1)S(1)} %get-tuple-element.23) | copy-start | bytes 147460
  31.6 10.0 %all-to-all-start.2 = ((bf16[32,8,96]{2,1,0:T(8,128)(2,1)}), bf16[32,8,96]{2,1,0:T(8,128)(2,1)S(1)}, u32[]{:S(2)}, u32[]{:S(2)}) async-start(bf16[32,8,96]{2,1,0:T(8,128)(2,1)} %copy-done.4), calls=%async_computation.2 | async-start | bytes 131072 | tf_op jit(solution)/shard_map/all_to_all | solution.py:297

commit v11 on v7

--- a/solution.py
+++ b/solution.py
@@ -62,6 +62,22 @@
     first = wide[:, : both // 2].reshape(groups * both // 2, width)
     second = wide[:, both // 2 :].reshape(groups * both // 2, width)
     return first.astype(BF16), second.astype(BF16)
+
+
+def centre_out(count):
+    return sorted(range(count), key=lambda i: (abs(2 * i - count + 1), i))
+
+
+def in_expert_order(ref):
+    order = centre_out(ref.shape[0])
+    return jnp.stack([ref[order.index(i)] for i in range(len(order))], axis=0)
+
+
+def exchange(chunks):
+    order = centre_out(lax.axis_size("expert"))
+    return lax.all_to_all(
+        chunks, "expert", split_axis=0, concat_axis=0, tiled=True, axis_index_groups=[order]
+    )
 
 
 def softmaxes(router, tokens, images):
@@ -94,7 +110,9 @@
     for load in second:
         load.wait()
     slot_grad = dot(combine_block.astype(BF16), grad_ref[...], 1, 0)
-    sent_ref[...] = pair_rows(slot_in, slot_grad, combine.shape[0])
+    pairs = pair_rows(slot_in, slot_grad, combine.shape[0])
+    for k, i in enumerate(centre_out(pairs.shape[0])):
+        sent_ref[k] = pairs[i]
 
 
 def stage_kernel(win_hbm, wout_hbm, win_ref, wout_ref, sems):
@@ -130,7 +148,7 @@
     tokens = tokens_ref[...]
     dispatch, combine, mask = softmaxes(router_ref[...], tokens, images)
     load.wait()
-    slot_out, slot_in_grad = split_rows(back_ref[...])
+    slot_out, slot_in_grad = split_rows(in_expert_order(back_ref))
     disp = jnp.where(mask, dot(slot_in_grad, tokens, 1, 1), 0.0)
     comb = fold_rows(jnp.where(mask, dot(slot_out, grad_ref[...], 1, 1), 0.0), images)
     mean = jnp.sum(dispatch * disp, axis=1, keepdims=True)
@@ -150,7 +168,7 @@
 def tokens_kernel(images, back_ref, tokens_ref, router_ref, logit_ref, out_ref):
     router = router_ref[...]
     dispatch, _, _ = softmaxes(router, tokens_ref[...], images)
-    _, slot_in_grad = split_rows(back_ref[...])
+    _, slot_in_grad = split_rows(in_expert_order(back_ref))
     out = dot(dispatch.astype(BF16), slot_in_grad, 0, 0)
     out = out + dot(logit_ref[...], router, 0, 0)
     out_ref[...] = out.astype(BF16)
@@ -257,7 +275,7 @@
         ),
         name="stage",
     )(w_in2, w_out2)
-    recv = lax.all_to_all(sent, "expert", split_axis=0, concat_axis=0, tiled=True)
+    recv = exchange(sent)
     back = pl.pallas_call(
         functools.partial(expert_kernel, step=512),
         out_shape=struct(recv.shape, BF16),
@@ -265,7 +283,7 @@
         name="expert",
     )(recv, w_in2, w_out2)
     recv, back = lax.optimization_barrier((recv, back))
-    slots_back = lax.all_to_all(back, "expert", split_axis=0, concat_axis=0, tiled=True)
+    slots_back = exchange(back)
     few = shares * owners * images <= 512
     if few:
         spread = [recv] + [

time: 42.7 us -> 40.8 us (0.956)
  waiting for transfers between devices: 11.3 us -> 6.66 us
  starting transfers between devices: 15.1 us -> 17.7 us
    all_to_all x2, waiting for transfers between devices: 9.21 us -> 4.61 us  [exchange(): lax.all_to_all(chunks, 'expert', split_axis=0, concat_axis=0, tiled=True,...]
    all_to_all x2, starting transfers between devices: 10.6 us -> 12.2 us  [exchange(): lax.all_to_all(chunks, 'expert', split_axis=0, concat_axis=0, tiled=True,...]
    all_to_all x1, starting transfers between devices: 2.54 us -> 3.69 us  [on_device(): lax.all_to_all(router_send, ('expert', 'dp'), split_axis=0, concat_axis=0...]
where the time goes in v11:
time: 40.8 us; the launch traced here: 40.3 us
  starting transfers between devices  17.7 us (43%)
  Pallas kernels  11.4 us (28%)
  waiting for transfers between devices  6.66 us (16%)
  local copies, waits for them, and re-layouts  3.17 us (8%)
  between operations  0.7 us (2%)
  other arithmetic  0.63 us (2%)
    all_to_all x2, starting transfers between devices, exchange(): lax.all_to_all(chunks, 'expert', split_axis=0, concat_axis=0, tiled=True,...  12.2 us
    all_to_all x2, waiting for transfers between devices, exchange(): lax.all_to_all(chunks, 'expert', split_axis=0, concat_axis=0, tiled=True,...  4.61 us
    pallas_call x1, Pallas kernels, on_device(): pl.pallas_call(functools.partial(weights_kernel, shares), in_specs=[in_sm...  3.8 us
    all_to_all x1, starting transfers between devices, on_device(): lax.all_to_all(router_send, ('expert', 'dp'), split_axis=0, concat_axis=0...  3.69 us
    unnamed x12, local copies, waits for them, and re-layouts  3.17 us
    pallas_call x1, Pallas kernels, on_device(): pl.pallas_call(functools.partial(slots_kernel, images), in_specs=[in_plac...  2.44 us
    all_to_all x1, waiting for transfers between devices, on_device(): lax.all_to_all(router_send, ('expert', 'dp'), split_axis=0, concat_axis=0...  2.04 us
    pallas_call x1, Pallas kernels, on_device(): pl.pallas_call(functools.partial(expert_kernel, step=512), out_shape=stru...  1.94 us
  transfers between devices with their start and end apart: 6, of which 3 were waited for; matrix products, arithmetic and copies ran while one was open for 0% of the time, Pallas kernels for 17%

profile of v11, /device:TPU:0, one launch (start us, length us, event | category | flops | bytes accessed | tf_op | source)
XLA Modules:
  0.0 40.3 jit_solution(11172314673001040876)
XLA Ops:
  0.6 2.4 %slots.1 = bf16[8,16,384]{2,1,0:T(8,128)(2,1)} custom-call(bf16[512,384]{1,0:T(8,128)(2,1)} %bitcast.10, bf16[8,384]{1,0:T(8,128)(2,1)} %bitcast.17, bf16[512,384]{1,0:T(8,128)(2,1)} %bitcast.13), custom_call_target="tpu_custom_call" | custom-call | tf_op jit(solution)/shard_map/slots/pallas_call | solution.py:253
  3.1 7.8 %all-to-all-start = ((bf16[8,16,384]{2,1,0:T(8,128)(2,1)}), bf16[8,16,384]{2,1,0:T(8,128)(2,1)S(1)}, u32[]{:S(2)}, u32[]{:S(2)}) async-start(bf16[8,16,384]{2,1,0:T(8,128)(2,1)} %slots.1), calls=%async_computation | async-start | bytes 196608 | tf_op jit(solution)/shard_map/all_to_all | solution.py:78
  10.9 0.0 copy-start.2
  10.9 1.3 %copy-done.2 = bf16[1,384,1536]{2,1,0:T(8,128)(2,1)S(1)} copy-done((bf16[1,384,1536]{2,1,0:T(8,128)(2,1)S(1)}, bf16[1,384,1536]{2,1,0:T(8,128)(2,1)}, u32[]{:S(2)}) %copy-start.2) | copy-done | bytes 1179672
  12.2 0.0 copy-start.3
  12.2 1.3 %copy-done.3 = bf16[1,384,1536]{2,1,0:T(8,128)(2,1)S(1)} copy-done((bf16[1,384,1536]{2,1,0:T(8,128)(2,1)S(1)}, bf16[1,384,1536]{2,1,0:T(8,128)(2,1)}, u32[]{:S(2)}) %copy-start.3) | copy-done | bytes 1179672
  13.4 0.5 %stage.1 = (bf16[384,1536]{1,0:T(8,128)(2,1)S(1)}, bf16[384,1536]{1,0:T(8,128)(2,1)S(1)}) custom-call(bf16[384,1536]{1,0:T(8,128)(2,1)S(1)} %bitcast.15, bf16[384,1536]{1,0:T(8,128)(2,1)S(1)} %bitcast.16), custom_call_target="tpu_custom_call" | custom-call | bytes 4718592 | tf_op jit(solution)/shard_map/stage/pallas_call | solution.py:266
  14.0 1.7 %all-to-all-done.recv_ref.refs_0_ = bf16[8,16,384]{2,1,0:T(8,128)(2,1)S(1)} async-done(((bf16[8,16,384]{2,1,0:T(8,128)(2,1)}), bf16[8,16,384]{2,1,0:T(8,128)(2,1)S(1)}, u32[]{:S(2)}, u32[]{:S(2)}) %all-to-all-start) | async-done | bytes 98336 | tf_op jit(solution)/shard_map/all_to_all | solution.py:78
  15.7 0.0 copy-start
  15.7 0.0 copy-start.1
  15.7 0.0 copy-start.5
  15.7 1.9 %expert.1 = bf16[8,16,384]{2,1,0:T(8,128)(2,1)} custom-call(bf16[8,16,384]{2,1,0:T(8,128)(2,1)S(1)} %all-to-all-done.recv_ref.refs_0_, bf16[384,1536]{1,0:T(8,128)(2,1)S(1)} %get-tuple-element.14.win_ref.refs_4_, bf16[384,1536]{1,0:T(8,128)(2,1)S(1)} %get-tuple-element.15.wout_ref.refs_5_), custom_call_target="tpu_custom_call" | custom-call | tf_op jit(solution)/shard_map/expert/pallas_call | solution.py:279
  17.6 4.4 %all-to-all-start.1 = ((bf16[8,16,384]{2,1,0:T(8,128)(2,1)}), bf16[8,16,384]{2,1,0:T(8,128)(2,1)S(1)}, u32[]{:S(2)}, u32[]{:S(2)}) async-start(bf16[8,16,384]{2,1,0:T(8,128)(2,1)} %expert.1), calls=%async_computation.1 | async-start | bytes 196608 | tf_op jit(solution)/shard_map/all_to_all | solution.py:78
  22.0 0.0 collective-permute-start.2
  22.0 1.5 %collective-permute-start.1 = (bf16[8,16,384]{2,1,0:T(8,128)(2,1)S(1)}, bf16[8,16,384]{2,1,0:T(8,128)(2,1)S(1)}, u32[]{:S(2)}, u32[]{:S(2)}) collective-permute-start(bf16[8,16,384]{2,1,0:T(8,128)(2,1)S(1)} %all-to-all-done.recv_ref.refs_0_), channel_id=1, source_target_pairs={{0,2},{1,3},{2,0},{3,1},{4,6},{5,7},{6,4},{7,5},{8,10},{9,11},{10,... | collective-permute-start | bytes 294920 | tf_op jit(solution)/shard_map/ppermute | solution.py:290
  23.5 0.3 collective-permute-start
  23.9 2.9 %all-to-all-done.1.back_hbm.back_ref = bf16[8,16,384]{2,1,0:T(8,128)(2,1)S(1)} async-done(((bf16[8,16,384]{2,1,0:T(8,128)(2,1)}), bf16[8,16,384]{2,1,0:T(8,128)(2,1)S(1)}, u32[]{:S(2)}, u32[]{:S(2)}) %all-to-all-start.1) | async-done | bytes 98336 | tf_op jit(solution)/shard_map/all_to_all | solution.py:78
  26.7 0.0 copy-done
  26.7 0.0 copy-done.1
  26.8 0.0 copy-done.5
  26.8 1.2 %logits.1 = (bf16[32,8,96]{2,1,0:T(8,128)(2,1)S(1)}, bf16[8,512]{1,0:T(8,128)(2,1)S(1)}) custom-call(bf16[8,16,384]{2,1,0:T(8,128)(2,1)S(1)} %all-to-all-done.1.back_hbm.back_ref, bf16[512,384]{1,0:T(8,128)(2,1)S(1)} %bitcast.11, bf16[8,384]{1,0:T(8,128)(2,1)S(1)} %bitcast.18, bf16[512,384]{1,0:T(8,128)(2,1)S(1)} %bitcast.14), custom_call_target="tpu_custom_call" | custom-call | tf_op jit(solution)/shard_map/logits/pallas_call | solution.py:297
  28.0 0.0 copy-start.4
  28.0 0.6 %copy-done.4 = bf16[32,8,96]{2,1,0:T(8,128)(2,1)} copy-done((bf16[32,8,96]{2,1,0:T(8,128)(2,1)}, bf16[32,8,96]{2,1,0:T(8,128)(2,1)S(1)}, u32[]{:S(2)}) %copy-start.4) | copy-done | bytes 49176
  28.6 3.7 %all-to-all-start.2 = ((bf16[32,8,96]{2,1,0:T(8,128)(2,1)}), bf16[32,8,96]{2,1,0:T(8,128)(2,1)S(1)}, u32[]{:S(2)}, u32[]{:S(2)}) async-start(bf16[32,8,96]{2,1,0:T(8,128)(2,1)} %copy-done.4), calls=%async_computation.2 | async-start | bytes 131072 | tf_op jit(solution)/shard_map/all_to_all | solution.py:309
  32.3 1.6 %tokens.1 = bf16[512,384]{1,0:T(8,128)(2,1)} custom-call(bf16[8,16,384]{2,1,0:T(8,128)(2,1)S(1)} %all-to-all-done.1.back_hbm.back_ref, bf16[512,384]{1,0:T(8,128)(2,1)S(1)} %bitcast.12, bf16[8,384]{1,0:T(8,128)(2,1)S(1)} %bitcast.19, bf16[8,512]{1,0:T(8,128)(2,1)S(1)} %get-tuple-element.17.logit_ref), custom_call_target="tpu_custom_call" | custom-call | tf_op jit(solution)/shard_map/tokens/pallas_call | solution.py:317
  33.8 0.0 collective-permute-done.2.refs_3_
  33.8 0.0 collective-permute-done.1.refs_2_
  33.8 0.0 collective-permute-done.refs_1_
  33.8 3.8 %weights.1 = (f32[96,1536]{1,0:T(8,128)}, f32[96,1536]{1,0:T(8,128)}) custom-call(s32[1]{0:T(128)} %bitcast.6.share_ref, bf16[8,16,384]{2,1,0:T(8,128)(2,1)S(1)} %all-to-all-done.recv_ref.refs_0_, bf16[8,16,384]{2,1,0:T(8,128)(2,1)} %collective-permute-done.refs_1_, bf16[8,16,384]{2,1,0:T(8,128)(2,1)S(1)} %collective-permute-done.1.refs_2_, ...), custom_call_target="tpu_custom_call" | custom-call | tf_op jit(solution)/shard_map/weights/pallas_call | solution.py:327
  37.6 2.0 %all-to-all-done.2 = bf16[32,8,96]{2,1,0:T(8,128)(2,1)S(1)} async-done(((bf16[32,8,96]{2,1,0:T(8,128)(2,1)}), bf16[32,8,96]{2,1,0:T(8,128)(2,1)S(1)}, u32[]{:S(2)}, u32[]{:S(2)}) %all-to-all-start.2) | async-done | bytes 49184 | tf_op jit(solution)/shard_map/all_to_all | solution.py:309
  39.7 0.6 %convert_reduce_fusion = f32[8,96]{1,0:T(8,128)} fusion(bf16[32,8,96]{2,1,0:T(8,128)(2,1)S(1)} %all-to-all-done.2), kind=kLoop, calls=%fused_computation | loop fusion | flops 48384 | bytes 52224 | tf_op jit(solution)/shard_map/reduce_sum | solution.py:357
Async XLA Ops:
  3.1 12.6 %all-to-all-start = ((bf16[8,16,384]{2,1,0:T(8,128)(2,1)}), bf16[8,16,384]{2,1,0:T(8,128)(2,1)S(1)}, u32[]{:S(2)}, u32[]{:S(2)}) async-start(bf16[8,16,384]{2,1,0:T(8,128)(2,1)} %slots.1), calls=%async_computation | async-start | bytes 196608 | tf_op jit(solution)/shard_map/all_to_all | solution.py:78
  10.9 1.3 %copy-start.2 = (bf16[1,384,1536]{2,1,0:T(8,128)(2,1)S(1)}, bf16[1,384,1536]{2,1,0:T(8,128)(2,1)}, u32[]{:S(2)}) copy-start(bf16[1,384,1536]{2,1,0:T(8,128)(2,1)} %param.7) | copy-start | bytes 3538948
  12.2 1.3 %copy-start.3 = (bf16[1,384,1536]{2,1,0:T(8,128)(2,1)S(1)}, bf16[1,384,1536]{2,1,0:T(8,128)(2,1)}, u32[]{:S(2)}) copy-start(bf16[1,384,1536]{2,1,0:T(8,128)(2,1)} %param.8) | copy-start | bytes 3538948
  15.7 11.1 %copy-start = (bf16[8,64,384]{2,1,0:T(8,128)(2,1)S(1)}, bf16[8,64,384]{2,1,0:T(8,128)(2,1)}, u32[]{:S(2)}) copy-start(bf16[8,64,384]{2,1,0:T(8,128)(2,1)} %param.5) | copy-start | bytes 1179652
  15.7 11.1 %copy-start.1 = (bf16[8,64,384]{2,1,0:T(8,128)(2,1)S(1)}, bf16[8,64,384]{2,1,0:T(8,128)(2,1)}, u32[]{:S(2)}) copy-start(bf16[8,64,384]{2,1,0:T(8,128)(2,1)} %param.9) | copy-start | bytes 1179652
  15.7 11.1 %copy-start.5 = (bf16[384,8]{0,1:T(8,128)(2,1)S(1)}, bf16[384,8]{0,1:T(8,128)(2,1)}, u32[]{:S(2)}) copy-start(bf16[384,8]{0,1:T(8,128)(2,1)} %param.6) | copy-start | bytes 18436
  17.6 9.1 %all-to-all-start.1 = ((bf16[8,16,384]{2,1,0:T(8,128)(2,1)}), bf16[8,16,384]{2,1,0:T(8,128)(2,1)S(1)}, u32[]{:S(2)}, u32[]{:S(2)}) async-start(bf16[8,16,384]{2,1,0:T(8,128)(2,1)} %expert.1), calls=%async_computation.1 | async-start | bytes 196608 | tf_op jit(solution)/shard_map/all_to_all | solution.py:78
  22.0 11.8 %collective-permute-start.2 = (bf16[8,16,384]{2,1,0:T(8,128)(2,1)S(1)}, bf16[8,16,384]{2,1,0:T(8,128)(2,1)S(1)}, u32[]{:S(2)}, u32[]{:S(2)}) collective-permute-start(bf16[8,16,384]{2,1,0:T(8,128)(2,1)S(1)} %all-to-all-done.recv_ref.refs_0_), channel_id=1, source_target_pairs={{0,3},{1,2},{2,1},{3,0},{4,7},{5,6},{6,5},{7,4},{8,11},{9,10},{10,... | collective-permute-start | bytes 294920 | tf_op jit(solution)/shard_map/ppermute | solution.py:290
  22.0 11.8 %collective-permute-start.1 = (bf16[8,16,384]{2,1,0:T(8,128)(2,1)S(1)}, bf16[8,16,384]{2,1,0:T(8,128)(2,1)S(1)}, u32[]{:S(2)}, u32[]{:S(2)}) collective-permute-start(bf16[8,16,384]{2,1,0:T(8,128)(2,1)S(1)} %all-to-all-done.recv_ref.refs_0_), channel_id=1, source_target_pairs={{0,2},{1,3},{2,0},{3,1},{4,6},{5,7},{6,4},{7,5},{8,10},{9,11},{10,... | collective-permute-start | bytes 294920 | tf_op jit(solution)/shard_map/ppermute | solution.py:290
  23.5 10.3 %collective-permute-start = (bf16[8,16,384]{2,1,0:T(8,128)(2,1)S(1)}, bf16[8,16,384]{2,1,0:T(8,128)(2,1)}, u32[]{:S(2)}, u32[]{:S(2)}) collective-permute-start(bf16[8,16,384]{2,1,0:T(8,128)(2,1)S(1)} %all-to-all-done.recv_ref.refs_0_), channel_id=1, source_target_pairs={{0,1},{1,0},{2,3},{3,2},{4,5},{5,4},{6,7},{7,6},{8,9},{9,8},{10,11... | collective-permute-start | bytes 294920 | tf_op jit(solution)/shard_map/ppermute | solution.py:290
  28.0 0.6 %copy-start.4 = (bf16[32,8,96]{2,1,0:T(8,128)(2,1)}, bf16[32,8,96]{2,1,0:T(8,128)(2,1)S(1)}, u32[]{:S(2)}) copy-start(bf16[32,8,96]{2,1,0:T(8,128)(2,1)S(1)} %get-tuple-element.23) | copy-start | bytes 147460
  28.6 11.1 %all-to-all-start.2 = ((bf16[32,8,96]{2,1,0:T(8,128)(2,1)}), bf16[32,8,96]{2,1,0:T(8,128)(2,1)S(1)}, u32[]{:S(2)}, u32[]{:S(2)}) async-start(bf16[32,8,96]{2,1,0:T(8,128)(2,1)} %copy-done.4), calls=%async_computation.2 | async-start | bytes 131072 | tf_op jit(solution)/shard_map/all_to_all | solution.py:309

commit v12 on v11

--- a/solution.py
+++ b/solution.py
@@ -73,10 +73,9 @@
     return jnp.stack([ref[order.index(i)] for i in range(len(order))], axis=0)
 
 
-def exchange(chunks):
-    order = centre_out(lax.axis_size("expert"))
+def exchange(chunks, axis, order):
     return lax.all_to_all(
-        chunks, "expert", split_axis=0, concat_axis=0, tiled=True, axis_index_groups=[order]
+        chunks, axis, split_axis=0, concat_axis=0, tiled=True, axis_index_groups=[order]
     )
 
 
@@ -141,7 +140,7 @@
 
 
 def logits_kernel(
-    images, back_hbm, tokens_ref, router_ref, grad_ref, send_ref, logit_ref, back_ref, sem
+    images, share_order, back_hbm, tokens_ref, router_ref, grad_ref, send_ref, logit_ref, back_ref, sem
 ):
     load = pltpu.make_async_copy(back_hbm, back_ref, sem)
     load.start()
@@ -158,10 +157,10 @@
     logit_ref[...] = logit_grad
     part = dot(logit_grad, tokens, 1, 0)
     devices, _, width = send_ref.shape
-    shares = part.shape[1] // width
-    for share in range(shares):
+    shares = len(share_order)
+    for place, share in enumerate(share_order):
         piece = part[:, share * width : (share + 1) * width].astype(BF16)
-        for device in range(share, devices, shares):
+        for device in range(place, devices, shares):
             send_ref[device] = piece
 
 
@@ -234,6 +233,8 @@
 
 def on_device(tokens, router, w_in, w_out, out_grad):
     owners, shares = lax.axis_size("expert"), lax.axis_size("dp")
+    experts_order = centre_out(owners)
+    share_order = [*range(1, shares, 2), *range(0, shares, 2)]
     images, per_image, width = tokens.shape
     experts = router.shape[1]
     hidden = w_in.shape[2]
@@ -275,7 +276,7 @@
         ),
         name="stage",
     )(w_in2, w_out2)
-    recv = exchange(sent)
+    recv = exchange(sent, "expert", experts_order)
     back = pl.pallas_call(
         functools.partial(expert_kernel, step=512),
         out_shape=struct(recv.shape, BF16),
@@ -283,7 +284,7 @@
         name="expert",
     )(recv, w_in2, w_out2)
     recv, back = lax.optimization_barrier((recv, back))
-    slots_back = exchange(back)
+    slots_back = exchange(back, "expert", experts_order)
     few = shares * owners * images <= 512
     if few:
         spread = [recv] + [
@@ -295,7 +296,7 @@
 
     in_vmem = pl.BlockSpec(memory_space=pltpu.VMEM)
     router_send, logit_grad = pl.pallas_call(
-        functools.partial(logits_kernel, images),
+        functools.partial(logits_kernel, images, share_order),
         in_specs=[in_place] + [in_vmem] * 3,
         out_shape=(
             struct((owners * shares, experts, row_count), BF16),
@@ -306,14 +307,11 @@
         name="logits",
     )(slots_back, tokens2, router_rows, grad2)
     share, router_send = lax.optimization_barrier((lax.axis_index("dp").reshape(1), router_send))
-    router_parts = lax.all_to_all(
+    router_parts = exchange(
         router_send,
         ("expert", "dp"),
-        split_axis=0,
-        concat_axis=0,
-        tiled=True,
-    )
-
+        [owner * shares + i for owner in experts_order for i in share_order],
+    )
     tokens_grad = pl.pallas_call(
         functools.partial(tokens_kernel, images),
         out_shape=struct((columns, width), BF16),

time: 40.8 us -> 40.6 us (level)
  transfers between devices with their start and end apart: 6 -> 6, of which waited for: 3 -> 3; matrix products, arithmetic and copies ran while one was open for 0% -> 0% of each run, Pallas kernels for 17% -> 18%
where the time goes in v12:
time: 40.6 us; the launch traced here: 40.1 us
  starting transfers between devices  17.7 us (44%)
  Pallas kernels  11.4 us (28%)
  waiting for transfers between devices  6.48 us (16%)
  local copies, waits for them, and re-layouts  3.17 us (8%)
  between operations  0.7 us (2%)
  other arithmetic  0.63 us (2%)
    all_to_all x3, starting transfers between devices, exchange(): lax.all_to_all(chunks, axis, split_axis=0, concat_axis=0, tiled=True, axi...  15.9 us
    all_to_all x3, waiting for transfers between devices, exchange(): lax.all_to_all(chunks, axis, split_axis=0, concat_axis=0, tiled=True, axi...  6.48 us
    pallas_call x1, Pallas kernels, on_device(): pl.pallas_call(functools.partial(weights_kernel, shares), in_specs=[in_sm...  3.8 us
    unnamed x12, local copies, waits for them, and re-layouts  3.17 us
    pallas_call x1, Pallas kernels, on_device(): pl.pallas_call(functools.partial(slots_kernel, images), in_specs=[in_plac...  2.44 us
    pallas_call x1, Pallas kernels, on_device(): pl.pallas_call(functools.partial(expert_kernel, step=512), out_shape=stru...  1.94 us
    ppermute x3, starting transfers between devices, on_device(): lax.ppermute(recv, 'dp', [(i, i ^ k) for i in range(shares)])  1.86 us
    pallas_call x1, Pallas kernels, on_device(): pl.pallas_call(functools.partial(tokens_kernel, images), out_shape=struct...  1.55 us
  transfers between devices with their start and end apart: 6, of which 3 were waited for; matrix products, arithmetic and copies ran while one was open for 0% of the time, Pallas kernels for 18%

profile of v12, /device:TPU:0, one launch (start us, length us, event | category | flops | bytes accessed | tf_op | source)
XLA Modules:
  0.0 40.1 jit_solution(17625893844410655746)
XLA Ops:
  0.6 2.4 %slots.1 = bf16[8,16,384]{2,1,0:T(8,128)(2,1)} custom-call(bf16[512,384]{1,0:T(8,128)(2,1)} %bitcast.10, bf16[8,384]{1,0:T(8,128)(2,1)} %bitcast.17, bf16[512,384]{1,0:T(8,128)(2,1)} %bitcast.13), custom_call_target="tpu_custom_call" | custom-call | tf_op jit(solution)/shard_map/slots/pallas_call | solution.py:254
  3.1 7.8 %all-to-all-start = ((bf16[8,16,384]{2,1,0:T(8,128)(2,1)}), bf16[8,16,384]{2,1,0:T(8,128)(2,1)S(1)}, u32[]{:S(2)}, u32[]{:S(2)}) async-start(bf16[8,16,384]{2,1,0:T(8,128)(2,1)} %slots.1), calls=%async_computation | async-start | bytes 196608 | tf_op jit(solution)/shard_map/all_to_all | solution.py:77
  10.9 0.0 copy-start.2
  10.9 1.3 %copy-done.2 = bf16[1,384,1536]{2,1,0:T(8,128)(2,1)S(1)} copy-done((bf16[1,384,1536]{2,1,0:T(8,128)(2,1)S(1)}, bf16[1,384,1536]{2,1,0:T(8,128)(2,1)}, u32[]{:S(2)}) %copy-start.2) | copy-done | bytes 1179672
  12.2 0.0 copy-start.3
  12.2 1.3 %copy-done.3 = bf16[1,384,1536]{2,1,0:T(8,128)(2,1)S(1)} copy-done((bf16[1,384,1536]{2,1,0:T(8,128)(2,1)S(1)}, bf16[1,384,1536]{2,1,0:T(8,128)(2,1)}, u32[]{:S(2)}) %copy-start.3) | copy-done | bytes 1179672
  13.4 0.5 %stage.1 = (bf16[384,1536]{1,0:T(8,128)(2,1)S(1)}, bf16[384,1536]{1,0:T(8,128)(2,1)S(1)}) custom-call(bf16[384,1536]{1,0:T(8,128)(2,1)S(1)} %bitcast.15, bf16[384,1536]{1,0:T(8,128)(2,1)S(1)} %bitcast.16), custom_call_target="tpu_custom_call" | custom-call | bytes 4718592 | tf_op jit(solution)/shard_map/stage/pallas_call | solution.py:267
  14.0 1.7 %all-to-all-done.recv_ref.refs_0_ = bf16[8,16,384]{2,1,0:T(8,128)(2,1)S(1)} async-done(((bf16[8,16,384]{2,1,0:T(8,128)(2,1)}), bf16[8,16,384]{2,1,0:T(8,128)(2,1)S(1)}, u32[]{:S(2)}, u32[]{:S(2)}) %all-to-all-start) | async-done | bytes 98336 | tf_op jit(solution)/shard_map/all_to_all | solution.py:77
  15.7 0.0 copy-start
  15.7 0.0 copy-start.1
  15.7 0.0 copy-start.5
  15.7 1.9 %expert.1 = bf16[8,16,384]{2,1,0:T(8,128)(2,1)} custom-call(bf16[8,16,384]{2,1,0:T(8,128)(2,1)S(1)} %all-to-all-done.recv_ref.refs_0_, bf16[384,1536]{1,0:T(8,128)(2,1)S(1)} %get-tuple-element.14.win_ref.refs_4_, bf16[384,1536]{1,0:T(8,128)(2,1)S(1)} %get-tuple-element.15.wout_ref.refs_5_), custom_call_target="tpu_custom_call" | custom-call | tf_op jit(solution)/shard_map/expert/pallas_call | solution.py:280
  17.6 4.4 %all-to-all-start.1 = ((bf16[8,16,384]{2,1,0:T(8,128)(2,1)}), bf16[8,16,384]{2,1,0:T(8,128)(2,1)S(1)}, u32[]{:S(2)}, u32[]{:S(2)}) async-start(bf16[8,16,384]{2,1,0:T(8,128)(2,1)} %expert.1), calls=%async_computation.1 | async-start | bytes 196608 | tf_op jit(solution)/shard_map/all_to_all | solution.py:77
  22.0 0.0 collective-permute-start.2
  22.0 1.5 %collective-permute-start.1 = (bf16[8,16,384]{2,1,0:T(8,128)(2,1)S(1)}, bf16[8,16,384]{2,1,0:T(8,128)(2,1)S(1)}, u32[]{:S(2)}, u32[]{:S(2)}) collective-permute-start(bf16[8,16,384]{2,1,0:T(8,128)(2,1)S(1)} %all-to-all-done.recv_ref.refs_0_), channel_id=1, source_target_pairs={{0,2},{1,3},{2,0},{3,1},{4,6},{5,7},{6,4},{7,5},{8,10},{9,11},{10,... | collective-permute-start | bytes 294920 | tf_op jit(solution)/shard_map/ppermute | solution.py:291
  23.5 0.3 collective-permute-start
  23.9 2.9 %all-to-all-done.1.back_hbm.back_ref = bf16[8,16,384]{2,1,0:T(8,128)(2,1)S(1)} async-done(((bf16[8,16,384]{2,1,0:T(8,128)(2,1)}), bf16[8,16,384]{2,1,0:T(8,128)(2,1)S(1)}, u32[]{:S(2)}, u32[]{:S(2)}) %all-to-all-start.1) | async-done | bytes 98336 | tf_op jit(solution)/shard_map/all_to_all | solution.py:77
  26.7 0.0 copy-done
  26.7 0.0 copy-done.1
  26.8 0.0 copy-done.5
  26.8 1.2 %logits.1 = (bf16[32,8,96]{2,1,0:T(8,128)(2,1)S(1)}, bf16[8,512]{1,0:T(8,128)(2,1)S(1)}) custom-call(bf16[8,16,384]{2,1,0:T(8,128)(2,1)S(1)} %all-to-all-done.1.back_hbm.back_ref, bf16[512,384]{1,0:T(8,128)(2,1)S(1)} %bitcast.11, bf16[8,384]{1,0:T(8,128)(2,1)S(1)} %bitcast.18, bf16[512,384]{1,0:T(8,128)(2,1)S(1)} %bitcast.14), custom_call_target="tpu_custom_call" | custom-call | tf_op jit(solution)/shard_map/logits/pallas_call | solution.py:298
  28.0 0.0 copy-start.4
  28.0 0.6 %copy-done.4 = bf16[32,8,96]{2,1,0:T(8,128)(2,1)} copy-done((bf16[32,8,96]{2,1,0:T(8,128)(2,1)}, bf16[32,8,96]{2,1,0:T(8,128)(2,1)S(1)}, u32[]{:S(2)}) %copy-start.4) | copy-done | bytes 49176
  28.6 3.7 %all-to-all-start.2 = ((bf16[32,8,96]{2,1,0:T(8,128)(2,1)}), bf16[32,8,96]{2,1,0:T(8,128)(2,1)S(1)}, u32[]{:S(2)}, u32[]{:S(2)}) async-start(bf16[32,8,96]{2,1,0:T(8,128)(2,1)} %copy-done.4), calls=%async_computation.2 | async-start | bytes 131072 | tf_op jit(solution)/shard_map/all_to_all | solution.py:77
  32.3 1.6 %tokens.1 = bf16[512,384]{1,0:T(8,128)(2,1)} custom-call(bf16[8,16,384]{2,1,0:T(8,128)(2,1)S(1)} %all-to-all-done.1.back_hbm.back_ref, bf16[512,384]{1,0:T(8,128)(2,1)S(1)} %bitcast.12, bf16[8,384]{1,0:T(8,128)(2,1)S(1)} %bitcast.19, bf16[8,512]{1,0:T(8,128)(2,1)S(1)} %get-tuple-element.17.logit_ref), custom_call_target="tpu_custom_call" | custom-call | tf_op jit(solution)/shard_map/tokens/pallas_call | solution.py:315
  33.8 0.0 collective-permute-done.2.refs_3_
  33.8 0.0 collective-permute-done.1.refs_2_
  33.8 0.0 collective-permute-done.refs_1_
  33.8 3.8 %weights.1 = (f32[96,1536]{1,0:T(8,128)}, f32[96,1536]{1,0:T(8,128)}) custom-call(s32[1]{0:T(128)} %bitcast.6.share_ref, bf16[8,16,384]{2,1,0:T(8,128)(2,1)S(1)} %all-to-all-done.recv_ref.refs_0_, bf16[8,16,384]{2,1,0:T(8,128)(2,1)} %collective-permute-done.refs_1_, bf16[8,16,384]{2,1,0:T(8,128)(2,1)S(1)} %collective-permute-done.1.refs_2_, ...), custom_call_target="tpu_custom_call" | custom-call | tf_op jit(solution)/shard_map/weights/pallas_call | solution.py:325
  37.6 1.9 %all-to-all-done.2 = bf16[32,8,96]{2,1,0:T(8,128)(2,1)S(1)} async-done(((bf16[32,8,96]{2,1,0:T(8,128)(2,1)}), bf16[32,8,96]{2,1,0:T(8,128)(2,1)S(1)}, u32[]{:S(2)}, u32[]{:S(2)}) %all-to-all-start.2) | async-done | bytes 49184 | tf_op jit(solution)/shard_map/all_to_all | solution.py:77
  39.5 0.6 %convert_reduce_fusion = f32[8,96]{1,0:T(8,128)} fusion(bf16[32,8,96]{2,1,0:T(8,128)(2,1)S(1)} %all-to-all-done.2), kind=kLoop, calls=%fused_computation | loop fusion | flops 48384 | bytes 52224 | tf_op jit(solution)/shard_map/reduce_sum | solution.py:355
Async XLA Ops:
  3.1 12.6 %all-to-all-start = ((bf16[8,16,384]{2,1,0:T(8,128)(2,1)}), bf16[8,16,384]{2,1,0:T(8,128)(2,1)S(1)}, u32[]{:S(2)}, u32[]{:S(2)}) async-start(bf16[8,16,384]{2,1,0:T(8,128)(2,1)} %slots.1), calls=%async_computation | async-start | bytes 196608 | tf_op jit(solution)/shard_map/all_to_all | solution.py:77
  10.9 1.3 %copy-start.2 = (bf16[1,384,1536]{2,1,0:T(8,128)(2,1)S(1)}, bf16[1,384,1536]{2,1,0:T(8,128)(2,1)}, u32[]{:S(2)}) copy-start(bf16[1,384,1536]{2,1,0:T(8,128)(2,1)} %param.7) | copy-start | bytes 3538948
  12.2 1.3 %copy-start.3 = (bf16[1,384,1536]{2,1,0:T(8,128)(2,1)S(1)}, bf16[1,384,1536]{2,1,0:T(8,128)(2,1)}, u32[]{:S(2)}) copy-start(bf16[1,384,1536]{2,1,0:T(8,128)(2,1)} %param.8) | copy-start | bytes 3538948
  15.7 11.1 %copy-start = (bf16[8,64,384]{2,1,0:T(8,128)(2,1)S(1)}, bf16[8,64,384]{2,1,0:T(8,128)(2,1)}, u32[]{:S(2)}) copy-start(bf16[8,64,384]{2,1,0:T(8,128)(2,1)} %param.5) | copy-start | bytes 1179652
  15.7 11.1 %copy-start.1 = (bf16[8,64,384]{2,1,0:T(8,128)(2,1)S(1)}, bf16[8,64,384]{2,1,0:T(8,128)(2,1)}, u32[]{:S(2)}) copy-start(bf16[8,64,384]{2,1,0:T(8,128)(2,1)} %param.9) | copy-start | bytes 1179652
  15.7 11.1 %copy-start.5 = (bf16[384,8]{0,1:T(8,128)(2,1)S(1)}, bf16[384,8]{0,1:T(8,128)(2,1)}, u32[]{:S(2)}) copy-start(bf16[384,8]{0,1:T(8,128)(2,1)} %param.6) | copy-start | bytes 18436
  17.6 9.1 %all-to-all-start.1 = ((bf16[8,16,384]{2,1,0:T(8,128)(2,1)}), bf16[8,16,384]{2,1,0:T(8,128)(2,1)S(1)}, u32[]{:S(2)}, u32[]{:S(2)}) async-start(bf16[8,16,384]{2,1,0:T(8,128)(2,1)} %expert.1), calls=%async_computation.1 | async-start | bytes 196608 | tf_op jit(solution)/shard_map/all_to_all | solution.py:77
  22.0 11.8 %collective-permute-start.2 = (bf16[8,16,384]{2,1,0:T(8,128)(2,1)S(1)}, bf16[8,16,384]{2,1,0:T(8,128)(2,1)S(1)}, u32[]{:S(2)}, u32[]{:S(2)}) collective-permute-start(bf16[8,16,384]{2,1,0:T(8,128)(2,1)S(1)} %all-to-all-done.recv_ref.refs_0_), channel_id=1, source_target_pairs={{0,3},{1,2},{2,1},{3,0},{4,7},{5,6},{6,5},{7,4},{8,11},{9,10},{10,... | collective-permute-start | bytes 294920 | tf_op jit(solution)/shard_map/ppermute | solution.py:291
  22.0 11.8 %collective-permute-start.1 = (bf16[8,16,384]{2,1,0:T(8,128)(2,1)S(1)}, bf16[8,16,384]{2,1,0:T(8,128)(2,1)S(1)}, u32[]{:S(2)}, u32[]{:S(2)}) collective-permute-start(bf16[8,16,384]{2,1,0:T(8,128)(2,1)S(1)} %all-to-all-done.recv_ref.refs_0_), channel_id=1, source_target_pairs={{0,2},{1,3},{2,0},{3,1},{4,6},{5,7},{6,4},{7,5},{8,10},{9,11},{10,... | collective-permute-start | bytes 294920 | tf_op jit(solution)/shard_map/ppermute | solution.py:291
  23.5 10.3 %collective-permute-start = (bf16[8,16,384]{2,1,0:T(8,128)(2,1)S(1)}, bf16[8,16,384]{2,1,0:T(8,128)(2,1)}, u32[]{:S(2)}, u32[]{:S(2)}) collective-permute-start(bf16[8,16,384]{2,1,0:T(8,128)(2,1)S(1)} %all-to-all-done.recv_ref.refs_0_), channel_id=1, source_target_pairs={{0,1},{1,0},{2,3},{3,2},{4,5},{5,4},{6,7},{7,6},{8,9},{9,8},{10,11... | collective-permute-start | bytes 294920 | tf_op jit(solution)/shard_map/ppermute | solution.py:291
  28.0 0.6 %copy-start.4 = (bf16[32,8,96]{2,1,0:T(8,128)(2,1)}, bf16[32,8,96]{2,1,0:T(8,128)(2,1)S(1)}, u32[]{:S(2)}) copy-start(bf16[32,8,96]{2,1,0:T(8,128)(2,1)S(1)} %get-tuple-element.23) | copy-start | bytes 147460
  28.6 10.9 %all-to-all-start.2 = ((bf16[32,8,96]{2,1,0:T(8,128)(2,1)}), bf16[32,8,96]{2,1,0:T(8,128)(2,1)S(1)}, u32[]{:S(2)}, u32[]{:S(2)}) async-start(bf16[32,8,96]{2,1,0:T(8,128)(2,1)} %copy-done.4), calls=%async_computation.2 | async-start | bytes 131072 | tf_op jit(solution)/shard_map/all_to_all | solution.py:77

commit v13 on v12

--- a/solution.py
+++ b/solution.py
@@ -64,12 +64,14 @@
     return first.astype(BF16), second.astype(BF16)
 
 
-def centre_out(count):
-    return sorted(range(count), key=lambda i: (abs(2 * i - count + 1), i))
+def exchange_order(count):
+    first = 5 * count // 8
+    others = sorted(range(count), key=lambda i: (-abs(2 * i - count + 1), i))
+    return [first] + [i for i in others if i != first]
 
 
 def in_expert_order(ref):
-    order = centre_out(ref.shape[0])
+    order = exchange_order(ref.shape[0])
     return jnp.stack([ref[order.index(i)] for i in range(len(order))], axis=0)
 
 
@@ -110,7 +112,7 @@
         load.wait()
     slot_grad = dot(combine_block.astype(BF16), grad_ref[...], 1, 0)
     pairs = pair_rows(slot_in, slot_grad, combine.shape[0])
-    for k, i in enumerate(centre_out(pairs.shape[0])):
+    for k, i in enumerate(exchange_order(pairs.shape[0])):
         sent_ref[k] = pairs[i]
 
 
@@ -233,7 +235,7 @@
 
 def on_device(tokens, router, w_in, w_out, out_grad):
     owners, shares = lax.axis_size("expert"), lax.axis_size("dp")
-    experts_order = centre_out(owners)
+    experts_order = exchange_order(owners)
     share_order = [*range(1, shares, 2), *range(0, shares, 2)]
     images, per_image, width = tokens.shape
     experts = router.shape[1]

time: 40.6 us -> 40.9 us (level)
  starting transfers between devices: 17.7 us -> 20 us
  waiting for transfers between devices: 6.48 us -> 4.46 us
    all_to_all x3, starting transfers between devices: 15.9 us -> 18.2 us  [exchange(): lax.all_to_all(chunks, axis, split_axis=0, concat_axis=0, tiled=True, axi...]
    all_to_all x3, waiting for transfers between devices: 6.48 us -> 4.46 us  [exchange(): lax.all_to_all(chunks, axis, split_axis=0, concat_axis=0, tiled=True, axi...]
  transfers between devices with their start and end apart: 6 -> 6, of which waited for: 3 -> 3; matrix products, arithmetic and copies ran while one was open for 0% -> 0% of each run, Pallas kernels for 18% -> 17%
where the time goes in v13:
time: 40.9 us; the launch traced here: 40.4 us
  starting transfers between devices  20 us (49%)
  Pallas kernels  11.4 us (28%)
  waiting for transfers between devices  4.46 us (11%)
  local copies, waits for them, and re-layouts  3.17 us (8%)
  between operations  0.7 us (2%)
  other arithmetic  0.63 us (2%)
    all_to_all x3, starting transfers between devices, exchange(): lax.all_to_all(chunks, axis, split_axis=0, concat_axis=0, tiled=True, axi...  18.2 us
    all_to_all x3, waiting for transfers between devices, exchange(): lax.all_to_all(chunks, axis, split_axis=0, concat_axis=0, tiled=True, axi...  4.46 us
    pallas_call x1, Pallas kernels, on_device(): pl.pallas_call(functools.partial(weights_kernel, shares), in_specs=[in_sm...  3.8 us
    unnamed x12, local copies, waits for them, and re-layouts  3.17 us
    pallas_call x1, Pallas kernels, on_device(): pl.pallas_call(functools.partial(slots_kernel, images), in_specs=[in_plac...  2.44 us
    pallas_call x1, Pallas kernels, on_device(): pl.pallas_call(functools.partial(expert_kernel, step=512), out_shape=stru...  1.94 us
    ppermute x3, starting transfers between devices, on_device(): lax.ppermute(recv, 'dp', [(i, i ^ k) for i in range(shares)])  1.86 us
    pallas_call x1, Pallas kernels, on_device(): pl.pallas_call(functools.partial(tokens_kernel, images), out_shape=struct...  1.55 us
  transfers between devices with their start and end apart: 6, of which 3 were waited for; matrix products, arithmetic and copies ran while one was open for 0% of the time, Pallas kernels for 17%

profile of v13, /device:TPU:0, one launch (start us, length us, event | category | flops | bytes accessed | tf_op | source)
XLA Modules:
  0.0 40.4 jit_solution(11129856900558449973)
XLA Ops:
  0.6 2.4 %slots.1 = bf16[8,16,384]{2,1,0:T(8,128)(2,1)} custom-call(bf16[512,384]{1,0:T(8,128)(2,1)} %bitcast.10, bf16[8,384]{1,0:T(8,128)(2,1)} %bitcast.17, bf16[512,384]{1,0:T(8,128)(2,1)} %bitcast.13), custom_call_target="tpu_custom_call" | custom-call | tf_op jit(solution)/shard_map/slots/pallas_call | solution.py:256
  3.1 8.2 %all-to-all-start = ((bf16[8,16,384]{2,1,0:T(8,128)(2,1)}), bf16[8,16,384]{2,1,0:T(8,128)(2,1)S(1)}, u32[]{:S(2)}, u32[]{:S(2)}) async-start(bf16[8,16,384]{2,1,0:T(8,128)(2,1)} %slots.1), calls=%async_computation | async-start | bytes 196608 | tf_op jit(solution)/shard_map/all_to_all | solution.py:79
  11.3 0.0 copy-start.2
  11.3 1.3 %copy-done.2 = bf16[1,384,1536]{2,1,0:T(8,128)(2,1)S(1)} copy-done((bf16[1,384,1536]{2,1,0:T(8,128)(2,1)S(1)}, bf16[1,384,1536]{2,1,0:T(8,128)(2,1)}, u32[]{:S(2)}) %copy-start.2) | copy-done | bytes 1179672
  12.6 0.0 copy-start.3
  12.6 1.3 %copy-done.3 = bf16[1,384,1536]{2,1,0:T(8,128)(2,1)S(1)} copy-done((bf16[1,384,1536]{2,1,0:T(8,128)(2,1)S(1)}, bf16[1,384,1536]{2,1,0:T(8,128)(2,1)}, u32[]{:S(2)}) %copy-start.3) | copy-done | bytes 1179672
  13.9 0.5 %stage.1 = (bf16[384,1536]{1,0:T(8,128)(2,1)S(1)}, bf16[384,1536]{1,0:T(8,128)(2,1)S(1)}) custom-call(bf16[384,1536]{1,0:T(8,128)(2,1)S(1)} %bitcast.15, bf16[384,1536]{1,0:T(8,128)(2,1)S(1)} %bitcast.16), custom_call_target="tpu_custom_call" | custom-call | bytes 4718592 | tf_op jit(solution)/shard_map/stage/pallas_call | solution.py:269
  14.4 0.7 %all-to-all-done.recv_ref.refs_0_ = bf16[8,16,384]{2,1,0:T(8,128)(2,1)S(1)} async-done(((bf16[8,16,384]{2,1,0:T(8,128)(2,1)}), bf16[8,16,384]{2,1,0:T(8,128)(2,1)S(1)}, u32[]{:S(2)}, u32[]{:S(2)}) %all-to-all-start) | async-done | bytes 98336 | tf_op jit(solution)/shard_map/all_to_all | solution.py:79
  15.1 0.0 copy-start
  15.1 0.0 copy-start.1
  15.1 0.0 copy-start.5
  15.1 1.9 %expert.1 = bf16[8,16,384]{2,1,0:T(8,128)(2,1)} custom-call(bf16[8,16,384]{2,1,0:T(8,128)(2,1)S(1)} %all-to-all-done.recv_ref.refs_0_, bf16[384,1536]{1,0:T(8,128)(2,1)S(1)} %get-tuple-element.14.win_ref.refs_4_, bf16[384,1536]{1,0:T(8,128)(2,1)S(1)} %get-tuple-element.15.wout_ref.refs_5_), custom_call_target="tpu_custom_call" | custom-call | tf_op jit(solution)/shard_map/expert/pallas_call | solution.py:282
  17.0 5.2 %all-to-all-start.1 = ((bf16[8,16,384]{2,1,0:T(8,128)(2,1)}), bf16[8,16,384]{2,1,0:T(8,128)(2,1)S(1)}, u32[]{:S(2)}, u32[]{:S(2)}) async-start(bf16[8,16,384]{2,1,0:T(8,128)(2,1)} %expert.1), calls=%async_computation.1 | async-start | bytes 196608 | tf_op jit(solution)/shard_map/all_to_all | solution.py:79
  22.2 0.0 collective-permute-start.2
  22.2 1.6 %collective-permute-start.1 = (bf16[8,16,384]{2,1,0:T(8,128)(2,1)S(1)}, bf16[8,16,384]{2,1,0:T(8,128)(2,1)S(1)}, u32[]{:S(2)}, u32[]{:S(2)}) collective-permute-start(bf16[8,16,384]{2,1,0:T(8,128)(2,1)S(1)} %all-to-all-done.recv_ref.refs_0_), channel_id=1, source_target_pairs={{0,2},{1,3},{2,0},{3,1},{4,6},{5,7},{6,4},{7,5},{8,10},{9,11},{10,... | collective-permute-start | bytes 294920 | tf_op jit(solution)/shard_map/ppermute | solution.py:293
  23.8 0.3 collective-permute-start
  24.1 1.9 %all-to-all-done.1.back_hbm.back_ref = bf16[8,16,384]{2,1,0:T(8,128)(2,1)S(1)} async-done(((bf16[8,16,384]{2,1,0:T(8,128)(2,1)}), bf16[8,16,384]{2,1,0:T(8,128)(2,1)S(1)}, u32[]{:S(2)}, u32[]{:S(2)}) %all-to-all-start.1) | async-done | bytes 98336 | tf_op jit(solution)/shard_map/all_to_all | solution.py:79
  26.0 0.0 copy-done
  26.0 0.0 copy-done.1
  26.0 0.0 copy-done.5
  26.0 1.2 %logits.1 = (bf16[32,8,96]{2,1,0:T(8,128)(2,1)S(1)}, bf16[8,512]{1,0:T(8,128)(2,1)S(1)}) custom-call(bf16[8,16,384]{2,1,0:T(8,128)(2,1)S(1)} %all-to-all-done.1.back_hbm.back_ref, bf16[512,384]{1,0:T(8,128)(2,1)S(1)} %bitcast.11, bf16[8,384]{1,0:T(8,128)(2,1)S(1)} %bitcast.18, bf16[512,384]{1,0:T(8,128)(2,1)S(1)} %bitcast.14), custom_call_target="tpu_custom_call" | custom-call | tf_op jit(solution)/shard_map/logits/pallas_call | solution.py:300
  27.2 0.0 copy-start.4
  27.2 0.6 %copy-done.4 = bf16[32,8,96]{2,1,0:T(8,128)(2,1)} copy-done((bf16[32,8,96]{2,1,0:T(8,128)(2,1)}, bf16[32,8,96]{2,1,0:T(8,128)(2,1)S(1)}, u32[]{:S(2)}) %copy-start.4) | copy-done | bytes 49176
  27.8 4.7 %all-to-all-start.2 = ((bf16[32,8,96]{2,1,0:T(8,128)(2,1)}), bf16[32,8,96]{2,1,0:T(8,128)(2,1)S(1)}, u32[]{:S(2)}, u32[]{:S(2)}) async-start(bf16[32,8,96]{2,1,0:T(8,128)(2,1)} %copy-done.4), calls=%async_computation.2 | async-start | bytes 131072 | tf_op jit(solution)/shard_map/all_to_all | solution.py:79
  32.5 1.6 %tokens.1 = bf16[512,384]{1,0:T(8,128)(2,1)} custom-call(bf16[8,16,384]{2,1,0:T(8,128)(2,1)S(1)} %all-to-all-done.1.back_hbm.back_ref, bf16[512,384]{1,0:T(8,128)(2,1)S(1)} %bitcast.12, bf16[8,384]{1,0:T(8,128)(2,1)S(1)} %bitcast.19, bf16[8,512]{1,0:T(8,128)(2,1)S(1)} %get-tuple-element.17.logit_ref), custom_call_target="tpu_custom_call" | custom-call | tf_op jit(solution)/shard_map/tokens/pallas_call | solution.py:317
  34.1 0.0 collective-permute-done.2.refs_3_
  34.1 0.0 collective-permute-done.1.refs_2_
  34.1 0.0 collective-permute-done.refs_1_
  34.1 3.8 %weights.1 = (f32[96,1536]{1,0:T(8,128)}, f32[96,1536]{1,0:T(8,128)}) custom-call(s32[1]{0:T(128)} %bitcast.6.share_ref, bf16[8,16,384]{2,1,0:T(8,128)(2,1)S(1)} %all-to-all-done.recv_ref.refs_0_, bf16[8,16,384]{2,1,0:T(8,128)(2,1)} %collective-permute-done.refs_1_, bf16[8,16,384]{2,1,0:T(8,128)(2,1)S(1)} %collective-permute-done.1.refs_2_, ...), custom_call_target="tpu_custom_call" | custom-call | tf_op jit(solution)/shard_map/weights/pallas_call | solution.py:327
  37.9 1.9 %all-to-all-done.2 = bf16[32,8,96]{2,1,0:T(8,128)(2,1)S(1)} async-done(((bf16[32,8,96]{2,1,0:T(8,128)(2,1)}), bf16[32,8,96]{2,1,0:T(8,128)(2,1)S(1)}, u32[]{:S(2)}, u32[]{:S(2)}) %all-to-all-start.2) | async-done | bytes 49184 | tf_op jit(solution)/shard_map/all_to_all | solution.py:79
  39.8 0.6 %convert_reduce_fusion = f32[8,96]{1,0:T(8,128)} fusion(bf16[32,8,96]{2,1,0:T(8,128)(2,1)S(1)} %all-to-all-done.2), kind=kLoop, calls=%fused_computation | loop fusion | flops 48384 | bytes 52224 | tf_op jit(solution)/shard_map/reduce_sum | solution.py:357
Async XLA Ops:
  3.1 12.0 %all-to-all-start = ((bf16[8,16,384]{2,1,0:T(8,128)(2,1)}), bf16[8,16,384]{2,1,0:T(8,128)(2,1)S(1)}, u32[]{:S(2)}, u32[]{:S(2)}) async-start(bf16[8,16,384]{2,1,0:T(8,128)(2,1)} %slots.1), calls=%async_computation | async-start | bytes 196608 | tf_op jit(solution)/shard_map/all_to_all | solution.py:79
  11.3 1.3 %copy-start.2 = (bf16[1,384,1536]{2,1,0:T(8,128)(2,1)S(1)}, bf16[1,384,1536]{2,1,0:T(8,128)(2,1)}, u32[]{:S(2)}) copy-start(bf16[1,384,1536]{2,1,0:T(8,128)(2,1)} %param.7) | copy-start | bytes 3538948
  12.6 1.3 %copy-start.3 = (bf16[1,384,1536]{2,1,0:T(8,128)(2,1)S(1)}, bf16[1,384,1536]{2,1,0:T(8,128)(2,1)}, u32[]{:S(2)}) copy-start(bf16[1,384,1536]{2,1,0:T(8,128)(2,1)} %param.8) | copy-start | bytes 3538948
  15.1 10.9 %copy-start = (bf16[8,64,384]{2,1,0:T(8,128)(2,1)S(1)}, bf16[8,64,384]{2,1,0:T(8,128)(2,1)}, u32[]{:S(2)}) copy-start(bf16[8,64,384]{2,1,0:T(8,128)(2,1)} %param.5) | copy-start | bytes 1179652
  15.1 10.9 %copy-start.1 = (bf16[8,64,384]{2,1,0:T(8,128)(2,1)S(1)}, bf16[8,64,384]{2,1,0:T(8,128)(2,1)}, u32[]{:S(2)}) copy-start(bf16[8,64,384]{2,1,0:T(8,128)(2,1)} %param.9) | copy-start | bytes 1179652
  15.1 10.9 %copy-start.5 = (bf16[384,8]{0,1:T(8,128)(2,1)S(1)}, bf16[384,8]{0,1:T(8,128)(2,1)}, u32[]{:S(2)}) copy-start(bf16[384,8]{0,1:T(8,128)(2,1)} %param.6) | copy-start | bytes 18436
  17.0 9.0 %all-to-all-start.1 = ((bf16[8,16,384]{2,1,0:T(8,128)(2,1)}), bf16[8,16,384]{2,1,0:T(8,128)(2,1)S(1)}, u32[]{:S(2)}, u32[]{:S(2)}) async-start(bf16[8,16,384]{2,1,0:T(8,128)(2,1)} %expert.1), calls=%async_computation.1 | async-start | bytes 196608 | tf_op jit(solution)/shard_map/all_to_all | solution.py:79
  22.2 11.8 %collective-permute-start.2 = (bf16[8,16,384]{2,1,0:T(8,128)(2,1)S(1)}, bf16[8,16,384]{2,1,0:T(8,128)(2,1)S(1)}, u32[]{:S(2)}, u32[]{:S(2)}) collective-permute-start(bf16[8,16,384]{2,1,0:T(8,128)(2,1)S(1)} %all-to-all-done.recv_ref.refs_0_), channel_id=1, source_target_pairs={{0,3},{1,2},{2,1},{3,0},{4,7},{5,6},{6,5},{7,4},{8,11},{9,10},{10,... | collective-permute-start | bytes 294920 | tf_op jit(solution)/shard_map/ppermute | solution.py:293
  22.2 11.8 %collective-permute-start.1 = (bf16[8,16,384]{2,1,0:T(8,128)(2,1)S(1)}, bf16[8,16,384]{2,1,0:T(8,128)(2,1)S(1)}, u32[]{:S(2)}, u32[]{:S(2)}) collective-permute-start(bf16[8,16,384]{2,1,0:T(8,128)(2,1)S(1)} %all-to-all-done.recv_ref.refs_0_), channel_id=1, source_target_pairs={{0,2},{1,3},{2,0},{3,1},{4,6},{5,7},{6,4},{7,5},{8,10},{9,11},{10,... | collective-permute-start | bytes 294920 | tf_op jit(solution)/shard_map/ppermute | solution.py:293
  23.8 10.3 %collective-permute-start = (bf16[8,16,384]{2,1,0:T(8,128)(2,1)S(1)}, bf16[8,16,384]{2,1,0:T(8,128)(2,1)}, u32[]{:S(2)}, u32[]{:S(2)}) collective-permute-start(bf16[8,16,384]{2,1,0:T(8,128)(2,1)S(1)} %all-to-all-done.recv_ref.refs_0_), channel_id=1, source_target_pairs={{0,1},{1,0},{2,3},{3,2},{4,5},{5,4},{6,7},{7,6},{8,9},{9,8},{10,11... | collective-permute-start | bytes 294920 | tf_op jit(solution)/shard_map/ppermute | solution.py:293
  27.2 0.6 %copy-start.4 = (bf16[32,8,96]{2,1,0:T(8,128)(2,1)}, bf16[32,8,96]{2,1,0:T(8,128)(2,1)S(1)}, u32[]{:S(2)}) copy-start(bf16[32,8,96]{2,1,0:T(8,128)(2,1)S(1)} %get-tuple-element.23) | copy-start | bytes 147460
  27.8 11.9 %all-to-all-start.2 = ((bf16[32,8,96]{2,1,0:T(8,128)(2,1)}), bf16[32,8,96]{2,1,0:T(8,128)(2,1)S(1)}, u32[]{:S(2)}, u32[]{:S(2)}) async-start(bf16[32,8,96]{2,1,0:T(8,128)(2,1)} %copy-done.4), calls=%async_computation.2 | async-start | bytes 131072 | tf_op jit(solution)/shard_map/all_to_all | solution.py:79

commit v14 on v12

--- a/solution.py
+++ b/solution.py
@@ -140,13 +140,10 @@
 
 
 def logits_kernel(
-    images, share_order, back_hbm, tokens_ref, router_ref, grad_ref, send_ref, logit_ref, back_ref, sem
+    images, share_order, back_ref, tokens_ref, router_ref, grad_ref, send_ref, logit_ref
 ):
-    load = pltpu.make_async_copy(back_hbm, back_ref, sem)
-    load.start()
     tokens = tokens_ref[...]
     dispatch, combine, mask = softmaxes(router_ref[...], tokens, images)
-    load.wait()
     slot_out, slot_in_grad = split_rows(in_expert_order(back_ref))
     disp = jnp.where(mask, dot(slot_in_grad, tokens, 1, 1), 0.0)
     comb = fold_rows(jnp.where(mask, dot(slot_out, grad_ref[...], 1, 1), 0.0), images)
@@ -297,12 +294,11 @@
     in_vmem = pl.BlockSpec(memory_space=pltpu.VMEM)
     router_send, logit_grad = pl.pallas_call(
         functools.partial(logits_kernel, images, share_order),
-        in_specs=[in_place] + [in_vmem] * 3,
+        in_specs=[in_vmem] * 4,
         out_shape=(
             struct((owners * shares, experts, row_count), BF16),
             struct((experts, columns), BF16),
         ),
-        scratch_shapes=[pltpu.VMEM(back.shape, BF16), pltpu.SemaphoreType.DMA],
         compiler_params=params,
         name="logits",
     )(slots_back, tokens2, router_rows, grad2)

time: 40.6 us -> 40.2 us (level)
    pallas_call x1, Pallas kernels: 1.19 us -> 0.77 us  [on_device(): pl.pallas_call(functools.partial(logits_kernel, images, share_order), in_...]
  transfers between devices with their start and end apart: 6 -> 6, of which waited for: 3 -> 3; matrix products, arithmetic and copies ran while one was open for 0% -> 0% of each run, Pallas kernels for 18% -> 17%
where the time goes in v14:
time: 40.2 us; the launch traced here: 39.7 us
  starting transfers between devices  17.7 us (44%)
  Pallas kernels  11 us (27%)
  waiting for transfers between devices  6.48 us (16%)
  local copies, waits for them, and re-layouts  3.18 us (8%)
  between operations  0.69 us (2%)
  other arithmetic  0.63 us (2%)
    all_to_all x3, starting transfers between devices, exchange(): lax.all_to_all(chunks, axis, split_axis=0, concat_axis=0, tiled=True, axi...  15.9 us
    all_to_all x3, waiting for transfers between devices, exchange(): lax.all_to_all(chunks, axis, split_axis=0, concat_axis=0, tiled=True, axi...  6.48 us
    pallas_call x1, Pallas kernels, on_device(): pl.pallas_call(functools.partial(weights_kernel, shares), in_specs=[in_sm...  3.8 us
    unnamed x12, local copies, waits for them, and re-layouts  3.18 us
    pallas_call x1, Pallas kernels, on_device(): pl.pallas_call(functools.partial(slots_kernel, images), in_specs=[in_plac...  2.44 us
    pallas_call x1, Pallas kernels, on_device(): pl.pallas_call(functools.partial(expert_kernel, step=512), out_shape=stru...  1.94 us
    ppermute x3, starting transfers between devices, on_device(): lax.ppermute(recv, 'dp', [(i, i ^ k) for i in range(shares)])  1.86 us
    pallas_call x1, Pallas kernels, on_device(): pl.pallas_call(functools.partial(tokens_kernel, images), out_shape=struct...  1.55 us
  transfers between devices with their start and end apart: 6, of which 3 were waited for; matrix products, arithmetic and copies ran while one was open for 0% of the time, Pallas kernels for 17%

profile of v14, /device:TPU:0, one launch (start us, length us, event | category | flops | bytes accessed | tf_op | source)
XLA Modules:
  0.0 39.7 jit_solution(3979033691839205830)
XLA Ops:
  0.6 2.4 %slots.1 = bf16[8,16,384]{2,1,0:T(8,128)(2,1)} custom-call(bf16[512,384]{1,0:T(8,128)(2,1)} %bitcast.10, bf16[8,384]{1,0:T(8,128)(2,1)} %bitcast.17, bf16[512,384]{1,0:T(8,128)(2,1)} %bitcast.13), custom_call_target="tpu_custom_call" | custom-call | tf_op jit(solution)/shard_map/slots/pallas_call | solution.py:251
  3.1 7.8 %all-to-all-start = ((bf16[8,16,384]{2,1,0:T(8,128)(2,1)}), bf16[8,16,384]{2,1,0:T(8,128)(2,1)S(1)}, u32[]{:S(2)}, u32[]{:S(2)}) async-start(bf16[8,16,384]{2,1,0:T(8,128)(2,1)} %slots.1), calls=%async_computation | async-start | bytes 196608 | tf_op jit(solution)/shard_map/all_to_all | solution.py:77
  10.9 0.0 copy-start.2
  10.9 1.3 %copy-done.2 = bf16[1,384,1536]{2,1,0:T(8,128)(2,1)S(1)} copy-done((bf16[1,384,1536]{2,1,0:T(8,128)(2,1)S(1)}, bf16[1,384,1536]{2,1,0:T(8,128)(2,1)}, u32[]{:S(2)}) %copy-start.2) | copy-done | bytes 1179672
  12.2 0.0 copy-start.3
  12.2 1.3 %copy-done.3 = bf16[1,384,1536]{2,1,0:T(8,128)(2,1)S(1)} copy-done((bf16[1,384,1536]{2,1,0:T(8,128)(2,1)S(1)}, bf16[1,384,1536]{2,1,0:T(8,128)(2,1)}, u32[]{:S(2)}) %copy-start.3) | copy-done | bytes 1179672
  13.4 0.5 %stage.1 = (bf16[384,1536]{1,0:T(8,128)(2,1)S(1)}, bf16[384,1536]{1,0:T(8,128)(2,1)S(1)}) custom-call(bf16[384,1536]{1,0:T(8,128)(2,1)S(1)} %bitcast.15, bf16[384,1536]{1,0:T(8,128)(2,1)S(1)} %bitcast.16), custom_call_target="tpu_custom_call" | custom-call | bytes 4718592 | tf_op jit(solution)/shard_map/stage/pallas_call | solution.py:264
  14.0 1.7 %all-to-all-done.recv_ref.refs_0_ = bf16[8,16,384]{2,1,0:T(8,128)(2,1)S(1)} async-done(((bf16[8,16,384]{2,1,0:T(8,128)(2,1)}), bf16[8,16,384]{2,1,0:T(8,128)(2,1)S(1)}, u32[]{:S(2)}, u32[]{:S(2)}) %all-to-all-start) | async-done | bytes 98336 | tf_op jit(solution)/shard_map/all_to_all | solution.py:77
  15.7 0.0 copy-start
  15.7 0.0 copy-start.1
  15.7 0.0 copy-start.5
  15.7 1.9 %expert.1 = bf16[8,16,384]{2,1,0:T(8,128)(2,1)} custom-call(bf16[8,16,384]{2,1,0:T(8,128)(2,1)S(1)} %all-to-all-done.recv_ref.refs_0_, bf16[384,1536]{1,0:T(8,128)(2,1)S(1)} %get-tuple-element.14.win_ref.refs_4_, bf16[384,1536]{1,0:T(8,128)(2,1)S(1)} %get-tuple-element.15.wout_ref.refs_5_), custom_call_target="tpu_custom_call" | custom-call | tf_op jit(solution)/shard_map/expert/pallas_call | solution.py:277
  17.6 4.4 %all-to-all-start.1 = ((bf16[8,16,384]{2,1,0:T(8,128)(2,1)}), bf16[8,16,384]{2,1,0:T(8,128)(2,1)S(1)}, u32[]{:S(2)}, u32[]{:S(2)}) async-start(bf16[8,16,384]{2,1,0:T(8,128)(2,1)} %expert.1), calls=%async_computation.1 | async-start | bytes 196608 | tf_op jit(solution)/shard_map/all_to_all | solution.py:77
  22.0 0.0 collective-permute-start.2
  22.0 1.5 %collective-permute-start.1 = (bf16[8,16,384]{2,1,0:T(8,128)(2,1)S(1)}, bf16[8,16,384]{2,1,0:T(8,128)(2,1)S(1)}, u32[]{:S(2)}, u32[]{:S(2)}) collective-permute-start(bf16[8,16,384]{2,1,0:T(8,128)(2,1)S(1)} %all-to-all-done.recv_ref.refs_0_), channel_id=1, source_target_pairs={{0,2},{1,3},{2,0},{3,1},{4,6},{5,7},{6,4},{7,5},{8,10},{9,11},{10,... | collective-permute-start | bytes 294920 | tf_op jit(solution)/shard_map/ppermute | solution.py:288
  23.5 0.3 collective-permute-start
  23.9 2.9 %all-to-all-done.1.back_ref = bf16[8,16,384]{2,1,0:T(8,128)(2,1)S(1)} async-done(((bf16[8,16,384]{2,1,0:T(8,128)(2,1)}), bf16[8,16,384]{2,1,0:T(8,128)(2,1)S(1)}, u32[]{:S(2)}, u32[]{:S(2)}) %all-to-all-start.1) | async-done | bytes 98336 | tf_op jit(solution)/shard_map/all_to_all | solution.py:77
  26.7 0.0 copy-done
  26.7 0.0 copy-done.1
  26.8 0.0 copy-done.5
  26.8 0.8 %logits.1 = (bf16[32,8,96]{2,1,0:T(8,128)(2,1)S(1)}, bf16[8,512]{1,0:T(8,128)(2,1)S(1)}) custom-call(bf16[8,16,384]{2,1,0:T(8,128)(2,1)S(1)} %all-to-all-done.1.back_ref, bf16[512,384]{1,0:T(8,128)(2,1)S(1)} %bitcast.11, bf16[8,384]{1,0:T(8,128)(2,1)S(1)} %bitcast.18, bf16[512,384]{1,0:T(8,128)(2,1)S(1)} %bitcast.14), custom_call_target="tpu_custom_call" | custom-call | tf_op jit(solution)/shard_map/logits/pallas_call | solution.py:295
  27.5 0.0 copy-start.4
  27.5 0.6 %copy-done.4 = bf16[32,8,96]{2,1,0:T(8,128)(2,1)} copy-done((bf16[32,8,96]{2,1,0:T(8,128)(2,1)}, bf16[32,8,96]{2,1,0:T(8,128)(2,1)S(1)}, u32[]{:S(2)}) %copy-start.4) | copy-done | bytes 49176
  28.2 3.7 %all-to-all-start.2 = ((bf16[32,8,96]{2,1,0:T(8,128)(2,1)}), bf16[32,8,96]{2,1,0:T(8,128)(2,1)S(1)}, u32[]{:S(2)}, u32[]{:S(2)}) async-start(bf16[32,8,96]{2,1,0:T(8,128)(2,1)} %copy-done.4), calls=%async_computation.2 | async-start | bytes 131072 | tf_op jit(solution)/shard_map/all_to_all | solution.py:77
  31.9 1.6 %tokens.1 = bf16[512,384]{1,0:T(8,128)(2,1)} custom-call(bf16[8,16,384]{2,1,0:T(8,128)(2,1)S(1)} %all-to-all-done.1.back_ref, bf16[512,384]{1,0:T(8,128)(2,1)S(1)} %bitcast.12, bf16[8,384]{1,0:T(8,128)(2,1)S(1)} %bitcast.19, bf16[8,512]{1,0:T(8,128)(2,1)S(1)} %get-tuple-element.17.logit_ref), custom_call_target="tpu_custom_call" | custom-call | tf_op jit(solution)/shard_map/tokens/pallas_call | solution.py:311
  33.4 0.0 collective-permute-done.2.refs_3_
  33.4 0.0 collective-permute-done.1.refs_2_
  33.4 0.0 collective-permute-done.refs_1_
  33.4 3.8 %weights.1 = (f32[96,1536]{1,0:T(8,128)}, f32[96,1536]{1,0:T(8,128)}) custom-call(s32[1]{0:T(128)} %bitcast.6.share_ref, bf16[8,16,384]{2,1,0:T(8,128)(2,1)S(1)} %all-to-all-done.recv_ref.refs_0_, bf16[8,16,384]{2,1,0:T(8,128)(2,1)} %collective-permute-done.refs_1_, bf16[8,16,384]{2,1,0:T(8,128)(2,1)S(1)} %collective-permute-done.1.refs_2_, ...), custom_call_target="tpu_custom_call" | custom-call | tf_op jit(solution)/shard_map/weights/pallas_call | solution.py:321
  37.2 1.9 %all-to-all-done.2 = bf16[32,8,96]{2,1,0:T(8,128)(2,1)S(1)} async-done(((bf16[32,8,96]{2,1,0:T(8,128)(2,1)}), bf16[32,8,96]{2,1,0:T(8,128)(2,1)S(1)}, u32[]{:S(2)}, u32[]{:S(2)}) %all-to-all-start.2) | async-done | bytes 49184 | tf_op jit(solution)/shard_map/all_to_all | solution.py:77
  39.1 0.6 %convert_reduce_fusion = f32[8,96]{1,0:T(8,128)} fusion(bf16[32,8,96]{2,1,0:T(8,128)(2,1)S(1)} %all-to-all-done.2), kind=kLoop, calls=%fused_computation | loop fusion | flops 48384 | bytes 52224 | tf_op jit(solution)/shard_map/reduce_sum | solution.py:351
Async XLA Ops:
  3.1 12.6 %all-to-all-start = ((bf16[8,16,384]{2,1,0:T(8,128)(2,1)}), bf16[8,16,384]{2,1,0:T(8,128)(2,1)S(1)}, u32[]{:S(2)}, u32[]{:S(2)}) async-start(bf16[8,16,384]{2,1,0:T(8,128)(2,1)} %slots.1), calls=%async_computation | async-start | bytes 196608 | tf_op jit(solution)/shard_map/all_to_all | solution.py:77
  10.9 1.3 %copy-start.2 = (bf16[1,384,1536]{2,1,0:T(8,128)(2,1)S(1)}, bf16[1,384,1536]{2,1,0:T(8,128)(2,1)}, u32[]{:S(2)}) copy-start(bf16[1,384,1536]{2,1,0:T(8,128)(2,1)} %param.7) | copy-start | bytes 3538948
  12.2 1.3 %copy-start.3 = (bf16[1,384,1536]{2,1,0:T(8,128)(2,1)S(1)}, bf16[1,384,1536]{2,1,0:T(8,128)(2,1)}, u32[]{:S(2)}) copy-start(bf16[1,384,1536]{2,1,0:T(8,128)(2,1)} %param.8) | copy-start | bytes 3538948
  15.7 11.1 %copy-start = (bf16[8,64,384]{2,1,0:T(8,128)(2,1)S(1)}, bf16[8,64,384]{2,1,0:T(8,128)(2,1)}, u32[]{:S(2)}) copy-start(bf16[8,64,384]{2,1,0:T(8,128)(2,1)} %param.5) | copy-start | bytes 1179652
  15.7 11.1 %copy-start.1 = (bf16[8,64,384]{2,1,0:T(8,128)(2,1)S(1)}, bf16[8,64,384]{2,1,0:T(8,128)(2,1)}, u32[]{:S(2)}) copy-start(bf16[8,64,384]{2,1,0:T(8,128)(2,1)} %param.9) | copy-start | bytes 1179652
  15.7 11.1 %copy-start.5 = (bf16[384,8]{0,1:T(8,128)(2,1)S(1)}, bf16[384,8]{0,1:T(8,128)(2,1)}, u32[]{:S(2)}) copy-start(bf16[384,8]{0,1:T(8,128)(2,1)} %param.6) | copy-start | bytes 18436
  17.6 9.1 %all-to-all-start.1 = ((bf16[8,16,384]{2,1,0:T(8,128)(2,1)}), bf16[8,16,384]{2,1,0:T(8,128)(2,1)S(1)}, u32[]{:S(2)}, u32[]{:S(2)}) async-start(bf16[8,16,384]{2,1,0:T(8,128)(2,1)} %expert.1), calls=%async_computation.1 | async-start | bytes 196608 | tf_op jit(solution)/shard_map/all_to_all | solution.py:77
  22.0 11.4 %collective-permute-start.2 = (bf16[8,16,384]{2,1,0:T(8,128)(2,1)S(1)}, bf16[8,16,384]{2,1,0:T(8,128)(2,1)S(1)}, u32[]{:S(2)}, u32[]{:S(2)}) collective-permute-start(bf16[8,16,384]{2,1,0:T(8,128)(2,1)S(1)} %all-to-all-done.recv_ref.refs_0_), channel_id=1, source_target_pairs={{0,3},{1,2},{2,1},{3,0},{4,7},{5,6},{6,5},{7,4},{8,11},{9,10},{10,... | collective-permute-start | bytes 294920 | tf_op jit(solution)/shard_map/ppermute | solution.py:288
  22.0 11.4 %collective-permute-start.1 = (bf16[8,16,384]{2,1,0:T(8,128)(2,1)S(1)}, bf16[8,16,384]{2,1,0:T(8,128)(2,1)S(1)}, u32[]{:S(2)}, u32[]{:S(2)}) collective-permute-start(bf16[8,16,384]{2,1,0:T(8,128)(2,1)S(1)} %all-to-all-done.recv_ref.refs_0_), channel_id=1, source_target_pairs={{0,2},{1,3},{2,0},{3,1},{4,6},{5,7},{6,4},{7,5},{8,10},{9,11},{10,... | collective-permute-start | bytes 294920 | tf_op jit(solution)/shard_map/ppermute | solution.py:288
  23.5 9.9 %collective-permute-start = (bf16[8,16,384]{2,1,0:T(8,128)(2,1)S(1)}, bf16[8,16,384]{2,1,0:T(8,128)(2,1)}, u32[]{:S(2)}, u32[]{:S(2)}) collective-permute-start(bf16[8,16,384]{2,1,0:T(8,128)(2,1)S(1)} %all-to-all-done.recv_ref.refs_0_), channel_id=1, source_target_pairs={{0,1},{1,0},{2,3},{3,2},{4,5},{5,4},{6,7},{7,6},{8,9},{9,8},{10,11... | collective-permute-start | bytes 294920 | tf_op jit(solution)/shard_map/ppermute | solution.py:288
  27.5 0.6 %copy-start.4 = (bf16[32,8,96]{2,1,0:T(8,128)(2,1)}, bf16[32,8,96]{2,1,0:T(8,128)(2,1)S(1)}, u32[]{:S(2)}) copy-start(bf16[32,8,96]{2,1,0:T(8,128)(2,1)S(1)} %get-tuple-element.23) | copy-start | bytes 147460
  28.2 10.9 %all-to-all-start.2 = ((bf16[32,8,96]{2,1,0:T(8,128)(2,1)}), bf16[32,8,96]{2,1,0:T(8,128)(2,1)S(1)}, u32[]{:S(2)}, u32[]{:S(2)}) async-start(bf16[32,8,96]{2,1,0:T(8,128)(2,1)} %copy-done.4), calls=%async_computation.2 | async-start | bytes 131072 | tf_op jit(solution)/shard_map/all_to_all | solution.py:77

commit v15 on v14

--- a/solution.py
+++ b/solution.py
@@ -93,21 +93,20 @@
 
 def slots_kernel(images, tokens_hbm, router_hbm, grad_hbm, sent_ref, *scratch):
     tokens_ref, router_ref, grad_ref, sems = scratch
-    first = [
-        pltpu.make_async_copy(tokens_hbm, tokens_ref, sems.at[0]),
-        pltpu.make_async_copy(router_hbm, router_ref, sems.at[1]),
+    loads = [
+        pltpu.make_async_copy(source, target, sems.at[i])
+        for i, (source, target) in enumerate(
+            ((tokens_hbm, tokens_ref), (router_hbm, router_ref), (grad_hbm, grad_ref))
+        )
     ]
-    second = [pltpu.make_async_copy(grad_hbm, grad_ref, sems.at[2])]
-    for load in first + second:
+    for load in loads:
         load.start()
-    for load in first:
+    for load in loads:
         load.wait()
     tokens = tokens_ref[...]
     block, combine, mask = softmaxes(router_ref[...], tokens, images)
     combine_block = jnp.where(mask, spread_rows(combine, images), 0.0)
     slot_in = dot(block.astype(BF16), tokens, 1, 0)
-    for load in second:
-        load.wait()
     slot_grad = dot(combine_block.astype(BF16), grad_ref[...], 1, 0)
     pairs = pair_rows(slot_in, slot_grad, combine.shape[0])
     for k, i in enumerate(centre_out(pairs.shape[0])):
@@ -248,9 +247,11 @@
         return jax.ShapeDtypeStruct(shape, dtype)
 
     in_place = pl.BlockSpec(memory_space=pl.ANY)
+    in_vmem = pl.BlockSpec(memory_space=pltpu.VMEM)
     sent = pl.pallas_call(
         functools.partial(slots_kernel, images),
         in_specs=[in_place] * 3,
+        out_specs=in_vmem,
         out_shape=struct((experts, 2 * images, width), BF16),
         scratch_shapes=[
             pltpu.VMEM((columns, width), BF16),
@@ -276,6 +277,8 @@
     recv = exchange(sent, "expert", experts_order)
     back = pl.pallas_call(
         functools.partial(expert_kernel, step=512),
+        in_specs=[in_vmem] * 3,
+        out_specs=in_vmem,
         out_shape=struct(recv.shape, BF16),
         compiler_params=params,
         name="expert",
@@ -291,10 +294,10 @@
     else:
         spread = [lax.all_gather(recv, "dp", axis=0, tiled=False)]
 
-    in_vmem = pl.BlockSpec(memory_space=pltpu.VMEM)
     router_send, logit_grad = pl.pallas_call(
         functools.partial(logits_kernel, images, share_order),
         in_specs=[in_vmem] * 4,
+        out_specs=(in_vmem, in_vmem),
         out_shape=(
             struct((owners * shares, experts, row_count), BF16),
             struct((experts, columns), BF16),
@@ -310,6 +313,8 @@
     )
     tokens_grad = pl.pallas_call(
         functools.partial(tokens_kernel, images),
+        in_specs=[in_vmem] * 4,
+        out_specs=in_vmem,
         out_shape=struct((columns, width), BF16),
         compiler_params=params,
         name="tokens",

time: 40.2 us -> 40.2 us (level)
  no operation moved by 1% of the time
where the time goes in v15:
time: 40.2 us; the launch traced here: 39.7 us
  starting transfers between devices  17.7 us (44%)
  Pallas kernels  11 us (27%)
  waiting for transfers between devices  6.48 us (16%)
  local copies, waits for them, and re-layouts  3.18 us (8%)
  between operations  0.69 us (2%)
  other arithmetic  0.63 us (2%)
    all_to_all x3, starting transfers between devices, exchange(): lax.all_to_all(chunks, axis, split_axis=0, concat_axis=0, tiled=True, axi...  15.9 us
    all_to_all x3, waiting for transfers between devices, exchange(): lax.all_to_all(chunks, axis, split_axis=0, concat_axis=0, tiled=True, axi...  6.48 us
    pallas_call x1, Pallas kernels, on_device(): pl.pallas_call(functools.partial(weights_kernel, shares), in_specs=[in_sm...  3.8 us
    unnamed x12, local copies, waits for them, and re-layouts  3.18 us
    pallas_call x1, Pallas kernels, on_device(): pl.pallas_call(functools.partial(slots_kernel, images), in_specs=[in_plac...  2.43 us
    pallas_call x1, Pallas kernels, on_device(): pl.pallas_call(functools.partial(expert_kernel, step=512), in_specs=[in_v...  1.94 us
    ppermute x3, starting transfers between devices, on_device(): lax.ppermute(recv, 'dp', [(i, i ^ k) for i in range(shares)])  1.86 us
    pallas_call x1, Pallas kernels, on_device(): pl.pallas_call(functools.partial(tokens_kernel, images), in_specs=[in_vme...  1.55 us
  transfers between devices with their start and end apart: 6, of which 3 were waited for; matrix products, arithmetic and copies ran while one was open for 0% of the time, Pallas kernels for 17%

profile of v15, /device:TPU:0, one launch (start us, length us, event | category | flops | bytes accessed | tf_op | source)
XLA Modules:
  0.0 39.7 jit_solution(14862264039434279341)
XLA Ops:
  0.6 2.4 %slots.1 = bf16[8,16,384]{2,1,0:T(8,128)(2,1)} custom-call(bf16[512,384]{1,0:T(8,128)(2,1)} %bitcast.10, bf16[8,384]{1,0:T(8,128)(2,1)} %bitcast.17, bf16[512,384]{1,0:T(8,128)(2,1)} %bitcast.13), custom_call_target="tpu_custom_call" | custom-call | tf_op jit(solution)/shard_map/slots/pallas_call | solution.py:251
  3.1 7.8 %all-to-all-start = ((bf16[8,16,384]{2,1,0:T(8,128)(2,1)}), bf16[8,16,384]{2,1,0:T(8,128)(2,1)S(1)}, u32[]{:S(2)}, u32[]{:S(2)}) async-start(bf16[8,16,384]{2,1,0:T(8,128)(2,1)} %slots.1), calls=%async_computation | async-start | bytes 196608 | tf_op jit(solution)/shard_map/all_to_all | solution.py:77
  10.9 0.0 copy-start.2
  10.9 1.3 %copy-done.2 = bf16[1,384,1536]{2,1,0:T(8,128)(2,1)S(1)} copy-done((bf16[1,384,1536]{2,1,0:T(8,128)(2,1)S(1)}, bf16[1,384,1536]{2,1,0:T(8,128)(2,1)}, u32[]{:S(2)}) %copy-start.2) | copy-done | bytes 1179672
  12.2 0.0 copy-start.3
  12.2 1.3 %copy-done.3 = bf16[1,384,1536]{2,1,0:T(8,128)(2,1)S(1)} copy-done((bf16[1,384,1536]{2,1,0:T(8,128)(2,1)S(1)}, bf16[1,384,1536]{2,1,0:T(8,128)(2,1)}, u32[]{:S(2)}) %copy-start.3) | copy-done | bytes 1179672
  13.4 0.5 %stage.1 = (bf16[384,1536]{1,0:T(8,128)(2,1)S(1)}, bf16[384,1536]{1,0:T(8,128)(2,1)S(1)}) custom-call(bf16[384,1536]{1,0:T(8,128)(2,1)S(1)} %bitcast.15, bf16[384,1536]{1,0:T(8,128)(2,1)S(1)} %bitcast.16), custom_call_target="tpu_custom_call" | custom-call | bytes 4718592 | tf_op jit(solution)/shard_map/stage/pallas_call | solution.py:265
  13.9 1.7 %all-to-all-done.recv_ref.refs_0_ = bf16[8,16,384]{2,1,0:T(8,128)(2,1)S(1)} async-done(((bf16[8,16,384]{2,1,0:T(8,128)(2,1)}), bf16[8,16,384]{2,1,0:T(8,128)(2,1)S(1)}, u32[]{:S(2)}, u32[]{:S(2)}) %all-to-all-start) | async-done | bytes 98336 | tf_op jit(solution)/shard_map/all_to_all | solution.py:77
  15.7 0.0 copy-start
  15.7 0.0 copy-start.1
  15.7 0.0 copy-start.5
  15.7 1.9 %expert.1 = bf16[8,16,384]{2,1,0:T(8,128)(2,1)} custom-call(bf16[8,16,384]{2,1,0:T(8,128)(2,1)S(1)} %all-to-all-done.recv_ref.refs_0_, bf16[384,1536]{1,0:T(8,128)(2,1)S(1)} %get-tuple-element.14.win_ref.refs_4_, bf16[384,1536]{1,0:T(8,128)(2,1)S(1)} %get-tuple-element.15.wout_ref.refs_5_), custom_call_target="tpu_custom_call" | custom-call | tf_op jit(solution)/shard_map/expert/pallas_call | solution.py:278
  17.6 4.4 %all-to-all-start.1 = ((bf16[8,16,384]{2,1,0:T(8,128)(2,1)}), bf16[8,16,384]{2,1,0:T(8,128)(2,1)S(1)}, u32[]{:S(2)}, u32[]{:S(2)}) async-start(bf16[8,16,384]{2,1,0:T(8,128)(2,1)} %expert.1), calls=%async_computation.1 | async-start | bytes 196608 | tf_op jit(solution)/shard_map/all_to_all | solution.py:77
  22.0 0.0 collective-permute-start.2
  22.0 1.5 %collective-permute-start.1 = (bf16[8,16,384]{2,1,0:T(8,128)(2,1)S(1)}, bf16[8,16,384]{2,1,0:T(8,128)(2,1)S(1)}, u32[]{:S(2)}, u32[]{:S(2)}) collective-permute-start(bf16[8,16,384]{2,1,0:T(8,128)(2,1)S(1)} %all-to-all-done.recv_ref.refs_0_), channel_id=1, source_target_pairs={{0,2},{1,3},{2,0},{3,1},{4,6},{5,7},{6,4},{7,5},{8,10},{9,11},{10,... | collective-permute-start | bytes 294920 | tf_op jit(solution)/shard_map/ppermute | solution.py:291
  23.5 0.3 collective-permute-start
  23.8 2.9 %all-to-all-done.1.back_ref = bf16[8,16,384]{2,1,0:T(8,128)(2,1)S(1)} async-done(((bf16[8,16,384]{2,1,0:T(8,128)(2,1)}), bf16[8,16,384]{2,1,0:T(8,128)(2,1)S(1)}, u32[]{:S(2)}, u32[]{:S(2)}) %all-to-all-start.1) | async-done | bytes 98336 | tf_op jit(solution)/shard_map/all_to_all | solution.py:77
  26.7 0.0 copy-done
  26.7 0.0 copy-done.1
  26.7 0.0 copy-done.5
  26.7 0.8 %logits.1 = (bf16[32,8,96]{2,1,0:T(8,128)(2,1)S(1)}, bf16[8,512]{1,0:T(8,128)(2,1)S(1)}) custom-call(bf16[8,16,384]{2,1,0:T(8,128)(2,1)S(1)} %all-to-all-done.1.back_ref, bf16[512,384]{1,0:T(8,128)(2,1)S(1)} %bitcast.11, bf16[8,384]{1,0:T(8,128)(2,1)S(1)} %bitcast.18, bf16[512,384]{1,0:T(8,128)(2,1)S(1)} %bitcast.14), custom_call_target="tpu_custom_call" | custom-call | tf_op jit(solution)/shard_map/logits/pallas_call | solution.py:297
  27.5 0.0 copy-start.4
  27.5 0.6 %copy-done.4 = bf16[32,8,96]{2,1,0:T(8,128)(2,1)} copy-done((bf16[32,8,96]{2,1,0:T(8,128)(2,1)}, bf16[32,8,96]{2,1,0:T(8,128)(2,1)S(1)}, u32[]{:S(2)}) %copy-start.4) | copy-done | bytes 49176
  28.2 3.7 %all-to-all-start.2 = ((bf16[32,8,96]{2,1,0:T(8,128)(2,1)}), bf16[32,8,96]{2,1,0:T(8,128)(2,1)S(1)}, u32[]{:S(2)}, u32[]{:S(2)}) async-start(bf16[32,8,96]{2,1,0:T(8,128)(2,1)} %copy-done.4), calls=%async_computation.2 | async-start | bytes 131072 | tf_op jit(solution)/shard_map/all_to_all | solution.py:77
  31.8 1.6 %tokens.1 = bf16[512,384]{1,0:T(8,128)(2,1)} custom-call(bf16[8,16,384]{2,1,0:T(8,128)(2,1)S(1)} %all-to-all-done.1.back_ref, bf16[512,384]{1,0:T(8,128)(2,1)S(1)} %bitcast.12, bf16[8,384]{1,0:T(8,128)(2,1)S(1)} %bitcast.19, bf16[8,512]{1,0:T(8,128)(2,1)S(1)} %get-tuple-element.17.logit_ref), custom_call_target="tpu_custom_call" | custom-call | tf_op jit(solution)/shard_map/tokens/pallas_call | solution.py:314
  33.4 0.0 collective-permute-done.2.refs_3_
  33.4 0.0 collective-permute-done.1.refs_2_
  33.4 0.0 collective-permute-done.refs_1_
  33.4 3.8 %weights.1 = (f32[96,1536]{1,0:T(8,128)}, f32[96,1536]{1,0:T(8,128)}) custom-call(s32[1]{0:T(128)} %bitcast.6.share_ref, bf16[8,16,384]{2,1,0:T(8,128)(2,1)S(1)} %all-to-all-done.recv_ref.refs_0_, bf16[8,16,384]{2,1,0:T(8,128)(2,1)} %collective-permute-done.refs_1_, bf16[8,16,384]{2,1,0:T(8,128)(2,1)S(1)} %collective-permute-done.1.refs_2_, ...), custom_call_target="tpu_custom_call" | custom-call | tf_op jit(solution)/shard_map/weights/pallas_call | solution.py:326
  37.2 1.9 %all-to-all-done.2 = bf16[32,8,96]{2,1,0:T(8,128)(2,1)S(1)} async-done(((bf16[32,8,96]{2,1,0:T(8,128)(2,1)}), bf16[32,8,96]{2,1,0:T(8,128)(2,1)S(1)}, u32[]{:S(2)}, u32[]{:S(2)}) %all-to-all-start.2) | async-done | bytes 49184 | tf_op jit(solution)/shard_map/all_to_all | solution.py:77
  39.1 0.6 %convert_reduce_fusion = f32[8,96]{1,0:T(8,128)} fusion(bf16[32,8,96]{2,1,0:T(8,128)(2,1)S(1)} %all-to-all-done.2), kind=kLoop, calls=%fused_computation | loop fusion | flops 48384 | bytes 52224 | tf_op jit(solution)/shard_map/reduce_sum | solution.py:356
Async XLA Ops:
  3.1 12.6 %all-to-all-start = ((bf16[8,16,384]{2,1,0:T(8,128)(2,1)}), bf16[8,16,384]{2,1,0:T(8,128)(2,1)S(1)}, u32[]{:S(2)}, u32[]{:S(2)}) async-start(bf16[8,16,384]{2,1,0:T(8,128)(2,1)} %slots.1), calls=%async_computation | async-start | bytes 196608 | tf_op jit(solution)/shard_map/all_to_all | solution.py:77
  10.9 1.3 %copy-start.2 = (bf16[1,384,1536]{2,1,0:T(8,128)(2,1)S(1)}, bf16[1,384,1536]{2,1,0:T(8,128)(2,1)}, u32[]{:S(2)}) copy-start(bf16[1,384,1536]{2,1,0:T(8,128)(2,1)} %param.7) | copy-start | bytes 3538948
  12.2 1.3 %copy-start.3 = (bf16[1,384,1536]{2,1,0:T(8,128)(2,1)S(1)}, bf16[1,384,1536]{2,1,0:T(8,128)(2,1)}, u32[]{:S(2)}) copy-start(bf16[1,384,1536]{2,1,0:T(8,128)(2,1)} %param.8) | copy-start | bytes 3538948
  15.7 11.1 %copy-start = (bf16[8,64,384]{2,1,0:T(8,128)(2,1)S(1)}, bf16[8,64,384]{2,1,0:T(8,128)(2,1)}, u32[]{:S(2)}) copy-start(bf16[8,64,384]{2,1,0:T(8,128)(2,1)} %param.5) | copy-start | bytes 1179652
  15.7 11.1 %copy-start.1 = (bf16[8,64,384]{2,1,0:T(8,128)(2,1)S(1)}, bf16[8,64,384]{2,1,0:T(8,128)(2,1)}, u32[]{:S(2)}) copy-start(bf16[8,64,384]{2,1,0:T(8,128)(2,1)} %param.9) | copy-start | bytes 1179652
  15.7 11.1 %copy-start.5 = (bf16[384,8]{0,1:T(8,128)(2,1)S(1)}, bf16[384,8]{0,1:T(8,128)(2,1)}, u32[]{:S(2)}) copy-start(bf16[384,8]{0,1:T(8,128)(2,1)} %param.6) | copy-start | bytes 18436
  17.6 9.1 %all-to-all-start.1 = ((bf16[8,16,384]{2,1,0:T(8,128)(2,1)}), bf16[8,16,384]{2,1,0:T(8,128)(2,1)S(1)}, u32[]{:S(2)}, u32[]{:S(2)}) async-start(bf16[8,16,384]{2,1,0:T(8,128)(2,1)} %expert.1), calls=%async_computation.1 | async-start | bytes 196608 | tf_op jit(solution)/shard_map/all_to_all | solution.py:77
  22.0 11.4 %collective-permute-start.2 = (bf16[8,16,384]{2,1,0:T(8,128)(2,1)S(1)}, bf16[8,16,384]{2,1,0:T(8,128)(2,1)S(1)}, u32[]{:S(2)}, u32[]{:S(2)}) collective-permute-start(bf16[8,16,384]{2,1,0:T(8,128)(2,1)S(1)} %all-to-all-done.recv_ref.refs_0_), channel_id=1, source_target_pairs={{0,3},{1,2},{2,1},{3,0},{4,7},{5,6},{6,5},{7,4},{8,11},{9,10},{10,... | collective-permute-start | bytes 294920 | tf_op jit(solution)/shard_map/ppermute | solution.py:291
  22.0 11.4 %collective-permute-start.1 = (bf16[8,16,384]{2,1,0:T(8,128)(2,1)S(1)}, bf16[8,16,384]{2,1,0:T(8,128)(2,1)S(1)}, u32[]{:S(2)}, u32[]{:S(2)}) collective-permute-start(bf16[8,16,384]{2,1,0:T(8,128)(2,1)S(1)} %all-to-all-done.recv_ref.refs_0_), channel_id=1, source_target_pairs={{0,2},{1,3},{2,0},{3,1},{4,6},{5,7},{6,4},{7,5},{8,10},{9,11},{10,... | collective-permute-start | bytes 294920 | tf_op jit(solution)/shard_map/ppermute | solution.py:291
  23.5 9.9 %collective-permute-start = (bf16[8,16,384]{2,1,0:T(8,128)(2,1)S(1)}, bf16[8,16,384]{2,1,0:T(8,128)(2,1)}, u32[]{:S(2)}, u32[]{:S(2)}) collective-permute-start(bf16[8,16,384]{2,1,0:T(8,128)(2,1)S(1)} %all-to-all-done.recv_ref.refs_0_), channel_id=1, source_target_pairs={{0,1},{1,0},{2,3},{3,2},{4,5},{5,4},{6,7},{7,6},{8,9},{9,8},{10,11... | collective-permute-start | bytes 294920 | tf_op jit(solution)/shard_map/ppermute | solution.py:291
  27.5 0.6 %copy-start.4 = (bf16[32,8,96]{2,1,0:T(8,128)(2,1)}, bf16[32,8,96]{2,1,0:T(8,128)(2,1)S(1)}, u32[]{:S(2)}) copy-start(bf16[32,8,96]{2,1,0:T(8,128)(2,1)S(1)} %get-tuple-element.23) | copy-start | bytes 147460
  28.2 10.9 %all-to-all-start.2 = ((bf16[32,8,96]{2,1,0:T(8,128)(2,1)}), bf16[32,8,96]{2,1,0:T(8,128)(2,1)S(1)}, u32[]{:S(2)}, u32[]{:S(2)}) async-start(bf16[32,8,96]{2,1,0:T(8,128)(2,1)} %copy-done.4), calls=%async_computation.2 | async-start | bytes 131072 | tf_op jit(solution)/shard_map/all_to_all | solution.py:77

commit v16 on v14

--- a/solution.py
+++ b/solution.py
@@ -87,7 +87,7 @@
     combine = combine / jnp.sum(combine, axis=0, keepdims=True)
     block = jnp.where(mask, spread_rows(logits, images), -jnp.inf)
     block = jnp.exp(block - jnp.max(block, axis=1, keepdims=True))
-    block = block / jnp.sum(block, axis=1, keepdims=True)
+    block = block * (1.0 / jnp.sum(block, axis=1, keepdims=True))
     return block, combine, mask
 
 
@@ -145,7 +145,7 @@
     tokens = tokens_ref[...]
     dispatch, combine, mask = softmaxes(router_ref[...], tokens, images)
     slot_out, slot_in_grad = split_rows(in_expert_order(back_ref))
-    disp = jnp.where(mask, dot(slot_in_grad, tokens, 1, 1), 0.0)
+    disp = dot(slot_in_grad, tokens, 1, 1)
     comb = fold_rows(jnp.where(mask, dot(slot_out, grad_ref[...], 1, 1), 0.0), images)
     mean = jnp.sum(dispatch * disp, axis=1, keepdims=True)
     from_dispatch = fold_rows(dispatch * (disp - mean), images)
@@ -275,7 +275,7 @@
     )(w_in2, w_out2)
     recv = exchange(sent, "expert", experts_order)
     back = pl.pallas_call(
-        functools.partial(expert_kernel, step=512),
+        functools.partial(expert_kernel, step=hidden),
         out_shape=struct(recv.shape, BF16),
         compiler_params=params,
         name="expert",

time: 40.2 us -> 40.2 us (level)
  no operation moved by 1% of the time
where the time goes in v16:
time: 40.2 us; the launch traced here: 39.7 us
  starting transfers between devices  17.7 us (44%)
  Pallas kernels  11 us (27%)
  waiting for transfers between devices  6.48 us (16%)
  local copies, waits for them, and re-layouts  3.18 us (8%)
  between operations  0.69 us (2%)
  other arithmetic  0.63 us (2%)
    all_to_all x3, starting transfers between devices, exchange(): lax.all_to_all(chunks, axis, split_axis=0, concat_axis=0, tiled=True, axi...  15.9 us
    all_to_all x3, waiting for transfers between devices, exchange(): lax.all_to_all(chunks, axis, split_axis=0, concat_axis=0, tiled=True, axi...  6.48 us
    pallas_call x1, Pallas kernels, on_device(): pl.pallas_call(functools.partial(weights_kernel, shares), in_specs=[in_sm...  3.8 us
    unnamed x12, local copies, waits for them, and re-layouts  3.18 us
    pallas_call x1, Pallas kernels, on_device(): pl.pallas_call(functools.partial(slots_kernel, images), in_specs=[in_plac...  2.44 us
    pallas_call x1, Pallas kernels, on_device(): pl.pallas_call(functools.partial(expert_kernel, step=hidden), out_shape=s...  1.92 us
    ppermute x3, starting transfers between devices, on_device(): lax.ppermute(recv, 'dp', [(i, i ^ k) for i in range(shares)])  1.86 us
    pallas_call x1, Pallas kernels, on_device(): pl.pallas_call(functools.partial(tokens_kernel, images), out_shape=struct...  1.55 us
  transfers between devices with their start and end apart: 6, of which 3 were waited for; matrix products, arithmetic and copies ran while one was open for 0% of the time, Pallas kernels for 17%

profile of v16, /device:TPU:0, one launch (start us, length us, event | category | flops | bytes accessed | tf_op | source)
XLA Modules:
  0.0 39.7 jit_solution(10189040123636605532)
XLA Ops:
  0.6 2.4 %slots.1 = bf16[8,16,384]{2,1,0:T(8,128)(2,1)} custom-call(bf16[512,384]{1,0:T(8,128)(2,1)} %bitcast.10, bf16[8,384]{1,0:T(8,128)(2,1)} %bitcast.17, bf16[512,384]{1,0:T(8,128)(2,1)} %bitcast.13), custom_call_target="tpu_custom_call" | custom-call | tf_op jit(solution)/shard_map/slots/pallas_call | solution.py:251
  3.1 7.8 %all-to-all-start = ((bf16[8,16,384]{2,1,0:T(8,128)(2,1)}), bf16[8,16,384]{2,1,0:T(8,128)(2,1)S(1)}, u32[]{:S(2)}, u32[]{:S(2)}) async-start(bf16[8,16,384]{2,1,0:T(8,128)(2,1)} %slots.1), calls=%async_computation | async-start | bytes 196608 | tf_op jit(solution)/shard_map/all_to_all | solution.py:77
  10.9 0.0 copy-start.2
  10.9 1.3 %copy-done.2 = bf16[1,384,1536]{2,1,0:T(8,128)(2,1)S(1)} copy-done((bf16[1,384,1536]{2,1,0:T(8,128)(2,1)S(1)}, bf16[1,384,1536]{2,1,0:T(8,128)(2,1)}, u32[]{:S(2)}) %copy-start.2) | copy-done | bytes 1179672
  12.2 0.0 copy-start.3
  12.2 1.3 %copy-done.3 = bf16[1,384,1536]{2,1,0:T(8,128)(2,1)S(1)} copy-done((bf16[1,384,1536]{2,1,0:T(8,128)(2,1)S(1)}, bf16[1,384,1536]{2,1,0:T(8,128)(2,1)}, u32[]{:S(2)}) %copy-start.3) | copy-done | bytes 1179672
  13.4 0.5 %stage.1 = (bf16[384,1536]{1,0:T(8,128)(2,1)S(1)}, bf16[384,1536]{1,0:T(8,128)(2,1)S(1)}) custom-call(bf16[384,1536]{1,0:T(8,128)(2,1)S(1)} %bitcast.15, bf16[384,1536]{1,0:T(8,128)(2,1)S(1)} %bitcast.16), custom_call_target="tpu_custom_call" | custom-call | bytes 4718592 | tf_op jit(solution)/shard_map/stage/pallas_call | solution.py:264
  14.0 1.7 %all-to-all-done.recv_ref.refs_0_ = bf16[8,16,384]{2,1,0:T(8,128)(2,1)S(1)} async-done(((bf16[8,16,384]{2,1,0:T(8,128)(2,1)}), bf16[8,16,384]{2,1,0:T(8,128)(2,1)S(1)}, u32[]{:S(2)}, u32[]{:S(2)}) %all-to-all-start) | async-done | bytes 98336 | tf_op jit(solution)/shard_map/all_to_all | solution.py:77
  15.7 0.0 copy-start
  15.7 0.0 copy-start.1
  15.7 0.0 copy-start.5
  15.7 1.9 %expert.1 = bf16[8,16,384]{2,1,0:T(8,128)(2,1)} custom-call(bf16[8,16,384]{2,1,0:T(8,128)(2,1)S(1)} %all-to-all-done.recv_ref.refs_0_, bf16[384,1536]{1,0:T(8,128)(2,1)S(1)} %get-tuple-element.14.win_ref.refs_4_, bf16[384,1536]{1,0:T(8,128)(2,1)S(1)} %get-tuple-element.15.wout_ref.refs_5_), custom_call_target="tpu_custom_call" | custom-call | tf_op jit(solution)/shard_map/expert/pallas_call | solution.py:277
  17.6 4.4 %all-to-all-start.1 = ((bf16[8,16,384]{2,1,0:T(8,128)(2,1)}), bf16[8,16,384]{2,1,0:T(8,128)(2,1)S(1)}, u32[]{:S(2)}, u32[]{:S(2)}) async-start(bf16[8,16,384]{2,1,0:T(8,128)(2,1)} %expert.1), calls=%async_computation.1 | async-start | bytes 196608 | tf_op jit(solution)/shard_map/all_to_all | solution.py:77
  22.0 0.0 collective-permute-start.2
  22.0 1.5 %collective-permute-start.1 = (bf16[8,16,384]{2,1,0:T(8,128)(2,1)S(1)}, bf16[8,16,384]{2,1,0:T(8,128)(2,1)S(1)}, u32[]{:S(2)}, u32[]{:S(2)}) collective-permute-start(bf16[8,16,384]{2,1,0:T(8,128)(2,1)S(1)} %all-to-all-done.recv_ref.refs_0_), channel_id=1, source_target_pairs={{0,2},{1,3},{2,0},{3,1},{4,6},{5,7},{6,4},{7,5},{8,10},{9,11},{10,... | collective-permute-start | bytes 294920 | tf_op jit(solution)/shard_map/ppermute | solution.py:288
  23.5 0.3 collective-permute-start
  23.8 2.9 %all-to-all-done.1.back_ref = bf16[8,16,384]{2,1,0:T(8,128)(2,1)S(1)} async-done(((bf16[8,16,384]{2,1,0:T(8,128)(2,1)}), bf16[8,16,384]{2,1,0:T(8,128)(2,1)S(1)}, u32[]{:S(2)}, u32[]{:S(2)}) %all-to-all-start.1) | async-done | bytes 98336 | tf_op jit(solution)/shard_map/all_to_all | solution.py:77
  26.7 0.0 copy-done
  26.7 0.0 copy-done.1
  26.7 0.0 copy-done.5
  26.7 0.8 %logits.1 = (bf16[32,8,96]{2,1,0:T(8,128)(2,1)S(1)}, bf16[8,512]{1,0:T(8,128)(2,1)S(1)}) custom-call(bf16[8,16,384]{2,1,0:T(8,128)(2,1)S(1)} %all-to-all-done.1.back_ref, bf16[512,384]{1,0:T(8,128)(2,1)S(1)} %bitcast.11, bf16[8,384]{1,0:T(8,128)(2,1)S(1)} %bitcast.18, bf16[512,384]{1,0:T(8,128)(2,1)S(1)} %bitcast.14), custom_call_target="tpu_custom_call" | custom-call | tf_op jit(solution)/shard_map/logits/pallas_call | solution.py:295
  27.5 0.0 copy-start.4
  27.5 0.6 %copy-done.4 = bf16[32,8,96]{2,1,0:T(8,128)(2,1)} copy-done((bf16[32,8,96]{2,1,0:T(8,128)(2,1)}, bf16[32,8,96]{2,1,0:T(8,128)(2,1)S(1)}, u32[]{:S(2)}) %copy-start.4) | copy-done | bytes 49176
  28.2 3.7 %all-to-all-start.2 = ((bf16[32,8,96]{2,1,0:T(8,128)(2,1)}), bf16[32,8,96]{2,1,0:T(8,128)(2,1)S(1)}, u32[]{:S(2)}, u32[]{:S(2)}) async-start(bf16[32,8,96]{2,1,0:T(8,128)(2,1)} %copy-done.4), calls=%async_computation.2 | async-start | bytes 131072 | tf_op jit(solution)/shard_map/all_to_all | solution.py:77
  31.8 1.6 %tokens.1 = bf16[512,384]{1,0:T(8,128)(2,1)} custom-call(bf16[8,16,384]{2,1,0:T(8,128)(2,1)S(1)} %all-to-all-done.1.back_ref, bf16[512,384]{1,0:T(8,128)(2,1)S(1)} %bitcast.12, bf16[8,384]{1,0:T(8,128)(2,1)S(1)} %bitcast.19, bf16[8,512]{1,0:T(8,128)(2,1)S(1)} %get-tuple-element.17.logit_ref), custom_call_target="tpu_custom_call" | custom-call | tf_op jit(solution)/shard_map/tokens/pallas_call | solution.py:311
  33.4 0.0 collective-permute-done.2.refs_3_
  33.4 0.0 collective-permute-done.1.refs_2_
  33.4 0.0 collective-permute-done.refs_1_
  33.4 3.8 %weights.1 = (f32[96,1536]{1,0:T(8,128)}, f32[96,1536]{1,0:T(8,128)}) custom-call(s32[1]{0:T(128)} %bitcast.6.share_ref, bf16[8,16,384]{2,1,0:T(8,128)(2,1)S(1)} %all-to-all-done.recv_ref.refs_0_, bf16[8,16,384]{2,1,0:T(8,128)(2,1)} %collective-permute-done.refs_1_, bf16[8,16,384]{2,1,0:T(8,128)(2,1)S(1)} %collective-permute-done.1.refs_2_, ...), custom_call_target="tpu_custom_call" | custom-call | tf_op jit(solution)/shard_map/weights/pallas_call | solution.py:321
  37.2 1.9 %all-to-all-done.2 = bf16[32,8,96]{2,1,0:T(8,128)(2,1)S(1)} async-done(((bf16[32,8,96]{2,1,0:T(8,128)(2,1)}), bf16[32,8,96]{2,1,0:T(8,128)(2,1)S(1)}, u32[]{:S(2)}, u32[]{:S(2)}) %all-to-all-start.2) | async-done | bytes 49184 | tf_op jit(solution)/shard_map/all_to_all | solution.py:77
  39.1 0.6 %convert_reduce_fusion = f32[8,96]{1,0:T(8,128)} fusion(bf16[32,8,96]{2,1,0:T(8,128)(2,1)S(1)} %all-to-all-done.2), kind=kLoop, calls=%fused_computation | loop fusion | flops 48384 | bytes 52224 | tf_op jit(solution)/shard_map/reduce_sum | solution.py:351
Async XLA Ops:
  3.1 12.6 %all-to-all-start = ((bf16[8,16,384]{2,1,0:T(8,128)(2,1)}), bf16[8,16,384]{2,1,0:T(8,128)(2,1)S(1)}, u32[]{:S(2)}, u32[]{:S(2)}) async-start(bf16[8,16,384]{2,1,0:T(8,128)(2,1)} %slots.1), calls=%async_computation | async-start | bytes 196608 | tf_op jit(solution)/shard_map/all_to_all | solution.py:77
  10.9 1.3 %copy-start.2 = (bf16[1,384,1536]{2,1,0:T(8,128)(2,1)S(1)}, bf16[1,384,1536]{2,1,0:T(8,128)(2,1)}, u32[]{:S(2)}) copy-start(bf16[1,384,1536]{2,1,0:T(8,128)(2,1)} %param.7) | copy-start | bytes 3538948
  12.2 1.3 %copy-start.3 = (bf16[1,384,1536]{2,1,0:T(8,128)(2,1)S(1)}, bf16[1,384,1536]{2,1,0:T(8,128)(2,1)}, u32[]{:S(2)}) copy-start(bf16[1,384,1536]{2,1,0:T(8,128)(2,1)} %param.8) | copy-start | bytes 3538948
  15.7 11.1 %copy-start = (bf16[8,64,384]{2,1,0:T(8,128)(2,1)S(1)}, bf16[8,64,384]{2,1,0:T(8,128)(2,1)}, u32[]{:S(2)}) copy-start(bf16[8,64,384]{2,1,0:T(8,128)(2,1)} %param.5) | copy-start | bytes 1179652
  15.7 11.1 %copy-start.1 = (bf16[8,64,384]{2,1,0:T(8,128)(2,1)S(1)}, bf16[8,64,384]{2,1,0:T(8,128)(2,1)}, u32[]{:S(2)}) copy-start(bf16[8,64,384]{2,1,0:T(8,128)(2,1)} %param.9) | copy-start | bytes 1179652
  15.7 11.1 %copy-start.5 = (bf16[384,8]{0,1:T(8,128)(2,1)S(1)}, bf16[384,8]{0,1:T(8,128)(2,1)}, u32[]{:S(2)}) copy-start(bf16[384,8]{0,1:T(8,128)(2,1)} %param.6) | copy-start | bytes 18436
  17.6 9.1 %all-to-all-start.1 = ((bf16[8,16,384]{2,1,0:T(8,128)(2,1)}), bf16[8,16,384]{2,1,0:T(8,128)(2,1)S(1)}, u32[]{:S(2)}, u32[]{:S(2)}) async-start(bf16[8,16,384]{2,1,0:T(8,128)(2,1)} %expert.1), calls=%async_computation.1 | async-start | bytes 196608 | tf_op jit(solution)/shard_map/all_to_all | solution.py:77
  22.0 11.4 %collective-permute-start.2 = (bf16[8,16,384]{2,1,0:T(8,128)(2,1)S(1)}, bf16[8,16,384]{2,1,0:T(8,128)(2,1)S(1)}, u32[]{:S(2)}, u32[]{:S(2)}) collective-permute-start(bf16[8,16,384]{2,1,0:T(8,128)(2,1)S(1)} %all-to-all-done.recv_ref.refs_0_), channel_id=1, source_target_pairs={{0,3},{1,2},{2,1},{3,0},{4,7},{5,6},{6,5},{7,4},{8,11},{9,10},{10,... | collective-permute-start | bytes 294920 | tf_op jit(solution)/shard_map/ppermute | solution.py:288
  22.0 11.4 %collective-permute-start.1 = (bf16[8,16,384]{2,1,0:T(8,128)(2,1)S(1)}, bf16[8,16,384]{2,1,0:T(8,128)(2,1)S(1)}, u32[]{:S(2)}, u32[]{:S(2)}) collective-permute-start(bf16[8,16,384]{2,1,0:T(8,128)(2,1)S(1)} %all-to-all-done.recv_ref.refs_0_), channel_id=1, source_target_pairs={{0,2},{1,3},{2,0},{3,1},{4,6},{5,7},{6,4},{7,5},{8,10},{9,11},{10,... | collective-permute-start | bytes 294920 | tf_op jit(solution)/shard_map/ppermute | solution.py:288
  23.5 9.9 %collective-permute-start = (bf16[8,16,384]{2,1,0:T(8,128)(2,1)S(1)}, bf16[8,16,384]{2,1,0:T(8,128)(2,1)}, u32[]{:S(2)}, u32[]{:S(2)}) collective-permute-start(bf16[8,16,384]{2,1,0:T(8,128)(2,1)S(1)} %all-to-all-done.recv_ref.refs_0_), channel_id=1, source_target_pairs={{0,1},{1,0},{2,3},{3,2},{4,5},{5,4},{6,7},{7,6},{8,9},{9,8},{10,11... | collective-permute-start | bytes 294920 | tf_op jit(solution)/shard_map/ppermute | solution.py:288
  27.5 0.6 %copy-start.4 = (bf16[32,8,96]{2,1,0:T(8,128)(2,1)}, bf16[32,8,96]{2,1,0:T(8,128)(2,1)S(1)}, u32[]{:S(2)}) copy-start(bf16[32,8,96]{2,1,0:T(8,128)(2,1)S(1)} %get-tuple-element.23) | copy-start | bytes 147460
  28.2 10.9 %all-to-all-start.2 = ((bf16[32,8,96]{2,1,0:T(8,128)(2,1)}), bf16[32,8,96]{2,1,0:T(8,128)(2,1)S(1)}, u32[]{:S(2)}, u32[]{:S(2)}) async-start(bf16[32,8,96]{2,1,0:T(8,128)(2,1)} %copy-done.4), calls=%async_computation.2 | async-start | bytes 131072 | tf_op jit(solution)/shard_map/all_to_all | solution.py:77

commit v17 on v16

--- a/solution.py
+++ b/solution.py
@@ -91,23 +91,11 @@
     return block, combine, mask
 
 
-def slots_kernel(images, tokens_hbm, router_hbm, grad_hbm, sent_ref, *scratch):
-    tokens_ref, router_ref, grad_ref, sems = scratch
-    first = [
-        pltpu.make_async_copy(tokens_hbm, tokens_ref, sems.at[0]),
-        pltpu.make_async_copy(router_hbm, router_ref, sems.at[1]),
-    ]
-    second = [pltpu.make_async_copy(grad_hbm, grad_ref, sems.at[2])]
-    for load in first + second:
-        load.start()
-    for load in first:
-        load.wait()
+def slots_kernel(images, tokens_ref, router_ref, grad_ref, sent_ref):
     tokens = tokens_ref[...]
     block, combine, mask = softmaxes(router_ref[...], tokens, images)
     combine_block = jnp.where(mask, spread_rows(combine, images), 0.0)
     slot_in = dot(block.astype(BF16), tokens, 1, 0)
-    for load in second:
-        load.wait()
     slot_grad = dot(combine_block.astype(BF16), grad_ref[...], 1, 0)
     pairs = pair_rows(slot_in, slot_grad, combine.shape[0])
     for k, i in enumerate(centre_out(pairs.shape[0])):
@@ -248,16 +236,11 @@
         return jax.ShapeDtypeStruct(shape, dtype)
 
     in_place = pl.BlockSpec(memory_space=pl.ANY)
+    in_vmem = pl.BlockSpec(memory_space=pltpu.VMEM)
     sent = pl.pallas_call(
         functools.partial(slots_kernel, images),
-        in_specs=[in_place] * 3,
+        in_specs=[in_vmem] * 3,
         out_shape=struct((experts, 2 * images, width), BF16),
-        scratch_shapes=[
-            pltpu.VMEM((columns, width), BF16),
-            pltpu.VMEM((experts, width), BF16),
-            pltpu.VMEM((columns, width), BF16),
-            pltpu.SemaphoreType.DMA((3,)),
-        ],
         compiler_params=whole,
         name="slots",
     )(tokens2, router_rows, grad2)
@@ -291,7 +274,6 @@
     else:
         spread = [lax.all_gather(recv, "dp", axis=0, tiled=False)]
 
-    in_vmem = pl.BlockSpec(memory_space=pltpu.VMEM)
     router_send, logit_grad = pl.pallas_call(
         functools.partial(logits_kernel, images, share_order),
         in_specs=[in_vmem] * 4,

time: 40.2 us -> 40.1 us (level)
  no operation moved by 1% of the time
where the time goes in v17:
time: 40.1 us; the launch traced here: 39.6 us
  starting transfers between devices  17.7 us (44%)
  Pallas kernels  10.9 us (27%)
  waiting for transfers between devices  6.48 us (16%)
  local copies, waits for them, and re-layouts  3.18 us (8%)
  between operations  0.68 us (2%)
  other arithmetic  0.63 us (2%)
    all_to_all x3, starting transfers between devices, exchange(): lax.all_to_all(chunks, axis, split_axis=0, concat_axis=0, tiled=True, axi...  15.9 us
    all_to_all x3, waiting for transfers between devices, exchange(): lax.all_to_all(chunks, axis, split_axis=0, concat_axis=0, tiled=True, axi...  6.48 us
    pallas_call x1, Pallas kernels, on_device(): pl.pallas_call(functools.partial(weights_kernel, shares), in_specs=[in_sm...  3.8 us
    unnamed x12, local copies, waits for them, and re-layouts  3.18 us
    pallas_call x1, Pallas kernels, on_device(): pl.pallas_call(functools.partial(slots_kernel, images), in_specs=[in_vmem...  2.4 us
    pallas_call x1, Pallas kernels, on_device(): pl.pallas_call(functools.partial(expert_kernel, step=hidden), out_shape=s...  1.92 us
    ppermute x3, starting transfers between devices, on_device(): lax.ppermute(recv, 'dp', [(i, i ^ k) for i in range(shares)])  1.86 us
    pallas_call x1, Pallas kernels, on_device(): pl.pallas_call(functools.partial(tokens_kernel, images), out_shape=struct...  1.55 us
  transfers between devices with their start and end apart: 6, of which 3 were waited for; matrix products, arithmetic and copies ran while one was open for 0% of the time, Pallas kernels for 17%

profile of v17, /device:TPU:0, one launch (start us, length us, event | category | flops | bytes accessed | tf_op | source)
XLA Modules:
  0.0 39.6 jit_solution(5959463650989276839)
XLA Ops:
  0.6 2.4 %slots.1 = bf16[8,16,384]{2,1,0:T(8,128)(2,1)} custom-call(bf16[512,384]{1,0:T(8,128)(2,1)} %bitcast.10, bf16[8,384]{1,0:T(8,128)(2,1)} %bitcast.17, bf16[512,384]{1,0:T(8,128)(2,1)} %bitcast.13), custom_call_target="tpu_custom_call" | custom-call | tf_op jit(solution)/shard_map/slots/pallas_call | solution.py:240
  3.0 7.8 %all-to-all-start = ((bf16[8,16,384]{2,1,0:T(8,128)(2,1)}), bf16[8,16,384]{2,1,0:T(8,128)(2,1)S(1)}, u32[]{:S(2)}, u32[]{:S(2)}) async-start(bf16[8,16,384]{2,1,0:T(8,128)(2,1)} %slots.1), calls=%async_computation | async-start | bytes 196608 | tf_op jit(solution)/shard_map/all_to_all | solution.py:77
  10.8 0.0 copy-start.2
  10.8 1.3 %copy-done.2 = bf16[1,384,1536]{2,1,0:T(8,128)(2,1)S(1)} copy-done((bf16[1,384,1536]{2,1,0:T(8,128)(2,1)S(1)}, bf16[1,384,1536]{2,1,0:T(8,128)(2,1)}, u32[]{:S(2)}) %copy-start.2) | copy-done | bytes 1179672
  12.1 0.0 copy-start.3
  12.1 1.3 %copy-done.3 = bf16[1,384,1536]{2,1,0:T(8,128)(2,1)S(1)} copy-done((bf16[1,384,1536]{2,1,0:T(8,128)(2,1)S(1)}, bf16[1,384,1536]{2,1,0:T(8,128)(2,1)}, u32[]{:S(2)}) %copy-start.3) | copy-done | bytes 1179672
  13.4 0.5 %stage.1 = (bf16[384,1536]{1,0:T(8,128)(2,1)S(1)}, bf16[384,1536]{1,0:T(8,128)(2,1)S(1)}) custom-call(bf16[384,1536]{1,0:T(8,128)(2,1)S(1)} %bitcast.15, bf16[384,1536]{1,0:T(8,128)(2,1)S(1)} %bitcast.16), custom_call_target="tpu_custom_call" | custom-call | bytes 4718592 | tf_op jit(solution)/shard_map/stage/pallas_call | solution.py:247
  13.9 1.7 %all-to-all-done.recv_ref.refs_0_ = bf16[8,16,384]{2,1,0:T(8,128)(2,1)S(1)} async-done(((bf16[8,16,384]{2,1,0:T(8,128)(2,1)}), bf16[8,16,384]{2,1,0:T(8,128)(2,1)S(1)}, u32[]{:S(2)}, u32[]{:S(2)}) %all-to-all-start) | async-done | bytes 98336 | tf_op jit(solution)/shard_map/all_to_all | solution.py:77
  15.6 0.0 copy-start
  15.6 0.0 copy-start.1
  15.6 0.0 copy-start.5
  15.6 1.9 %expert.1 = bf16[8,16,384]{2,1,0:T(8,128)(2,1)} custom-call(bf16[8,16,384]{2,1,0:T(8,128)(2,1)S(1)} %all-to-all-done.recv_ref.refs_0_, bf16[384,1536]{1,0:T(8,128)(2,1)S(1)} %get-tuple-element.14.win_ref.refs_4_, bf16[384,1536]{1,0:T(8,128)(2,1)S(1)} %get-tuple-element.15.wout_ref.refs_5_), custom_call_target="tpu_custom_call" | custom-call | tf_op jit(solution)/shard_map/expert/pallas_call | solution.py:260
  17.5 4.4 %all-to-all-start.1 = ((bf16[8,16,384]{2,1,0:T(8,128)(2,1)}), bf16[8,16,384]{2,1,0:T(8,128)(2,1)S(1)}, u32[]{:S(2)}, u32[]{:S(2)}) async-start(bf16[8,16,384]{2,1,0:T(8,128)(2,1)} %expert.1), calls=%async_computation.1 | async-start | bytes 196608 | tf_op jit(solution)/shard_map/all_to_all | solution.py:77
  21.9 0.0 collective-permute-start.2
  21.9 1.5 %collective-permute-start.1 = (bf16[8,16,384]{2,1,0:T(8,128)(2,1)S(1)}, bf16[8,16,384]{2,1,0:T(8,128)(2,1)S(1)}, u32[]{:S(2)}, u32[]{:S(2)}) collective-permute-start(bf16[8,16,384]{2,1,0:T(8,128)(2,1)S(1)} %all-to-all-done.recv_ref.refs_0_), channel_id=1, source_target_pairs={{0,2},{1,3},{2,0},{3,1},{4,6},{5,7},{6,4},{7,5},{8,10},{9,11},{10,... | collective-permute-start | bytes 294920 | tf_op jit(solution)/shard_map/ppermute | solution.py:271
  23.5 0.3 collective-permute-start
  23.8 2.9 %all-to-all-done.1.back_ref = bf16[8,16,384]{2,1,0:T(8,128)(2,1)S(1)} async-done(((bf16[8,16,384]{2,1,0:T(8,128)(2,1)}), bf16[8,16,384]{2,1,0:T(8,128)(2,1)S(1)}, u32[]{:S(2)}, u32[]{:S(2)}) %all-to-all-start.1) | async-done | bytes 98336 | tf_op jit(solution)/shard_map/all_to_all | solution.py:77
  26.7 0.0 copy-done
  26.7 0.0 copy-done.1
  26.7 0.0 copy-done.5
  26.7 0.8 %logits.1 = (bf16[32,8,96]{2,1,0:T(8,128)(2,1)S(1)}, bf16[8,512]{1,0:T(8,128)(2,1)S(1)}) custom-call(bf16[8,16,384]{2,1,0:T(8,128)(2,1)S(1)} %all-to-all-done.1.back_ref, bf16[512,384]{1,0:T(8,128)(2,1)S(1)} %bitcast.11, bf16[8,384]{1,0:T(8,128)(2,1)S(1)} %bitcast.18, bf16[512,384]{1,0:T(8,128)(2,1)S(1)} %bitcast.14), custom_call_target="tpu_custom_call" | custom-call | tf_op jit(solution)/shard_map/logits/pallas_call | solution.py:277
  27.4 0.0 copy-start.4
  27.5 0.6 %copy-done.4 = bf16[32,8,96]{2,1,0:T(8,128)(2,1)} copy-done((bf16[32,8,96]{2,1,0:T(8,128)(2,1)}, bf16[32,8,96]{2,1,0:T(8,128)(2,1)S(1)}, u32[]{:S(2)}) %copy-start.4) | copy-done | bytes 49176
  28.1 3.7 %all-to-all-start.2 = ((bf16[32,8,96]{2,1,0:T(8,128)(2,1)}), bf16[32,8,96]{2,1,0:T(8,128)(2,1)S(1)}, u32[]{:S(2)}, u32[]{:S(2)}) async-start(bf16[32,8,96]{2,1,0:T(8,128)(2,1)} %copy-done.4), calls=%async_computation.2 | async-start | bytes 131072 | tf_op jit(solution)/shard_map/all_to_all | solution.py:77
  31.8 1.6 %tokens.1 = bf16[512,384]{1,0:T(8,128)(2,1)} custom-call(bf16[8,16,384]{2,1,0:T(8,128)(2,1)S(1)} %all-to-all-done.1.back_ref, bf16[512,384]{1,0:T(8,128)(2,1)S(1)} %bitcast.12, bf16[8,384]{1,0:T(8,128)(2,1)S(1)} %bitcast.19, bf16[8,512]{1,0:T(8,128)(2,1)S(1)} %get-tuple-element.17.logit_ref), custom_call_target="tpu_custom_call" | custom-call | tf_op jit(solution)/shard_map/tokens/pallas_call | solution.py:293
  33.3 0.0 collective-permute-done.2.refs_3_
  33.3 0.0 collective-permute-done.1.refs_2_
  33.3 0.0 collective-permute-done.refs_1_
  33.3 3.8 %weights.1 = (f32[96,1536]{1,0:T(8,128)}, f32[96,1536]{1,0:T(8,128)}) custom-call(s32[1]{0:T(128)} %bitcast.6.share_ref, bf16[8,16,384]{2,1,0:T(8,128)(2,1)S(1)} %all-to-all-done.recv_ref.refs_0_, bf16[8,16,384]{2,1,0:T(8,128)(2,1)} %collective-permute-done.refs_1_, bf16[8,16,384]{2,1,0:T(8,128)(2,1)S(1)} %collective-permute-done.1.refs_2_, ...), custom_call_target="tpu_custom_call" | custom-call | tf_op jit(solution)/shard_map/weights/pallas_call | solution.py:303
  37.1 1.9 %all-to-all-done.2 = bf16[32,8,96]{2,1,0:T(8,128)(2,1)S(1)} async-done(((bf16[32,8,96]{2,1,0:T(8,128)(2,1)}), bf16[32,8,96]{2,1,0:T(8,128)(2,1)S(1)}, u32[]{:S(2)}, u32[]{:S(2)}) %all-to-all-start.2) | async-done | bytes 49184 | tf_op jit(solution)/shard_map/all_to_all | solution.py:77
  39.0 0.6 %convert_reduce_fusion = f32[8,96]{1,0:T(8,128)} fusion(bf16[32,8,96]{2,1,0:T(8,128)(2,1)S(1)} %all-to-all-done.2), kind=kLoop, calls=%fused_computation | loop fusion | flops 48384 | bytes 52224 | tf_op jit(solution)/shard_map/reduce_sum | solution.py:333
Async XLA Ops:
  3.0 12.6 %all-to-all-start = ((bf16[8,16,384]{2,1,0:T(8,128)(2,1)}), bf16[8,16,384]{2,1,0:T(8,128)(2,1)S(1)}, u32[]{:S(2)}, u32[]{:S(2)}) async-start(bf16[8,16,384]{2,1,0:T(8,128)(2,1)} %slots.1), calls=%async_computation | async-start | bytes 196608 | tf_op jit(solution)/shard_map/all_to_all | solution.py:77
  10.8 1.3 %copy-start.2 = (bf16[1,384,1536]{2,1,0:T(8,128)(2,1)S(1)}, bf16[1,384,1536]{2,1,0:T(8,128)(2,1)}, u32[]{:S(2)}) copy-start(bf16[1,384,1536]{2,1,0:T(8,128)(2,1)} %param.7) | copy-start | bytes 3538948
  12.1 1.3 %copy-start.3 = (bf16[1,384,1536]{2,1,0:T(8,128)(2,1)S(1)}, bf16[1,384,1536]{2,1,0:T(8,128)(2,1)}, u32[]{:S(2)}) copy-start(bf16[1,384,1536]{2,1,0:T(8,128)(2,1)} %param.8) | copy-start | bytes 3538948
  15.6 11.1 %copy-start = (bf16[8,64,384]{2,1,0:T(8,128)(2,1)S(1)}, bf16[8,64,384]{2,1,0:T(8,128)(2,1)}, u32[]{:S(2)}) copy-start(bf16[8,64,384]{2,1,0:T(8,128)(2,1)} %param.5) | copy-start | bytes 1179652
  15.6 11.1 %copy-start.1 = (bf16[8,64,384]{2,1,0:T(8,128)(2,1)S(1)}, bf16[8,64,384]{2,1,0:T(8,128)(2,1)}, u32[]{:S(2)}) copy-start(bf16[8,64,384]{2,1,0:T(8,128)(2,1)} %param.9) | copy-start | bytes 1179652
  15.6 11.1 %copy-start.5 = (bf16[384,8]{0,1:T(8,128)(2,1)S(1)}, bf16[384,8]{0,1:T(8,128)(2,1)}, u32[]{:S(2)}) copy-start(bf16[384,8]{0,1:T(8,128)(2,1)} %param.6) | copy-start | bytes 18436
  17.5 9.1 %all-to-all-start.1 = ((bf16[8,16,384]{2,1,0:T(8,128)(2,1)}), bf16[8,16,384]{2,1,0:T(8,128)(2,1)S(1)}, u32[]{:S(2)}, u32[]{:S(2)}) async-start(bf16[8,16,384]{2,1,0:T(8,128)(2,1)} %expert.1), calls=%async_computation.1 | async-start | bytes 196608 | tf_op jit(solution)/shard_map/all_to_all | solution.py:77
  21.9 11.4 %collective-permute-start.2 = (bf16[8,16,384]{2,1,0:T(8,128)(2,1)S(1)}, bf16[8,16,384]{2,1,0:T(8,128)(2,1)S(1)}, u32[]{:S(2)}, u32[]{:S(2)}) collective-permute-start(bf16[8,16,384]{2,1,0:T(8,128)(2,1)S(1)} %all-to-all-done.recv_ref.refs_0_), channel_id=1, source_target_pairs={{0,3},{1,2},{2,1},{3,0},{4,7},{5,6},{6,5},{7,4},{8,11},{9,10},{10,... | collective-permute-start | bytes 294920 | tf_op jit(solution)/shard_map/ppermute | solution.py:271
  21.9 11.4 %collective-permute-start.1 = (bf16[8,16,384]{2,1,0:T(8,128)(2,1)S(1)}, bf16[8,16,384]{2,1,0:T(8,128)(2,1)S(1)}, u32[]{:S(2)}, u32[]{:S(2)}) collective-permute-start(bf16[8,16,384]{2,1,0:T(8,128)(2,1)S(1)} %all-to-all-done.recv_ref.refs_0_), channel_id=1, source_target_pairs={{0,2},{1,3},{2,0},{3,1},{4,6},{5,7},{6,4},{7,5},{8,10},{9,11},{10,... | collective-permute-start | bytes 294920 | tf_op jit(solution)/shard_map/ppermute | solution.py:271
  23.5 9.9 %collective-permute-start = (bf16[8,16,384]{2,1,0:T(8,128)(2,1)S(1)}, bf16[8,16,384]{2,1,0:T(8,128)(2,1)}, u32[]{:S(2)}, u32[]{:S(2)}) collective-permute-start(bf16[8,16,384]{2,1,0:T(8,128)(2,1)S(1)} %all-to-all-done.recv_ref.refs_0_), channel_id=1, source_target_pairs={{0,1},{1,0},{2,3},{3,2},{4,5},{5,4},{6,7},{7,6},{8,9},{9,8},{10,11... | collective-permute-start | bytes 294920 | tf_op jit(solution)/shard_map/ppermute | solution.py:271
  27.4 0.6 %copy-start.4 = (bf16[32,8,96]{2,1,0:T(8,128)(2,1)}, bf16[32,8,96]{2,1,0:T(8,128)(2,1)S(1)}, u32[]{:S(2)}) copy-start(bf16[32,8,96]{2,1,0:T(8,128)(2,1)S(1)} %get-tuple-element.23) | copy-start | bytes 147460
  28.1 10.9 %all-to-all-start.2 = ((bf16[32,8,96]{2,1,0:T(8,128)(2,1)}), bf16[32,8,96]{2,1,0:T(8,128)(2,1)S(1)}, u32[]{:S(2)}, u32[]{:S(2)}) async-start(bf16[32,8,96]{2,1,0:T(8,128)(2,1)} %copy-done.4), calls=%async_computation.2 | async-start | bytes 131072 | tf_op jit(solution)/shard_map/all_to_all | solution.py:77

commit v18 on v17

--- a/solution.py
+++ b/solution.py
@@ -65,7 +65,7 @@
 
 
 def centre_out(count):
-    return sorted(range(count), key=lambda i: (abs(2 * i - count + 1), i))
+    return sorted(range(count), key=lambda i: (abs(2 * i - count + 1), -i))
 
 
 def in_expert_order(ref):

time: 40.1 us -> 40.5 us (level)
  no operation moved by 1% of the time
where the time goes in v18:
time: 40.5 us; the launch traced here: 40 us
  starting transfers between devices  17.7 us (44%)
  Pallas kernels  10.9 us (27%)
  waiting for transfers between devices  6.86 us (17%)
  local copies, waits for them, and re-layouts  3.18 us (8%)
  between operations  0.68 us (2%)
  other arithmetic  0.63 us (2%)
    all_to_all x3, starting transfers between devices, exchange(): lax.all_to_all(chunks, axis, split_axis=0, concat_axis=0, tiled=True, axi...  15.9 us
    all_to_all x3, waiting for transfers between devices, exchange(): lax.all_to_all(chunks, axis, split_axis=0, concat_axis=0, tiled=True, axi...  6.85 us
    pallas_call x1, Pallas kernels, on_device(): pl.pallas_call(functools.partial(weights_kernel, shares), in_specs=[in_sm...  3.8 us
    unnamed x12, local copies, waits for them, and re-layouts  3.18 us
    pallas_call x1, Pallas kernels, on_device(): pl.pallas_call(functools.partial(slots_kernel, images), in_specs=[in_vmem...  2.4 us
    pallas_call x1, Pallas kernels, on_device(): pl.pallas_call(functools.partial(expert_kernel, step=hidden), out_shape=s...  1.93 us
    ppermute x3, starting transfers between devices, on_device(): lax.ppermute(recv, 'dp', [(i, i ^ k) for i in range(shares)])  1.86 us
    pallas_call x1, Pallas kernels, on_device(): pl.pallas_call(functools.partial(tokens_kernel, images), out_shape=struct...  1.55 us
  transfers between devices with their start and end apart: 6, of which 3 were waited for; matrix products, arithmetic and copies ran while one was open for 0% of the time, Pallas kernels for 17%

profile of v18, /device:TPU:0, one launch (start us, length us, event | category | flops | bytes accessed | tf_op | source)
XLA Modules:
  0.0 40.0 jit_solution(8476327368230436506)
XLA Ops:
  0.6 2.4 %slots.1 = bf16[8,16,384]{2,1,0:T(8,128)(2,1)} custom-call(bf16[512,384]{1,0:T(8,128)(2,1)} %bitcast.10, bf16[8,384]{1,0:T(8,128)(2,1)} %bitcast.17, bf16[512,384]{1,0:T(8,128)(2,1)} %bitcast.13), custom_call_target="tpu_custom_call" | custom-call | tf_op jit(solution)/shard_map/slots/pallas_call | solution.py:240
  3.0 7.8 %all-to-all-start = ((bf16[8,16,384]{2,1,0:T(8,128)(2,1)}), bf16[8,16,384]{2,1,0:T(8,128)(2,1)S(1)}, u32[]{:S(2)}, u32[]{:S(2)}) async-start(bf16[8,16,384]{2,1,0:T(8,128)(2,1)} %slots.1), calls=%async_computation | async-start | bytes 196608 | tf_op jit(solution)/shard_map/all_to_all | solution.py:77
  10.8 0.0 copy-start.2
  10.8 1.3 %copy-done.2 = bf16[1,384,1536]{2,1,0:T(8,128)(2,1)S(1)} copy-done((bf16[1,384,1536]{2,1,0:T(8,128)(2,1)S(1)}, bf16[1,384,1536]{2,1,0:T(8,128)(2,1)}, u32[]{:S(2)}) %copy-start.2) | copy-done | bytes 1179672
  12.1 0.0 copy-start.3
  12.1 1.3 %copy-done.3 = bf16[1,384,1536]{2,1,0:T(8,128)(2,1)S(1)} copy-done((bf16[1,384,1536]{2,1,0:T(8,128)(2,1)S(1)}, bf16[1,384,1536]{2,1,0:T(8,128)(2,1)}, u32[]{:S(2)}) %copy-start.3) | copy-done | bytes 1179672
  13.4 0.5 %stage.1 = (bf16[384,1536]{1,0:T(8,128)(2,1)S(1)}, bf16[384,1536]{1,0:T(8,128)(2,1)S(1)}) custom-call(bf16[384,1536]{1,0:T(8,128)(2,1)S(1)} %bitcast.15, bf16[384,1536]{1,0:T(8,128)(2,1)S(1)} %bitcast.16), custom_call_target="tpu_custom_call" | custom-call | bytes 4718592 | tf_op jit(solution)/shard_map/stage/pallas_call | solution.py:247
  13.9 1.7 %all-to-all-done.recv_ref.refs_0_ = bf16[8,16,384]{2,1,0:T(8,128)(2,1)S(1)} async-done(((bf16[8,16,384]{2,1,0:T(8,128)(2,1)}), bf16[8,16,384]{2,1,0:T(8,128)(2,1)S(1)}, u32[]{:S(2)}, u32[]{:S(2)}) %all-to-all-start) | async-done | bytes 98336 | tf_op jit(solution)/shard_map/all_to_all | solution.py:77
  15.6 0.0 copy-start
  15.6 0.0 copy-start.1
  15.6 0.0 copy-start.5
  15.6 1.9 %expert.1 = bf16[8,16,384]{2,1,0:T(8,128)(2,1)} custom-call(bf16[8,16,384]{2,1,0:T(8,128)(2,1)S(1)} %all-to-all-done.recv_ref.refs_0_, bf16[384,1536]{1,0:T(8,128)(2,1)S(1)} %get-tuple-element.14.win_ref.refs_4_, bf16[384,1536]{1,0:T(8,128)(2,1)S(1)} %get-tuple-element.15.wout_ref.refs_5_), custom_call_target="tpu_custom_call" | custom-call | tf_op jit(solution)/shard_map/expert/pallas_call | solution.py:260
  17.5 4.4 %all-to-all-start.1 = ((bf16[8,16,384]{2,1,0:T(8,128)(2,1)}), bf16[8,16,384]{2,1,0:T(8,128)(2,1)S(1)}, u32[]{:S(2)}, u32[]{:S(2)}) async-start(bf16[8,16,384]{2,1,0:T(8,128)(2,1)} %expert.1), calls=%async_computation.1 | async-start | bytes 196608 | tf_op jit(solution)/shard_map/all_to_all | solution.py:77
  21.9 0.0 collective-permute-start.2
  21.9 1.5 %collective-permute-start.1 = (bf16[8,16,384]{2,1,0:T(8,128)(2,1)S(1)}, bf16[8,16,384]{2,1,0:T(8,128)(2,1)S(1)}, u32[]{:S(2)}, u32[]{:S(2)}) collective-permute-start(bf16[8,16,384]{2,1,0:T(8,128)(2,1)S(1)} %all-to-all-done.recv_ref.refs_0_), channel_id=1, source_target_pairs={{0,2},{1,3},{2,0},{3,1},{4,6},{5,7},{6,4},{7,5},{8,10},{9,11},{10,... | collective-permute-start | bytes 294920 | tf_op jit(solution)/shard_map/ppermute | solution.py:271
  23.5 0.3 collective-permute-start
  23.8 2.9 %all-to-all-done.1.back_ref = bf16[8,16,384]{2,1,0:T(8,128)(2,1)S(1)} async-done(((bf16[8,16,384]{2,1,0:T(8,128)(2,1)}), bf16[8,16,384]{2,1,0:T(8,128)(2,1)S(1)}, u32[]{:S(2)}, u32[]{:S(2)}) %all-to-all-start.1) | async-done | bytes 98336 | tf_op jit(solution)/shard_map/all_to_all | solution.py:77
  26.7 0.0 copy-done
  26.7 0.0 copy-done.1
  26.7 0.0 copy-done.5
  26.7 0.8 %logits.1 = (bf16[32,8,96]{2,1,0:T(8,128)(2,1)S(1)}, bf16[8,512]{1,0:T(8,128)(2,1)S(1)}) custom-call(bf16[8,16,384]{2,1,0:T(8,128)(2,1)S(1)} %all-to-all-done.1.back_ref, bf16[512,384]{1,0:T(8,128)(2,1)S(1)} %bitcast.11, bf16[8,384]{1,0:T(8,128)(2,1)S(1)} %bitcast.18, bf16[512,384]{1,0:T(8,128)(2,1)S(1)} %bitcast.14), custom_call_target="tpu_custom_call" | custom-call | tf_op jit(solution)/shard_map/logits/pallas_call | solution.py:277
  27.5 0.0 copy-start.4
  27.5 0.6 %copy-done.4 = bf16[32,8,96]{2,1,0:T(8,128)(2,1)} copy-done((bf16[32,8,96]{2,1,0:T(8,128)(2,1)}, bf16[32,8,96]{2,1,0:T(8,128)(2,1)S(1)}, u32[]{:S(2)}) %copy-start.4) | copy-done | bytes 49176
  28.1 3.7 %all-to-all-start.2 = ((bf16[32,8,96]{2,1,0:T(8,128)(2,1)}), bf16[32,8,96]{2,1,0:T(8,128)(2,1)S(1)}, u32[]{:S(2)}, u32[]{:S(2)}) async-start(bf16[32,8,96]{2,1,0:T(8,128)(2,1)} %copy-done.4), calls=%async_computation.2 | async-start | bytes 131072 | tf_op jit(solution)/shard_map/all_to_all | solution.py:77
  31.8 1.5 %tokens.1 = bf16[512,384]{1,0:T(8,128)(2,1)} custom-call(bf16[8,16,384]{2,1,0:T(8,128)(2,1)S(1)} %all-to-all-done.1.back_ref, bf16[512,384]{1,0:T(8,128)(2,1)S(1)} %bitcast.12, bf16[8,384]{1,0:T(8,128)(2,1)S(1)} %bitcast.19, bf16[8,512]{1,0:T(8,128)(2,1)S(1)} %get-tuple-element.17.logit_ref), custom_call_target="tpu_custom_call" | custom-call | tf_op jit(solution)/shard_map/tokens/pallas_call | solution.py:293
  33.3 0.0 collective-permute-done.2.refs_3_
  33.3 0.0 collective-permute-done.1.refs_2_
  33.3 0.0 collective-permute-done.refs_1_
  33.3 3.8 %weights.1 = (f32[96,1536]{1,0:T(8,128)}, f32[96,1536]{1,0:T(8,128)}) custom-call(s32[1]{0:T(128)} %bitcast.6.share_ref, bf16[8,16,384]{2,1,0:T(8,128)(2,1)S(1)} %all-to-all-done.recv_ref.refs_0_, bf16[8,16,384]{2,1,0:T(8,128)(2,1)} %collective-permute-done.refs_1_, bf16[8,16,384]{2,1,0:T(8,128)(2,1)S(1)} %collective-permute-done.1.refs_2_, ...), custom_call_target="tpu_custom_call" | custom-call | tf_op jit(solution)/shard_map/weights/pallas_call | solution.py:303
  37.1 2.2 %all-to-all-done.2 = bf16[32,8,96]{2,1,0:T(8,128)(2,1)S(1)} async-done(((bf16[32,8,96]{2,1,0:T(8,128)(2,1)}), bf16[32,8,96]{2,1,0:T(8,128)(2,1)S(1)}, u32[]{:S(2)}, u32[]{:S(2)}) %all-to-all-start.2) | async-done | bytes 49184 | tf_op jit(solution)/shard_map/all_to_all | solution.py:77
  39.4 0.6 %convert_reduce_fusion = f32[8,96]{1,0:T(8,128)} fusion(bf16[32,8,96]{2,1,0:T(8,128)(2,1)S(1)} %all-to-all-done.2), kind=kLoop, calls=%fused_computation | loop fusion | flops 48384 | bytes 52224 | tf_op jit(solution)/shard_map/reduce_sum | solution.py:333
Async XLA Ops:
  3.0 12.6 %all-to-all-start = ((bf16[8,16,384]{2,1,0:T(8,128)(2,1)}), bf16[8,16,384]{2,1,0:T(8,128)(2,1)S(1)}, u32[]{:S(2)}, u32[]{:S(2)}) async-start(bf16[8,16,384]{2,1,0:T(8,128)(2,1)} %slots.1), calls=%async_computation | async-start | bytes 196608 | tf_op jit(solution)/shard_map/all_to_all | solution.py:77
  10.8 1.3 %copy-start.2 = (bf16[1,384,1536]{2,1,0:T(8,128)(2,1)S(1)}, bf16[1,384,1536]{2,1,0:T(8,128)(2,1)}, u32[]{:S(2)}) copy-start(bf16[1,384,1536]{2,1,0:T(8,128)(2,1)} %param.7) | copy-start | bytes 3538948
  12.1 1.3 %copy-start.3 = (bf16[1,384,1536]{2,1,0:T(8,128)(2,1)S(1)}, bf16[1,384,1536]{2,1,0:T(8,128)(2,1)}, u32[]{:S(2)}) copy-start(bf16[1,384,1536]{2,1,0:T(8,128)(2,1)} %param.8) | copy-start | bytes 3538948
  15.6 11.1 %copy-start = (bf16[8,64,384]{2,1,0:T(8,128)(2,1)S(1)}, bf16[8,64,384]{2,1,0:T(8,128)(2,1)}, u32[]{:S(2)}) copy-start(bf16[8,64,384]{2,1,0:T(8,128)(2,1)} %param.5) | copy-start | bytes 1179652
  15.6 11.1 %copy-start.1 = (bf16[8,64,384]{2,1,0:T(8,128)(2,1)S(1)}, bf16[8,64,384]{2,1,0:T(8,128)(2,1)}, u32[]{:S(2)}) copy-start(bf16[8,64,384]{2,1,0:T(8,128)(2,1)} %param.9) | copy-start | bytes 1179652
  15.6 11.1 %copy-start.5 = (bf16[384,8]{0,1:T(8,128)(2,1)S(1)}, bf16[384,8]{0,1:T(8,128)(2,1)}, u32[]{:S(2)}) copy-start(bf16[384,8]{0,1:T(8,128)(2,1)} %param.6) | copy-start | bytes 18436
  17.5 9.1 %all-to-all-start.1 = ((bf16[8,16,384]{2,1,0:T(8,128)(2,1)}), bf16[8,16,384]{2,1,0:T(8,128)(2,1)S(1)}, u32[]{:S(2)}, u32[]{:S(2)}) async-start(bf16[8,16,384]{2,1,0:T(8,128)(2,1)} %expert.1), calls=%async_computation.1 | async-start | bytes 196608 | tf_op jit(solution)/shard_map/all_to_all | solution.py:77
  21.9 11.4 %collective-permute-start.2 = (bf16[8,16,384]{2,1,0:T(8,128)(2,1)S(1)}, bf16[8,16,384]{2,1,0:T(8,128)(2,1)S(1)}, u32[]{:S(2)}, u32[]{:S(2)}) collective-permute-start(bf16[8,16,384]{2,1,0:T(8,128)(2,1)S(1)} %all-to-all-done.recv_ref.refs_0_), channel_id=1, source_target_pairs={{0,3},{1,2},{2,1},{3,0},{4,7},{5,6},{6,5},{7,4},{8,11},{9,10},{10,... | collective-permute-start | bytes 294920 | tf_op jit(solution)/shard_map/ppermute | solution.py:271
  21.9 11.4 %collective-permute-start.1 = (bf16[8,16,384]{2,1,0:T(8,128)(2,1)S(1)}, bf16[8,16,384]{2,1,0:T(8,128)(2,1)S(1)}, u32[]{:S(2)}, u32[]{:S(2)}) collective-permute-start(bf16[8,16,384]{2,1,0:T(8,128)(2,1)S(1)} %all-to-all-done.recv_ref.refs_0_), channel_id=1, source_target_pairs={{0,2},{1,3},{2,0},{3,1},{4,6},{5,7},{6,4},{7,5},{8,10},{9,11},{10,... | collective-permute-start | bytes 294920 | tf_op jit(solution)/shard_map/ppermute | solution.py:271
  23.5 9.9 %collective-permute-start = (bf16[8,16,384]{2,1,0:T(8,128)(2,1)S(1)}, bf16[8,16,384]{2,1,0:T(8,128)(2,1)}, u32[]{:S(2)}, u32[]{:S(2)}) collective-permute-start(bf16[8,16,384]{2,1,0:T(8,128)(2,1)S(1)} %all-to-all-done.recv_ref.refs_0_), channel_id=1, source_target_pairs={{0,1},{1,0},{2,3},{3,2},{4,5},{5,4},{6,7},{7,6},{8,9},{9,8},{10,11... | collective-permute-start | bytes 294920 | tf_op jit(solution)/shard_map/ppermute | solution.py:271
  27.5 0.6 %copy-start.4 = (bf16[32,8,96]{2,1,0:T(8,128)(2,1)}, bf16[32,8,96]{2,1,0:T(8,128)(2,1)S(1)}, u32[]{:S(2)}) copy-start(bf16[32,8,96]{2,1,0:T(8,128)(2,1)S(1)} %get-tuple-element.23) | copy-start | bytes 147460
  28.1 11.3 %all-to-all-start.2 = ((bf16[32,8,96]{2,1,0:T(8,128)(2,1)}), bf16[32,8,96]{2,1,0:T(8,128)(2,1)S(1)}, u32[]{:S(2)}, u32[]{:S(2)}) async-start(bf16[32,8,96]{2,1,0:T(8,128)(2,1)} %copy-done.4), calls=%async_computation.2 | async-start | bytes 131072 | tf_op jit(solution)/shard_map/all_to_all | solution.py:77

commit v19 on v17

--- a/solution.py
+++ b/solution.py
@@ -127,11 +127,16 @@
     back_ref[...] = pair_rows(out, back, recv_ref.shape[0])
 
 
+def soft_kernel(images, tokens_ref, router_ref, block_ref, combine_ref):
+    block_ref[...], combine_ref[...], _ = softmaxes(router_ref[...], tokens_ref[...], images)
+
+
 def logits_kernel(
-    images, share_order, back_ref, tokens_ref, router_ref, grad_ref, send_ref, logit_ref
+    images, share_order, back_ref, tokens_ref, block_ref, combine_ref, grad_ref, send_ref, logit_ref
 ):
     tokens = tokens_ref[...]
-    dispatch, combine, mask = softmaxes(router_ref[...], tokens, images)
+    dispatch, combine = block_ref[...], combine_ref[...]
+    mask = own_image(combine.shape[0], images, tokens.shape[0])
     slot_out, slot_in_grad = split_rows(in_expert_order(back_ref))
     disp = dot(slot_in_grad, tokens, 1, 1)
     comb = fold_rows(jnp.where(mask, dot(slot_out, grad_ref[...], 1, 1), 0.0), images)
@@ -149,9 +154,9 @@
             send_ref[device] = piece
 
 
-def tokens_kernel(images, back_ref, tokens_ref, router_ref, logit_ref, out_ref):
+def tokens_kernel(back_ref, block_ref, router_ref, logit_ref, out_ref):
     router = router_ref[...]
-    dispatch, _, _ = softmaxes(router, tokens_ref[...], images)
+    dispatch = block_ref[...]
     _, slot_in_grad = split_rows(in_expert_order(back_ref))
     out = dot(dispatch.astype(BF16), slot_in_grad, 0, 0)
     out = out + dot(logit_ref[...], router, 0, 0)
@@ -265,6 +270,14 @@
     )(recv, w_in2, w_out2)
     recv, back = lax.optimization_barrier((recv, back))
     slots_back = exchange(back, "expert", experts_order)
+    soft_rows, _ = lax.optimization_barrier((router_rows, back))
+    block, combine = pl.pallas_call(
+        functools.partial(soft_kernel, images),
+        in_specs=[in_vmem] * 2,
+        out_shape=(struct((experts * images, columns), F32), struct((experts, columns), F32)),
+        compiler_params=params,
+        name="soft",
+    )(tokens2, soft_rows)
     few = shares * owners * images <= 512
     if few:
         spread = [recv] + [
@@ -276,14 +289,14 @@
 
     router_send, logit_grad = pl.pallas_call(
         functools.partial(logits_kernel, images, share_order),
-        in_specs=[in_vmem] * 4,
+        in_specs=[in_vmem] * 5,
         out_shape=(
             struct((owners * shares, experts, row_count), BF16),
             struct((experts, columns), BF16),
         ),
         compiler_params=params,
         name="logits",
-    )(slots_back, tokens2, router_rows, grad2)
+    )(slots_back, tokens2, block, combine, grad2)
     share, router_send = lax.optimization_barrier((lax.axis_index("dp").reshape(1), router_send))
     router_parts = exchange(
         router_send,
@@ -291,11 +304,11 @@
         [owner * shares + i for owner in experts_order for i in share_order],
     )
     tokens_grad = pl.pallas_call(
-        functools.partial(tokens_kernel, images),
+        tokens_kernel,
         out_shape=struct((columns, width), BF16),
         compiler_params=params,
         name="tokens",
-    )(slots_back, tokens2, router_rows, logit_grad)
+    )(slots_back, block, router_rows, logit_grad)
     in_smem = pl.BlockSpec(memory_space=pltpu.SMEM)
     out_shape = [struct((row_count, hidden), F32)] * 2
     if few:

time: 40.1 us -> 40 us (level)
  local copies, waits for them, and re-layouts: 3.18 us -> 2.55 us
  Pallas kernels: 10.9 us -> 11.5 us
    unnamed x12 -> x10, local copies, waits for them, and re-layouts: 3.18 us -> 2.55 us
    pallas_call x1, Pallas kernels: 0.77 us -> 1.26 us  [on_device(): pl.pallas_call(functools.partial(logits_kernel, images, share_order), in_...]
    pallas_call x1 -> x2, Pallas kernels: 1.55 us -> 1.56 us  [the longest x1 1.15 us: on_device(): pl.pallas_call(tokens_kernel, out_shape=struct((columns, width), BF16), c...]
  transfers between devices with their start and end apart: 6 -> 6, of which waited for: 3 -> 3; matrix products, arithmetic and copies ran while one was open for 0% -> 0% of each run, Pallas kernels for 17% -> 18%
where the time goes in v19:
time: 40 us; the launch traced here: 39.5 us
  starting transfers between devices  17.7 us (44%)
  Pallas kernels  11.5 us (29%)
  waiting for transfers between devices  6.37 us (16%)
  local copies, waits for them, and re-layouts  2.55 us (6%)
  between operations  0.68 us (2%)
  other arithmetic  0.63 us (2%)
    all_to_all x3, starting transfers between devices, exchange(): lax.all_to_all(chunks, axis, split_axis=0, concat_axis=0, tiled=True, axi...  15.9 us
    all_to_all x3, waiting for transfers between devices, exchange(): lax.all_to_all(chunks, axis, split_axis=0, concat_axis=0, tiled=True, axi...  6.37 us
    pallas_call x1, Pallas kernels, on_device(): pl.pallas_call(functools.partial(weights_kernel, shares), in_specs=[in_sm...  3.89 us
    unnamed x10, local copies, waits for them, and re-layouts  2.55 us
    pallas_call x1, Pallas kernels, on_device(): pl.pallas_call(functools.partial(slots_kernel, images), in_specs=[in_vmem...  2.4 us
    pallas_call x1, Pallas kernels, on_device(): pl.pallas_call(functools.partial(expert_kernel, step=hidden), out_shape=s...  1.93 us
    ppermute x3, starting transfers between devices, on_device(): lax.ppermute(recv, 'dp', [(i, i ^ k) for i in range(shares)])  1.86 us
    pallas_call x1, Pallas kernels, on_device(): pl.pallas_call(functools.partial(logits_kernel, images, share_order), in_...  1.26 us
  transfers between devices with their start and end apart: 6, of which 3 were waited for; matrix products, arithmetic and copies ran while one was open for 0% of the time, Pallas kernels for 18%

profile of v19, /device:TPU:0, one launch (start us, length us, event | category | flops | bytes accessed | tf_op | source)
XLA Modules:
  0.0 39.5 jit_solution(11840842650291996062)
XLA Ops:
  0.6 2.4 %slots.1 = bf16[8,16,384]{2,1,0:T(8,128)(2,1)} custom-call(bf16[512,384]{1,0:T(8,128)(2,1)} %bitcast.10, bf16[8,384]{1,0:T(8,128)(2,1)} %bitcast.17, bf16[512,384]{1,0:T(8,128)(2,1)} %bitcast.13), custom_call_target="tpu_custom_call" | custom-call | tf_op jit(solution)/shard_map/slots/pallas_call | solution.py:245
  3.0 7.8 %all-to-all-start = ((bf16[8,16,384]{2,1,0:T(8,128)(2,1)}), bf16[8,16,384]{2,1,0:T(8,128)(2,1)S(1)}, u32[]{:S(2)}, u32[]{:S(2)}) async-start(bf16[8,16,384]{2,1,0:T(8,128)(2,1)} %slots.1), calls=%async_computation | async-start | bytes 196608 | tf_op jit(solution)/shard_map/all_to_all | solution.py:77
  10.8 0.0 copy-start.2
  10.8 1.3 %copy-done.2 = bf16[1,384,1536]{2,1,0:T(8,128)(2,1)S(1)} copy-done((bf16[1,384,1536]{2,1,0:T(8,128)(2,1)S(1)}, bf16[1,384,1536]{2,1,0:T(8,128)(2,1)}, u32[]{:S(2)}) %copy-start.2) | copy-done | bytes 1179672
  12.1 0.0 copy-start.3
  12.1 1.3 %copy-done.3 = bf16[1,384,1536]{2,1,0:T(8,128)(2,1)S(1)} copy-done((bf16[1,384,1536]{2,1,0:T(8,128)(2,1)S(1)}, bf16[1,384,1536]{2,1,0:T(8,128)(2,1)}, u32[]{:S(2)}) %copy-start.3) | copy-done | bytes 1179672
  13.4 0.5 %stage.1 = (bf16[384,1536]{1,0:T(8,128)(2,1)S(1)}, bf16[384,1536]{1,0:T(8,128)(2,1)S(1)}) custom-call(bf16[384,1536]{1,0:T(8,128)(2,1)S(1)} %bitcast.15, bf16[384,1536]{1,0:T(8,128)(2,1)S(1)} %bitcast.16), custom_call_target="tpu_custom_call" | custom-call | bytes 4718592 | tf_op jit(solution)/shard_map/stage/pallas_call | solution.py:252
  13.9 1.7 %all-to-all-done.recv_ref.refs_0_ = bf16[8,16,384]{2,1,0:T(8,128)(2,1)S(1)} async-done(((bf16[8,16,384]{2,1,0:T(8,128)(2,1)}), bf16[8,16,384]{2,1,0:T(8,128)(2,1)S(1)}, u32[]{:S(2)}, u32[]{:S(2)}) %all-to-all-start) | async-done | bytes 98336 | tf_op jit(solution)/shard_map/all_to_all | solution.py:77
  15.6 0.0 copy-start
  15.6 0.0 copy-start.4
  15.6 0.0 copy-start.1
  15.6 1.9 %expert.1 = bf16[8,16,384]{2,1,0:T(8,128)(2,1)} custom-call(bf16[8,16,384]{2,1,0:T(8,128)(2,1)S(1)} %all-to-all-done.recv_ref.refs_0_, bf16[384,1536]{1,0:T(8,128)(2,1)S(1)} %get-tuple-element.17.win_ref.refs_4_, bf16[384,1536]{1,0:T(8,128)(2,1)S(1)} %get-tuple-element.18.wout_ref.refs_5_), custom_call_target="tpu_custom_call" | custom-call | tf_op jit(solution)/shard_map/expert/pallas_call | solution.py:265
  17.5 4.4 %all-to-all-start.1 = ((bf16[8,16,384]{2,1,0:T(8,128)(2,1)}), bf16[8,16,384]{2,1,0:T(8,128)(2,1)S(1)}, u32[]{:S(2)}, u32[]{:S(2)}) async-start(bf16[8,16,384]{2,1,0:T(8,128)(2,1)} %expert.1), calls=%async_computation.1 | async-start | bytes 196608 | tf_op jit(solution)/shard_map/all_to_all | solution.py:77
  21.9 0.0 collective-permute-start.2
  21.9 1.6 %collective-permute-start.1 = (bf16[8,16,384]{2,1,0:T(8,128)(2,1)S(1)}, bf16[8,16,384]{2,1,0:T(8,128)(2,1)}, u32[]{:S(2)}, u32[]{:S(2)}) collective-permute-start(bf16[8,16,384]{2,1,0:T(8,128)(2,1)S(1)} %all-to-all-done.recv_ref.refs_0_), channel_id=1, source_target_pairs={{0,2},{1,3},{2,0},{3,1},{4,6},{5,7},{6,4},{7,5},{8,10},{9,11},{10,... | collective-permute-start | bytes 294920 | tf_op jit(solution)/shard_map/ppermute | solution.py:284
  23.5 0.3 collective-permute-start
  23.8 0.0 copy-done
  23.8 0.0 copy-done.4
  23.8 0.4 %soft.1 = (f32[64,512]{1,0:T(8,128)S(1)}, f32[8,512]{1,0:T(8,128)S(1)}) custom-call(bf16[512,384]{1,0:T(8,128)(2,1)S(1)} %bitcast.11, bf16[8,384]{1,0:T(8,128)(2,1)S(1)} %bitcast.18), custom_call_target="tpu_custom_call" | custom-call | tf_op jit(solution)/shard_map/soft/pallas_call | solution.py:274
  24.2 2.5 %all-to-all-done.1.back_ref = bf16[8,16,384]{2,1,0:T(8,128)(2,1)S(1)} async-done(((bf16[8,16,384]{2,1,0:T(8,128)(2,1)}), bf16[8,16,384]{2,1,0:T(8,128)(2,1)S(1)}, u32[]{:S(2)}, u32[]{:S(2)}) %all-to-all-start.1) | async-done | bytes 98336 | tf_op jit(solution)/shard_map/all_to_all | solution.py:77
  26.7 0.0 copy-done.1
  26.7 1.3 %logits.1 = (bf16[32,8,96]{2,1,0:T(8,128)(2,1)}, bf16[8,512]{1,0:T(8,128)(2,1)S(1)}) custom-call(bf16[8,16,384]{2,1,0:T(8,128)(2,1)S(1)} %all-to-all-done.1.back_ref, bf16[512,384]{1,0:T(8,128)(2,1)S(1)} %bitcast.12, f32[64,512]{1,0:T(8,128)S(1)} %get-tuple-element.21.block_ref, f32[8,512]{1,0:T(8,128)S(1)} %get-tuple-element.22.combine_ref, ...), custom_call_target="tpu_custom_call" | custom-call | tf_op jit(solution)/shard_map/logits/pallas_call | solution.py:290
  27.9 3.7 %all-to-all-start.2 = ((bf16[32,8,96]{2,1,0:T(8,128)(2,1)}), bf16[32,8,96]{2,1,0:T(8,128)(2,1)S(1)}, u32[]{:S(2)}, u32[]{:S(2)}) async-start(bf16[32,8,96]{2,1,0:T(8,128)(2,1)} %get-tuple-element.29), calls=%async_computation.2 | async-start | bytes 131072 | tf_op jit(solution)/shard_map/all_to_all | solution.py:77
  31.6 1.1 %tokens.1 = bf16[512,384]{1,0:T(8,128)(2,1)} custom-call(bf16[8,16,384]{2,1,0:T(8,128)(2,1)S(1)} %all-to-all-done.1.back_ref, f32[64,512]{1,0:T(8,128)S(1)} %get-tuple-element.21.block_ref, bf16[8,384]{1,0:T(8,128)(2,1)S(1)} %bitcast.19, bf16[8,512]{1,0:T(8,128)(2,1)S(1)} %get-tuple-element.23.logit_ref), custom_call_target="tpu_custom_call" | custom-call | tf_op jit(solution)/shard_map/tokens/pallas_call | solution.py:306
  32.8 0.0 collective-permute-done.2.refs_3_
  32.8 0.0 collective-permute-done.1.refs_2_
  32.8 0.0 collective-permute-done.refs_1_
  32.8 3.9 %weights.1 = (f32[96,1536]{1,0:T(8,128)}, f32[96,1536]{1,0:T(8,128)}) custom-call(s32[1]{0:T(128)} %bitcast.6.share_ref, bf16[8,16,384]{2,1,0:T(8,128)(2,1)S(1)} %all-to-all-done.recv_ref.refs_0_, bf16[8,16,384]{2,1,0:T(8,128)(2,1)} %collective-permute-done.refs_1_, bf16[8,16,384]{2,1,0:T(8,128)(2,1)} %collective-permute-done.1.refs_2_, ...), custom_call_target="tpu_custom_call" | custom-call | tf_op jit(solution)/shard_map/weights/pallas_call | solution.py:316
  36.7 2.2 %all-to-all-done.2 = bf16[32,8,96]{2,1,0:T(8,128)(2,1)S(1)} async-done(((bf16[32,8,96]{2,1,0:T(8,128)(2,1)}), bf16[32,8,96]{2,1,0:T(8,128)(2,1)S(1)}, u32[]{:S(2)}, u32[]{:S(2)}) %all-to-all-start.2) | async-done | bytes 49184 | tf_op jit(solution)/shard_map/all_to_all | solution.py:77
  38.9 0.6 %convert_reduce_fusion = f32[8,96]{1,0:T(8,128)} fusion(bf16[32,8,96]{2,1,0:T(8,128)(2,1)S(1)} %all-to-all-done.2), kind=kLoop, calls=%fused_computation | loop fusion | flops 48384 | bytes 52224 | tf_op jit(solution)/shard_map/reduce_sum | solution.py:346
Async XLA Ops:
  3.0 12.6 %all-to-all-start = ((bf16[8,16,384]{2,1,0:T(8,128)(2,1)}), bf16[8,16,384]{2,1,0:T(8,128)(2,1)S(1)}, u32[]{:S(2)}, u32[]{:S(2)}) async-start(bf16[8,16,384]{2,1,0:T(8,128)(2,1)} %slots.1), calls=%async_computation | async-start | bytes 196608 | tf_op jit(solution)/shard_map/all_to_all | solution.py:77
  10.8 1.3 %copy-start.2 = (bf16[1,384,1536]{2,1,0:T(8,128)(2,1)S(1)}, bf16[1,384,1536]{2,1,0:T(8,128)(2,1)}, u32[]{:S(2)}) copy-start(bf16[1,384,1536]{2,1,0:T(8,128)(2,1)} %param.7) | copy-start | bytes 3538948
  12.1 1.3 %copy-start.3 = (bf16[1,384,1536]{2,1,0:T(8,128)(2,1)S(1)}, bf16[1,384,1536]{2,1,0:T(8,128)(2,1)}, u32[]{:S(2)}) copy-start(bf16[1,384,1536]{2,1,0:T(8,128)(2,1)} %param.8) | copy-start | bytes 3538948
  15.6 8.2 %copy-start = (bf16[8,64,384]{2,1,0:T(8,128)(2,1)S(1)}, bf16[8,64,384]{2,1,0:T(8,128)(2,1)}, u32[]{:S(2)}) copy-start(bf16[8,64,384]{2,1,0:T(8,128)(2,1)} %param.5) | copy-start | bytes 1179652
  15.6 8.2 %copy-start.4 = (bf16[384,8]{0,1:T(8,128)(2,1)S(1)}, bf16[384,8]{0,1:T(8,128)(2,1)}, u32[]{:S(2)}) copy-start(bf16[384,8]{0,1:T(8,128)(2,1)} %param.6) | copy-start | bytes 18436
  15.6 11.1 %copy-start.1 = (bf16[8,64,384]{2,1,0:T(8,128)(2,1)S(1)}, bf16[8,64,384]{2,1,0:T(8,128)(2,1)}, u32[]{:S(2)}) copy-start(bf16[8,64,384]{2,1,0:T(8,128)(2,1)} %param.9) | copy-start | bytes 1179652
  17.5 9.1 %all-to-all-start.1 = ((bf16[8,16,384]{2,1,0:T(8,128)(2,1)}), bf16[8,16,384]{2,1,0:T(8,128)(2,1)S(1)}, u32[]{:S(2)}, u32[]{:S(2)}) async-start(bf16[8,16,384]{2,1,0:T(8,128)(2,1)} %expert.1), calls=%async_computation.1 | async-start | bytes 196608 | tf_op jit(solution)/shard_map/all_to_all | solution.py:77
  21.9 10.9 %collective-permute-start.2 = (bf16[8,16,384]{2,1,0:T(8,128)(2,1)S(1)}, bf16[8,16,384]{2,1,0:T(8,128)(2,1)}, u32[]{:S(2)}, u32[]{:S(2)}) collective-permute-start(bf16[8,16,384]{2,1,0:T(8,128)(2,1)S(1)} %all-to-all-done.recv_ref.refs_0_), channel_id=1, source_target_pairs={{0,3},{1,2},{2,1},{3,0},{4,7},{5,6},{6,5},{7,4},{8,11},{9,10},{10,... | collective-permute-start | bytes 294920 | tf_op jit(solution)/shard_map/ppermute | solution.py:284
  21.9 10.9 %collective-permute-start.1 = (bf16[8,16,384]{2,1,0:T(8,128)(2,1)S(1)}, bf16[8,16,384]{2,1,0:T(8,128)(2,1)}, u32[]{:S(2)}, u32[]{:S(2)}) collective-permute-start(bf16[8,16,384]{2,1,0:T(8,128)(2,1)S(1)} %all-to-all-done.recv_ref.refs_0_), channel_id=1, source_target_pairs={{0,2},{1,3},{2,0},{3,1},{4,6},{5,7},{6,4},{7,5},{8,10},{9,11},{10,... | collective-permute-start | bytes 294920 | tf_op jit(solution)/shard_map/ppermute | solution.py:284
  23.5 9.3 %collective-permute-start = (bf16[8,16,384]{2,1,0:T(8,128)(2,1)S(1)}, bf16[8,16,384]{2,1,0:T(8,128)(2,1)}, u32[]{:S(2)}, u32[]{:S(2)}) collective-permute-start(bf16[8,16,384]{2,1,0:T(8,128)(2,1)S(1)} %all-to-all-done.recv_ref.refs_0_), channel_id=1, source_target_pairs={{0,1},{1,0},{2,3},{3,2},{4,5},{5,4},{6,7},{7,6},{8,9},{9,8},{10,11... | collective-permute-start | bytes 294920 | tf_op jit(solution)/shard_map/ppermute | solution.py:284
  27.9 10.9 %all-to-all-start.2 = ((bf16[32,8,96]{2,1,0:T(8,128)(2,1)}), bf16[32,8,96]{2,1,0:T(8,128)(2,1)S(1)}, u32[]{:S(2)}, u32[]{:S(2)}) async-start(bf16[32,8,96]{2,1,0:T(8,128)(2,1)} %get-tuple-element.29), calls=%async_computation.2 | async-start | bytes 131072 | tf_op jit(solution)/shard_map/all_to_all | solution.py:77
